TPU v7x, 128 devices: a whole 4x4x4 slice. The times are simulated.
128 devices in a mesh: ts: 32 (over z, x_lo, y), gz: 4 (over x_hi, core).
Axes of the slice: x: 4 (x_hi: 2, x_lo: 2; x = x_hi * 2 + x_lo), y: 4, z: 4, core: 2. Of those that a mesh axis runs over, the one named last changes fastest.
Arguments:
- eigvecs: bfloat16 [2, 3, 4, 32, 64, 32, 128], P(None, None, None, 'ts', 'gz'), may hold values from -0.25 to 0.25
- gauge_links: bfloat16 [3, 18, 4, 32, 64, 32], P(None, None, None, 'ts', 'gz'), may hold values from -3.5 to 3.5
- momenta: int32 [2, 3], replicated, may hold values from -2 to 2
- directions: int32 [3], replicated, may hold values from 0 to 2, each once
Outputs:
- elementals: float32 [128, 4, 2, 2, 384], P('ts', 'gz')
Inputs may be any that keep to these rules, and one draw needn't show every extreme that they name: Each of the three directions exactly once.
All inputs are finite; a program needn't handle non-finite values.
Results may differ from a plain program's by a relative error of at most 0.0045.
Values may be sent and summed in bfloat16 or wider, within the bound.
No kernel may reach another device: no remote copies, remote signals or barrier semaphores. Data moves between devices by JAX's collectives and lax.ppermute only.
A program may use at most 128 MiB of HBM per device.

v0:
```python
import math

import jax
import jax.numpy as jnp
from jax import lax
from jax.sharding import PartitionSpec as P


def from_behind(value, axis, steps):
    count = lax.axis_size(axis)
    pairs = [(source, (source + steps) % count) for source in range(count)]
    return lax.ppermute(value, axis, pairs)


def transport(link, vectors, adjoint):
    real_in = vectors[0]
    imag_in = vectors[1]
    real_out = []
    imag_out = []
    for a in range(3):
        real_sum = jnp.float32(0.0)
        imag_sum = jnp.float32(0.0)
        for b in range(3):
            if adjoint:
                entry = (b * 3 + a) * 2
                link_re = link[entry][..., None].astype(jnp.float32)
                link_im = -link[entry + 1][..., None].astype(jnp.float32)
            else:
                entry = (a * 3 + b) * 2
                link_re = link[entry][..., None].astype(jnp.float32)
                link_im = link[entry + 1][..., None].astype(jnp.float32)
            vec_re = real_in[b].astype(jnp.float32)
            vec_im = imag_in[b].astype(jnp.float32)
            real_sum = real_sum + link_re * vec_re - link_im * vec_im
            imag_sum = imag_sum + link_re * vec_im + link_im * vec_re
        real_out.append(real_sum)
        imag_out.append(imag_sum)
    return jnp.stack([jnp.stack(real_out), jnp.stack(imag_out)])


def fraction(component, coords, length):
    return jnp.mod(component[:, None] * coords[None, :], length).astype(jnp.float32) / length


def phase_angle(momenta, x_first, z_first, count_x, count_z, count_y, total_x, total_z, total_y):
    coord_x = x_first + jnp.arange(count_x, dtype=jnp.int32)
    coord_z = z_first + jnp.arange(count_z, dtype=jnp.int32)
    coord_y = jnp.arange(count_y, dtype=jnp.int32)
    frac_x = fraction(momenta[:, 0], coord_x, total_x)
    frac_y = fraction(momenta[:, 1], coord_y, total_y)
    frac_z = fraction(momenta[:, 2], coord_z, total_z)
    return (
        2.0
        * math.pi
        * (frac_x[:, :, None, None] + frac_y[:, None, None, :] + frac_z[:, None, :, None])
    )


def x_upper(values):
    plane = from_behind(values, "ts", -1)
    return jnp.concatenate([values[:, :, :, 1:], plane], axis=3)


def x_lower(values):
    plane = from_behind(values, "ts", 1)
    return jnp.concatenate([plane, values[:, :, :, :-1]], axis=3)


def y_upper(values):
    return jnp.roll(values, -1, axis=5)


def y_lower(values):
    return jnp.roll(values, 1, axis=5)


def elementals_block(vectors, links, momenta, directions, z_up, z_down, z_first, total_z):
    uppers = (x_upper, y_upper, z_up)
    lowers = (x_lower, y_lower, z_down)
    shifted = []
    for k in range(3):
        backward = transport(links[k], vectors, True).astype(jnp.bfloat16)
        ahead = uppers[k](vectors)
        behind = lowers[k](backward)
        shifted.append(
            (0.5 * (transport(links[k], ahead, False) - behind.astype(jnp.float32))).astype(
                jnp.bfloat16
            )
        )
    stacked = jnp.stack(shifted)
    count_x = vectors.shape[3]
    count_z = vectors.shape[4]
    count_y = vectors.shape[5]
    x_first = lax.axis_index("ts") * count_x
    angle = phase_angle(
        momenta,
        x_first,
        z_first,
        count_x,
        count_z,
        count_y,
        count_x * lax.axis_size("ts"),
        total_z,
        count_y,
    )
    cosine = jnp.cos(angle)[:, None, None, :, :, :, None]
    sine = jnp.sin(angle)[:, None, None, :, :, :, None]
    real_in = vectors[0].astype(jnp.float32)
    imag_in = vectors[1].astype(jnp.float32)
    phased = jnp.stack(
        [cosine * real_in - sine * imag_in, sine * real_in + cosine * imag_in], axis=1
    ).astype(jnp.bfloat16)
    products = jnp.einsum(
        "pqctxzyi,ksctxzyj->itpqksj", phased, stacked, preferred_element_type=jnp.float32
    )
    real_part = products[:, :, :, 0, :, 0] + products[:, :, :, 1, :, 1]
    imag_part = products[:, :, :, 0, :, 1] - products[:, :, :, 1, :, 0]
    joined = jnp.stack([real_part, imag_part], axis=3)
    chosen = jnp.take(joined, directions, axis=4)
    nev = vectors.shape[6]
    return chosen.reshape(nev, vectors.shape[2], momenta.shape[0], 2, directions.shape[0] * nev)


def shards(eigvecs, gauge_links, momenta, directions):

    def z_plane_upper(values):
        plane = from_behind(values[:, :, :, :, :1], "gz", -1)
        return jnp.concatenate([values[:, :, :, :, 1:], plane], axis=4)

    def z_plane_lower(values):
        plane = from_behind(values[:, :, :, :, -1:], "gz", 1)
        return jnp.concatenate([plane, values[:, :, :, :, :-1]], axis=4)

    planes = eigvecs.shape[4]
    block_terms = elementals_block(
        eigvecs,
        gauge_links,
        momenta,
        directions,
        z_plane_upper,
        z_plane_lower,
        lax.axis_index("gz") * planes,
        planes * lax.axis_size("gz"),
    )
    totals = lax.psum(block_terms, "gz")
    partial_rows = lax.dynamic_slice_in_dim(totals, lax.axis_index("gz"), 1, 1)
    return lax.psum_scatter(partial_rows, "ts", scatter_dimension=0, tiled=True)


def solution(mesh):
    in_specs = (
        P(None, None, None, "ts", "gz", None, None),
        P(None, None, None, "ts", "gz", None),
        P(),
        P(),
    )
    out_specs = P("ts", "gz", None, None, None)
    return jax.shard_map(shards, mesh=mesh, in_specs=in_specs, out_specs=out_specs, check_vma=False)
```

profile of v0, /device:TPU:0, one launch (start us, length us, event | category | flops | bytes accessed | tf_op | source)
XLA Modules:
  0.0 521.7 jit_solution(4573191188997885710)
XLA Ops:
  6.5 7.5 %collective-permute-start = (bf16[2,3,4,1,16,32,128]{6,5,4,2,3,1,0:T(8,128)(2,1)}, bf16[2,3,4,1,16,32,128]{6,5,4,2,3,1,0:T(8,128)(2,1)}, u32[]{:S(2)}, u32[]{:S(2)}) collective-permute-start(bf16[2,3,4,1,16,32,128]{6,5,4,2,3,1,0:T(8,128)(2,1)} %bitcast.690), channel_id=1, source_target_pairs={{0,124},{4,0},{8,4},{12,8},{16,12},{20,16},{24,20},{28,24},{32,28}... | collective-permute-start | bytes 9437192 | tf_op jit(solution)/shard_map/ppermute | solution.py:12
  22.2 3.9 fusion.198
  33.2 2.0 fusion.126
  41.4 3.5 bitcast_convert_fusion.1
  44.9 2.1 fusion.162
  51.4 2.4 fusion.13
  54.2 3.5 slice.710
  61.0 4.1 fusion.53
  67.4 3.6 fusion.58
  75.7 3.4 subtract_convert_fusion
  81.2 4.7 collective-permute-done.2
  86.0 3.1 fusion.83
  91.2 3.8 fusion.88
  95.9 3.2 fusion.9
  99.1 3.9 fusion.33
  103.1 3.9 fusion.28
  107.1 3.9 fusion.23
  111.0 3.5 maximum_bitcast_fusion.4
  115.8 8.7 %fusion.15 = f32[128,4,2,2,3,2,128]{0,6,3,2,5,4,1:T(8,128)S(1)} fusion(bf16[2,1,3,4,16,32,128]{6,5,4,2,1,0,3:T(8,128)(2,1)} %get-tuple-element.22, bf16[2,1,3,4,16,32,128]{6,5,4,2,1,0,3:T(8,128)(2,1)S(1)} %get-tuple-element.21, bf16[1,2,3,4,1,16,32,128]{7,6,5,2,1,0,3,4:T(8,128)(2,1)} %fusion.9, bf16[1,2,3,4,1,16,32,128]{7,6,5,2,1,0,3,4:T(8,128)(2,1)S(1)} %fusion.11, ...), kind=kOutput, calls=%fused_computation.154 | convolution fusion | flops 4880596992 | bytes 28311552 | tf_op jit(solution)/shard_map/pqctxzyi,ksctxzyj->itpqksj/dot_general | solution.py:113
  125.1 2.4 gather_fusion
  127.5 2.2 copy.75
  129.8 2.0 bitcast_select_fusion
  131.9 71.7 %all-reduce.4.cloned.1.call-done = f32[128,4,2,2,384]{0,4,3,2,1:T(8,128)} async-done(((f32[128,4,2,2,384]{0,4,3,2,1:T(8,128)}), f32[128,4,2,2,384]{0,4,3,2,1:T(8,128)}) %all-reduce.4.cloned.1.call-update) | async-done | bytes 3145744 | tf_op jit(solution)/shard_map/psum | solution.py:145
  207.2 306.3 %all-reduce.6.cloned.1.call-done = f32[128,1,2,2,384]{4,3,2,1,0:T(2,128)} async-done(((f32[128,1,2,2,384]{4,3,2,1,0:T(2,128)}), f32[128,1,2,2,384]{4,3,2,1,0:T(2,128)}) %all-reduce.6.cloned.1.call-update) | async-done | bytes 786448
  (241 shorter events, 46.9 us)
Async XLA Ops:
  6.5 197.0 %all-reduce.4.cloned.1.call-start = ((), (), s32[]{:S(2)}) async-start(), calls=%async_computation | async-start | bytes 6291456 | tf_op jit(solution)/shard_map/psum | solution.py:145
  6.5 92.5 %collective-permute-start = (bf16[2,3,4,1,16,32,128]{6,5,4,2,3,1,0:T(8,128)(2,1)}, bf16[2,3,4,1,16,32,128]{6,5,4,2,3,1,0:T(8,128)(2,1)}, u32[]{:S(2)}, u32[]{:S(2)}) collective-permute-start(bf16[2,3,4,1,16,32,128]{6,5,4,2,3,1,0:T(8,128)(2,1)} %bitcast.690), channel_id=1, source_target_pairs={{0,124},{4,0},{8,4},{12,8},{16,12},{20,16},{24,20},{28,24},{32,28}... | collective-permute-start | bytes 9437192 | tf_op jit(solution)/shard_map/ppermute | solution.py:12
  15.7 70.2 %collective-permute-start.2 = (bf16[2,3,4,1,1,32,128]{6,5,4,2,3,1,0:T(8,128)(2,1)}, bf16[2,3,4,1,1,32,128]{6,5,4,2,3,1,0:T(8,128)(2,1)}, u32[]{:S(2)}, u32[]{:S(2)}) collective-permute-start(bf16[2,3,4,1,1,32,128]{6,5,4,2,3,1,0:T(8,128)(2,1)} %slice.723), channel_id=1, source_target_pairs={{0,3},{1,0},{2,1},{3,2},{4,7},{5,4},{6,5},{7,6},{8,11},{9,8},{10,9... | collective-permute-start | bytes 589832 | tf_op jit(solution)/shard_map/ppermute | solution.py:12
  19.3 25.6 %copy-start.54 = (f32[4,16,32]{2,1,0:T(8,128)}, f32[4,16,32]{2,1,0:T(8,128)S(1)}, u32[]{:S(2)}) copy-start(f32[4,16,32]{2,1,0:T(8,128)S(1)} %get-tuple-element.79) | copy-start | bytes 24580
  21.1 12.1 %copy-start.21 = (f32[4,16,32]{2,1,0:T(8,128)}, f32[4,16,32]{2,1,0:T(8,128)S(1)}, u32[]{:S(2)}) copy-start(f32[4,16,32]{2,1,0:T(8,128)S(1)} %get-tuple-element.110) | copy-start | bytes 24580
  21.1 12.1 %copy-start.27 = (f32[4,16,32]{2,1,0:T(8,128)}, f32[4,16,32]{2,1,0:T(8,128)S(1)}, u32[]{:S(2)}) copy-start(f32[4,16,32]{2,1,0:T(8,128)S(1)} %get-tuple-element.105) | copy-start | bytes 24580
  21.1 14.1 %copy-start.23 = (f32[4,16,32]{2,1,0:T(8,128)}, f32[4,16,32]{2,1,0:T(8,128)S(1)}, u32[]{:S(2)}) copy-start(f32[4,16,32]{2,1,0:T(8,128)S(1)} %get-tuple-element.111) | copy-start | bytes 24580
  21.1 14.1 %copy-start.29 = (f32[4,16,32]{2,1,0:T(8,128)}, f32[4,16,32]{2,1,0:T(8,128)S(1)}, u32[]{:S(2)}) copy-start(f32[4,16,32]{2,1,0:T(8,128)S(1)} %get-tuple-element.107) | copy-start | bytes 24580
  21.1 14.1 %copy-start.33 = (f32[4,16,32]{2,1,0:T(8,128)}, f32[4,16,32]{2,1,0:T(8,128)S(1)}, u32[]{:S(2)}) copy-start(f32[4,16,32]{2,1,0:T(8,128)S(1)} %get-tuple-element.101) | copy-start | bytes 24580
  21.1 16.1 %copy-start.25 = (f32[4,16,32]{2,1,0:T(8,128)}, f32[4,16,32]{2,1,0:T(8,128)S(1)}, u32[]{:S(2)}) copy-start(f32[4,16,32]{2,1,0:T(8,128)S(1)} %get-tuple-element.112) | copy-start | bytes 24580
  21.1 16.1 %copy-start.31 = (f32[4,16,32]{2,1,0:T(8,128)}, f32[4,16,32]{2,1,0:T(8,128)S(1)}, u32[]{:S(2)}) copy-start(f32[4,16,32]{2,1,0:T(8,128)S(1)} %get-tuple-element.109) | copy-start | bytes 24580
  21.1 16.1 %copy-start.35 = (f32[4,16,32]{2,1,0:T(8,128)}, f32[4,16,32]{2,1,0:T(8,128)S(1)}, u32[]{:S(2)}) copy-start(f32[4,16,32]{2,1,0:T(8,128)S(1)} %get-tuple-element.103) | copy-start | bytes 24580
  31.2 64.6 %collective-permute-start.3 = (bf16[2,3,4,1,1,32,128]{6,5,1,2,0,4,3:T(8,128)(2,1)}, bf16[2,3,4,1,1,32,128]{6,5,1,2,0,4,3:T(8,128)(2,1)}, u32[]{:S(2)}, u32[]{:S(2)}) collective-permute-start(bf16[2,3,4,1,1,32,128]{6,5,1,2,0,4,3:T(8,128)(2,1)} %maximum_bitcast_fusion.20), channel_id=1, source_target_pairs={{0,1},{1,2},{2,3},{3,0},{4,5},{5,6},{6,7},{7,4},{8,9},{9,10},{10,1... | collective-permute-start | bytes 589832 | tf_op jit(solution)/shard_map/ppermute | solution.py:12
  33.1 11.9 %copy-start.15 = (f32[4,16,32]{2,1,0:T(8,128)}, f32[4,16,32]{2,1,0:T(8,128)S(1)}, u32[]{:S(2)}) copy-start(f32[4,16,32]{2,1,0:T(8,128)S(1)} %get-tuple-element.92) | copy-start | bytes 24580
  33.1 11.9 %copy-start.60 = (f32[4,16,32]{2,1,0:T(8,128)}, f32[4,16,32]{2,1,0:T(8,128)S(1)}, u32[]{:S(2)}) copy-start(f32[4,16,32]{2,1,0:T(8,128)S(1)} %get-tuple-element.86) | copy-start | bytes 24580
  33.1 14.0 %copy-start.17 = (f32[4,16,32]{2,1,0:T(8,128)}, f32[4,16,32]{2,1,0:T(8,128)S(1)}, u32[]{:S(2)}) copy-start(f32[4,16,32]{2,1,0:T(8,128)S(1)} %get-tuple-element.94) | copy-start | bytes 24580
  33.1 14.0 %copy-start.56 = (f32[4,16,32]{2,1,0:T(8,128)}, f32[4,16,32]{2,1,0:T(8,128)S(1)}, u32[]{:S(2)}) copy-start(f32[4,16,32]{2,1,0:T(8,128)S(1)} %get-tuple-element.82) | copy-start | bytes 24580
  33.1 14.0 %copy-start.62 = (f32[4,16,32]{2,1,0:T(8,128)}, f32[4,16,32]{2,1,0:T(8,128)S(1)}, u32[]{:S(2)}) copy-start(f32[4,16,32]{2,1,0:T(8,128)S(1)} %get-tuple-element.88) | copy-start | bytes 24580
  33.1 16.0 %copy-start.19 = (f32[4,16,32]{2,1,0:T(8,128)}, f32[4,16,32]{2,1,0:T(8,128)S(1)}, u32[]{:S(2)}) copy-start(f32[4,16,32]{2,1,0:T(8,128)S(1)} %get-tuple-element.96) | copy-start | bytes 24580
  33.1 16.0 %copy-start.58 = (f32[4,16,32]{2,1,0:T(8,128)}, f32[4,16,32]{2,1,0:T(8,128)S(1)}, u32[]{:S(2)}) copy-start(f32[4,16,32]{2,1,0:T(8,128)S(1)} %get-tuple-element.84) | copy-start | bytes 24580
  33.1 16.0 %copy-start.64 = (f32[4,16,32]{2,1,0:T(8,128)}, f32[4,16,32]{2,1,0:T(8,128)S(1)}, u32[]{:S(2)}) copy-start(f32[4,16,32]{2,1,0:T(8,128)S(1)} %get-tuple-element.90) | copy-start | bytes 24580
  41.4 74.4 %collective-permute-start.1 = (bf16[2,3,4,1,16,32,128]{6,5,4,1,2,3,0:T(8,128)(2,1)}, bf16[2,3,4,1,16,32,128]{6,5,4,1,2,3,0:T(8,128)(2,1)}, u32[]{:S(2)}, u32[]{:S(2)}) collective-permute-start(bf16[2,3,4,1,16,32,128]{6,5,4,1,2,3,0:T(8,128)(2,1)} %pad_maximum_fusion.2), channel_id=1, source_target_pairs={{0,4},{4,8},{8,12},{12,16},{16,20},{20,24},{24,28},{28,32},{32,36}... | collective-permute-start | bytes 9437192 | tf_op jit(solution)/shard_map/ppermute | solution.py:12
  131.8 74.1 %copy-start.92 = (u32[128]{0:T(128)S(1)}, u32[128]{0:T(128)}, u32[]{:S(2)}) copy-start(u32[128]{0:T(128)} %constant.82) | copy-start | bytes 1540
  131.8 381.7 %all-reduce.6.cloned.1.call-start = ((), (), s32[]{:S(2)}) async-start(), calls=%async_computation.1 | async-start | bytes 1572864
  (75 other events, 292.2 us)
Sparse Core Ops, SparseCore 0:
  132.0 71.5 all-reduce.3
  206.1 307.4 all-reduce.5
where the time goes:
time: 523 us; the launch traced here: 522 us
  waiting for transfers between devices  384 us (73%)
  other arithmetic  83.5 us (16%)
  local copies, waits for them, and re-layouts  20.5 us (4%)
  between operations  15.6 us (3%)
  starting transfers between devices  9.44 us (2%)
  matrix products  8.68 us (2%)
    unnamed x3, waiting for transfers between devices  306 us
    psum x1, waiting for transfers between devices, shards(): totals = lax.psum(block_terms, 'gz')  71.7 us
    sub x7, other arithmetic, transport(): real_sum = real_sum + link_re * vec_re - link_im * vec_im  26.2 us
    another operation x10, other arithmetic  23.1 us
  transfers between devices with their start and end apart: 6, of which 4 were waited for; matrix products, arithmetic and copies ran while one was open for 17% of the time, Pallas kernels for 0%

commit v1 on v0

v1 whole, which is shorter than its diff:
```python
import functools
import math

import jax
import jax.numpy as jnp
from jax import lax
from jax.experimental import pallas as pl
from jax.experimental.pallas import tpu as pltpu
from jax.sharding import PartitionSpec as P

BF16 = jnp.bfloat16
F32 = jnp.float32


def link_rows(entries, adjoint, width):
    rows = []
    for r in range(2):
        for a in range(3):
            pieces = []
            for q in range(2):
                for b in range(3):
                    first = ((b * 3 + a) if adjoint else (a * 3 + b)) * 2
                    if r == q:
                        pieces.append(entries[first])
                    elif (q == 1) == adjoint:
                        pieces.append(entries[first + 1])
                    else:
                        pieces.append(-entries[first + 1])
            lanes = sum(piece.shape[1] for piece in pieces)
            if lanes < width:
                pieces.append(jnp.zeros((pieces[0].shape[0], width - lanes), F32))
            rows.append(jnp.concatenate(pieces, axis=1))
    return rows


def site_masks(count_y, lanes):
    row = lax.broadcasted_iota(jnp.int32, (count_y, lanes), 0)
    lane = lax.broadcasted_iota(jnp.int32, (count_y, lanes), 1) % count_y
    same = jnp.where(lane == row, 1.0, 0.0).astype(BF16)
    above = jnp.where(lane == (row + 1) % count_y, 1.0, 0.0).astype(BF16)
    below = jnp.where(lane == (row + count_y - 1) % count_y, 1.0, 0.0).astype(BF16)
    return same, above, below


def spread(rows_ref, kind, row, mask):
    count_y, lanes = mask.shape
    blocks = []
    for ra in range(6):
        line = rows_ref[kind, ra, pl.ds(row, 1), :lanes]
        blocks.append(jnp.broadcast_to(line, (count_y, lanes)).astype(BF16) * mask)
    return jnp.concatenate(blocks, axis=0)


def write_phased(vectors, table_ref, x_at, out_ref, first):
    _, _, count_z, count_y, nev = vectors.shape
    planes = nev // count_y
    for b in range(3):
        for block in range(count_z // planes):
            sites = pl.ds(block * planes, planes)
            real = vectors[0, b, sites].reshape(nev, nev).T.astype(F32)
            imag = vectors[1, b, sites].reshape(nev, nev).T.astype(F32)
            lanes = pl.ds(first + b * count_z * count_y + block * nev, nev)
            for p in range(2):
                cosine = table_ref[x_at, 2 * p : 2 * p + 1, block * nev : (block + 1) * nev]
                sine = table_ref[x_at, 2 * p + 1 : 2 * p + 2, block * nev : (block + 1) * nev]
                out_ref[pl.ds(2 * p * nev, nev), lanes] = (cosine * real - sine * imag).astype(BF16)
                out_ref[pl.ds((2 * p + 1) * nev, nev), lanes] = (sine * real + cosine * imag).astype(BF16)


def put_displaced(out_ref, where, z, terms, count_y, nev):
    for r in range(2):
        for a in range(3):
            rows = terms[(r * 3 + a) * count_y : (r * 3 + a + 1) * count_y]
            out_ref[where, a, z, :, r * nev : (r + 1) * nev] = rows.astype(BF16)


def combine(products, nev):
    parts = []
    for p in range(2):
        rr = products[2 * p * nev : (2 * p + 1) * nev, :nev]
        ri = products[2 * p * nev : (2 * p + 1) * nev, nev:]
        ir = products[(2 * p + 1) * nev : (2 * p + 2) * nev, :nev]
        ii = products[(2 * p + 1) * nev : (2 * p + 2) * nev, nev:]
        parts.append(rr + ii)
        parts.append(ri - ir)
    return parts


def yz_kernel(v_ref, up_ref, down_ref, link_ref, below_ref, table_ref, out_ref, rows, padded, phased, moved):
    count_z, count_y, nev = v_ref.shape[3:]
    lanes = 6 * count_y
    same, above, below = site_masks(count_y, lanes)
    padded[:, :, 0] = down_ref[:, :, 0, 0]
    padded[:, :, pl.ds(1, count_z)] = v_ref[:, :, 0]
    padded[:, :, count_z + 1] = up_ref[:, :, 0, 0]

    wide = rows.shape[3]
    lane = lax.broadcasted_iota(jnp.int32, (count_z, wide), 1) % count_y
    link_y = [0.5 * link_ref[1, e, 0].astype(F32) for e in range(18)]
    for ra, line in enumerate(link_rows(link_y, False, wide)):
        shifted = jnp.where(lane == 0, pltpu.roll(line, wide - (count_y - 1), 1), pltpu.roll(line, 1, 1))
        rows[0, ra, pl.ds(8, count_z), :] = shifted
    for ra, line in enumerate(link_rows(link_y, True, wide)):
        rows[1, ra, pl.ds(8, count_z), :] = -line
    link_z = [0.5 * link_ref[2, e, 0].astype(F32) for e in range(18)]
    for ra, line in enumerate(link_rows(link_z, False, wide)):
        rows[2, ra, pl.ds(8, count_z), :] = line
    for ra, line in enumerate(link_rows(link_z, True, wide)):
        rows[3, ra, pl.ds(8, count_z), :] = -line
    link_b = [0.5 * below_ref[e, 0].astype(F32) for e in range(18)]
    for ra, line in enumerate(link_rows(link_b, True, wide)):
        rows[3, ra, 7:8, :] = -line

    write_phased(v_ref.at[:, :, 0], table_ref, 0, phased, 0)

    def plane(z, carry):
        here = padded[:, :, z + 1].reshape(lanes, nev)
        ahead = padded[:, :, z + 2].reshape(lanes, nev)
        behind = padded[:, :, z].reshape(lanes, nev)
        in_y = spread(rows, 0, z + 8, above) + spread(rows, 1, z + 8, below)
        terms = jnp.dot(in_y, here, preferred_element_type=F32)
        put_displaced(moved, 0, z, terms, count_y, nev)
        terms = jnp.dot(spread(rows, 2, z + 8, same), ahead, preferred_element_type=F32)
        terms += jnp.dot(spread(rows, 3, z + 7, same), behind, preferred_element_type=F32)
        put_displaced(moved, 1, z, terms, count_y, nev)
        return carry

    lax.fori_loop(0, count_z, plane, 0, unroll=2)
    for k in range(2):
        products = jnp.dot(
            phased[...], moved[k].reshape(-1, 2 * nev), preferred_element_type=F32
        )
        for at, part in enumerate(combine(products, nev)):
            out_ref[0, :, (2 * at + k) * nev : (2 * at + k + 1) * nev] = part.astype(BF16)


def x_terms(low, high, link, table_ref, x_low, x_high, out_ref, at_t, rows, phased, moved):
    count_z, count_y, nev = low.shape[2:]
    lanes = 6 * count_y
    same = site_masks(count_y, lanes)[0]
    entries = [0.5 * link[e].astype(F32) for e in range(18)]
    for ra, line in enumerate(link_rows(entries, False, lanes)):
        rows[0, ra] = line
    for ra, line in enumerate(link_rows(entries, True, lanes)):
        rows[1, ra] = -line
    sites = 3 * count_z * count_y
    write_phased(low, table_ref, x_low, phased, 0)
    write_phased(high, table_ref, x_high, phased, sites)

    def plane(z, carry):
        terms = jnp.dot(spread(rows, 0, z, same), high[:, :, z].reshape(lanes, nev), preferred_element_type=F32)
        put_displaced(moved, 0, z, terms, count_y, nev)
        terms = jnp.dot(spread(rows, 1, z, same), low[:, :, z].reshape(lanes, nev), preferred_element_type=F32)
        put_displaced(moved, 1, z, terms, count_y, nev)
        return carry

    lax.fori_loop(0, count_z, plane, 0, unroll=2)
    products = jnp.dot(phased[...], moved[...].reshape(-1, 2 * nev), preferred_element_type=F32)
    for at, part in enumerate(combine(products, nev)):
        out_ref[at_t, :, at * nev : (at + 1) * nev] = part.astype(BF16)


def x_kernel(own_up, recv_up, own_down, recv_down, link_up, link_down, table_ref, out_ref, rows, phased, moved):
    x_terms(
        own_up.at[:, :, 0], recv_up.at[:, :, 0], link_up.at[0, :, 0], table_ref, 0, 1, out_ref, 0, rows, phased, moved
    )
    x_terms(
        recv_down.at[:, :, 0], own_down.at[:, :, 0], link_down.at[:, 0], table_ref, 2, 0, out_ref, 1, rows, phased, moved
    )


def fraction(component, coords, length):
    return jnp.mod(component[:, None] * coords[None, :], length).astype(F32) / length


def phase_table(momenta, coord_x, coord_z, coord_y, total_x, total_z, total_y):
    frac_x = fraction(momenta[:, 0], coord_x, total_x)
    frac_y = fraction(momenta[:, 1], coord_y, total_y)
    frac_z = fraction(momenta[:, 2], coord_z, total_z)
    angle = 2.0 * math.pi * (
        (frac_x[:, :, None, None] + frac_y[:, None, None, :]) + frac_z[:, None, :, None]
    )
    table = jnp.stack([jnp.cos(angle), jnp.sin(angle)], axis=1)
    table = jnp.transpose(table, (2, 0, 1, 3, 4))
    return table.reshape(coord_x.shape[0], 4, coord_z.shape[0] * coord_y.shape[0])


def shift(value, axis, steps):
    count = lax.axis_size(axis)
    return lax.ppermute(value, axis, [(source, (source + steps) % count) for source in range(count)])


def shards(eigvecs, gauge_links, momenta, directions):
    _, _, count_t, _, count_z, count_y, nev = eigvecs.shape
    vectors = eigvecs.reshape(2, 3, count_t, count_z, count_y, nev)
    links = gauge_links.reshape(3, 18, count_t, count_z, count_y)
    size_x, size_g = lax.axis_size("ts"), lax.axis_size("gz")
    half = count_t // 2

    recv_up, recv_down = [], []
    for c in range(half):
        recv_up.append(shift(vectors[:, :, c : c + 1], "ts", -1))
        recv_down.append(shift(vectors[:, :, half + c : half + c + 1], "ts", 1))
    link_down = shift(links[0, :, half:], "ts", 1)
    up = shift(vectors[:, :, :, :1], "gz", -1)
    down = shift(vectors[:, :, :, -1:], "gz", 1)
    below = shift(links[2, :, :, -1:], "gz", 1)

    x = lax.axis_index("ts")
    coord_x = x + jnp.array([0, 1, -1], jnp.int32)
    coord_z = lax.axis_index("gz") * count_z + jnp.arange(count_z, dtype=jnp.int32)
    coord_y = jnp.arange(count_y, dtype=jnp.int32)
    table = phase_table(momenta, coord_x, coord_z, coord_y, size_x, count_z * size_g, count_y)

    sites = 3 * count_z * count_y
    table_spec = pl.BlockSpec(table.shape, lambda t: (0, 0, 0))
    yz = pl.pallas_call(
        yz_kernel,
        grid=(count_t,),
        in_specs=[
            pl.BlockSpec((2, 3, 1, count_z, count_y, nev), lambda t: (0, 0, t, 0, 0, 0)),
            pl.BlockSpec((2, 3, 1, 1, count_y, nev), lambda t: (0, 0, t, 0, 0, 0)),
            pl.BlockSpec((2, 3, 1, 1, count_y, nev), lambda t: (0, 0, t, 0, 0, 0)),
            pl.BlockSpec((3, 18, 1, count_z, count_y), lambda t: (0, 0, t, 0, 0)),
            pl.BlockSpec((18, 1, 1, count_y), lambda t: (0, t, 0, 0)),
            table_spec,
        ],
        out_specs=pl.BlockSpec((1, nev, 8 * nev), lambda t: (t, 0, 0)),
        out_shape=jax.ShapeDtypeStruct((count_t, nev, 8 * nev), BF16),
        scratch_shapes=[
            pltpu.VMEM((4, 6, count_z + 8, 256), F32),
            pltpu.VMEM((2, 3, count_z + 2, count_y, nev), BF16),
            pltpu.VMEM((4 * nev, sites), BF16),
            pltpu.VMEM((2, 3, count_z, count_y, 2 * nev), BF16),
        ],
        compiler_params=pltpu.CompilerParams(vmem_limit_bytes=40 * 1024 * 1024),
        cost_estimate=pl.CostEstimate(flops=12_000_000_000, bytes_accessed=6_000_000, transcendentals=0),
        name="yz_terms",
    )(vectors, up, down, links, below, table)

    x_parts = []
    for c in range(half):
        x_parts.append(
            pl.pallas_call(
                x_kernel,
                grid=(1,),
                in_specs=[
                    pl.BlockSpec((2, 3, 1, count_z, count_y, nev), functools.partial(lambda c, i: (0, 0, c, 0, 0, 0), c)),
                    pl.BlockSpec((2, 3, 1, count_z, count_y, nev), lambda i: (0, 0, 0, 0, 0, 0)),
                    pl.BlockSpec((2, 3, 1, count_z, count_y, nev), functools.partial(lambda c, i: (0, 0, c, 0, 0, 0), half + c)),
                    pl.BlockSpec((2, 3, 1, count_z, count_y, nev), lambda i: (0, 0, 0, 0, 0, 0)),
                    pl.BlockSpec((1, 18, 1, count_z, count_y), functools.partial(lambda c, i: (0, 0, c, 0, 0), c)),
                    pl.BlockSpec((18, 1, count_z, count_y), functools.partial(lambda c, i: (0, c, 0, 0), c)),
                    table_spec,
                ],
                out_specs=pl.BlockSpec((2, nev, 4 * nev), lambda i: (0, 0, 0)),
                out_shape=jax.ShapeDtypeStruct((2, nev, 4 * nev), BF16),
                scratch_shapes=[
                    pltpu.VMEM((2, 6, count_z, 6 * count_y), F32),
                    pltpu.VMEM((4 * nev, 2 * sites), BF16),
                    pltpu.VMEM((2, 3, count_z, count_y, 2 * nev), BF16),
                ],
                compiler_params=pltpu.CompilerParams(vmem_limit_bytes=40 * 1024 * 1024),
                cost_estimate=pl.CostEstimate(flops=6_000_000_000, bytes_accessed=4_000_000, transcendentals=0),
                name="x_terms",
            )(vectors, recv_up[c], vectors, recv_down[c], links, link_down, table)
        )
    order = [part[0] for part in x_parts] + [part[1] for part in x_parts]
    in_x = jnp.stack(order)

    group = nev // size_x
    both = jnp.concatenate([in_x, yz], axis=2).reshape(count_t, size_x, group, 12 * nev)
    sent = jnp.transpose(both, (1, 0, 2, 3)).reshape(size_x * count_t, group, 12 * nev)
    got = lax.all_to_all(sent, ("ts", "gz"), 0, 0, tiled=True)
    total = jnp.sum(got.astype(F32), axis=0)
    in_x = total[:, : 4 * nev].reshape(group, 4, 1, nev)
    in_yz = total[:, 4 * nev :].reshape(group, 4, 2, nev)
    chosen = jnp.take(jnp.concatenate([in_x, in_yz], axis=2), directions, axis=2)
    return chosen.reshape(group, 1, 2, 2, 3 * nev)


def solution(mesh):
    in_specs = (
        P(None, None, None, "ts", "gz", None, None),
        P(None, None, None, "ts", "gz", None),
        P(),
        P(),
    )
    out_specs = P("ts", "gz", None, None, None)
    return jax.shard_map(shards, mesh=mesh, in_specs=in_specs, out_specs=out_specs, check_vma=False)
```

time: 523 us -> 117 us (0.22)
  waiting for transfers between devices: 384 us -> 41 us
  other arithmetic: 83.5 us -> 2.02 us
  Pallas kernels: 0 us -> 36.1 us
  starting transfers between devices: 9.44 us -> 24.8 us
  between operations: 15.6 us -> 0.24 us
  matrix products: 8.68 us -> 0 us
  local copies, waits for them, and re-layouts: 20.5 us -> 12 us
    unnamed x3 -> x0, waiting for transfers between devices: 306 us -> none
    psum x1 -> x0, waiting for transfers between devices: 71.7 us -> none  [shards(): totals = lax.psum(block_terms, 'gz')]
    pallas_call x0 -> x3, Pallas kernels: none -> 36.1 us  [the longest x1 18.5 us: shards(): pl.pallas_call(yz_kernel, grid=(count_t,), in_specs=[pl.BlockSpec((2, 3,...]
    another operation x18 -> x0, other arithmetic: 31.5 us -> none
    sub x8 -> x0, other arithmetic: 26.4 us -> none  [the longest x7 26.2 us: transport(): real_sum = real_sum + link_re * vec_re - link_im * vec_im]
    all_to_all x0 -> x1, waiting for transfers between devices: none -> 24.2 us  [shards(): got = lax.all_to_all(sent, ('ts', 'gz'), 0, 0, tiled=True)]
    ppermute x4 -> x8, waiting for transfers between devices: 6 us -> 16.9 us  [shift(): lax.ppermute(value, axis, [(source, (source + steps) % count) for source...]
    convert_element_type x5 -> x0, other arithmetic: 9.12 us -> none  [the longest x2 5.01 us: elementals_block(): (0.5 * (transport(links[k], ahead, False) - behind.astype(jnp.float32)))....]
  transfers between devices with their start and end apart: 6 -> 9, of which waited for: 4 -> 2; matrix products, arithmetic and copies ran while one was open for 17% -> 4% of each run, Pallas kernels for 0% -> 24%
where the time goes in v1:
time: 117 us; the launch traced here: 116 us
  waiting for transfers between devices  41 us (35%)
  Pallas kernels  36.1 us (31%)
  starting transfers between devices  24.8 us (21%)
  local copies, waits for them, and re-layouts  12 us (10%)
  other arithmetic  2.02 us (2%)
    all_to_all x1, waiting for transfers between devices, shards(): got = lax.all_to_all(sent, ('ts', 'gz'), 0, 0, tiled=True)  24.2 us
    pallas_call x1, Pallas kernels, shards(): pl.pallas_call(yz_kernel, grid=(count_t,), in_specs=[pl.BlockSpec((2, 3,...  18.5 us
    pallas_call x2, Pallas kernels, shards(): pl.pallas_call(x_kernel, grid=(1,), in_specs=[pl.BlockSpec((2, 3, 1, coun...  17.6 us
    ppermute x8, waiting for transfers between devices, shift(): lax.ppermute(value, axis, [(source, (source + steps) % count) for source...  16.9 us
    ppermute x8, starting transfers between devices, shift(): lax.ppermute(value, axis, [(source, (source + steps) % count) for source...  16.7 us
    all_to_all x1, starting transfers between devices, shards(): got = lax.all_to_all(sent, ('ts', 'gz'), 0, 0, tiled=True)  8.17 us
    slice x1, local copies, waits for them, and re-layouts, shards(): recv_down.append(shift(vectors[:, :, half + c:half + c + 1], 'ts', 1))  4.04 us
    reshape x2, local copies, waits for them, and re-layouts, shards(): jnp.concatenate([in_x, yz], axis=2)  2.39 us
  transfers between devices with their start and end apart: 9, of which 2 were waited for; matrix products, arithmetic and copies ran while one was open for 4% of the time, Pallas kernels for 24%

profile of v1, /device:TPU:0, one launch (start us, length us, event | category | flops | bytes accessed | tf_op | source)
XLA Modules:
  0.0 116.3 jit_solution(2882140427858240873)
XLA Ops:
  0.0 4.0 %fusion.11 = (bf16[2,3,1,16,32,128]{5,4,3,2,1,0:T(8,128)(2,1)}, bf16[2,3,1,16,32,128]{5,4,3,2,1,0:T(8,128)(2,1)}, bf16[2,3,1,16,32,128]{5,4,3,2,1,0:T(8,128)(2,1)}, bf16[2,3,1,16,32,128]{5,4,3,2,1,0:T(8,128)(2,1)}) fusion(bf16[2,3,4,16,32,128]{5,4,3,2,1,0:T(8,128)(2,1)} %bitcast.18), kind=kLoop, calls=%fused_computation.42 | loop fusion | bytes 6291456 | tf_op jit(solution)/shard_map/slice | solution.py:203
  4.0 7.5 %collective-permute-start = (bf16[2,3,1,16,32,128]{5,4,3,2,1,0:T(8,128)(2,1)}, bf16[2,3,1,16,32,128]{5,4,3,2,1,0:T(8,128)(2,1)}, u32[]{:S(2)}, u32[]{:S(2)}) collective-permute-start(bf16[2,3,1,16,32,128]{5,4,3,2,1,0:T(8,128)(2,1)} %get-tuple-element.11), channel_id=1, source_target_pairs={{0,124},{4,0},{8,4},{12,8},{16,12},{20,16},{24,20},{28,24},{32,28}... | collective-permute-start | bytes 2359304 | tf_op jit(solution)/shard_map/ppermute | solution.py:190
  11.6 0.8 fusion.12
  12.4 1.9 %collective-permute-start.5 = (bf16[2,3,4,1,32,128]{5,4,3,2,1,0:T(8,128)(2,1)}, bf16[2,3,4,1,32,128]{5,4,3,2,1,0:T(8,128)(2,1)S(1)}, u32[]{:S(2)}, u32[]{:S(2)}) collective-permute-start(bf16[2,3,4,1,32,128]{5,4,3,2,1,0:T(8,128)(2,1)} %get-tuple-element.13), channel_id=1, source_target_pairs={{0,3},{1,0},{2,1},{3,2},{4,7},{5,4},{6,5},{7,6},{8,11},{9,8},{10,9... | collective-permute-start | bytes 589832 | tf_op jit(solution)/shard_map/ppermute | solution.py:190
  14.3 1.0 slice_bitcast_fusion.1
  15.2 1.0 collective-permute-start.7
  16.3 1.6 %slice_bitcast_fusion = bf16[18,2,16,32]{3,2,1,0:T(8,128)(2,1)} fusion(bf16[3,18,4,16,32]{4,3,2,1,0:T(8,128)(2,1)} %bitcast.26), kind=kLoop, calls=%fused_computation.3 | loop fusion | bytes 73728 | tf_op jit(solution)/shard_map/squeeze | solution.py:204
  17.8 0.2 slice_reduce_fusion.2
  18.4 0.3 fusion.1
  18.7 0.1 reshape.174.table_ref
  18.8 16.8 %collective-permute-done.7.below_ref = bf16[18,4,1,32]{3,2,1,0:T(2,128)(2,1)S(1)} collective-permute-done((bf16[18,4,1,32]{3,2,1,0:T(2,128)(2,1)S(1)}, bf16[18,4,1,32]{3,2,1,0:T(2,128)(2,1)S(1)}, u32[]{:S(2)}, u32[]{:S(2)}) %collective-permute-start.7) | collective-permute-done | bytes 4640 | tf_op jit(solution)/shard_map/ppermute | solution.py:190
  35.6 6.2 %collective-permute-start.3 = (bf16[2,3,1,16,32,128]{5,4,3,2,1,0:T(8,128)(2,1)}, bf16[2,3,1,16,32,128]{5,4,3,2,1,0:T(8,128)(2,1)S(1)}, u32[]{:S(2)}, u32[]{:S(2)}) collective-permute-start(bf16[2,3,1,16,32,128]{5,4,3,2,1,0:T(8,128)(2,1)} %get-tuple-element.10), channel_id=1, source_target_pairs={{0,124},{4,0},{8,4},{12,8},{16,12},{20,16},{24,20},{28,24},{32,28}... | collective-permute-start | bytes 2359304 | tf_op jit(solution)/shard_map/ppermute | solution.py:190
  41.9 1.2 %copy-done.1 = bf16[3,18,4,1,16,32]{5,4,3,2,1,0:T(8,128)(2,1)S(1)} copy-done((bf16[3,18,4,1,16,32]{5,4,3,2,1,0:T(8,128)(2,1)S(1)}, bf16[3,18,4,1,16,32]{5,4,3,2,1,0:T(8,128)(2,1)}, u32[]{:S(2)}) %copy-start.1) | copy-done | bytes 221208
  43.0 18.5 %yz_terms.1 = bf16[4,128,1024]{2,1,0:T(8,128)(2,1)S(1)} custom-call(bf16[2,3,4,16,32,128]{5,4,3,2,1,0:T(8,128)(2,1)S(1)} %bitcast.20, bf16[2,3,4,1,32,128]{5,4,3,2,1,0:T(8,128)(2,1)S(1)} %collective-permute-done.5.up_ref, bf16[2,3,4,1,32,128]{5,4,3,2,1,0:T(8,128)(2,1)} %collective-permute-done.6.down_ref, bf16[3,18,4,16,32]{4,3,2,1,0:T(8,128)(2,1)S(1)} %bitcast.27, ...), custom_call_target="tpu_custom_call" | custom-call | flops 12000000000 | bytes 6000000 | tf_op jit(solution)/shard_map/yz_terms/pallas_call | solution.py:217
  61.6 9.5 %x_terms.2 = bf16[2,128,512]{2,1,0:T(8,128)(2,1)S(1)} custom-call(bf16[2,3,4,16,32,128]{5,4,3,2,1,0:T(8,128)(2,1)S(1)} %bitcast.21, bf16[2,3,1,16,32,128]{5,4,3,2,1,0:T(8,128)(2,1)} %collective-permute-done.recv_up, bf16[2,3,4,16,32,128]{5,4,3,2,1,0:T(8,128)(2,1)S(1)} %bitcast.22, bf16[2,3,1,16,32,128]{5,4,3,2,1,0:T(8,128)(2,1)} %collective-permute-done.1.recv_down, ...), custom_call_target="tpu_custom_call" | custom-call | flops 6000000000 | bytes 4000000 | tf_op jit(solution)/shard_map/x_terms/pallas_call | solution.py:244
  71.1 8.1 %x_terms.3 = bf16[2,128,512]{2,1,0:T(8,128)(2,1)S(1)} custom-call(bf16[2,3,4,16,32,128]{5,4,3,2,1,0:T(8,128)(2,1)S(1)} %bitcast.23, bf16[2,3,1,16,32,128]{5,4,3,2,1,0:T(8,128)(2,1)S(1)} %collective-permute-done.3.recv_up, bf16[2,3,4,16,32,128]{5,4,3,2,1,0:T(8,128)(2,1)S(1)} %bitcast.24, ...), custom_call_target="tpu_custom_call" | custom-call | flops 6000000000 | bytes 4000000 | tf_op jit(solution)/shard_map/x_terms/pallas_call | solution.py:244
  79.3 0.1 pad_maximum_fusion
  79.4 0.4 reshape.175
  79.8 2.0 %copy.18 = bf16[4,32,4,1536]{3,2,0,1:T(4,128)(2,1)} copy(bf16[4,32,4,1536]{3,2,1,0:T(4,128)(2,1)S(1)} %reshape.175) | data formatting | bytes 3145728 | tf_op jit(solution)/shard_map/reshape | solution.py:272
  81.8 8.2 %all-to-all-start = ((bf16[128,4,1536]{2,1,0:T(4,128)(2,1)}), bf16[128,4,1536]{2,1,0:T(4,128)(2,1)S(1)}, u32[]{:S(2)}, u32[]{:S(2)}) async-start(bf16[128,4,1536]{2,1,0:T(4,128)(2,1)} %bitcast.7), calls=%async_computation | async-start | bytes 3145728 | tf_op jit(solution)/shard_map/all_to_all | solution.py:274
  90.1 24.2 %all-to-all-done = bf16[128,4,1536]{2,1,0:T(4,128)(2,1)S(1)} async-done(((bf16[128,4,1536]{2,1,0:T(4,128)(2,1)}), bf16[128,4,1536]{2,1,0:T(4,128)(2,1)S(1)}, u32[]{:S(2)}, u32[]{:S(2)}) %all-to-all-start) | async-done | bytes 1572896 | tf_op jit(solution)/shard_map/all_to_all | solution.py:274
  114.3 0.7 convert_reduce_fusion
  115.0 0.6 gather_fusion
  115.7 0.6 select_bitcast_fusion
  (43 shorter events, 0.6 us)
Async XLA Ops:
  0.0 11.6 %copy-start = (bf16[2,3,4,1,16,32,128]{6,5,4,3,2,1,0:T(8,128)(2,1)S(1)}, bf16[2,3,4,1,16,32,128]{6,5,4,3,2,1,0:T(8,128)(2,1)}, u32[]{:S(2)}) copy-start(bf16[2,3,4,1,16,32,128]{6,5,4,3,2,1,0:T(8,128)(2,1)} %param.5) | copy-start | bytes 9437188
  0.0 17.8 %copy-start.3 = (s32[2,3]{1,0:T(2,128)S(1)}, s32[2,3]{1,0:T(2,128)}, u32[]{:S(2)}) copy-start(s32[2,3]{1,0:T(2,128)} %param.7) | copy-start | bytes 76
  0.0 18.1 %copy-start.5 = (s32[3]{0:T(128)S(1)}, s32[3]{0:T(128)}, u32[]{:S(2)}) copy-start(s32[3]{0:T(128)} %constant.77.clone) | copy-start | bytes 40
  4.0 57.5 %collective-permute-start = (bf16[2,3,1,16,32,128]{5,4,3,2,1,0:T(8,128)(2,1)}, bf16[2,3,1,16,32,128]{5,4,3,2,1,0:T(8,128)(2,1)}, u32[]{:S(2)}, u32[]{:S(2)}) collective-permute-start(bf16[2,3,1,16,32,128]{5,4,3,2,1,0:T(8,128)(2,1)} %get-tuple-element.11), channel_id=1, source_target_pairs={{0,124},{4,0},{8,4},{12,8},{16,12},{20,16},{24,20},{28,24},{32,28}... | collective-permute-start | bytes 2359304 | tf_op jit(solution)/shard_map/ppermute | solution.py:190
  11.6 50.0 %collective-permute-start.1 = (bf16[2,3,1,16,32,128]{5,4,3,2,1,0:T(8,128)(2,1)}, bf16[2,3,1,16,32,128]{5,4,3,2,1,0:T(8,128)(2,1)}, u32[]{:S(2)}, u32[]{:S(2)}) collective-permute-start(bf16[2,3,1,16,32,128]{5,4,3,2,1,0:T(8,128)(2,1)} %get-tuple-element.8), channel_id=1, source_target_pairs={{0,4},{4,8},{8,12},{12,16},{16,20},{20,24},{24,28},{28,32},{32,36}... | collective-permute-start | bytes 2359304 | tf_op jit(solution)/shard_map/ppermute | solution.py:190
  12.4 23.2 %collective-permute-start.5 = (bf16[2,3,4,1,32,128]{5,4,3,2,1,0:T(8,128)(2,1)}, bf16[2,3,4,1,32,128]{5,4,3,2,1,0:T(8,128)(2,1)S(1)}, u32[]{:S(2)}, u32[]{:S(2)}) collective-permute-start(bf16[2,3,4,1,32,128]{5,4,3,2,1,0:T(8,128)(2,1)} %get-tuple-element.13), channel_id=1, source_target_pairs={{0,3},{1,0},{2,1},{3,2},{4,7},{5,4},{6,5},{7,6},{8,11},{9,8},{10,9... | collective-permute-start | bytes 589832 | tf_op jit(solution)/shard_map/ppermute | solution.py:190
  14.3 27.6 %collective-permute-start.6 = (bf16[2,3,4,1,32,128]{5,4,3,2,1,0:T(8,128)(2,1)}, bf16[2,3,4,1,32,128]{5,4,3,2,1,0:T(8,128)(2,1)}, u32[]{:S(2)}, u32[]{:S(2)}) collective-permute-start(bf16[2,3,4,1,32,128]{5,4,3,2,1,0:T(8,128)(2,1)} %get-tuple-element.12), channel_id=1, source_target_pairs={{0,1},{1,2},{2,3},{3,0},{4,5},{5,6},{6,7},{7,4},{8,9},{9,10},{10,1... | collective-permute-start | bytes 589832 | tf_op jit(solution)/shard_map/ppermute | solution.py:190
  15.2 20.4 %collective-permute-start.7 = (bf16[18,4,1,32]{3,2,1,0:T(2,128)(2,1)S(1)}, bf16[18,4,1,32]{3,2,1,0:T(2,128)(2,1)S(1)}, u32[]{:S(2)}, u32[]{:S(2)}) collective-permute-start(bf16[18,4,1,32]{3,2,1,0:T(2,128)(2,1)S(1)} %slice_bitcast_fusion.1), channel_id=1, source_target_pairs={{0,1},{1,2},{2,3},{3,0},{4,5},{5,6},{6,7},{7,4},{8,9},{9,10},{10,1... | collective-permute-start | bytes 13832 | tf_op jit(solution)/shard_map/ppermute | solution.py:190
  35.6 25.9 %collective-permute-start.2 = (bf16[18,2,16,32]{3,2,1,0:T(8,128)(2,1)}, bf16[18,2,16,32]{3,2,1,0:T(8,128)(2,1)S(1)}, u32[]{:S(2)}, u32[]{:S(2)}) collective-permute-start(bf16[18,2,16,32]{3,2,1,0:T(8,128)(2,1)} %slice_bitcast_fusion), channel_id=1, source_target_pairs={{0,4},{4,8},{8,12},{12,16},{16,20},{20,24},{24,28},{28,32},{32,36}... | collective-permute-start | bytes 110600 | tf_op jit(solution)/shard_map/ppermute | solution.py:190
  35.6 35.5 %collective-permute-start.3 = (bf16[2,3,1,16,32,128]{5,4,3,2,1,0:T(8,128)(2,1)}, bf16[2,3,1,16,32,128]{5,4,3,2,1,0:T(8,128)(2,1)S(1)}, u32[]{:S(2)}, u32[]{:S(2)}) collective-permute-start(bf16[2,3,1,16,32,128]{5,4,3,2,1,0:T(8,128)(2,1)} %get-tuple-element.10), channel_id=1, source_target_pairs={{0,124},{4,0},{8,4},{12,8},{16,12},{20,16},{24,20},{28,24},{32,28}... | collective-permute-start | bytes 2359304 | tf_op jit(solution)/shard_map/ppermute | solution.py:190
  41.9 29.2 %collective-permute-start.4 = (bf16[2,3,1,16,32,128]{5,4,3,2,1,0:T(8,128)(2,1)}, bf16[2,3,1,16,32,128]{5,4,3,2,1,0:T(8,128)(2,1)S(1)}, u32[]{:S(2)}, u32[]{:S(2)}) collective-permute-start(bf16[2,3,1,16,32,128]{5,4,3,2,1,0:T(8,128)(2,1)} %get-tuple-element.9), channel_id=1, source_target_pairs={{0,4},{4,8},{8,12},{12,16},{16,20},{20,24},{24,28},{28,32},{32,36}... | collective-permute-start | bytes 2359304 | tf_op jit(solution)/shard_map/ppermute | solution.py:190
  41.9 1.2 %copy-start.1 = (bf16[3,18,4,1,16,32]{5,4,3,2,1,0:T(8,128)(2,1)S(1)}, bf16[3,18,4,1,16,32]{5,4,3,2,1,0:T(8,128)(2,1)}, u32[]{:S(2)}) copy-start(bf16[3,18,4,1,16,32]{5,4,3,2,1,0:T(8,128)(2,1)} %param.6) | copy-start | bytes 663556
  43.0 18.5 %copy-start.2 = (bf16[3,18,4,1,16,32]{5,4,3,2,1,0:T(8,128)(2,1)S(1)}, bf16[3,18,4,1,16,32]{5,4,3,2,1,0:T(8,128)(2,1)}, u32[]{:S(2)}) copy-start(bf16[3,18,4,1,16,32]{5,4,3,2,1,0:T(8,128)(2,1)} %param.6) | copy-start | bytes 663556
  79.8 10.2 %copy-start.4 = (s32[3]{0:T(128)S(1)}, s32[3]{0:T(128)}, u32[]{:S(2)}) copy-start(s32[3]{0:T(128)} %param.8) | copy-start | bytes 40
  81.8 32.5 %all-to-all-start = ((bf16[128,4,1536]{2,1,0:T(4,128)(2,1)}), bf16[128,4,1536]{2,1,0:T(4,128)(2,1)S(1)}, u32[]{:S(2)}, u32[]{:S(2)}) async-start(bf16[128,4,1536]{2,1,0:T(4,128)(2,1)} %bitcast.7), calls=%async_computation | async-start | bytes 3145728 | tf_op jit(solution)/shard_map/all_to_all | solution.py:274

commit v2 on v1

v2 whole, which is shorter than its diff:
```python
import functools
import math

import jax
import jax.numpy as jnp
from jax import lax
from jax.experimental import pallas as pl
from jax.experimental.pallas import tpu as pltpu
from jax.sharding import PartitionSpec as P

BF16 = jnp.bfloat16
F32 = jnp.float32


def link_rows(entries, adjoint, width):
    rows = []
    for r in range(2):
        for a in range(3):
            pieces = []
            for q in range(2):
                for b in range(3):
                    first = ((b * 3 + a) if adjoint else (a * 3 + b)) * 2
                    if r == q:
                        pieces.append(entries[first])
                    elif (q == 1) == adjoint:
                        pieces.append(entries[first + 1])
                    else:
                        pieces.append(-entries[first + 1])
            lanes = sum(piece.shape[1] for piece in pieces)
            if lanes < width:
                pieces.append(jnp.zeros((pieces[0].shape[0], width - lanes), F32))
            rows.append(jnp.concatenate(pieces, axis=1))
    return rows


def site_masks(count_y, lanes):
    row = lax.broadcasted_iota(jnp.int32, (count_y, lanes), 0)
    lane = lax.broadcasted_iota(jnp.int32, (count_y, lanes), 1) % count_y
    same = jnp.where(lane == row, 1.0, 0.0).astype(BF16)
    above = jnp.where(lane == (row + 1) % count_y, 1.0, 0.0).astype(BF16)
    below = jnp.where(lane == (row + count_y - 1) % count_y, 1.0, 0.0).astype(BF16)
    return same, above, below


def spread(rows_ref, kind, row, mask):
    count_y, lanes = mask.shape
    blocks = []
    for ra in range(6):
        line = rows_ref[kind, ra, pl.ds(row, 1), :lanes]
        blocks.append(jnp.broadcast_to(line, (count_y, lanes)).astype(BF16) * mask)
    return jnp.concatenate(blocks, axis=0)


def write_phased(planes_of, table, table_first, blocks, out_ref, first, colour_stride):
    for b in range(3):
        for block in range(blocks):
            real = planes_of(0, b, block).T.astype(F32)
            imag = planes_of(1, b, block).T.astype(F32)
            nev, sites = real.shape
            at = first + b * colour_stride + block * sites
            put_phased(real, imag, table, table_first + block * sites, out_ref, at)


def put_phased(real, imag, table, table_at, out_ref, at):
    nev, sites = real.shape
    for p in range(2):
        cosine = table[2 * p : 2 * p + 1, table_at : table_at + sites]
        sine = table[2 * p + 1 : 2 * p + 2, table_at : table_at + sites]
        out_ref[2 * p * nev : (2 * p + 1) * nev, at : at + sites] = (cosine * real - sine * imag).astype(BF16)
        out_ref[(2 * p + 1) * nev : (2 * p + 2) * nev, at : at + sites] = (sine * real + cosine * imag).astype(BF16)


def put_displaced(out_ref, z, terms, count_y, nev):
    for r in range(2):
        for a in range(3):
            rows = terms[(r * 3 + a) * count_y : (r * 3 + a + 1) * count_y]
            out_ref[a, z, :, r * nev : (r + 1) * nev] = rows.astype(BF16)


def combine(products, nev):
    real, imag = [], []
    for p in range(2):
        rr = products[2 * p * nev : (2 * p + 1) * nev, :nev]
        ri = products[2 * p * nev : (2 * p + 1) * nev, nev:]
        ir = products[(2 * p + 1) * nev : (2 * p + 2) * nev, :nev]
        ii = products[(2 * p + 1) * nev : (2 * p + 2) * nev, nev:]
        real.append(rr + ii)
        imag.append(ri - ir)
    return real + imag


def by_owner(first, second):
    nev, lanes = first.shape
    a = first.reshape(nev // 8, 8, lanes)
    b = second.reshape(nev // 8, 8, lanes)
    upper = lax.broadcasted_iota(jnp.int32, a.shape, 1) < 4
    even = jnp.where(upper, a, pltpu.roll(b, 4, 1))
    odd = jnp.where(upper, pltpu.roll(a, 4, 1), b)
    return jnp.stack([even, odd], axis=1).reshape(nev // 4, 8, lanes)


def put_partials(out_ref, m, at, parts):
    real = by_owner(parts[0], parts[1])
    imag = by_owner(parts[2], parts[3])
    nev = parts[0].shape[1]
    out_ref[:, m, :, at * nev : (at + 1) * nev] = jnp.concatenate([real, imag], axis=1).astype(BF16)


def yz_kernel(core_ref, v_ref, swap0_ref, swap1_ref, halo_ref, link_ref, swap_link_ref, table_ref, out_ref,
              rows, padded, phased, moved_y, moved_z, extra):
    m = pl.program_id(0)
    core = core_ref[0]
    count_z, count_y, nev = v_ref.shape[3:]
    deep = 2 * count_z
    lanes = 6 * count_y
    sites = deep * count_y
    same, above, below = site_masks(count_y, lanes)
    mine = pl.multiple_of(core * count_z, count_z)
    theirs = pl.multiple_of((1 - core) * count_z, count_z)
    padded[:, :, pl.ds(mine, count_z)] = v_ref[:, :, 0]

    @pl.when(m == 0)
    def _():
        padded[:, :, pl.ds(theirs, count_z)] = swap0_ref[:, :, 0]

    @pl.when(m == 1)
    def _():
        padded[:, :, pl.ds(theirs, count_z)] = swap1_ref[:, :, 0]

    padded[:, :, deep] = halo_ref[:, :, 0]

    wide = rows.shape[3]
    lane = lax.broadcasted_iota(jnp.int32, (count_z, wide), 1) % count_y
    for links, start in ((link_ref, mine), (swap_link_ref, theirs)):
        at = pl.ds(start, count_z)
        link_y = [0.5 * links[1, e, 0].astype(F32) for e in range(18)]
        for ra, line in enumerate(link_rows(link_y, False, wide)):
            rows[0, ra, at, :] = jnp.where(
                lane == 0, pltpu.roll(line, wide - (count_y - 1), 1), pltpu.roll(line, 1, 1)
            )
        for ra, line in enumerate(link_rows(link_y, True, wide)):
            rows[1, ra, at, :] = -line
        link_z = [0.5 * links[2, e, 0].astype(F32) for e in range(18)]
        for ra, line in enumerate(link_rows(link_z, False, wide)):
            rows[2, ra, at, :] = line
        for ra, line in enumerate(link_rows(link_z, True, wide)):
            rows[3, ra, at, :] = -line

    table = table_ref[0]
    step = nev // count_y
    write_phased(
        lambda q, b, block: padded[q, b, block * step : (block + 1) * step].reshape(nev, nev),
        table, 0, sites // nev, phased, 0, sites,
    )
    put_phased(
        padded[0, :, deep].reshape(3 * count_y, nev).T.astype(F32),
        padded[1, :, deep].reshape(3 * count_y, nev).T.astype(F32),
        table, sites, phased, 3 * sites,
    )

    def forward(z):
        return jnp.dot(
            spread(rows, 2, z, same), padded[:, :, z + 1].reshape(lanes, nev), preferred_element_type=F32
        )

    def backward(z):
        return jnp.dot(
            spread(rows, 3, z - 1, same), padded[:, :, z - 1].reshape(lanes, nev), preferred_element_type=F32
        )

    def plane(z, carry):
        in_y = spread(rows, 0, z, above) + spread(rows, 1, z, below)
        terms = jnp.dot(in_y, padded[:, :, z].reshape(lanes, nev), preferred_element_type=F32)
        put_displaced(moved_y, z, terms, count_y, nev)
        return carry

    def between(z, carry):
        put_displaced(moved_z, z, forward(z) + backward(z), count_y, nev)
        return carry

    lax.fori_loop(0, deep, plane, 0, unroll=16)
    put_displaced(moved_z, 0, forward(0), count_y, nev)
    lax.fori_loop(1, deep, between, 0, unroll=16)
    terms = backward(deep)
    for r in range(2):
        half = terms[r * 3 * count_y : (r + 1) * 3 * count_y]
        extra[:, r * nev : (r + 1) * nev] = half.astype(BF16)

    products = jnp.dot(
        phased[:, : 3 * sites], moved_y[...].reshape(3 * sites, 2 * nev), preferred_element_type=F32
    )
    put_partials(out_ref, 0, 0, combine(products, nev))
    products = jnp.dot(
        phased[:, : 3 * sites], moved_z[...].reshape(3 * sites, 2 * nev), preferred_element_type=F32
    ) + jnp.dot(phased[:, 3 * sites : 3 * sites + 3 * count_y], extra[...], preferred_element_type=F32)
    put_partials(out_ref, 0, 1, combine(products, nev))


def x_terms(low, high, link, table_low, table_high, rows, phased, moved):
    count_z, count_y, nev = low.shape[2:]
    lanes = 6 * count_y
    same = site_masks(count_y, lanes)[0]
    entries = [0.5 * link[e].astype(F32) for e in range(18)]
    for ra, line in enumerate(link_rows(entries, False, lanes)):
        rows[0, ra] = line
    for ra, line in enumerate(link_rows(entries, True, lanes)):
        rows[1, ra] = -line
    sites = count_z * count_y
    step = nev // count_y
    for vectors, table, first in ((low, table_low, 0), (high, table_high, 3 * sites)):
        write_phased(
            lambda q, b, block: vectors[q, b, block * step : (block + 1) * step].reshape(nev, nev),
            table, 0, sites // nev, phased, first, sites,
        )

    def plane(z, carry):
        terms = jnp.dot(spread(rows, 0, z, same), high[:, :, z].reshape(lanes, nev), preferred_element_type=F32)
        put_displaced(moved.at[0], z, terms, count_y, nev)
        terms = jnp.dot(spread(rows, 1, z, same), low[:, :, z].reshape(lanes, nev), preferred_element_type=F32)
        put_displaced(moved.at[1], z, terms, count_y, nev)
        return carry

    lax.fori_loop(0, count_z, plane, 0, unroll=16)
    products = jnp.dot(phased[...], moved[...].reshape(6 * sites, 2 * nev), preferred_element_type=F32)
    return combine(products, nev)


def x_pairs(own_up, recv_up, own_down, recv_down, link_up, link_down, table_ref, rows, phased, moved):
    yield 0, x_terms(
        own_up.at[:, :, 0], recv_up.at[:, :, 0], link_up.at[0, :, 0], table_ref[0], table_ref[1], rows, phased, moved
    )
    yield 1, x_terms(
        recv_down.at[:, :, 0], own_down.at[:, :, 0], link_down.at[:, 0], table_ref[2], table_ref[0], rows, phased, moved
    )


def x_first_kernel(core_ref, own_up, recv_up, own_down, recv_down, link_up, link_down, table_ref, out_ref, *scratch):
    for m, parts in x_pairs(own_up, recv_up, own_down, recv_down, link_up, link_down, table_ref, *scratch):
        for at, part in enumerate(parts):
            out_ref[m, at] = part


def x_last_kernel(core_ref, own_up, recv_up, own_down, recv_down, link_up, link_down, table_ref, before, _, out_ref, *scratch):
    for m, parts in x_pairs(own_up, recv_up, own_down, recv_down, link_up, link_down, table_ref, *scratch):
        put_partials(out_ref, m, 0, [part + before[m, at] for at, part in enumerate(parts)])


def total_kernel(directions_ref, got_ref, out_ref):
    total = jnp.sum(got_ref[...].astype(F32), axis=0)
    nev = total.shape[1] // 3
    group = out_ref.shape[0]
    in_y, in_z, in_x = (total[:, k * nev : (k + 1) * nev] for k in range(3))
    for d in range(3):
        direction = directions_ref[d]
        chosen = jnp.where(direction == 0, in_x, jnp.where(direction == 1, in_y, in_z))
        for r in range(2):
            for p in range(2):
                for i in range(group):
                    row = (r * 2 + p) * group + i
                    out_ref[i, 0, p, r : r + 1, d * nev : (d + 1) * nev] = chosen[row : row + 1]


def fraction(component, coords, length):
    return jnp.mod(component[:, None] * coords[None, :], length).astype(F32) / length


def phase_table(momenta, coord_x, coord_z, coord_y, total_x, total_z, total_y):
    frac_x = fraction(momenta[:, 0], coord_x, total_x)
    frac_y = fraction(momenta[:, 1], coord_y, total_y)
    frac_z = fraction(momenta[:, 2], coord_z, total_z)
    angle = 2.0 * math.pi * (
        (frac_x[:, :, None, None] + frac_y[:, None, None, :]) + frac_z[:, None, :, None]
    )
    table = jnp.stack([jnp.cos(angle), jnp.sin(angle)], axis=1)
    table = jnp.transpose(table, (2, 0, 1, 3, 4))
    return table.reshape(coord_x.shape[0], 4, coord_z.shape[0] * coord_y.shape[0])


def shift(value, steps):
    count = lax.axis_size("ts")
    return lax.ppermute(value, "ts", [(source, (source + steps) % count) for source in range(count)])


def shards(eigvecs, gauge_links, momenta, directions):
    _, _, count_t, _, count_z, count_y, nev = eigvecs.shape
    vectors = eigvecs.reshape(2, 3, count_t, count_z, count_y, nev)
    links = gauge_links.reshape(3, 18, count_t, count_z, count_y)
    size_x, size_g = lax.axis_size("ts"), lax.axis_size("gz")
    x, g = lax.axis_index("ts"), lax.axis_index("gz")
    core, chip = g % 2, g // 2
    deep = 2 * count_z
    sites = count_z * count_y
    group = nev // size_x

    lowest = vectors[:, :, :, 0].reshape(2, 3, 2, 2, count_y, nev)
    halo = lax.ppermute(lowest[:, :, :, 0], "gz", [(0, 2), (2, 0)])
    halo += lax.ppermute(lowest[:, :, :, 1], "gz", [(0, 3), (2, 1)])

    def times(array, axis, at):
        return lax.dynamic_slice_in_dim(array, at, 1, axis)

    swap = [(0, 1), (1, 0), (2, 3), (3, 2)]
    recv_up = [shift(times(vectors, 2, core), -1)]
    recv_down = [shift(times(vectors, 2, core + 2), 1)]
    swap0 = lax.ppermute(times(vectors, 2, 1 - core), "gz", swap)
    swap1 = lax.ppermute(times(vectors, 2, 3 - core), "gz", swap)
    given = lax.dynamic_index_in_dim(links.reshape(3, 18, 2, 2, count_z, count_y), 1 - core, 3, keepdims=False)
    swap_links = lax.ppermute(given, "gz", swap)
    link_down = shift(jnp.concatenate([times(links[0], 1, core + 2), swap_links[0, :, 1:]], axis=1), 1)
    recv_up.append(shift(swap0, -1))
    recv_down.append(shift(swap1, 1))

    coord_x = x + jnp.array([0, 1, -1], jnp.int32)
    coord_z = chip * deep + jnp.arange(deep + 1, dtype=jnp.int32)
    coord_y = jnp.arange(count_y, dtype=jnp.int32)
    table = phase_table(momenta, coord_x, coord_z, coord_y, size_x, count_z * size_g, count_y)
    top = table[:1, :, 2 * sites :]
    table_yz = jnp.concatenate([table[:1, :, : 2 * sites], top, top, top], axis=2)
    table_x = [lax.dynamic_slice_in_dim(table, at * sites, sites, 2) for at in (core, 1 - core)]

    core_at = jnp.reshape(core, (1,)).astype(jnp.int32)
    limit = pltpu.CompilerParams(vmem_limit_bytes=48 * 1024 * 1024)
    whole = lambda shape: pl.BlockSpec(shape, lambda i, core: (0,) * len(shape))
    one_time = (2, 3, 1, count_z, count_y, nev)
    sent = pl.pallas_call(
        yz_kernel,
        grid_spec=pltpu.PrefetchScalarGridSpec(
            num_scalar_prefetch=1,
            grid=(2,),
            in_specs=[
                pl.BlockSpec(one_time, lambda m, core: (0, 0, core[0] + 2 * m, 0, 0, 0)),
                whole(one_time),
                whole(one_time),
                pl.BlockSpec((2, 3, 1, count_y, nev), lambda m, core: (0, 0, m, 0, 0)),
                pl.BlockSpec((3, 18, 1, count_z, count_y), lambda m, core: (0, 0, core[0] + 2 * m, 0, 0)),
                pl.BlockSpec((3, 18, 1, count_z, count_y), lambda m, core: (0, 0, m, 0, 0)),
                whole(table_yz.shape),
            ],
            out_specs=pl.BlockSpec((size_x, 1, 4 * group, 2 * nev), lambda m, core: (0, m, 0, 0)),
            scratch_shapes=[
                pltpu.VMEM((4, 6, deep, 256), F32),
                pltpu.VMEM((2, 3, deep + 1, count_y, nev), BF16),
                pltpu.VMEM((4 * nev, 6 * sites + nev), BF16),
                pltpu.VMEM((3, deep, count_y, 2 * nev), BF16),
                pltpu.VMEM((3, deep, count_y, 2 * nev), BF16),
                pltpu.VMEM((3 * count_y, 2 * nev), BF16),
            ],
        ),
        out_shape=jax.ShapeDtypeStruct((size_x, 2, 4 * group, 3 * nev), BF16),
        compiler_params=limit,
        cost_estimate=pl.CostEstimate(flops=9_000_000_000, bytes_accessed=6_000_000, transcendentals=0),
        name="yz_terms",
    )(core_at, vectors, swap0, swap1, halo, links, swap_links, table_yz)

    part = None
    for c in range(2):
        if c == 0:
            own = [vectors, vectors]
            own_specs = [
                pl.BlockSpec(one_time, lambda i, core: (0, 0, core[0], 0, 0, 0)),
                pl.BlockSpec(one_time, lambda i, core: (0, 0, core[0] + 2, 0, 0, 0)),
            ]
            link, link_spec = links, pl.BlockSpec((1, 18, 1, count_z, count_y), lambda i, core: (0, 0, core[0], 0, 0))
        else:
            own = [swap0, swap1]
            own_specs = [whole(one_time), whole(one_time)]
            link, link_spec = swap_links, whole((1, 18, 1, count_z, count_y))
        operands = [core_at, own[0], recv_up[c], own[1], recv_down[c], link, link_down, table_x[c]]
        in_specs = [
            own_specs[0],
            whole(one_time),
            own_specs[1],
            whole(one_time),
            link_spec,
            pl.BlockSpec((18, 1, count_z, count_y), functools.partial(lambda c, i, core: (0, c, 0, 0), c)),
            whole(table_x[c].shape),
        ]
        scratch = [
            pltpu.VMEM((2, 6, count_z, 6 * count_y), F32),
            pltpu.VMEM((4 * nev, 6 * sites), BF16),
            pltpu.VMEM((2, 3, count_z, count_y, 2 * nev), BF16),
        ]
        cost = pl.CostEstimate(flops=5_000_000_000, bytes_accessed=4_000_000, transcendentals=0)
        if c == 0:
            shape = (2, 4, nev, nev)
            part = pl.pallas_call(
                x_first_kernel,
                grid_spec=pltpu.PrefetchScalarGridSpec(
                    num_scalar_prefetch=1, grid=(1,), in_specs=in_specs, out_specs=whole(shape), scratch_shapes=scratch
                ),
                out_shape=jax.ShapeDtypeStruct(shape, F32),
                compiler_params=limit,
                cost_estimate=cost,
                name="x_first",
            )(*operands)
        else:
            sent = pl.pallas_call(
                x_last_kernel,
                grid_spec=pltpu.PrefetchScalarGridSpec(
                    num_scalar_prefetch=1,
                    grid=(1,),
                    in_specs=in_specs + [whole(part.shape), pl.BlockSpec(memory_space=pl.ANY)],
                    out_specs=pl.BlockSpec((size_x, 2, 4 * group, nev), lambda i, core: (0, 0, 0, 2)),
                    scratch_shapes=scratch,
                ),
                out_shape=jax.ShapeDtypeStruct(sent.shape, BF16),
                input_output_aliases={len(operands) + 1: 0},
                compiler_params=limit,
                cost_estimate=cost,
                name="x_last",
            )(*operands, part, sent)

    pieces = sent.reshape(2 * size_x, 4 * group, 3 * nev)
    groups = [[(ts * 2 + h) * 2 + c for ts in range(size_x) for h in range(2)] for c in range(2)]
    got = lax.all_to_all(pieces, ("ts", "gz"), 0, 0, tiled=True, axis_index_groups=groups)
    return pl.pallas_call(
        total_kernel,
        in_specs=[pl.BlockSpec(memory_space=pltpu.SMEM), pl.BlockSpec(memory_space=pltpu.VMEM)],
        out_specs=pl.BlockSpec(memory_space=pltpu.VMEM),
        out_shape=jax.ShapeDtypeStruct((group, 1, 2, 2, 3 * nev), F32),
        name="total",
    )(directions, got)


def solution(mesh):
    in_specs = (
        P(None, None, None, "ts", "gz", None, None),
        P(None, None, None, "ts", "gz", None),
        P(),
        P(),
    )
    out_specs = P("ts", "gz", None, None, None)
    return jax.shard_map(shards, mesh=mesh, in_specs=in_specs, out_specs=out_specs, check_vma=False)
```

time: 117 us -> 110 us (0.940); the launches traced: 116 us -> 108 us
  waiting for transfers between devices: 41 us -> 13.3 us
  blocking collectives: 0 us -> 24 us
  starting transfers between devices: 24.8 us -> 20.3 us
  Pallas kernels: 36.1 us -> 34.3 us
    all_to_all x1 -> x0, waiting for transfers between devices: 24.2 us -> none  [shards(): got = lax.all_to_all(sent, ('ts', 'gz'), 0, 0, tiled=True)]
    all_to_all x0 -> x1, blocking collectives: none -> 24 us  [shards(): lax.all_to_all(pieces, ('ts', 'gz'), 0, 0, tiled=True, axis_index_groups=...]
    all_to_all x1 -> x0, starting transfers between devices: 8.17 us -> none  [shards(): got = lax.all_to_all(sent, ('ts', 'gz'), 0, 0, tiled=True)]
    dynamic_slice x0 -> x3, local copies, waits for them, and re-layouts: none -> 4.96 us  [the longest x2 4.87 us: times(): return lax.dynamic_slice_in_dim(array, at, 1, axis)]
    ppermute x8 -> x10, starting transfers between devices: 16.7 us -> 20.3 us  [the longest x5 13.8 us: shift(): lax.ppermute(value, 'ts', [(source, (source + steps) % count) for source...]
    ppermute x8 -> x10, waiting for transfers between devices: 16.9 us -> 13.3 us  [the longest x1 10.9 us: shards(): halo = lax.ppermute(lowest[:, :, :, 0], 'gz', [(0, 2), (2, 0)])]
    reshape x5 -> x0, local copies, waits for them, and re-layouts: 2.43 us -> none  [the longest x2 2.39 us: shards(): jnp.concatenate([in_x, yz], axis=2)]
    pallas_call x3 -> x4, Pallas kernels: 36.1 us -> 34.3 us  [the longest x1 19.3 us: shards(): pl.pallas_call(yz_kernel, grid_spec=pltpu.PrefetchScalarGridSpec(num_scal...]
  transfers between devices with their start and end apart: 9 -> 10, of which waited for: 2 -> 3; matrix products, arithmetic and copies ran while one was open for 4% -> 11% of each run, Pallas kernels for 24% -> 25%
where the time goes in v2:
time: 110 us; the launch traced here: 108 us
  Pallas kernels  34.3 us (31%)
  blocking collectives  24 us (22%)
  starting transfers between devices  20.3 us (18%)
  waiting for transfers between devices  13.3 us (12%)
  local copies, waits for them, and re-layouts  13.1 us (12%)
  other arithmetic  2.52 us (2%)
    all_to_all x1, blocking collectives, shards(): lax.all_to_all(pieces, ('ts', 'gz'), 0, 0, tiled=True, axis_index_groups=...  24 us
    pallas_call x1, Pallas kernels, shards(): pl.pallas_call(yz_kernel, grid_spec=pltpu.PrefetchScalarGridSpec(num_scal...  19.3 us
    ppermute x5, starting transfers between devices, shift(): lax.ppermute(value, 'ts', [(source, (source + steps) % count) for source...  13.8 us
    ppermute x1, waiting for transfers between devices, shards(): halo = lax.ppermute(lowest[:, :, :, 0], 'gz', [(0, 2), (2, 0)])  10.9 us
    pallas_call x1, Pallas kernels, shards(): pl.pallas_call(x_first_kernel, grid_spec=pltpu.PrefetchScalarGridSpec(num...  7.33 us
    pallas_call x1, Pallas kernels, shards(): pl.pallas_call(x_last_kernel, grid_spec=pltpu.PrefetchScalarGridSpec(num_...  5.78 us
    dynamic_slice x2, local copies, waits for them, and re-layouts, times(): return lax.dynamic_slice_in_dim(array, at, 1, axis)  4.87 us
    ppermute x1, starting transfers between devices, shards(): halo = lax.ppermute(lowest[:, :, :, 0], 'gz', [(0, 2), (2, 0)])  4.63 us
  transfers between devices with their start and end apart: 10, of which 3 were waited for; matrix products, arithmetic and copies ran while one was open for 11% of the time, Pallas kernels for 25%

profile of v2, /device:TPU:0, one launch (start us, length us, event | category | flops | bytes accessed | tf_op | source)
XLA Modules:
  0.0 107.6 jit_solution(13394430627838645007)
XLA Ops:
  0.0 4.0 %dynamic-slice_bitcast_fusion = (bf16[2,3,1,16,32,128]{5,4,3,2,1,0:T(8,128)(2,1)}, bf16[2,3,1,16,32,128]{5,4,3,2,1,0:T(8,128)(2,1)}, bf16[2,3,1,16,32,128]{5,4,3,2,1,0:T(8,128)(2,1)}, bf16[2,3,1,16,32,128]{5,4,3,2,1,0:T(8,128)(2,1)}) fusion(bf16[2,3,4,1,16,32,128]{6,5,4,3,2,1,0:T(8,128)(2,1)} %param.5, s32[]{:T(128)S(6)} %select_n.68, s32[]{:T(128)S(6)} %select_n.66, ...), kind=kLoop, calls=%fused_computation | loop fusion | bytes 6291472 | tf_op jit(solution)/shard_map/dynamic_slice | solution.py:300
  4.5 0.8 copy_bitcast_fusion
  5.3 7.5 %collective-permute-start.6 = (bf16[2,3,1,16,32,128]{5,4,3,2,1,0:T(8,128)(2,1)}, bf16[2,3,1,16,32,128]{5,4,3,2,1,0:T(8,128)(2,1)S(1)}, u32[]{:S(2)}, u32[]{:S(2)}) collective-permute-start(bf16[2,3,1,16,32,128]{5,4,3,2,1,0:T(8,128)(2,1)} %get-tuple-element.11), channel_id=1, source_target_pairs={{0,124},{4,0},{8,4},{12,8},{16,12},{20,16},{24,20},{28,24},{32,28}... | collective-permute-start | bytes 2359304 | tf_op jit(solution)/shard_map/ppermute | solution.py:281
  12.8 0.7 slice.37
  14.8 1.6 %slice.50 = bf16[2,3,4,1,32,128]{5,4,3,2,1,0:T(8,128)(2,1)} slice(bf16[2,3,4,16,32,128]{5,4,3,2,1,0:T(8,128)(2,1)} %bitcast.34), slice={[0:2], [0:3], [0:4], [0:1], [0:32], [0:128]} | slice | bytes 393216 | tf_op jit(solution)/shard_map/slice | solution.py:295
  16.4 1.0 slice_bitcast_fusion
  17.4 0.9 dynamic-slice_bitcast_fusion.4
  18.3 4.6 %collective-permute-start.8 = (bf16[2,3,2,32,128]{4,3,2,1,0:T(8,128)(2,1)S(1)}, bf16[2,3,2,32,128]{4,3,2,1,0:T(8,128)(2,1)S(1)}, u32[]{:S(2)}, u32[]{:S(2)}) collective-permute-start(bf16[2,3,2,32,128]{4,3,2,1,0:T(8,128)(2,1)S(1)} %get-tuple-element.13), channel_id=1, source_target_pairs={{0,2},{2,0},{4,6},{6,4},{8,10},{10,8},{12,14},{14,12},{16,18},{18,... | collective-permute-start | bytes 294920 | tf_op jit(solution)/shard_map/ppermute | solution.py:296
  22.9 0.9 slice_bitcast_fusion.2
  23.8 10.9 %collective-permute-done.8 = bf16[2,3,2,32,128]{4,3,2,1,0:T(8,128)(2,1)S(1)} collective-permute-done((bf16[2,3,2,32,128]{4,3,2,1,0:T(8,128)(2,1)S(1)}, bf16[2,3,2,32,128]{4,3,2,1,0:T(8,128)(2,1)S(1)}, u32[]{:S(2)}, u32[]{:S(2)}) %collective-permute-start.8) | collective-permute-done | bytes 98336 | tf_op jit(solution)/shard_map/ppermute | solution.py:296
  34.7 1.3 %collective-permute-start.9 = (bf16[2,3,2,32,128]{4,3,2,1,0:T(8,128)(2,1)S(1)}, bf16[2,3,2,32,128]{4,3,2,1,0:T(8,128)(2,1)S(1)}, u32[]{:S(2)}, u32[]{:S(2)}) collective-permute-start(bf16[2,3,2,32,128]{4,3,2,1,0:T(8,128)(2,1)S(1)} %get-tuple-element.12), channel_id=1, source_target_pairs={{0,3},{2,1},{4,7},{6,5},{8,11},{10,9},{12,15},{14,13},{16,19},{18,... | collective-permute-start | bytes 294920 | tf_op jit(solution)/shard_map/ppermute | solution.py:297
  36.0 0.7 pad_maximum_fusion
  36.7 1.5 %collective-permute-done.9 = bf16[2,3,2,32,128]{4,3,2,1,0:T(8,128)(2,1)S(1)} collective-permute-done((bf16[2,3,2,32,128]{4,3,2,1,0:T(8,128)(2,1)S(1)}, bf16[2,3,2,32,128]{4,3,2,1,0:T(8,128)(2,1)S(1)}, u32[]{:S(2)}, u32[]{:S(2)}) %collective-permute-start.9) | collective-permute-done | bytes 98336 | tf_op jit(solution)/shard_map/ppermute | solution.py:297
  38.3 0.9 slice.53
  39.2 0.7 slice.54
  40.1 1.0 add.147.halo_ref
  41.1 1.0 copy.14.swap_link_ref.link_up
  42.1 6.3 %collective-permute-start.1 = (bf16[2,3,1,16,32,128]{5,4,3,2,1,0:T(8,128)(2,1)S(1)}, bf16[2,3,1,16,32,128]{5,4,3,2,1,0:T(8,128)(2,1)S(1)}, u32[]{:S(2)}, u32[]{:S(2)}) collective-permute-start(bf16[2,3,1,16,32,128]{5,4,3,2,1,0:T(8,128)(2,1)S(1)} %collective-permute-done.swap0_ref.own_up), channel_id=1, source_target_pairs={{0,124},{4,0},{8,4},{12,8},{16,12},{20,16},{24,20},{28,24},{32,28}... | collective-permute-start | bytes 2359304 | tf_op jit(solution)/shard_map/ppermute | solution.py:281
  48.4 0.9 collective-permute-done.5.link_down
  49.3 7.3 %x_first.1.before = f32[2,4,128,128]{3,2,1,0:T(8,128)S(1)} custom-call(s32[1]{0:T(128)} %bitcast.core_ref, bf16[2,3,4,16,32,128]{5,4,3,2,1,0:T(8,128)(2,1)} %bitcast.35, bf16[2,3,1,16,32,128]{5,4,3,2,1,0:T(8,128)(2,1)S(1)} %collective-permute-done.6.recv_up, bf16[2,3,4,16,32,128]{5,4,3,2,1,0:T(8,128)(2,1)} %bitcast.36, ...), custom_call_target="tpu_custom_call" | custom-call | flops 5000000000 | bytes 4000000 | tf_op jit(solution)/shard_map/x_first/pallas_call | solution.py:386
  56.7 19.3 %yz_terms.1._ = bf16[32,2,16,384]{3,2,1,0:T(8,128)(2,1)S(1)} custom-call(s32[1]{0:T(128)} %bitcast.core_ref, bf16[2,3,4,16,32,128]{5,4,3,2,1,0:T(8,128)(2,1)} %bitcast.37, bf16[2,3,1,16,32,128]{5,4,3,2,1,0:T(8,128)(2,1)S(1)} %collective-permute-done.swap0_ref.own_up, bf16[2,3,1,16,32,128]{5,4,3,2,1,0:T(8,128)(2,1)S(1)} %collective-permute-done.2.swap1_ref.own_down, ...), custom_call_target="tpu_custom_call" | custom-call | flops 8999999488 | bytes 6000000 | tf_op jit(solution)/shard_map/yz_terms/pallas_call | solution.py:325
  76.0 5.8 %x_last.1 = bf16[32,2,16,384]{3,2,1,0:T(8,128)(2,1)S(1)} custom-call(s32[1]{0:T(128)} %bitcast.core_ref, bf16[2,3,1,16,32,128]{5,4,3,2,1,0:T(8,128)(2,1)S(1)} %collective-permute-done.swap0_ref.own_up, bf16[2,3,1,16,32,128]{5,4,3,2,1,0:T(8,128)(2,1)S(1)} %collective-permute-done.1.recv_up, ...), custom_call_target="tpu_custom_call", output_to_operand_aliasing={{}: (9, {})} | custom-call | flops 5000000000 | bytes 4000000 | tf_op jit(solution)/shard_map/x_last/pallas_call | solution.py:397
  81.8 24.0 %all_to_all.5.got_ref = bf16[64,16,384]{2,1,0:T(8,128)(2,1)} all-to-all(bf16[64,16,384]{2,1,0:T(8,128)(2,1)S(1)} %bitcast.30), channel_id=1, replica_groups={{0,2,4,6,8,10,12,14,16,18,20,22,24,26,28,30,32,34,36,38,40,42,44,46,48,..., dimensions={0} | all-to-all | bytes 1572864 | tf_op jit(solution)/shard_map/all_to_all | solution.py:415
  105.8 1.9 %total.1 = f32[4,1,2,2,384]{4,3,2,1,0:T(2,128)} custom-call(s32[3]{0:T(128)} %directions_ref.1, bf16[64,16,384]{2,1,0:T(8,128)(2,1)} %all_to_all.5.got_ref), custom_call_target="tpu_custom_call" | custom-call | tf_op jit(solution)/shard_map/total/pallas_call | solution.py:416
  (40 shorter events, 2.0 us)
Async XLA Ops:
  0.0 4.5 %copy-start = (bf16[3,18,4,1,16,32]{5,4,3,2,1,0:T(8,128)(2,1)S(1)}, bf16[3,18,4,1,16,32]{5,4,3,2,1,0:T(8,128)(2,1)}, u32[]{:S(2)}) copy-start(bf16[3,18,4,1,16,32]{5,4,3,2,1,0:T(8,128)(2,1)} %param.6) | copy-start | bytes 663556
  0.0 13.6 %copy-start.5 = (s32[2,3]{1,0:T(2,128)S(1)}, s32[2,3]{1,0:T(2,128)}, u32[]{:S(2)}) copy-start(s32[2,3]{1,0:T(2,128)} %param.7) | copy-start | bytes 76
  0.0 13.9 %copy-start.6 = (s32[3]{0:T(128)S(1)}, s32[3]{0:T(128)}, u32[]{:S(2)}) copy-start(s32[3]{0:T(128)} %constant.107.clone) | copy-start | bytes 40
  4.0 38.1 %collective-permute-start = (bf16[2,3,1,16,32,128]{5,4,3,2,1,0:T(8,128)(2,1)}, bf16[2,3,1,16,32,128]{5,4,3,2,1,0:T(8,128)(2,1)S(1)}, u32[]{:S(2)}, u32[]{:S(2)}) collective-permute-start(bf16[2,3,1,16,32,128]{5,4,3,2,1,0:T(8,128)(2,1)} %get-tuple-element.10), channel_id=1, source_target_pairs={{0,1},{1,0},{2,3},{3,2},{4,5},{5,4},{6,7},{7,6},{8,9},{9,8},{10,11... | collective-permute-start | bytes 2359304 | tf_op jit(solution)/shard_map/ppermute | solution.py:305
  4.0 44.4 %collective-permute-start.2 = (bf16[2,3,1,16,32,128]{5,4,3,2,1,0:T(8,128)(2,1)}, bf16[2,3,1,16,32,128]{5,4,3,2,1,0:T(8,128)(2,1)S(1)}, u32[]{:S(2)}, u32[]{:S(2)}) collective-permute-start(bf16[2,3,1,16,32,128]{5,4,3,2,1,0:T(8,128)(2,1)} %get-tuple-element.9), channel_id=1, source_target_pairs={{0,1},{1,0},{2,3},{3,2},{4,5},{5,4},{6,7},{7,6},{8,9},{9,8},{10,11... | collective-permute-start | bytes 2359304 | tf_op jit(solution)/shard_map/ppermute | solution.py:306
  5.3 13.0 %collective-permute-start.4 = (bf16[3,18,2,16,32]{4,3,1,2,0:T(8,128)(2,1)}, bf16[3,18,2,16,32]{4,3,1,2,0:T(8,128)(2,1)}, u32[]{:S(2)}, u32[]{:S(2)}) collective-permute-start(bf16[3,18,2,16,32]{4,3,1,2,0:T(8,128)(2,1)} %copy_bitcast_fusion), channel_id=1, source_target_pairs={{0,1},{1,0},{2,3},{3,2},{4,5},{5,4},{6,7},{7,6},{8,9},{9,8},{10,11... | collective-permute-start | bytes 331784 | tf_op jit(solution)/shard_map/ppermute | solution.py:308
  5.3 44.0 %collective-permute-start.6 = (bf16[2,3,1,16,32,128]{5,4,3,2,1,0:T(8,128)(2,1)}, bf16[2,3,1,16,32,128]{5,4,3,2,1,0:T(8,128)(2,1)S(1)}, u32[]{:S(2)}, u32[]{:S(2)}) collective-permute-start(bf16[2,3,1,16,32,128]{5,4,3,2,1,0:T(8,128)(2,1)} %get-tuple-element.11), channel_id=1, source_target_pairs={{0,124},{4,0},{8,4},{12,8},{16,12},{20,16},{24,20},{28,24},{32,28}... | collective-permute-start | bytes 2359304 | tf_op jit(solution)/shard_map/ppermute | solution.py:281
  12.8 36.5 %collective-permute-start.7 = (bf16[2,3,1,16,32,128]{5,4,3,2,1,0:T(8,128)(2,1)}, bf16[2,3,1,16,32,128]{5,4,3,2,1,0:T(8,128)(2,1)}, u32[]{:S(2)}, u32[]{:S(2)}) collective-permute-start(bf16[2,3,1,16,32,128]{5,4,3,2,1,0:T(8,128)(2,1)} %get-tuple-element.8), channel_id=1, source_target_pairs={{0,4},{4,8},{8,12},{12,16},{16,20},{20,24},{24,28},{28,32},{32,36}... | collective-permute-start | bytes 2359304 | tf_op jit(solution)/shard_map/ppermute | solution.py:281
  14.6 22.1 %copy-start.1 = (f32[3,2,2,33,32]{4,3,2,1,0:T(8,128)}, f32[3,2,2,33,32]{4,3,2,1,0:T(8,128)S(1)}, u32[]{:S(2)}) copy-start(f32[3,2,2,33,32]{4,3,2,1,0:T(8,128)S(1)} %maximum_bitcast_fusion) | copy-start | bytes 152068
  14.7 23.5 %copy-start.2 = (f32[3,4,1056]{2,1,0:T(4,128)}, f32[3,4,1056]{2,1,0:T(4,128)S(1)}, u32[]{:S(2)}) copy-start(f32[3,4,1056]{2,1,0:T(4,128)S(1)} %reshape.158) | copy-start | bytes 152068
  18.3 16.5 %collective-permute-start.8 = (bf16[2,3,2,32,128]{4,3,2,1,0:T(8,128)(2,1)S(1)}, bf16[2,3,2,32,128]{4,3,2,1,0:T(8,128)(2,1)S(1)}, u32[]{:S(2)}, u32[]{:S(2)}) collective-permute-start(bf16[2,3,2,32,128]{4,3,2,1,0:T(8,128)(2,1)S(1)} %get-tuple-element.13), channel_id=1, source_target_pairs={{0,2},{2,0},{4,6},{6,4},{8,10},{10,8},{12,14},{14,12},{16,18},{18,... | collective-permute-start | bytes 294920 | tf_op jit(solution)/shard_map/ppermute | solution.py:296
  34.7 3.6 %copy-start.3 = (bf16[2,3,2,32,128]{4,3,2,1,0:T(8,128)(2,1)}, bf16[2,3,2,32,128]{4,3,2,1,0:T(8,128)(2,1)S(1)}, u32[]{:S(2)}) copy-start(bf16[2,3,2,32,128]{4,3,2,1,0:T(8,128)(2,1)S(1)} %collective-permute-done.8) | copy-start | bytes 294916
  34.7 3.5 %collective-permute-start.9 = (bf16[2,3,2,32,128]{4,3,2,1,0:T(8,128)(2,1)S(1)}, bf16[2,3,2,32,128]{4,3,2,1,0:T(8,128)(2,1)S(1)}, u32[]{:S(2)}, u32[]{:S(2)}) collective-permute-start(bf16[2,3,2,32,128]{4,3,2,1,0:T(8,128)(2,1)S(1)} %get-tuple-element.12), channel_id=1, source_target_pairs={{0,3},{2,1},{4,7},{6,5},{8,11},{10,9},{12,15},{14,13},{16,19},{18,... | collective-permute-start | bytes 294920 | tf_op jit(solution)/shard_map/ppermute | solution.py:297
  38.2 1.0 copy-start.4
  38.2 11.1 %collective-permute-start.5 = (bf16[18,2,16,32]{3,2,1,0:T(8,128)(2,1)}, bf16[18,2,16,32]{3,2,1,0:T(8,128)(2,1)S(1)}, u32[]{:S(2)}, u32[]{:S(2)}) collective-permute-start(bf16[18,2,16,32]{3,2,1,0:T(8,128)(2,1)} %pad_maximum_fusion), channel_id=1, source_target_pairs={{0,4},{4,8},{8,12},{12,16},{16,20},{20,24},{24,28},{28,32},{32,36}... | collective-permute-start | bytes 110600 | tf_op jit(solution)/shard_map/ppermute | solution.py:281
  42.1 33.8 %collective-permute-start.1 = (bf16[2,3,1,16,32,128]{5,4,3,2,1,0:T(8,128)(2,1)S(1)}, bf16[2,3,1,16,32,128]{5,4,3,2,1,0:T(8,128)(2,1)S(1)}, u32[]{:S(2)}, u32[]{:S(2)}) collective-permute-start(bf16[2,3,1,16,32,128]{5,4,3,2,1,0:T(8,128)(2,1)S(1)} %collective-permute-done.swap0_ref.own_up), channel_id=1, source_target_pairs={{0,124},{4,0},{8,4},{12,8},{16,12},{20,16},{24,20},{28,24},{32,28}... | collective-permute-start | bytes 2359304 | tf_op jit(solution)/shard_map/ppermute | solution.py:281
  48.4 27.5 %collective-permute-start.3 = (bf16[2,3,1,16,32,128]{5,4,3,2,1,0:T(8,128)(2,1)S(1)}, bf16[2,3,1,16,32,128]{5,4,3,2,1,0:T(8,128)(2,1)S(1)}, u32[]{:S(2)}, u32[]{:S(2)}) collective-permute-start(bf16[2,3,1,16,32,128]{5,4,3,2,1,0:T(8,128)(2,1)S(1)} %collective-permute-done.2.swap1_ref.own_down), channel_id=1, source_target_pairs={{0,4},{4,8},{8,12},{12,16},{16,20},{20,24},{24,28},{28,32},{32,36}... | collective-permute-start | bytes 2359304 | tf_op jit(solution)/shard_map/ppermute | solution.py:281

commit v3 on v2

v3 whole, which is shorter than its diff:
```python
import functools
import math

import jax
import jax.numpy as jnp
from jax import lax
from jax.experimental import pallas as pl
from jax.experimental.pallas import tpu as pltpu
from jax.sharding import PartitionSpec as P

BF16 = jnp.bfloat16
F32 = jnp.float32


def link_rows(entries, adjoint, width):
    rows = []
    for r in range(2):
        for a in range(3):
            pieces = []
            for q in range(2):
                for b in range(3):
                    first = ((b * 3 + a) if adjoint else (a * 3 + b)) * 2
                    if r == q:
                        pieces.append(entries[first])
                    elif (q == 1) == adjoint:
                        pieces.append(entries[first + 1])
                    else:
                        pieces.append(-entries[first + 1])
            lanes = sum(piece.shape[1] for piece in pieces)
            if lanes < width:
                pieces.append(jnp.zeros((pieces[0].shape[0], width - lanes), F32))
            rows.append(jnp.concatenate(pieces, axis=1))
    return rows


def site_masks(count_y, lanes):
    row = lax.broadcasted_iota(jnp.int32, (count_y, lanes), 0)
    lane = lax.broadcasted_iota(jnp.int32, (count_y, lanes), 1) % count_y
    same = jnp.where(lane == row, 1.0, 0.0).astype(BF16)
    above = jnp.where(lane == (row + 1) % count_y, 1.0, 0.0).astype(BF16)
    below = jnp.where(lane == (row + count_y - 1) % count_y, 1.0, 0.0).astype(BF16)
    return same, above, below


def spread(rows_ref, kind, row, mask):
    count_y, lanes = mask.shape
    blocks = []
    for ra in range(6):
        line = rows_ref[kind, ra, pl.ds(row, 1), :lanes]
        blocks.append(jnp.broadcast_to(line, (count_y, lanes)).astype(BF16) * mask)
    return jnp.concatenate(blocks, axis=0)


def write_phased(planes_of, table, x_at, table_first, blocks, out_ref, first, colour_stride):
    for b in range(3):
        for block in range(blocks):
            real = planes_of(0, b, block).T.astype(F32)
            imag = planes_of(1, b, block).T.astype(F32)
            nev, sites = real.shape
            at = first + b * colour_stride + block * sites
            put_phased(real, imag, table, x_at, table_first + block * sites, out_ref, at)


def put_phased(real, imag, table, x_at, table_at, out_ref, at):
    nev, sites = real.shape
    for p in range(2):
        cosine, sine = (values[2 * x_at + p : 2 * x_at + p + 1, pl.ds(table_at, sites)] for values in table)
        out_ref[2 * p * nev : (2 * p + 1) * nev, at : at + sites] = (cosine * real - sine * imag).astype(BF16)
        out_ref[(2 * p + 1) * nev : (2 * p + 2) * nev, at : at + sites] = (sine * real + cosine * imag).astype(BF16)


def put_displaced(out_ref, z, terms, count_y, nev):
    for r in range(2):
        for a in range(3):
            rows = terms[(r * 3 + a) * count_y : (r * 3 + a + 1) * count_y]
            out_ref[a, z, :, r * nev : (r + 1) * nev] = rows.astype(BF16)


def combine(products, nev):
    real, imag = [], []
    for p in range(2):
        rr = products[2 * p * nev : (2 * p + 1) * nev, :nev]
        ri = products[2 * p * nev : (2 * p + 1) * nev, nev:]
        ir = products[(2 * p + 1) * nev : (2 * p + 2) * nev, :nev]
        ii = products[(2 * p + 1) * nev : (2 * p + 2) * nev, nev:]
        real.append(rr + ii)
        imag.append(ri - ir)
    return real + imag


def by_owner(first, second):
    nev, lanes = first.shape
    a = first.reshape(nev // 8, 8, lanes)
    b = second.reshape(nev // 8, 8, lanes)
    upper = lax.broadcasted_iota(jnp.int32, a.shape, 1) < 4
    even = jnp.where(upper, a, pltpu.roll(b, 4, 1))
    odd = jnp.where(upper, pltpu.roll(a, 4, 1), b)
    return jnp.stack([even, odd], axis=1).reshape(nev // 4, 8, lanes)


def put_partials(out_ref, m, at, parts):
    real = by_owner(parts[0], parts[1])
    imag = by_owner(parts[2], parts[3])
    nev = parts[0].shape[1]
    out_ref[:, m, :, at * nev : (at + 1) * nev] = jnp.concatenate([real, imag], axis=1).astype(BF16)


def packed_plane(packed, q, b, z, count, count_z, count_y):
    first = ((q * 3 + b) * count_z + z) * count_y
    return packed[first : first + count * count_y]


def link_planes(nev, count_z, count_y):
    return -(-18 * count_y * count_z // (nev * count_y))


def packed_link(packed, k, e, count_z, count_y):
    nev = packed.shape[1]
    per_row = nev // count_y
    first = (6 * count_z + k * link_planes(nev, count_z, count_y)) * count_y + e // per_row * count_z
    lane = e % per_row * count_y
    return packed[first : first + count_z, lane : lane + count_y]


def copy_vectors(v_ref, out_ref, at):
    _, _, _, count_z, count_y, nev = v_ref.shape
    for i in range(6):
        out_ref[at, i * count_z : (i + 1) * count_z] = v_ref[i // 3, i % 3, 0]


def pack_up_kernel(core_ref, v_ref, low_ref, up_ref, low0_ref, low1_ref):
    copy_vectors(v_ref, up_ref, 0)
    for m in range(2):
        low0_ref[:, :, m] = low_ref[:, :, 2 * m, 0]
        low1_ref[:, :, m] = low_ref[:, :, 2 * m + 1, 0]


def pack_links_kernel(directions, core_ref, v_ref, link_ref, out_ref):
    _, _, _, count_z, count_y, nev = v_ref.shape
    copy_vectors(v_ref, out_ref, 0)
    per_row = nev // count_y
    planes = link_planes(nev, count_z, count_y)
    per_plane = count_y // count_z
    for k in range(directions):
        for at in range(planes * per_plane):
            held = [link_ref[k, e, 0] for e in range(at * per_row, min(18, (at + 1) * per_row))]
            held += [jnp.zeros((count_z, count_y), BF16)] * (per_row - len(held))
            first = at % per_plane * count_z
            out_ref[0, 6 * count_z + k * planes + at // per_plane, first : first + count_z] = jnp.concatenate(
                held, axis=1
            )


def yz_kernel(core_ref, v_ref, swap_ref, halo_ref, link_ref, cosine_ref, sine_ref, out_ref,
              rows, padded, phased, moved_y, moved_z, extra):
    core = core_ref[0]
    count_z, count_y, nev = v_ref.shape[3:]
    deep = 2 * count_z
    lanes = 6 * count_y
    sites = deep * count_y
    same, above, below = site_masks(count_y, lanes)
    mine = pl.multiple_of(core * count_z, count_z)
    theirs = pl.multiple_of((1 - core) * count_z, count_z)
    wide = rows.shape[3]
    lane = lax.broadcasted_iota(jnp.int32, (count_z, wide), 1) % count_y

    def fill_rows(link, start):
        at = pl.ds(start, count_z)
        link_y = [0.5 * link(1, e).astype(F32) for e in range(18)]
        for ra, line in enumerate(link_rows(link_y, False, wide)):
            rows[0, ra, at, :] = jnp.where(
                lane == 0, pltpu.roll(line, wide - (count_y - 1), 1), pltpu.roll(line, 1, 1)
            )
        for ra, line in enumerate(link_rows(link_y, True, wide)):
            rows[1, ra, at, :] = -line
        link_z = [0.5 * link(2, e).astype(F32) for e in range(18)]
        for ra, line in enumerate(link_rows(link_z, False, wide)):
            rows[2, ra, at, :] = line
        for ra, line in enumerate(link_rows(link_z, True, wide)):
            rows[3, ra, at, :] = -line

    padded[:, :, pl.ds(mine, count_z)] = v_ref[:, :, 0]
    padded[:, :, deep] = halo_ref[:, :, 0]
    swapped = swap_ref.at[0]
    for q in range(2):
        for b in range(3):
            block = packed_plane(swapped, q, b, 0, count_z, count_z, count_y)
            padded[q, b, pl.ds(theirs, count_z)] = block.reshape(count_z, count_y, nev)
    fill_rows(lambda k, e: packed_link(swapped, k, e, count_z, count_y), theirs)
    fill_rows(lambda k, e: link_ref[k, e, 0], mine)

    table = cosine_ref, sine_ref
    step = nev // count_y
    write_phased(
        lambda q, b, block: padded[q, b, block * step : (block + 1) * step].reshape(nev, nev),
        table, 0, 0, sites // nev, phased, 0, sites,
    )
    put_phased(
        padded[0, :, deep].reshape(3 * count_y, nev).T.astype(F32),
        padded[1, :, deep].reshape(3 * count_y, nev).T.astype(F32),
        table, 0, sites, phased, 3 * sites,
    )

    def forward(z):
        return jnp.dot(
            spread(rows, 2, z, same), padded[:, :, z + 1].reshape(lanes, nev), preferred_element_type=F32
        )

    def backward(z):
        return jnp.dot(
            spread(rows, 3, z - 1, same), padded[:, :, z - 1].reshape(lanes, nev), preferred_element_type=F32
        )

    for z in range(deep):
        in_y = spread(rows, 0, z, above) + spread(rows, 1, z, below)
        terms = jnp.dot(in_y, padded[:, :, z].reshape(lanes, nev), preferred_element_type=F32)
        put_displaced(moved_y, z, terms, count_y, nev)
        terms = forward(z)
        if z > 0:
            terms += backward(z)
        put_displaced(moved_z, z, terms, count_y, nev)
    terms = backward(deep)
    for r in range(2):
        half = terms[r * 3 * count_y : (r + 1) * 3 * count_y]
        extra[:, r * nev : (r + 1) * nev] = half.astype(BF16)

    products = jnp.dot(
        phased[:, : 3 * sites], moved_y[...].reshape(3 * sites, 2 * nev), preferred_element_type=F32
    )
    put_partials(out_ref, 0, 0, combine(products, nev))
    products = jnp.dot(
        phased[:, : 3 * sites], moved_z[...].reshape(3 * sites, 2 * nev), preferred_element_type=F32
    ) + jnp.dot(phased[:, 3 * sites : 3 * sites + 3 * count_y], extra[...], preferred_element_type=F32)
    put_partials(out_ref, 0, 1, combine(products, nev))


def x_terms(low, high, link, table, table_first, x_low, x_high, rows, phased, moved):
    count_z, lanes = rows.shape[2:]
    count_y = lanes // 6
    nev = low.shape[1]
    same = site_masks(count_y, lanes)[0]
    entries = [0.5 * link(e).astype(F32) for e in range(18)]
    for ra, line in enumerate(link_rows(entries, False, lanes)):
        rows[0, ra] = line
    for ra, line in enumerate(link_rows(entries, True, lanes)):
        rows[1, ra] = -line
    sites = count_z * count_y
    for vectors, x_at, first in ((low, x_low, 0), (high, x_high, 3 * sites)):
        write_phased(
            lambda q, b, block: vectors[(q * 3 + b) * sites + block * nev : (q * 3 + b) * sites + (block + 1) * nev],
            table, x_at, table_first, sites // nev, phased, first, sites,
        )

    def plane(vectors, z):
        return jnp.concatenate(
            [packed_plane(vectors, q, b, z, 1, count_z, count_y) for q in range(2) for b in range(3)], axis=0
        )

    for z in range(count_z):
        terms = jnp.dot(spread(rows, 0, z, same), plane(high, z), preferred_element_type=F32)
        put_displaced(moved.at[0], z, terms, count_y, nev)
        terms = jnp.dot(spread(rows, 1, z, same), plane(low, z), preferred_element_type=F32)
        put_displaced(moved.at[1], z, terms, count_y, nev)
    products = jnp.dot(phased[...], moved[...].reshape(6 * sites, 2 * nev), preferred_element_type=F32)
    return combine(products, nev)


def x_first_kernel(core_ref, own_up, recv_up, own_down, recv_down, link_ref, cosine_ref, sine_ref, out_ref, rows, phased, moved):
    count_z, count_y = link_ref.shape[3:]
    table = cosine_ref, sine_ref
    at_table = pl.multiple_of(core_ref[0] * (count_z * count_y), count_z * count_y)
    parts = x_terms(
        own_up.at[0], recv_up.at[0], lambda e: link_ref[0, e, 0], table, at_table, 0, 1, rows, phased, moved
    )
    for at, part in enumerate(parts):
        out_ref[0, at] = part
    received = recv_down.at[0]
    parts = x_terms(
        received, own_down.at[0], lambda e: packed_link(received, 0, e, count_z, count_y),
        table, at_table, 2, 0, rows, phased, moved,
    )
    for at, part in enumerate(parts):
        out_ref[1, at] = part


def x_last_kernel(core_ref, swap_ref, recv_up, recv_down, cosine_ref, sine_ref, before, _, out_ref, rows, phased, moved):
    count_z, lanes = rows.shape[2:]
    count_y = lanes // 6
    table = cosine_ref, sine_ref
    at_table = pl.multiple_of((1 - core_ref[0]) * (count_z * count_y), count_z * count_y)
    first = swap_ref.at[0]
    parts = x_terms(
        first, recv_up.at[0], lambda e: packed_link(first, 0, e, count_z, count_y),
        table, at_table, 0, 1, rows, phased, moved,
    )
    put_partials(out_ref, 0, 0, [part + before[0, at] for at, part in enumerate(parts)])
    received = recv_down.at[0]
    parts = x_terms(
        received, swap_ref.at[1], lambda e: packed_link(received, 0, e, count_z, count_y),
        table, at_table, 2, 0, rows, phased, moved,
    )
    put_partials(out_ref, 1, 0, [part + before[1, at] for at, part in enumerate(parts)])


def total_kernel(directions_ref, got_ref, out_ref):
    total = jnp.sum(got_ref[...].astype(F32), axis=0)
    nev = total.shape[1] // 3
    group = out_ref.shape[0]
    in_y, in_z, in_x = (total[:, k * nev : (k + 1) * nev] for k in range(3))
    for d in range(3):
        direction = directions_ref[d]
        chosen = jnp.where(direction == 0, in_x, jnp.where(direction == 1, in_y, in_z))
        for r in range(2):
            for p in range(2):
                for i in range(group):
                    row = (r * 2 + p) * group + i
                    out_ref[i, 0, p, r : r + 1, d * nev : (d + 1) * nev] = chosen[row : row + 1]


def fraction(component, coords, length):
    return jnp.mod(component * coords, length).astype(F32) / length


def table_kernel(lengths, deep, place_ref, momenta_ref, cosine_ref, sine_ref):
    length_x, length_z, length_y = lengths
    shape = cosine_ref.shape
    row = lax.broadcasted_iota(jnp.int32, shape, 0)
    lane = lax.broadcasted_iota(jnp.int32, shape, 1)
    x_at = row // 2
    x = place_ref[0] + jnp.where(x_at == 2, -1, x_at)
    z = place_ref[1] + jnp.minimum(lane // length_y, deep)
    y = lane % length_y
    first = row % 2 == 0
    m_x, m_y, m_z = (jnp.where(first, momenta_ref[0, i], momenta_ref[1, i]) for i in range(3))
    angle = 2.0 * math.pi * (
        (fraction(m_x, x, length_x) + fraction(m_y, y, length_y)) + fraction(m_z, z, length_z)
    )
    cosine_ref[...] = jnp.cos(angle)
    sine_ref[...] = jnp.sin(angle)


def shift(value, steps):
    count = lax.axis_size("ts")
    return lax.ppermute(value, "ts", [(source, (source + steps) % count) for source in range(count)])


def shards(eigvecs, gauge_links, momenta, directions):
    _, _, count_t, _, count_z, count_y, nev = eigvecs.shape
    vectors = eigvecs.reshape(2, 3, count_t, count_z, count_y, nev)
    links = gauge_links.reshape(3, 18, count_t, count_z, count_y)
    size_x, size_g = lax.axis_size("ts"), lax.axis_size("gz")
    x, g = lax.axis_index("ts"), lax.axis_index("gz")
    core, chip = g % 2, g // 2
    deep = 2 * count_z
    sites = count_z * count_y
    full = 6 * sites
    group = nev // size_x

    small = pl.CostEstimate(flops=1_000_000, bytes_accessed=100_000, transcendentals=0)
    limit = pltpu.CompilerParams(vmem_limit_bytes=48 * 1024 * 1024)
    in_vmem = pl.BlockSpec(memory_space=pltpu.VMEM)
    anywhere = pl.BlockSpec(memory_space=pl.ANY)
    planes = link_planes(nev, count_z, count_y)

    core_at = jnp.reshape(core, (1,)).astype(jnp.int32)
    one_time = (2, 3, 1, count_z, count_y, nev)

    def whole(shape):
        return pl.BlockSpec(shape, lambda i, core: (0,) * len(shape))

    lowest = (2, 3, 2, count_y, nev)
    up, low0, low1 = pl.pallas_call(
        pack_up_kernel,
        grid_spec=pltpu.PrefetchScalarGridSpec(
            num_scalar_prefetch=1,
            grid=(1,),
            in_specs=[
                pl.BlockSpec(one_time, lambda i, core: (0, 0, core[0], 0, 0, 0)),
                pl.BlockSpec((2, 3, count_t, 1, count_y, nev), lambda i, core: (0, 0, 0, 0, 0, 0)),
            ],
            out_specs=[whole((1, 6 * count_z, count_y, nev)), whole(lowest), whole(lowest)],
        ),
        out_shape=[
            jax.ShapeDtypeStruct((1, 6 * count_z, count_y, nev), BF16),
            jax.ShapeDtypeStruct(lowest, BF16),
            jax.ShapeDtypeStruct(lowest, BF16),
        ],
        compiler_params=limit,
        cost_estimate=small,
        name="pack_up",
    )(core_at, vectors, vectors)

    def pack_links(kept, times, first_of, core_at):
        shape = (times, 6 * count_z + kept * planes, count_y, nev)
        packed = pl.pallas_call(
            functools.partial(pack_links_kernel, kept),
            grid_spec=pltpu.PrefetchScalarGridSpec(
                num_scalar_prefetch=1,
                grid=(times,),
                in_specs=[
                    pl.BlockSpec(one_time, lambda m, core: (0, 0, first_of(core[0]) + 2 * m, 0, 0, 0)),
                    pl.BlockSpec(
                        (kept, 18, 1, count_z, count_y), lambda m, core: (0, 0, first_of(core[0]) + 2 * m, 0, 0)
                    ),
                ],
                out_specs=pl.BlockSpec((1,) + shape[1:], lambda m, core: (m, 0, 0, 0)),
            ),
            out_shape=jax.ShapeDtypeStruct(shape, BF16),
            compiler_params=limit,
            cost_estimate=small,
            name="pack_links",
        )(core_at, vectors, links)
        return packed.reshape(times, -1, nev)

    halo = lax.ppermute(low0, "gz", [(0, 2), (2, 0)]) + lax.ppermute(low1, "gz", [(0, 3), (2, 1)])
    up, halo = lax.optimization_barrier((up.reshape(1, full, nev), halo))
    recv_up = [shift(up, -1)]
    down = pack_links(1, 1, lambda core: core + 2, core_at)
    down, _ = lax.optimization_barrier((down, halo))
    recv_down = [shift(down, 1)]
    given = pack_links(3, 2, lambda core: 1 - core, core_at)
    swapped = lax.ppermute(given, "gz", [(0, 1), (1, 0), (2, 3), (3, 2)])
    recv_up.append(shift(swapped[:1, :full], -1))
    recv_down.append(shift(swapped[1:, : full + planes * count_y], 1))

    shape = jax.ShapeDtypeStruct((8, 2 * sites + nev), F32)
    table = pl.pallas_call(
        functools.partial(table_kernel, (size_x, count_z * size_g, count_y), deep),
        in_specs=[pl.BlockSpec(memory_space=pltpu.SMEM)] * 2,
        out_specs=[in_vmem] * 2,
        out_shape=[shape, shape],
        cost_estimate=small,
        name="phase_table",
    )(jnp.stack([x, chip * deep]).astype(jnp.int32), momenta)

    sent = pl.pallas_call(
        yz_kernel,
        grid_spec=pltpu.PrefetchScalarGridSpec(
            num_scalar_prefetch=1,
            grid=(2,),
            in_specs=[
                pl.BlockSpec((2, 3, 1, count_z, count_y, nev), lambda m, core: (0, 0, core[0] + 2 * m, 0, 0, 0)),
                pl.BlockSpec((1,) + swapped.shape[1:], lambda m, core: (m, 0, 0)),
                pl.BlockSpec((2, 3, 1, count_y, nev), lambda m, core: (0, 0, m, 0, 0)),
                pl.BlockSpec((3, 18, 1, count_z, count_y), lambda m, core: (0, 0, core[0] + 2 * m, 0, 0)),
                whole(shape.shape),
                whole(shape.shape),
            ],
            out_specs=pl.BlockSpec((size_x, 1, 4 * group, 2 * nev), lambda m, core: (0, m, 0, 0)),
            scratch_shapes=[
                pltpu.VMEM((4, 6, deep, 256), F32),
                pltpu.VMEM((2, 3, deep + 1, count_y, nev), BF16),
                pltpu.VMEM((4 * nev, 6 * sites + nev), BF16),
                pltpu.VMEM((3, deep, count_y, 2 * nev), BF16),
                pltpu.VMEM((3, deep, count_y, 2 * nev), BF16),
                pltpu.VMEM((3 * count_y, 2 * nev), BF16),
            ],
        ),
        out_shape=jax.ShapeDtypeStruct((size_x, 2, 4 * group, 3 * nev), BF16),
        compiler_params=limit,
        cost_estimate=small,
        name="yz_terms",
    )(core_at, vectors, swapped, halo, links, *table)

    core_at, _ = lax.optimization_barrier((core_at, sent))
    scratch = [
        pltpu.VMEM((2, 6, count_z, 6 * count_y), F32),
        pltpu.VMEM((4 * nev, 6 * sites), BF16),
        pltpu.VMEM((2, 3, count_z, count_y, 2 * nev), BF16),
    ]
    part = pl.pallas_call(
        x_first_kernel,
        grid_spec=pltpu.PrefetchScalarGridSpec(
            num_scalar_prefetch=1,
            grid=(1,),
            in_specs=[
                whole(up.shape),
                whole(up.shape),
                whole(down.shape),
                whole(down.shape),
                pl.BlockSpec((1, 18, 1, count_z, count_y), lambda i, core: (0, 0, core[0], 0, 0)),
                whole(shape.shape),
                whole(shape.shape),
            ],
            out_specs=whole((2, 4, nev, nev)),
            scratch_shapes=scratch,
        ),
        out_shape=jax.ShapeDtypeStruct((2, 4, nev, nev), F32),
        compiler_params=limit,
        cost_estimate=small,
        name="x_first",
    )(core_at, up, recv_up[0], down, recv_down[0], links, *table)
    sent = pl.pallas_call(
        x_last_kernel,
        grid=(1,),
        in_specs=[pl.BlockSpec(memory_space=pltpu.SMEM)] + [in_vmem] * 6 + [anywhere],
        out_specs=pl.BlockSpec((size_x, 2, 4 * group, nev), lambda i: (0, 0, 0, 2)),
        out_shape=jax.ShapeDtypeStruct(sent.shape, BF16),
        scratch_shapes=scratch,
        input_output_aliases={7: 0},
        compiler_params=limit,
        cost_estimate=small,
        name="x_last",
    )(core_at, swapped, recv_up[1], recv_down[1], *table, part, sent)

    pieces = sent.reshape(2 * size_x, 4 * group, 3 * nev)
    groups = [[(ts * 2 + h) * 2 + c for ts in range(size_x) for h in range(2)] for c in range(2)]
    got = lax.all_to_all(pieces, ("ts", "gz"), 0, 0, tiled=True, axis_index_groups=groups)
    return pl.pallas_call(
        total_kernel,
        in_specs=[pl.BlockSpec(memory_space=pltpu.SMEM), in_vmem],
        out_specs=in_vmem,
        out_shape=jax.ShapeDtypeStruct((group, 1, 2, 2, 3 * nev), F32),
        name="total",
    )(directions, got)


def solution(mesh):
    in_specs = (
        P(None, None, None, "ts", "gz", None, None),
        P(None, None, None, "ts", "gz", None),
        P(),
        P(),
    )
    out_specs = P("ts", "gz", None, None, None)
    return jax.shard_map(shards, mesh=mesh, in_specs=in_specs, out_specs=out_specs, check_vma=False)
```

time: 110 us -> 93 us (0.85); the launches traced: 108 us -> 92.4 us
  local copies, waits for them, and re-layouts: 13.1 us -> 6.49 us
  starting transfers between devices: 20.3 us -> 15.5 us
  Pallas kernels: 34.3 us -> 30.8 us
  blocking collectives: 24 us -> 26.9 us
  other arithmetic: 2.52 us -> 0.62 us
  waiting for transfers between devices: 13.3 us -> 12 us
    ppermute x5 -> x3, waiting for transfers between devices: 12.4 us -> 2.05 us  [the longest x1 1.55 us: shards(): lax.ppermute(low0, 'gz', [(0, 2), (2, 0)])]
    ppermute x5 -> x4, waiting for transfers between devices: 0.91 us -> 9.98 us  [shift(): lax.ppermute(value, 'ts', [(source, (source + steps) % count) for source...]
    pallas_call x1, Pallas kernels: 19.3 us -> 11.3 us  [shards(): pl.pallas_call(yz_kernel, grid_spec=pltpu.PrefetchScalarGridSpec(num_scal...]
    dynamic_slice x3 -> x0, local copies, waits for them, and re-layouts: 4.96 us -> none  [the longest x2 4.87 us: times(): return lax.dynamic_slice_in_dim(array, at, 1, axis)]
    ppermute x5 -> x4, starting transfers between devices: 13.8 us -> 9.12 us  [shift(): lax.ppermute(value, 'ts', [(source, (source + steps) % count) for source...]
    unnamed x14 -> x10, local copies, waits for them, and re-layouts: 0.03 us -> 4.6 us
    pallas_call x1 -> x5, Pallas kernels: 5.78 us -> 10.2 us  [the longest x1 7.13 us: shards(): pl.pallas_call(x_last_kernel, grid=(1,), in_specs=[pl.BlockSpec(memory_sp...]
    all_to_all x1, blocking collectives: 24 us -> 26.9 us  [shards(): lax.all_to_all(pieces, ('ts', 'gz'), 0, 0, tiled=True, axis_index_groups=...]
  transfers between devices with their start and end apart: 10 -> 7, of which waited for: 3 -> 4; matrix products, arithmetic and copies ran while one was open for 11% -> 3% of each run, Pallas kernels for 25% -> 23%
where the time goes in v3:
time: 93 us; the launch traced here: 92.4 us
  Pallas kernels  30.8 us (33%)
  blocking collectives  26.9 us (29%)
  starting transfers between devices  15.5 us (17%)
  waiting for transfers between devices  12 us (13%)
  local copies, waits for them, and re-layouts  6.49 us (7%)
    all_to_all x1, blocking collectives, shards(): lax.all_to_all(pieces, ('ts', 'gz'), 0, 0, tiled=True, axis_index_groups=...  26.9 us
    pallas_call x1, Pallas kernels, shards(): pl.pallas_call(yz_kernel, grid_spec=pltpu.PrefetchScalarGridSpec(num_scal...  11.3 us
    ppermute x4, waiting for transfers between devices, shift(): lax.ppermute(value, 'ts', [(source, (source + steps) % count) for source...  9.98 us
    ppermute x4, starting transfers between devices, shift(): lax.ppermute(value, 'ts', [(source, (source + steps) % count) for source...  9.12 us
    pallas_call x1, Pallas kernels, shards(): pl.pallas_call(x_first_kernel, grid_spec=pltpu.PrefetchScalarGridSpec(num...  7.31 us
    pallas_call x1, Pallas kernels, shards(): pl.pallas_call(x_last_kernel, grid=(1,), in_specs=[pl.BlockSpec(memory_sp...  7.13 us
    ppermute x1, starting transfers between devices, shards(): lax.ppermute(low0, 'gz', [(0, 2), (2, 0)])  5 us
    unnamed x10, local copies, waits for them, and re-layouts  4.6 us
  transfers between devices with their start and end apart: 7, of which 4 were waited for; matrix products, arithmetic and copies ran while one was open for 3% of the time, Pallas kernels for 23%

profile of v3, /device:TPU:0, one launch (start us, length us, event | category | flops | bytes accessed | tf_op | source)
XLA Modules:
  0.0 92.4 jit_solution(6388424583203490757)
XLA Ops:
  0.0 1.9 %copy-done = bf16[2,3,4,1,16,32,128]{6,5,4,3,2,1,0:T(8,128)(2,1)S(1)} copy-done((bf16[2,3,4,1,16,32,128]{6,5,4,3,2,1,0:T(8,128)(2,1)S(1)}, bf16[2,3,4,1,16,32,128]{6,5,4,3,2,1,0:T(8,128)(2,1)}, u32[]{:S(2)}) %copy-start) | copy-done | bytes 3145752
  1.9 1.2 %copy-done.1 = bf16[3,18,4,1,16,32]{5,4,3,2,1,0:T(8,128)(2,1)S(1)} copy-done((bf16[3,18,4,1,16,32]{5,4,3,2,1,0:T(8,128)(2,1)S(1)}, bf16[3,18,4,1,16,32]{5,4,3,2,1,0:T(8,128)(2,1)}, u32[]{:S(2)}) %copy-start.1) | copy-done | bytes 221208
  3.6 1.0 %pack_up.1 = (bf16[1,96,32,128]{3,2,1,0:T(8,128)(2,1)}, bf16[2,3,2,32,128]{4,3,2,1,0:T(8,128)(2,1)S(1)}, bf16[2,3,2,32,128]{4,3,2,1,0:T(8,128)(2,1)S(1)}) custom-call(s32[1]{0:T(128)} %bitcast.core_ref, bf16[2,3,4,16,32,128]{5,4,3,2,1,0:T(8,128)(2,1)S(1)} %bitcast.11, bf16[2,3,4,16,32,128]{5,4,3,2,1,0:T(8,128)(2,1)S(1)} %bitcast.12), custom_call_target="tpu_custom_call" | custom-call | flops 1000000 | bytes 100000 | tf_op jit(solution)/shard_map/pack_up/pallas_call | solution.py:372
  4.6 5.0 %collective-permute-start.1 = (bf16[2,3,2,32,128]{4,3,2,1,0:T(8,128)(2,1)S(1)}, bf16[2,3,2,32,128]{4,3,2,1,0:T(8,128)(2,1)S(1)}, u32[]{:S(2)}, u32[]{:S(2)}) collective-permute-start(bf16[2,3,2,32,128]{4,3,2,1,0:T(8,128)(2,1)S(1)} %get-tuple-element.15), channel_id=1, source_target_pairs={{0,2},{2,0},{4,6},{6,4},{8,10},{10,8},{12,14},{14,12},{16,18},{18,... | collective-permute-start | bytes 294920 | tf_op jit(solution)/shard_map/ppermute | solution.py:415
  9.6 1.3 %collective-permute-start.2 = (bf16[2,3,2,32,128]{4,3,2,1,0:T(8,128)(2,1)S(1)}, bf16[2,3,2,32,128]{4,3,2,1,0:T(8,128)(2,1)S(1)}, u32[]{:S(2)}, u32[]{:S(2)}) collective-permute-start(bf16[2,3,2,32,128]{4,3,2,1,0:T(8,128)(2,1)S(1)} %get-tuple-element.16), channel_id=1, source_target_pairs={{0,3},{2,1},{4,7},{6,5},{8,11},{10,9},{12,15},{14,13},{16,19},{18,... | collective-permute-start | bytes 294920 | tf_op jit(solution)/shard_map/ppermute | solution.py:415
  11.1 1.6 %collective-permute-done.1 = bf16[2,3,2,32,128]{4,3,2,1,0:T(8,128)(2,1)S(1)} collective-permute-done((bf16[2,3,2,32,128]{4,3,2,1,0:T(8,128)(2,1)S(1)}, bf16[2,3,2,32,128]{4,3,2,1,0:T(8,128)(2,1)S(1)}, u32[]{:S(2)}, u32[]{:S(2)}) %collective-permute-start.1) | collective-permute-done | bytes 98336 | tf_op jit(solution)/shard_map/ppermute | solution.py:415
  12.6 0.5 collective-permute-done.2
  13.2 1.6 %collective-permute-start.6 = (bf16[1,3168,128]{2,1,0:T(8,128)(2,1)S(1)}, bf16[1,3168,128]{2,1,0:T(8,128)(2,1)}, u32[]{:S(2)}, u32[]{:S(2)}) collective-permute-start(bf16[1,3168,128]{2,1,0:T(8,128)(2,1)S(1)} %bitcast.19), channel_id=1, source_target_pairs={{0,4},{4,8},{8,12},{12,16},{16,20},{20,24},{24,28},{28,32},{32,36}... | collective-permute-start | bytes 2433032 | tf_op jit(solution)/shard_map/ppermute | solution.py:344
  14.8 1.0 %slice.9 = bf16[1,3168,128]{2,1,0:T(8,128)(2,1)} slice(bf16[2,3360,128]{2,1,0:T(8,128)(2,1)S(1)} %collective-permute-done.swap_ref), slice={[1:2], [0:3168], [0:128]} | slice | bytes 1622016 | tf_op jit(solution)/shard_map/slice | solution.py:424
  15.8 1.6 %collective-permute-start.4 = (bf16[1,3168,128]{2,1,0:T(8,128)(2,1)}, bf16[1,3168,128]{2,1,0:T(8,128)(2,1)}, u32[]{:S(2)}, u32[]{:S(2)}) collective-permute-start(bf16[1,3168,128]{2,1,0:T(8,128)(2,1)} %slice.9), channel_id=1, source_target_pairs={{0,4},{4,8},{8,12},{12,16},{16,20},{20,24},{24,28},{28,32},{32,36}... | collective-permute-start | bytes 2433032 | tf_op jit(solution)/shard_map/ppermute | solution.py:344
  17.4 4.7 %collective-permute-start.5 = (bf16[1,3072,128]{2,1,0:T(8,128)(2,1)}, bf16[1,3072,128]{2,1,0:T(8,128)(2,1)}, u32[]{:S(2)}, u32[]{:S(2)}) collective-permute-start(bf16[1,3072,128]{2,1,0:T(8,128)(2,1)} %bitcast.4.own_up), channel_id=1, source_target_pairs={{0,124},{4,0},{8,4},{12,8},{16,12},{20,16},{24,20},{28,24},{32,28}... | collective-permute-start | bytes 2359304 | tf_op jit(solution)/shard_map/ppermute | solution.py:344
  22.0 0.9 %slice.8 = bf16[1,3072,128]{2,1,0:T(8,128)(2,1)} slice(bf16[2,3360,128]{2,1,0:T(8,128)(2,1)S(1)} %collective-permute-done.swap_ref), slice={[0:1], [0:3072], [0:128]} | slice | bytes 1572864 | tf_op jit(solution)/shard_map/slice | solution.py:423
  23.0 1.2 %collective-permute-start.3 = (bf16[1,3072,128]{2,1,0:T(8,128)(2,1)}, bf16[1,3072,128]{2,1,0:T(8,128)(2,1)}, u32[]{:S(2)}, u32[]{:S(2)}) collective-permute-start(bf16[1,3072,128]{2,1,0:T(8,128)(2,1)} %slice.8), channel_id=1, source_target_pairs={{0,124},{4,0},{8,4},{12,8},{16,12},{20,16},{24,20},{28,24},{32,28}... | collective-permute-start | bytes 2359304 | tf_op jit(solution)/shard_map/ppermute | solution.py:344
  24.2 0.6 pad_add_fusion.place_ref
  24.8 1.5 %phase_table.1 = (f32[8,1152]{1,0:T(8,128)}, f32[8,1152]{1,0:T(8,128)}) custom-call(s32[2]{0:T(128)} %pad_add_fusion.place_ref, s32[2,3]{1,0:T(2,128)} %momenta_ref.1), custom_call_target="tpu_custom_call" | custom-call | flops 1000000 | bytes 100000 | tf_op jit(solution)/shard_map/phase_table/pallas_call | solution.py:427
  26.3 0.8 copy-done.3
  27.1 0.8 copy-done.4
  27.9 11.3 %yz_terms.1._ = bf16[32,2,16,384]{3,2,1,0:T(8,128)(2,1)S(1)} custom-call(s32[1]{0:T(128)} %bitcast.core_ref, bf16[2,3,4,16,32,128]{5,4,3,2,1,0:T(8,128)(2,1)} %bitcast.9, bf16[2,3360,128]{2,1,0:T(8,128)(2,1)S(1)} %collective-permute-done.swap_ref, bf16[2,3,2,32,128]{4,3,2,1,0:T(8,128)(2,1)S(1)} %add.9.halo_ref, bf16[3,18,4,16,32]{4,3,2,1,0:T(8,128)(2,1)S(1)} %bitcast.16, ...), custom_call_target="tpu_custom_call" | custom-call | flops 1000000 | bytes 100000 | tf_op jit(solution)/shard_map/yz_terms/pallas_call | solution.py:436
  39.2 1.0 %collective-permute-done.5.recv_up = bf16[1,3072,128]{2,1,0:T(8,128)(2,1)} collective-permute-done((bf16[1,3072,128]{2,1,0:T(8,128)(2,1)}, bf16[1,3072,128]{2,1,0:T(8,128)(2,1)}, u32[]{:S(2)}, u32[]{:S(2)}) %collective-permute-start.5) | collective-permute-done | bytes 786464 | tf_op jit(solution)/shard_map/ppermute | solution.py:344
  40.2 7.3 %x_first.1.before = f32[2,4,128,128]{3,2,1,0:T(8,128)S(1)} custom-call(s32[1]{0:T(128)} %bitcast.core_ref, bf16[1,3072,128]{2,1,0:T(8,128)(2,1)} %bitcast.4.own_up, bf16[1,3072,128]{2,1,0:T(8,128)(2,1)} %collective-permute-done.5.recv_up, bf16[1,3168,128]{2,1,0:T(8,128)(2,1)S(1)} %bitcast.20, bf16[1,3168,128]{2,1,0:T(8,128)(2,1)} %collective-permute-done.6.recv_down, ...), custom_call_target="tpu_custom_call" | custom-call | flops 1000000 | bytes 100000 | tf_op jit(solution)/shard_map/x_first/pallas_call | solution.py:471
  47.6 8.9 %collective-permute-done.3.recv_up = bf16[1,3072,128]{2,1,0:T(8,128)(2,1)} collective-permute-done((bf16[1,3072,128]{2,1,0:T(8,128)(2,1)}, bf16[1,3072,128]{2,1,0:T(8,128)(2,1)}, u32[]{:S(2)}, u32[]{:S(2)}) %collective-permute-start.3) | collective-permute-done | bytes 786464 | tf_op jit(solution)/shard_map/ppermute | solution.py:344
  56.5 7.1 %x_last.1 = bf16[32,2,16,384]{3,2,1,0:T(8,128)(2,1)S(1)} custom-call(s32[1]{0:T(128)} %bitcast.core_ref, bf16[2,3360,128]{2,1,0:T(8,128)(2,1)S(1)} %collective-permute-done.swap_ref, bf16[1,3072,128]{2,1,0:T(8,128)(2,1)} %collective-permute-done.3.recv_up, bf16[1,3168,128]{2,1,0:T(8,128)(2,1)} %collective-permute-done.4.recv_down, ...), custom_call_target="tpu_custom_call", output_to_operand_aliasing={{}: (7, {})} | custom-call | flops 1000000 | bytes 100000 | tf_op jit(solution)/shard_map/x_last/pallas_call | solution.py:493
  63.6 26.9 %all_to_all.5.got_ref = bf16[64,16,384]{2,1,0:T(8,128)(2,1)} all-to-all(bf16[64,16,384]{2,1,0:T(8,128)(2,1)S(1)} %bitcast.18), channel_id=1, replica_groups={{0,2,4,6,8,10,12,14,16,18,20,22,24,26,28,30,32,34,36,38,40,42,44,46,48,..., dimensions={0} | all-to-all | bytes 1572864 | tf_op jit(solution)/shard_map/all_to_all | solution.py:508
  90.6 1.9 %total.1 = f32[4,1,2,2,384]{4,3,2,1,0:T(2,128)} custom-call(s32[3]{0:T(128)} %directions_ref.1, bf16[64,16,384]{2,1,0:T(8,128)(2,1)} %all_to_all.5.got_ref), custom_call_target="tpu_custom_call" | custom-call | tf_op jit(solution)/shard_map/total/pallas_call | solution.py:509
  (13 shorter events, 0.7 us)
Async XLA Ops:
  0.0 1.9 %copy-start = (bf16[2,3,4,1,16,32,128]{6,5,4,3,2,1,0:T(8,128)(2,1)S(1)}, bf16[2,3,4,1,16,32,128]{6,5,4,3,2,1,0:T(8,128)(2,1)}, u32[]{:S(2)}) copy-start(bf16[2,3,4,1,16,32,128]{6,5,4,3,2,1,0:T(8,128)(2,1)} %param.4) | copy-start | bytes 9437188
  1.9 1.2 %copy-start.1 = (bf16[3,18,4,1,16,32]{5,4,3,2,1,0:T(8,128)(2,1)S(1)}, bf16[3,18,4,1,16,32]{5,4,3,2,1,0:T(8,128)(2,1)}, u32[]{:S(2)}) copy-start(bf16[3,18,4,1,16,32]{5,4,3,2,1,0:T(8,128)(2,1)} %param.5) | copy-start | bytes 663556
  3.5 7.4 %copy-start.2 = (bf16[3,18,4,1,16,32]{5,4,3,2,1,0:T(8,128)(2,1)S(1)}, bf16[3,18,4,1,16,32]{5,4,3,2,1,0:T(8,128)(2,1)}, u32[]{:S(2)}) copy-start(bf16[3,18,4,1,16,32]{5,4,3,2,1,0:T(8,128)(2,1)} %param.5) | copy-start | bytes 663556
  3.5 11.3 %collective-permute-start = (bf16[2,3360,128]{2,1,0:T(8,128)(2,1)S(1)}, bf16[2,3360,128]{2,1,0:T(8,128)(2,1)S(1)}, u32[]{:S(2)}, u32[]{:S(2)}) collective-permute-start(bf16[2,3360,128]{2,1,0:T(8,128)(2,1)S(1)} %bitcast.21), channel_id=1, source_target_pairs={{0,1},{1,0},{2,3},{3,2},{4,5},{5,4},{6,7},{7,6},{8,9},{9,8},{10,11... | collective-permute-start | bytes 5160968 | tf_op jit(solution)/shard_map/ppermute | solution.py:422
  4.6 8.0 %collective-permute-start.1 = (bf16[2,3,2,32,128]{4,3,2,1,0:T(8,128)(2,1)S(1)}, bf16[2,3,2,32,128]{4,3,2,1,0:T(8,128)(2,1)S(1)}, u32[]{:S(2)}, u32[]{:S(2)}) collective-permute-start(bf16[2,3,2,32,128]{4,3,2,1,0:T(8,128)(2,1)S(1)} %get-tuple-element.15), channel_id=1, source_target_pairs={{0,2},{2,0},{4,6},{6,4},{8,10},{10,8},{12,14},{14,12},{16,18},{18,... | collective-permute-start | bytes 294920 | tf_op jit(solution)/shard_map/ppermute | solution.py:415
  9.6 3.5 %collective-permute-start.2 = (bf16[2,3,2,32,128]{4,3,2,1,0:T(8,128)(2,1)S(1)}, bf16[2,3,2,32,128]{4,3,2,1,0:T(8,128)(2,1)S(1)}, u32[]{:S(2)}, u32[]{:S(2)}) collective-permute-start(bf16[2,3,2,32,128]{4,3,2,1,0:T(8,128)(2,1)S(1)} %get-tuple-element.16), channel_id=1, source_target_pairs={{0,3},{2,1},{4,7},{6,5},{8,11},{10,9},{12,15},{14,13},{16,19},{18,... | collective-permute-start | bytes 294920 | tf_op jit(solution)/shard_map/ppermute | solution.py:415
  13.2 27.1 %collective-permute-start.6 = (bf16[1,3168,128]{2,1,0:T(8,128)(2,1)S(1)}, bf16[1,3168,128]{2,1,0:T(8,128)(2,1)}, u32[]{:S(2)}, u32[]{:S(2)}) collective-permute-start(bf16[1,3168,128]{2,1,0:T(8,128)(2,1)S(1)} %bitcast.19), channel_id=1, source_target_pairs={{0,4},{4,8},{8,12},{12,16},{16,20},{20,24},{24,28},{28,32},{32,36}... | collective-permute-start | bytes 2433032 | tf_op jit(solution)/shard_map/ppermute | solution.py:344
  15.8 40.7 %collective-permute-start.4 = (bf16[1,3168,128]{2,1,0:T(8,128)(2,1)}, bf16[1,3168,128]{2,1,0:T(8,128)(2,1)}, u32[]{:S(2)}, u32[]{:S(2)}) collective-permute-start(bf16[1,3168,128]{2,1,0:T(8,128)(2,1)} %slice.9), channel_id=1, source_target_pairs={{0,4},{4,8},{8,12},{12,16},{16,20},{20,24},{24,28},{28,32},{32,36}... | collective-permute-start | bytes 2433032 | tf_op jit(solution)/shard_map/ppermute | solution.py:344
  17.4 22.9 %collective-permute-start.5 = (bf16[1,3072,128]{2,1,0:T(8,128)(2,1)}, bf16[1,3072,128]{2,1,0:T(8,128)(2,1)}, u32[]{:S(2)}, u32[]{:S(2)}) collective-permute-start(bf16[1,3072,128]{2,1,0:T(8,128)(2,1)} %bitcast.4.own_up), channel_id=1, source_target_pairs={{0,124},{4,0},{8,4},{12,8},{16,12},{20,16},{24,20},{28,24},{32,28}... | collective-permute-start | bytes 2359304 | tf_op jit(solution)/shard_map/ppermute | solution.py:344
  23.0 33.5 %collective-permute-start.3 = (bf16[1,3072,128]{2,1,0:T(8,128)(2,1)}, bf16[1,3072,128]{2,1,0:T(8,128)(2,1)}, u32[]{:S(2)}, u32[]{:S(2)}) collective-permute-start(bf16[1,3072,128]{2,1,0:T(8,128)(2,1)} %slice.8), channel_id=1, source_target_pairs={{0,124},{4,0},{8,4},{12,8},{16,12},{20,16},{24,20},{28,24},{32,28}... | collective-permute-start | bytes 2359304 | tf_op jit(solution)/shard_map/ppermute | solution.py:344
  26.3 0.8 copy-start.3
  27.1 0.8 copy-start.4

commit v4 on v3

v4 whole, which is shorter than its diff:
```python
import functools
import math

import jax
import jax.numpy as jnp
from jax import lax
from jax.experimental import pallas as pl
from jax.experimental.pallas import tpu as pltpu
from jax.sharding import PartitionSpec as P

BF16 = jnp.bfloat16
F32 = jnp.float32


def link_rows(entries, adjoint, width):
    rows = []
    for r in range(2):
        for a in range(3):
            pieces = []
            for q in range(2):
                for b in range(3):
                    first = ((b * 3 + a) if adjoint else (a * 3 + b)) * 2
                    if r == q:
                        pieces.append(entries[first])
                    elif (q == 1) == adjoint:
                        pieces.append(entries[first + 1])
                    else:
                        pieces.append(-entries[first + 1])
            lanes = sum(piece.shape[1] for piece in pieces)
            if lanes < width:
                pieces.append(jnp.zeros((pieces[0].shape[0], width - lanes), F32))
            rows.append(jnp.concatenate(pieces, axis=1))
    return rows


def site_masks(count_y, lanes):
    row = lax.broadcasted_iota(jnp.int32, (count_y, lanes), 0)
    lane = lax.broadcasted_iota(jnp.int32, (count_y, lanes), 1) % count_y
    same = jnp.where(lane == row, 1.0, 0.0).astype(BF16)
    above = jnp.where(lane == (row + 1) % count_y, 1.0, 0.0).astype(BF16)
    below = jnp.where(lane == (row + count_y - 1) % count_y, 1.0, 0.0).astype(BF16)
    return same, above, below


def spread(rows_ref, kind, row, mask):
    count_y, lanes = mask.shape
    blocks = []
    for ra in range(6):
        line = rows_ref[kind, ra, pl.ds(row, 1), :lanes]
        blocks.append(jnp.broadcast_to(line, (count_y, lanes)).astype(BF16) * mask)
    return jnp.concatenate(blocks, axis=0)


def fraction(component, coords, length):
    return jnp.mod(component * coords, length).astype(F32) / length


def fill_table(lengths, deep, place_ref, momenta_ref, table_ref):
    length_x, length_z, length_y = lengths
    rows = table_ref.shape[0] // 2
    shape = rows, table_ref.shape[1]
    row = lax.broadcasted_iota(jnp.int32, shape, 0)
    lane = lax.broadcasted_iota(jnp.int32, shape, 1)
    x_at = row // 2
    x = place_ref[1] + jnp.where(x_at == 2, -1, x_at)
    plane = lane // length_y
    above = deep + (shape[1] // length_y - deep) // 2
    z = place_ref[2] + jnp.where(plane < deep, plane, jnp.where(plane < above, deep, deep - 1))
    y = lane % length_y
    first = row % 2 == 0
    m_x, m_y, m_z = (jnp.where(first, momenta_ref[0, i], momenta_ref[1, i]) for i in range(3))
    angle = 2.0 * math.pi * (
        (fraction(m_x, x, length_x) + fraction(m_y, y, length_y)) + fraction(m_z, z, length_z)
    )
    table_ref[:rows] = jnp.cos(angle)
    table_ref[rows:] = jnp.sin(angle)


def write_phased(planes_of, table, x_at, table_first, blocks, out_ref, first, colour_stride):
    for b in range(3):
        for block in range(blocks):
            real = planes_of(0, b, block).T.astype(F32)
            imag = planes_of(1, b, block).T.astype(F32)
            nev, sites = real.shape
            at = first + b * colour_stride + block * sites
            put_phased(real, imag, table, x_at, table_first + block * sites, out_ref, at)


def put_phased(real, imag, table, x_at, table_at, out_ref, at):
    nev, sites = real.shape
    for p in range(2):
        cosine, sine = (table[pl.ds(half + 2 * x_at + p, 1), pl.ds(table_at, sites)] for half in (0, table.shape[0] // 2))
        out_ref[2 * p * nev : (2 * p + 1) * nev, at : at + sites] = (cosine * real - sine * imag).astype(BF16)
        out_ref[(2 * p + 1) * nev : (2 * p + 2) * nev, at : at + sites] = (sine * real + cosine * imag).astype(BF16)


def put_displaced(out_ref, z, terms, count_y, nev):
    for r in range(2):
        for a in range(3):
            rows = terms[(r * 3 + a) * count_y : (r * 3 + a + 1) * count_y]
            out_ref[a, z, :, r * nev : (r + 1) * nev] = rows.astype(BF16)


def combine(products, nev):
    real, imag = [], []
    for p in range(2):
        rr = products[2 * p * nev : (2 * p + 1) * nev, :nev]
        ri = products[2 * p * nev : (2 * p + 1) * nev, nev:]
        ir = products[(2 * p + 1) * nev : (2 * p + 2) * nev, :nev]
        ii = products[(2 * p + 1) * nev : (2 * p + 2) * nev, nev:]
        real.append(rr + ii)
        imag.append(ri - ir)
    return real + imag


def by_owner(first, second):
    nev, lanes = first.shape
    a = first.reshape(nev // 8, 8, lanes)
    b = second.reshape(nev // 8, 8, lanes)
    upper = lax.broadcasted_iota(jnp.int32, a.shape, 1) < 4
    even = jnp.where(upper, a, pltpu.roll(b, 4, 1))
    odd = jnp.where(upper, pltpu.roll(a, 4, 1), b)
    return jnp.stack([even, odd], axis=1).reshape(nev // 4, 8, lanes)


def partial_rows(parts):
    return jnp.concatenate([by_owner(parts[0], parts[1]), by_owner(parts[2], parts[3])], axis=1)


def packed_plane(packed, depth, q, b, z, count, count_y):
    first = ((q * 3 + b) * depth + z) * count_y
    return packed[first : first + count * count_y]


def link_planes(nev, count_z, count_y):
    return -(-18 * count_y * count_z // (nev * count_y))


def packed_link(packed, depth, k, e, count_z, count_y):
    nev = packed.shape[1]
    per_row = nev // count_y
    first = (6 * depth + k * link_planes(nev, count_z, count_y)) * count_y + e // per_row * count_z
    lane = e % per_row * count_y
    return packed[first : first + count_z, lane : lane + count_y]


def pack_kernel(times, core_ref, v_ref, link_ref, *out_refs):
    _, _, _, count_z, count_y, nev = v_ref.shape
    per_row = nev // count_y
    planes = link_planes(nev, count_z, count_y)
    per_plane = count_y // count_z
    step = pl.program_id(0)

    def put(out_ref, directions):
        for i in range(6):
            out_ref[0, i * count_z : (i + 1) * count_z] = v_ref[i // 3, i % 3, 0]
        for k in range(directions):
            for at in range(planes * per_plane):
                held = [link_ref[k, e, 0] for e in range(at * per_row, min(18, (at + 1) * per_row))]
                held += [jnp.zeros((count_z, count_y), BF16)] * (per_row - len(held))
                plane = 6 * count_z + k * planes + at // per_plane
                first = at % per_plane * count_z
                out_ref[0, plane, first : first + count_z] = jnp.concatenate(held, axis=1)

    if times == 1:
        pl.when(step == 0)(lambda: put(out_refs[0], 0))
        pl.when(step == 1)(lambda: put(out_refs[1], 1))
    else:
        put(out_refs[0], 3)


def split(swap_ref, start, count_z, up_ref, down_ref):
    depth = up_ref.shape[1] // 6
    for i in range(6):
        first = i * count_z + start
        up_ref[0, i * depth : (i + 1) * depth] = swap_ref[0, first : first + depth]
        down_ref[0, i * depth : (i + 1) * depth] = swap_ref[1, first : first + depth]
    planes = down_ref.shape[1] - 6 * depth
    down_ref[0, 6 * depth :] = swap_ref[1, 6 * count_z : 6 * count_z + planes]


def split_first_kernel(count_z, core_ref, swap_ref, low_ref, up_ref, down_ref, lowest_ref):
    split(swap_ref, 0, count_z, up_ref, down_ref)
    core = core_ref[0]
    for m in range(2):
        for i in range(6):
            own = low_ref[i // 3, i % 3, core + 2 * m, 0]
            lowest_ref[m, i] = jnp.where(core == 0, own, swap_ref[m, i * count_z])


def split_last_kernel(count_z, core_ref, swap_ref, up_ref, down_ref):
    split(swap_ref, count_z - up_ref.shape[1] // 6, count_z, up_ref, down_ref)


def yz_kernel(lengths, place_ref, v_ref, swap_ref, link_ref, momenta_ref, out_ref, top_ref, line_ref, table_ref,
              rows, padded, phased, moved_y, moved_z):
    core = place_ref[0]
    count_z, count_y, nev = v_ref.shape[3:]
    deep = 2 * count_z
    lanes = 6 * count_y
    sites = deep * count_y
    same, above, below = site_masks(count_y, lanes)
    mine = pl.multiple_of(core * count_z, count_z)
    theirs = pl.multiple_of((1 - core) * count_z, count_z)
    wide = rows.shape[3]
    lane = lax.broadcasted_iota(jnp.int32, (count_z, wide), 1) % count_y

    def fill_rows(link, start):
        at = pl.ds(start, count_z)
        link_y = [0.5 * link(1, e).astype(F32) for e in range(18)]
        for ra, line in enumerate(link_rows(link_y, False, wide)):
            rows[0, ra, at, :] = jnp.where(
                lane == 0, pltpu.roll(line, wide - (count_y - 1), 1), pltpu.roll(line, 1, 1)
            )
        for ra, line in enumerate(link_rows(link_y, True, wide)):
            rows[1, ra, at, :] = -line
        link_z = [0.5 * link(2, e).astype(F32) for e in range(18)]
        for ra, line in enumerate(link_rows(link_z, False, wide)):
            rows[2, ra, at, :] = line
        for ra, line in enumerate(link_rows(link_z, True, wide)):
            rows[3, ra, at, :] = -line

    padded[:, :, pl.ds(mine, count_z)] = v_ref[:, :, 0]
    swapped = swap_ref.at[0]
    for q in range(2):
        for b in range(3):
            block = packed_plane(swapped, count_z, q, b, 0, count_z, count_y)
            padded[q, b, pl.ds(theirs, count_z)] = block.reshape(count_z, count_y, nev)
    fill_rows(lambda k, e: packed_link(swapped, count_z, k, e, count_z, count_y), theirs)
    fill_rows(lambda k, e: link_ref[k, e, 0], mine)

    pl.when(pl.program_id(0) == 0)(lambda: fill_table(lengths, deep, place_ref, momenta_ref, table_ref))
    table = table_ref
    step = nev // count_y
    write_phased(
        lambda q, b, block: padded[q, b, block * step : (block + 1) * step].reshape(nev, nev),
        table, 0, 0, sites // nev, phased, 0, sites,
    )
    def forward(z):
        return jnp.dot(
            spread(rows, 2, z, same), padded[:, :, z + 1].reshape(lanes, nev), preferred_element_type=F32
        )

    def backward(z):
        return jnp.dot(
            spread(rows, 3, z - 1, same), padded[:, :, z - 1].reshape(lanes, nev), preferred_element_type=F32
        )

    for z in range(deep):
        in_y = spread(rows, 0, z, above) + spread(rows, 1, z, below)
        terms = jnp.dot(in_y, padded[:, :, z].reshape(lanes, nev), preferred_element_type=F32)
        put_displaced(moved_y, z, terms, count_y, nev)
        terms = forward(z) if z + 1 < deep else 0.0
        if z > 0:
            terms += backward(z)
        put_displaced(moved_z, z, terms, count_y, nev)
    for at, moved in enumerate((moved_y, moved_z)):
        products = jnp.dot(phased[...], moved[...].reshape(3 * sites, 2 * nev), preferred_element_type=F32)
        out_ref[:, 0, :, at * nev : (at + 1) * nev] = partial_rows(combine(products, nev)).astype(BF16)
    top_ref[0] = padded[:, :, deep - 1].reshape(lanes, nev)
    for kind in range(2):
        for ra in range(6):
            line_ref[0, kind * 8 + ra : kind * 8 + ra + 1] = rows[2 + kind, ra, deep - 1 : deep]


def x_terms(low, high, link, table, table_first, x_low, x_high, rows, phased, moved):
    held_z, lanes = rows.shape[2:]
    count_z, count_y = moved.shape[2:4]
    nev = low[0].shape[1]
    same = site_masks(count_y, lanes)[0]
    entries = [0.5 * link(e).astype(F32) for e in range(18)]
    for ra, line in enumerate(link_rows(entries, False, lanes)):
        rows[0, ra] = line
    for ra, line in enumerate(link_rows(entries, True, lanes)):
        rows[1, ra] = -line
    sites = count_z * count_y
    step = nev // count_y
    for (vectors, depth, z), x_at, first in ((low, x_low, 0), (high, x_high, 3 * sites)):
        write_phased(
            lambda q, b, block: packed_plane(vectors, depth, q, b, z + block * step, step, count_y),
            table, x_at, table_first, sites // nev, phased, first, sites,
        )

    def plane(held, at):
        vectors, depth, z = held
        return jnp.concatenate(
            [packed_plane(vectors, depth, q, b, z + at, 1, count_y) for q in range(2) for b in range(3)], axis=0
        )

    first = max(low[2], high[2])
    for z in range(count_z):
        terms = jnp.dot(spread(rows, 0, first + z, same), plane(high, z), preferred_element_type=F32)
        put_displaced(moved.at[0], z, terms, count_y, nev)
        terms = jnp.dot(spread(rows, 1, first + z, same), plane(low, z), preferred_element_type=F32)
        put_displaced(moved.at[1], z, terms, count_y, nev)
    products = jnp.dot(phased[...], moved[...].reshape(6 * sites, 2 * nev), preferred_element_type=F32)
    return combine(products, nev)


def x_first_kernel(core_ref, own_up, recv_up, own_down, recv_down, link_ref, table, out_ref, *scratch):
    count_z, count_y = link_ref.shape[3:]
    at_table = pl.multiple_of(core_ref[0] * (count_z * count_y), count_z * count_y)
    received = recv_down.at[0]
    up = x_terms(
        (own_up.at[0], count_z, 0), (recv_up.at[0], count_z, 0), lambda e: link_ref[0, e, 0],
        table, at_table, 0, 1, *scratch,
    )
    down = x_terms(
        (received, count_z, 0), (own_down.at[0], count_z, 0),
        lambda e: packed_link(received, count_z, 0, e, count_z, count_y),
        table, at_table, 2, 0, *scratch,
    )
    for m, parts in enumerate((up, down)):
        for at, part in enumerate(parts):
            out_ref[m, at] = part


def x_part(last, core_ref, swap_ref, recv_up, recv_down, table, rows, phased, moved):
    held_z = rows.shape[2]
    depth, count_y = moved.shape[2:4]
    first = held_z - depth if last else 0
    nev = swap_ref.shape[2]
    at_table = pl.multiple_of((1 - core_ref[0]) * (held_z * count_y) + first * count_y, nev)
    own_up, own_down, received = swap_ref.at[0], swap_ref.at[1], recv_down.at[0]
    up = x_terms(
        (own_up, held_z, first), (recv_up.at[0], depth, 0),
        lambda e: packed_link(own_up, held_z, 0, e, held_z, count_y),
        table, at_table, 0, 1, rows, phased, moved,
    )
    down = x_terms(
        (received, depth, 0), (own_down, held_z, first),
        lambda e: packed_link(received, depth, 0, e, held_z, count_y),
        table, at_table, 2, 0, rows, phased, moved,
    )
    return up, down


def x_middle_kernel(core_ref, swap_ref, recv_up, recv_down, table, before, out_ref, *scratch):
    both = x_part(False, core_ref, swap_ref, recv_up, recv_down, table, *scratch)
    for m, parts in enumerate(both):
        for at, part in enumerate(parts):
            out_ref[m, at] = part + before[m, at]


def boundary(top, halo, lines, table, edge):
    lanes, nev = top.shape
    count_y = lanes // 6
    wide = lanes // 2
    same = site_masks(count_y, lanes)[0]

    def matrix(kind):
        blocks = []
        for ra in range(6):
            line = lines[kind * 8 + ra : kind * 8 + ra + 1, :lanes]
            blocks.append(jnp.broadcast_to(line, (count_y, lanes)).astype(BF16) * same)
        return jnp.concatenate(blocks, axis=0)

    products = 0.0
    for at, (phased, moved, kind) in enumerate(((top, halo, 0), (halo, top, 1))):
        put_phased(
            phased[:wide].T.astype(F32), phased[wide:].T.astype(F32), table, 0,
            table.shape[1] - (at + 1) * nev, edge, at * nev,
        )
        terms = jnp.dot(matrix(kind), moved[...], preferred_element_type=F32).astype(BF16)
        displaced = jnp.concatenate([terms[:wide], terms[wide:]], axis=1)
        products += jnp.dot(edge[:, at * nev : at * nev + wide], displaced, preferred_element_type=F32)
    return combine(products, nev)


def x_last_kernel(core_ref, swap_ref, recv_up, recv_down, table, before, sent_ref,
                  top_ref, halo_ref, line_ref, out_ref, rows, phased, moved, edge):
    nev = before.shape[3]
    out_ref[:, :, :, :nev] = sent_ref[:, :, :, :nev]
    for m in range(2):
        above = partial_rows(boundary(top_ref.at[m], halo_ref.at[m], line_ref.at[m], table, edge))
        out_ref[:, m, :, nev : 2 * nev] = (sent_ref[:, m, :, nev:].astype(F32) + above).astype(BF16)
    both = x_part(True, core_ref, swap_ref, recv_up, recv_down, table, rows, phased, moved)
    for m, parts in enumerate(both):
        parts = [part + before[m, at] for at, part in enumerate(parts)]
        out_ref[:, m, :, 2 * nev :] = partial_rows(parts).astype(BF16)


def total_kernel(directions_ref, got_ref, out_ref):
    total = jnp.sum(got_ref[...].astype(F32), axis=0)
    nev = total.shape[1] // 3
    group = out_ref.shape[0]
    in_y, in_z, in_x = (total[:, k * nev : (k + 1) * nev] for k in range(3))
    for d in range(3):
        direction = directions_ref[d]
        chosen = jnp.where(direction == 0, in_x, jnp.where(direction == 1, in_y, in_z))
        for r in range(2):
            for p in range(2):
                for i in range(group):
                    row = (r * 2 + p) * group + i
                    out_ref[i, 0, p, r : r + 1, d * nev : (d + 1) * nev] = chosen[row : row + 1]


def shift(value, steps):
    count = lax.axis_size("ts")
    return lax.ppermute(value, "ts", [(source, (source + steps) % count) for source in range(count)])


def shards(eigvecs, gauge_links, momenta, directions):
    _, _, count_t, _, count_z, count_y, nev = eigvecs.shape
    vectors = eigvecs.reshape(2, 3, count_t, count_z, count_y, nev)
    links = gauge_links.reshape(3, 18, count_t, count_z, count_y)
    size_x, size_g = lax.axis_size("ts"), lax.axis_size("gz")
    x, g = lax.axis_index("ts"), lax.axis_index("gz")
    core, chip = g % 2, g // 2
    deep = 2 * count_z
    sites = count_z * count_y
    group = nev // size_x

    small = pl.CostEstimate(flops=1_000_000, bytes_accessed=100_000, transcendentals=0)
    limit = pltpu.CompilerParams(vmem_limit_bytes=28 * 1024 * 1024)
    in_vmem = pl.BlockSpec(memory_space=pltpu.VMEM)
    in_smem = pl.BlockSpec(memory_space=pltpu.SMEM)
    planes = link_planes(nev, count_z, count_y)

    core_at = jnp.reshape(core, (1,)).astype(jnp.int32)
    one_time = (2, 3, 1, count_z, count_y, nev)

    def whole(shape):
        return pl.BlockSpec(shape, lambda i, core: (0,) * len(shape))

    def packed(times, depth, directions):
        return times, 6 * depth + directions * planes, count_y, nev

    def arrays(*shapes):
        return [jax.ShapeDtypeStruct(array, BF16) for array in shapes]

    def rows(array):
        return array.reshape(array.shape[0], -1, nev)

    def pack(name, first_of, shapes, times):
        if times == 1:
            out_specs = [whole(shape) for shape in shapes]
        else:
            out_specs = [pl.BlockSpec((1,) + shapes[0][1:], lambda i, core: (i, 0, 0, 0))]
        return pl.pallas_call(
            functools.partial(pack_kernel, times),
            grid_spec=pltpu.PrefetchScalarGridSpec(
                num_scalar_prefetch=1,
                grid=(2,),
                in_specs=[
                    pl.BlockSpec(one_time, lambda i, core: (0, 0, first_of(core[0]) + 2 * i, 0, 0, 0)),
                    pl.BlockSpec((3, 18, 1, count_z, count_y), lambda i, core: (0, 0, first_of(core[0]) + 2 * i, 0, 0)),
                ],
                out_specs=out_specs,
            ),
            out_shape=arrays(*shapes),
            compiler_params=pltpu.CompilerParams(vmem_limit_bytes=28 * 1024 * 1024),
            cost_estimate=small,
            name=name,
        )

    up, down = pack("pack_own", lambda core: core, (packed(1, count_z, 0), packed(1, count_z, 1)), 1)(
        core_at, vectors, links
    )
    after, _ = lax.optimization_barrier((core_at, up))
    (given,) = pack("pack_given", lambda core: 1 - core, (packed(2, count_z, 3),), 2)(after, vectors, links)
    recv_up = [shift(rows(up), -1)]
    recv_down = [shift(rows(down), 1)]
    swapped = lax.ppermute(given, "gz", [(0, 1), (1, 0), (2, 3), (3, 2)])
    tail = nev // count_y
    lead = count_z - tail
    shapes = packed(1, lead, 0), packed(1, lead, 1), (2, 6, count_y, nev)
    up_a, down_a, lowest = pl.pallas_call(
        functools.partial(split_first_kernel, count_z),
        grid_spec=pltpu.PrefetchScalarGridSpec(
            num_scalar_prefetch=1,
            grid=(1,),
            in_specs=[
                whole(swapped.shape),
                pl.BlockSpec((2, 3, count_t, 1, count_y, nev), lambda i, core: (0, 0, 0, 0, 0, 0)),
            ],
            out_specs=[whole(shape) for shape in shapes],
        ),
        out_shape=arrays(*shapes),
        compiler_params=limit,
        cost_estimate=small,
        name="split_first",
    )(core_at, swapped, vectors)
    recv_up.append(shift(rows(up_a), -1))
    recv_down.append(shift(rows(down_a), 1))
    halo = lax.ppermute(rows(lowest), "gz", [(0, 2), (2, 0), (1, 3), (3, 1)])

    place = jnp.stack([core, x, chip * deep]).astype(jnp.int32)
    place, _ = lax.optimization_barrier((place, up_a))
    wide = jax.ShapeDtypeStruct((16, 2 * sites + 2 * nev), F32)
    sent, top, lines, table = pl.pallas_call(
        functools.partial(yz_kernel, (size_x, count_z * size_g, count_y)),
        grid_spec=pltpu.PrefetchScalarGridSpec(
            num_scalar_prefetch=1,
            grid=(2,),
            in_specs=[
                pl.BlockSpec(one_time, lambda m, core: (0, 0, core[0] + 2 * m, 0, 0, 0)),
                pl.BlockSpec((1,) + rows(swapped).shape[1:], lambda m, core: (m, 0, 0)),
                pl.BlockSpec((3, 18, 1, count_z, count_y), lambda m, core: (0, 0, core[0] + 2 * m, 0, 0)),
                in_smem,
            ],
            out_specs=[
                pl.BlockSpec((size_x, 1, 4 * group, 2 * nev), lambda m, core: (0, m, 0, 0)),
                pl.BlockSpec((1, 6 * count_y, nev), lambda m, core: (m, 0, 0)),
                pl.BlockSpec((1, 16, 2 * nev), lambda m, core: (m, 0, 0)),
                whole(wide.shape),
            ],
            scratch_shapes=[
                pltpu.VMEM((4, 6, deep, 2 * nev), F32),
                pltpu.VMEM((2, 3, deep, count_y, nev), BF16),
                pltpu.VMEM((4 * nev, 6 * sites), BF16),
                pltpu.VMEM((3, deep, count_y, 2 * nev), BF16),
                pltpu.VMEM((3, deep, count_y, 2 * nev), BF16),
            ],
        ),
        out_shape=[
            jax.ShapeDtypeStruct((size_x, 2, 4 * group, 2 * nev), BF16),
            jax.ShapeDtypeStruct((2, 6 * count_y, nev), BF16),
            jax.ShapeDtypeStruct((2, 16, 2 * nev), F32),
            wide,
        ],
        compiler_params=limit,
        cost_estimate=small,
        name="yz_terms",
    )(place, vectors, rows(swapped), links, momenta)

    core_at, _ = lax.optimization_barrier((core_at, sent))
    shapes = packed(1, tail, 0), packed(1, tail, 1)
    up_b, down_b = pl.pallas_call(
        functools.partial(split_last_kernel, count_z),
        in_specs=[in_smem, in_vmem],
        out_specs=[in_vmem] * 2,
        out_shape=arrays(*shapes),
        compiler_params=limit,
        cost_estimate=small,
        name="split_last",
    )(core_at, swapped)
    recv_up.append(shift(rows(up_b), -1))
    recv_down.append(shift(rows(down_b), 1))

    def scratch(depth):
        return [
            pltpu.VMEM((2, 6, count_z, 6 * count_y), F32),
            pltpu.VMEM((4 * nev, 6 * depth * count_y), BF16),
            pltpu.VMEM((2, 3, depth, count_y, 2 * nev), BF16),
        ]

    parts = jax.ShapeDtypeStruct((2, 4, nev, nev), F32)
    part = pl.pallas_call(
        x_first_kernel,
        grid_spec=pltpu.PrefetchScalarGridSpec(
            num_scalar_prefetch=1,
            grid=(1,),
            in_specs=[whole(array.shape) for array in (rows(up), recv_up[0], rows(down), recv_down[0])]
            + [pl.BlockSpec((1, 18, 1, count_z, count_y), lambda i, core: (0, 0, core[0], 0, 0))]
            + [whole(wide.shape)],
            out_specs=whole(parts.shape),
            scratch_shapes=scratch(count_z),
        ),
        out_shape=parts,
        compiler_params=limit,
        cost_estimate=small,
        name="x_first",
    )(core_at, rows(up), recv_up[0], rows(down), recv_down[0], links, table)
    part = pl.pallas_call(
        x_middle_kernel,
        in_specs=[in_smem] + [in_vmem] * 5,
        out_specs=in_vmem,
        out_shape=parts,
        scratch_shapes=scratch(lead),
        compiler_params=limit,
        cost_estimate=small,
        name="x_middle",
    )(core_at, rows(swapped), recv_up[1], recv_down[1], table, part)
    sent = pl.pallas_call(
        x_last_kernel,
        in_specs=[in_smem] + [in_vmem] * 9,
        out_specs=in_vmem,
        out_shape=jax.ShapeDtypeStruct((size_x, 2, 4 * group, 3 * nev), BF16),
        scratch_shapes=scratch(tail) + [pltpu.VMEM((4 * nev, 2 * nev), BF16)],
        compiler_params=limit,
        cost_estimate=small,
        name="x_last",
    )(core_at, rows(swapped), recv_up[2], recv_down[2], table, part, sent, top, halo, lines)

    pieces = sent.reshape(2 * size_x, 4 * group, 3 * nev)
    groups = [[(ts * 2 + h) * 2 + c for ts in range(size_x) for h in range(2)] for c in range(2)]
    got = lax.all_to_all(pieces, ("ts", "gz"), 0, 0, tiled=True, axis_index_groups=groups)
    return pl.pallas_call(
        total_kernel,
        in_specs=[in_smem, in_vmem],
        out_specs=in_vmem,
        out_shape=jax.ShapeDtypeStruct((group, 1, 2, 2, 3 * nev), F32),
        name="total",
    )(directions, got)


def solution(mesh):
    in_specs = (
        P(None, None, None, "ts", "gz", None, None),
        P(None, None, None, "ts", "gz", None),
        P(),
        P(),
    )
    out_specs = P("ts", "gz", None, None, None)
    return jax.shard_map(shards, mesh=mesh, in_specs=in_specs, out_specs=out_specs, check_vma=False)
```

time: 93 us -> 81.8 us (0.88)
  waiting for transfers between devices: 12 us -> 0.02 us
  starting transfers between devices: 15.5 us -> 22.9 us
  blocking collectives: 26.9 us -> 20.2 us
  Pallas kernels: 30.8 us -> 31.9 us
    ppermute x4 -> x6, starting transfers between devices: 9.12 us -> 20.1 us  [shift(): lax.ppermute(value, 'ts', [(source, (source + steps) % count) for source...]
    ppermute x4 -> x6, waiting for transfers between devices: 9.98 us -> 0.02 us  [shift(): lax.ppermute(value, 'ts', [(source, (source + steps) % count) for source...]
    all_to_all x1, blocking collectives: 26.9 us -> 20.2 us  [shards(): lax.all_to_all(pieces, ('ts', 'gz'), 0, 0, tiled=True, axis_index_groups=...]
    ppermute x2 -> x1, starting transfers between devices: 6.3 us -> 2.73 us  [shards(): halo = lax.ppermute(rows(lowest), 'gz', [(0, 2), (2, 0), (1, 3), (3, 1)])]
    ppermute x2 -> x1, waiting for transfers between devices: 2.05 us -> 0.01 us  [shards(): halo = lax.ppermute(rows(lowest), 'gz', [(0, 2), (2, 0), (1, 3), (3, 1)])]
    slice x2 -> x0, local copies, waits for them, and re-layouts: 1.9 us -> none  [the longest x1 0.97 us: shards(): recv_down.append(shift(swapped[1:, :full + planes * count_y], 1))]
    unnamed x10 -> x18, local copies, waits for them, and re-layouts: 4.6 us -> 6.18 us
    pallas_call x7 -> x8, Pallas kernels: 23.5 us -> 24.2 us  [the longest x1 11.5 us: shards(): pl.pallas_call(functools.partial(yz_kernel, (size_x, count_z * size_g, co...]
  transfers between devices with their start and end apart: 7 -> 8, of which waited for: 4 -> 0; matrix products, arithmetic and copies ran while one was open for 3% -> 0% of each run, Pallas kernels for 23% -> 32%
where the time goes in v4:
time: 81.8 us; the launch traced here: 81.4 us
  Pallas kernels  31.9 us (39%)
  starting transfers between devices  22.9 us (28%)
  blocking collectives  20.2 us (25%)
  local copies, waits for them, and re-layouts  6.18 us (8%)
    all_to_all x1, blocking collectives, shards(): lax.all_to_all(pieces, ('ts', 'gz'), 0, 0, tiled=True, axis_index_groups=...  20.2 us
    ppermute x6, starting transfers between devices, shift(): lax.ppermute(value, 'ts', [(source, (source + steps) % count) for source...  20.1 us
    pallas_call x1, Pallas kernels, shards(): pl.pallas_call(functools.partial(yz_kernel, (size_x, count_z * size_g, co...  11.5 us
    pallas_call x1, Pallas kernels, shards(): pl.pallas_call(x_first_kernel, grid_spec=pltpu.PrefetchScalarGridSpec(num...  7.69 us
    unnamed x18, local copies, waits for them, and re-layouts  6.18 us
    pallas_call x1, Pallas kernels, shards(): pl.pallas_call(x_middle_kernel, in_specs=[in_smem] + [in_vmem] * 5, out_s...  5.41 us
    ppermute x1, starting transfers between devices, shards(): halo = lax.ppermute(rows(lowest), 'gz', [(0, 2), (2, 0), (1, 3), (3, 1)])  2.73 us
    pallas_call x1, Pallas kernels, shards(): pl.pallas_call(x_last_kernel, in_specs=[in_smem] + [in_vmem] * 9, out_spe...  2.26 us
  transfers between devices with their start and end apart: 8, of which 0 were waited for; matrix products, arithmetic and copies ran while one was open for 0% of the time, Pallas kernels for 32%

profile of v4, /device:TPU:0, one launch (start us, length us, event | category | flops | bytes accessed | tf_op | source)
XLA Modules:
  0.0 81.4 jit_solution(4456668679613262102)
XLA Ops:
  0.0 1.9 %copy-done = bf16[2,3,4,1,16,32,128]{6,5,4,3,2,1,0:T(8,128)(2,1)S(1)} copy-done((bf16[2,3,4,1,16,32,128]{6,5,4,3,2,1,0:T(8,128)(2,1)S(1)}, bf16[2,3,4,1,16,32,128]{6,5,4,3,2,1,0:T(8,128)(2,1)}, u32[]{:S(2)}) %copy-start) | copy-done | bytes 3145752
  1.9 1.2 %copy-done.5 = bf16[3,18,4,1,16,32]{5,4,3,2,1,0:T(8,128)(2,1)S(1)} copy-done((bf16[3,18,4,1,16,32]{5,4,3,2,1,0:T(8,128)(2,1)S(1)}, bf16[3,18,4,1,16,32]{5,4,3,2,1,0:T(8,128)(2,1)}, u32[]{:S(2)}) %copy-start.5) | copy-done | bytes 221208
  3.1 1.5 %pack_own.1 = (bf16[1,96,32,128]{3,2,1,0:T(8,128)(2,1)}, bf16[1,99,32,128]{3,2,1,0:T(8,128)(2,1)}) custom-call(s32[1]{0:T(128)} %bitcast.core_ref, bf16[2,3,4,16,32,128]{5,4,3,2,1,0:T(8,128)(2,1)S(1)} %bitcast.14, bf16[3,18,4,16,32]{4,3,2,1,0:T(8,128)(2,1)S(1)} %bitcast.21), custom_call_target="tpu_custom_call" | custom-call | flops 1000000 | bytes 100000 | tf_op jit(solution)/shard_map/pack_own/pallas_call | solution.py:457
  4.6 0.4 pack_given.1
  5.0 0.1 collective-permute-start
  5.1 7.6 %collective-permute-start.5 = (bf16[1,3072,128]{2,1,0:T(8,128)(2,1)}, bf16[1,3072,128]{2,1,0:T(8,128)(2,1)}, u32[]{:S(2)}, u32[]{:S(2)}) collective-permute-start(bf16[1,3072,128]{2,1,0:T(8,128)(2,1)} %bitcast.10.own_up), channel_id=1, source_target_pairs={{0,124},{4,0},{8,4},{12,8},{16,12},{20,16},{24,20},{28,24},{32,28}... | collective-permute-start | bytes 2359304 | tf_op jit(solution)/shard_map/ppermute | solution.py:400
  12.7 1.1 %split_first.1 = (bf16[1,72,32,128]{3,2,1,0:T(8,128)(2,1)}, bf16[1,75,32,128]{3,2,1,0:T(8,128)(2,1)}, bf16[2,6,32,128]{3,2,1,0:T(8,128)(2,1)S(1)}) custom-call(s32[1]{0:T(128)} %bitcast.core_ref, bf16[2,105,32,128]{3,2,1,0:T(8,128)(2,1)S(1)} %collective-permute-done.swap_ref, bf16[2,3,4,16,32,128]{5,4,3,2,1,0:T(8,128)(2,1)S(1)} %bitcast.16), custom_call_target="tpu_custom_call" | custom-call | flops 1000000 | bytes 100000 | tf_op jit(solution)/shard_map/split_first/pallas_call | solution.py:468
  13.9 0.5 copy-done.2
  14.3 6.2 %collective-permute-start.3 = (bf16[1,2304,128]{2,1,0:T(8,128)(2,1)}, bf16[1,2304,128]{2,1,0:T(8,128)(2,1)}, u32[]{:S(2)}, u32[]{:S(2)}) collective-permute-start(bf16[1,2304,128]{2,1,0:T(8,128)(2,1)} %bitcast.8), channel_id=1, source_target_pairs={{0,124},{4,0},{8,4},{12,8},{16,12},{20,16},{24,20},{28,24},{32,28}... | collective-permute-start | bytes 1769480 | tf_op jit(solution)/shard_map/ppermute | solution.py:400
  20.6 0.1 pad_add_fusion.place_ref
  20.7 1.5 %copy-done.3 = bf16[2,105,32,128]{3,2,1,0:T(8,128)(2,1)S(1)} copy-done((bf16[2,105,32,128]{3,2,1,0:T(8,128)(2,1)S(1)}, bf16[2,105,32,128]{3,2,1,0:T(8,128)(2,1)}, u32[]{:S(2)}) %copy-start.3) | copy-done | bytes 1720344
  22.1 1.2 %copy-done.6 = bf16[3,18,4,1,16,32]{5,4,3,2,1,0:T(8,128)(2,1)S(1)} copy-done((bf16[3,18,4,1,16,32]{5,4,3,2,1,0:T(8,128)(2,1)S(1)}, bf16[3,18,4,1,16,32]{5,4,3,2,1,0:T(8,128)(2,1)}, u32[]{:S(2)}) %copy-start.6) | copy-done | bytes 221208
  23.3 11.5 %yz_terms.1 = (bf16[32,2,16,256]{3,2,1,0:T(8,128)(2,1)S(1)}, bf16[2,192,128]{2,1,0:T(8,128)(2,1)S(1)}, f32[2,16,256]{2,1,0:T(8,128)S(1)}, f32[16,1280]{1,0:T(8,128)S(1)}) custom-call(s32[3]{0:T(128)S(1)} %pad_add_fusion.place_ref, bf16[2,3,4,16,32,128]{5,4,3,2,1,0:T(8,128)(2,1)S(1)} %bitcast.17, bf16[2,3360,128]{2,1,0:T(8,128)(2,1)S(1)} %bitcast.18, ...), custom_call_target="tpu_custom_call" | custom-call | flops 1000000 | bytes 100000 | tf_op jit(solution)/shard_map/yz_terms/pallas_call | solution.py:491
  34.8 0.0 copy-start.7
  34.9 0.1 collective-permute-start.2
  35.0 6.2 %collective-permute-start.1 = (bf16[1,768,128]{2,1,0:T(8,128)(2,1)S(1)}, bf16[1,768,128]{2,1,0:T(8,128)(2,1)S(1)}, u32[]{:S(2)}, u32[]{:S(2)}) collective-permute-start(bf16[1,768,128]{2,1,0:T(8,128)(2,1)S(1)} %bitcast.27), channel_id=1, source_target_pairs={{0,124},{4,0},{8,4},{12,8},{16,12},{20,16},{24,20},{28,24},{32,28}... | collective-permute-start | bytes 589832 | tf_op jit(solution)/shard_map/ppermute | solution.py:400
  41.2 0.0 collective-permute-done.6.recv_down
  41.2 2.7 %collective-permute-start.7 = (bf16[2,192,128]{2,1,0:T(8,128)(2,1)S(1)}, bf16[2,192,128]{2,1,0:T(8,128)(2,1)S(1)}, u32[]{:S(2)}, u32[]{:S(2)}) collective-permute-start(bf16[2,192,128]{2,1,0:T(8,128)(2,1)S(1)} %bitcast.28), channel_id=1, source_target_pairs={{0,2},{2,0},{1,3},{3,1},{4,6},{6,4},{5,7},{7,5},{8,10},{10,8},{9,1... | collective-permute-start | bytes 294920 | tf_op jit(solution)/shard_map/ppermute | solution.py:486
  43.9 7.7 %x_first.1.before = f32[2,4,128,128]{3,2,1,0:T(8,128)S(1)} custom-call(s32[1]{0:T(128)} %bitcast.core_ref, bf16[1,3072,128]{2,1,0:T(8,128)(2,1)} %bitcast.10.own_up, bf16[1,3072,128]{2,1,0:T(8,128)(2,1)} %collective-permute-done.5.recv_up, bf16[1,3168,128]{2,1,0:T(8,128)(2,1)} %bitcast.11.own_down, bf16[1,3168,128]{2,1,0:T(8,128)(2,1)} %collective-permute-done.6.recv_down, ...), custom_call_target="tpu_custom_call" | custom-call | flops 1000000 | bytes 100000 | tf_op jit(solution)/shard_map/x_first/pallas_call | solution.py:549
  51.6 0.0 collective-permute-done.3.recv_up
  51.6 5.4 %x_middle.1.before = f32[2,4,128,128]{3,2,1,0:T(8,128)S(1)} custom-call(s32[1]{0:T(128)} %bitcast.core_ref, bf16[2,3360,128]{2,1,0:T(8,128)(2,1)S(1)} %bitcast.19, bf16[1,2304,128]{2,1,0:T(8,128)(2,1)} %collective-permute-done.3.recv_up, bf16[1,2400,128]{2,1,0:T(8,128)(2,1)} %collective-permute-done.4.recv_down, f32[16,1280]{1,0:T(8,128)S(1)} %get-tuple-element.27.table, ...), custom_call_target="tpu_custom_call" | custom-call | flops 1000000 | bytes 100000 | tf_op jit(solution)/shard_map/x_middle/pallas_call | solution.py:565
  57.1 2.3 %x_last.1 = bf16[32,2,16,384]{3,2,1,0:T(8,128)(2,1)S(1)} custom-call(s32[1]{0:T(128)} %bitcast.core_ref, bf16[2,3360,128]{2,1,0:T(8,128)(2,1)S(1)} %bitcast.20, bf16[1,768,128]{2,1,0:T(8,128)(2,1)S(1)} %collective-permute-done.1.recv_up, bf16[1,864,128]{2,1,0:T(8,128)(2,1)S(1)} %collective-permute-done.2.recv_down, f32[16,1280]{1,0:T(8,128)S(1)} %get-tuple-element.27.table, ...), custom_call_target="tpu_custom_call" | custom-call | flops 1000000 | bytes 100000 | tf_op jit(solution)/shard_map/x_last/pallas_call | solution.py:575
  59.4 20.2 %all_to_all.5.got_ref = bf16[64,16,384]{2,1,0:T(8,128)(2,1)} all-to-all(bf16[64,16,384]{2,1,0:T(8,128)(2,1)S(1)} %bitcast.25), channel_id=1, replica_groups={{0,2,4,6,8,10,12,14,16,18,20,22,24,26,28,30,32,34,36,38,40,42,44,46,48,..., dimensions={0} | all-to-all | bytes 1572864 | tf_op jit(solution)/shard_map/all_to_all | solution.py:588
  79.5 1.9 %total.1 = f32[4,1,2,2,384]{4,3,2,1,0:T(2,128)} custom-call(s32[3]{0:T(128)} %directions_ref.1, bf16[64,16,384]{2,1,0:T(8,128)(2,1)} %all_to_all.5.got_ref), custom_call_target="tpu_custom_call" | custom-call | tf_op jit(solution)/shard_map/total/pallas_call | solution.py:589
  (21 shorter events, 0.1 us)
Async XLA Ops:
  0.0 1.9 %copy-start = (bf16[2,3,4,1,16,32,128]{6,5,4,3,2,1,0:T(8,128)(2,1)S(1)}, bf16[2,3,4,1,16,32,128]{6,5,4,3,2,1,0:T(8,128)(2,1)}, u32[]{:S(2)}) copy-start(bf16[2,3,4,1,16,32,128]{6,5,4,3,2,1,0:T(8,128)(2,1)} %param.4) | copy-start | bytes 9437188
  1.9 1.2 %copy-start.5 = (bf16[3,18,4,1,16,32]{5,4,3,2,1,0:T(8,128)(2,1)S(1)}, bf16[3,18,4,1,16,32]{5,4,3,2,1,0:T(8,128)(2,1)}, u32[]{:S(2)}) copy-start(bf16[3,18,4,1,16,32]{5,4,3,2,1,0:T(8,128)(2,1)} %param.5) | copy-start | bytes 663556
  5.0 7.7 %collective-permute-start = (bf16[2,105,32,128]{3,2,1,0:T(8,128)(2,1)S(1)}, bf16[2,105,32,128]{3,2,1,0:T(8,128)(2,1)S(1)}, u32[]{:S(2)}, u32[]{:S(2)}) collective-permute-start(bf16[2,105,32,128]{3,2,1,0:T(8,128)(2,1)S(1)} %pack_given.1), channel_id=1, source_target_pairs={{0,1},{1,0},{2,3},{3,2},{4,5},{5,4},{6,7},{7,6},{8,9},{9,8},{10,11... | collective-permute-start | bytes 5160968 | tf_op jit(solution)/shard_map/ppermute | solution.py:464
  5.1 29.8 %collective-permute-start.5 = (bf16[1,3072,128]{2,1,0:T(8,128)(2,1)}, bf16[1,3072,128]{2,1,0:T(8,128)(2,1)}, u32[]{:S(2)}, u32[]{:S(2)}) collective-permute-start(bf16[1,3072,128]{2,1,0:T(8,128)(2,1)} %bitcast.10.own_up), channel_id=1, source_target_pairs={{0,124},{4,0},{8,4},{12,8},{16,12},{20,16},{24,20},{28,24},{32,28}... | collective-permute-start | bytes 2359304 | tf_op jit(solution)/shard_map/ppermute | solution.py:400
  12.7 8.0 %copy-start.1 = (bf16[2,3,4,1,16,32,128]{6,5,4,3,2,1,0:T(8,128)(2,1)S(1)}, bf16[2,3,4,1,16,32,128]{6,5,4,3,2,1,0:T(8,128)(2,1)}, u32[]{:S(2)}) copy-start(bf16[2,3,4,1,16,32,128]{6,5,4,3,2,1,0:T(8,128)(2,1)} %param.4) | copy-start | bytes 9437188
  12.7 8.0 %copy-start.8 = (s32[2,3]{1,0:T(2,128)S(1)}, s32[2,3]{1,0:T(2,128)}, u32[]{:S(2)}) copy-start(s32[2,3]{1,0:T(2,128)} %momenta_ref.1) | copy-start | bytes 76
  12.7 28.5 %collective-permute-start.6 = (bf16[1,3168,128]{2,1,0:T(8,128)(2,1)}, bf16[1,3168,128]{2,1,0:T(8,128)(2,1)}, u32[]{:S(2)}, u32[]{:S(2)}) collective-permute-start(bf16[1,3168,128]{2,1,0:T(8,128)(2,1)} %bitcast.11.own_down), channel_id=1, source_target_pairs={{0,4},{4,8},{8,12},{12,16},{16,20},{20,24},{24,28},{28,32},{32,36}... | collective-permute-start | bytes 2433032 | tf_op jit(solution)/shard_map/ppermute | solution.py:400
  12.7 1.6 %copy-start.2 = (bf16[2,105,32,128]{3,2,1,0:T(8,128)(2,1)}, bf16[2,105,32,128]{3,2,1,0:T(8,128)(2,1)S(1)}, u32[]{:S(2)}) copy-start(bf16[2,105,32,128]{3,2,1,0:T(8,128)(2,1)S(1)} %collective-permute-done.swap_ref) | copy-start | bytes 5160964
  14.3 37.3 %collective-permute-start.4 = (bf16[1,2400,128]{2,1,0:T(8,128)(2,1)}, bf16[1,2400,128]{2,1,0:T(8,128)(2,1)}, u32[]{:S(2)}, u32[]{:S(2)}) collective-permute-start(bf16[1,2400,128]{2,1,0:T(8,128)(2,1)} %bitcast.9), channel_id=1, source_target_pairs={{0,4},{4,8},{8,12},{12,16},{16,20},{20,24},{24,28},{28,32},{32,36}... | collective-permute-start | bytes 1843208 | tf_op jit(solution)/shard_map/ppermute | solution.py:400
  14.3 37.3 %collective-permute-start.3 = (bf16[1,2304,128]{2,1,0:T(8,128)(2,1)}, bf16[1,2304,128]{2,1,0:T(8,128)(2,1)}, u32[]{:S(2)}, u32[]{:S(2)}) collective-permute-start(bf16[1,2304,128]{2,1,0:T(8,128)(2,1)} %bitcast.8), channel_id=1, source_target_pairs={{0,124},{4,0},{8,4},{12,8},{16,12},{20,16},{24,20},{28,24},{32,28}... | collective-permute-start | bytes 1769480 | tf_op jit(solution)/shard_map/ppermute | solution.py:400
  20.7 1.5 %copy-start.3 = (bf16[2,105,32,128]{3,2,1,0:T(8,128)(2,1)S(1)}, bf16[2,105,32,128]{3,2,1,0:T(8,128)(2,1)}, u32[]{:S(2)}) copy-start(bf16[2,105,32,128]{3,2,1,0:T(8,128)(2,1)} %copy-done.2) | copy-start | bytes 5160964
  22.1 1.2 %copy-start.6 = (bf16[3,18,4,1,16,32]{5,4,3,2,1,0:T(8,128)(2,1)S(1)}, bf16[3,18,4,1,16,32]{5,4,3,2,1,0:T(8,128)(2,1)}, u32[]{:S(2)}) copy-start(bf16[3,18,4,1,16,32]{5,4,3,2,1,0:T(8,128)(2,1)} %param.5) | copy-start | bytes 663556
  34.8 9.1 %copy-start.7 = (bf16[3,18,4,1,16,32]{5,4,3,2,1,0:T(8,128)(2,1)S(1)}, bf16[3,18,4,1,16,32]{5,4,3,2,1,0:T(8,128)(2,1)}, u32[]{:S(2)}) copy-start(bf16[3,18,4,1,16,32]{5,4,3,2,1,0:T(8,128)(2,1)} %param.5) | copy-start | bytes 663556
  34.9 22.2 %collective-permute-start.2 = (bf16[1,864,128]{2,1,0:T(8,128)(2,1)S(1)}, bf16[1,864,128]{2,1,0:T(8,128)(2,1)S(1)}, u32[]{:S(2)}, u32[]{:S(2)}) collective-permute-start(bf16[1,864,128]{2,1,0:T(8,128)(2,1)S(1)} %bitcast.26), channel_id=1, source_target_pairs={{0,4},{4,8},{8,12},{12,16},{16,20},{20,24},{24,28},{28,32},{32,36}... | collective-permute-start | bytes 663560 | tf_op jit(solution)/shard_map/ppermute | solution.py:400
  35.0 22.1 %collective-permute-start.1 = (bf16[1,768,128]{2,1,0:T(8,128)(2,1)S(1)}, bf16[1,768,128]{2,1,0:T(8,128)(2,1)S(1)}, u32[]{:S(2)}, u32[]{:S(2)}) collective-permute-start(bf16[1,768,128]{2,1,0:T(8,128)(2,1)S(1)} %bitcast.27), channel_id=1, source_target_pairs={{0,124},{4,0},{8,4},{12,8},{16,12},{20,16},{24,20},{28,24},{32,28}... | collective-permute-start | bytes 589832 | tf_op jit(solution)/shard_map/ppermute | solution.py:400
  41.2 15.9 %collective-permute-start.7 = (bf16[2,192,128]{2,1,0:T(8,128)(2,1)S(1)}, bf16[2,192,128]{2,1,0:T(8,128)(2,1)S(1)}, u32[]{:S(2)}, u32[]{:S(2)}) collective-permute-start(bf16[2,192,128]{2,1,0:T(8,128)(2,1)S(1)} %bitcast.28), channel_id=1, source_target_pairs={{0,2},{2,0},{1,3},{3,1},{4,6},{6,4},{5,7},{7,5},{8,10},{10,8},{9,1... | collective-permute-start | bytes 294920 | tf_op jit(solution)/shard_map/ppermute | solution.py:486
  43.9 7.7 %copy-start.4 = (bf16[2,105,32,128]{3,2,1,0:T(8,128)(2,1)S(1)}, bf16[2,105,32,128]{3,2,1,0:T(8,128)(2,1)}, u32[]{:S(2)}) copy-start(bf16[2,105,32,128]{3,2,1,0:T(8,128)(2,1)} %copy-done.2) | copy-start | bytes 5160964

commit v5 on v4

v5 whole, which is shorter than its diff:
```python
import functools
import math

import jax
import jax.numpy as jnp
from jax import lax
from jax.experimental import pallas as pl
from jax.experimental.pallas import tpu as pltpu
from jax.sharding import PartitionSpec as P

BF16 = jnp.bfloat16
F32 = jnp.float32


def link_rows(entries, adjoint, width):
    rows = []
    for r in range(2):
        for a in range(3):
            pieces = []
            for q in range(2):
                for b in range(3):
                    first = ((b * 3 + a) if adjoint else (a * 3 + b)) * 2
                    if r == q:
                        pieces.append(entries[first])
                    elif (q == 1) == adjoint:
                        pieces.append(entries[first + 1])
                    else:
                        pieces.append(-entries[first + 1])
            lanes = sum(piece.shape[1] for piece in pieces)
            if lanes < width:
                pieces.append(jnp.zeros((pieces[0].shape[0], width - lanes), F32))
            rows.append(jnp.concatenate(pieces, axis=1))
    return rows


def site_masks(count_y, lanes):
    row = lax.broadcasted_iota(jnp.int32, (count_y, lanes), 0)
    lane = lax.broadcasted_iota(jnp.int32, (count_y, lanes), 1) % count_y
    same = jnp.where(lane == row, 1.0, 0.0).astype(BF16)
    above = jnp.where(lane == (row + 1) % count_y, 1.0, 0.0).astype(BF16)
    below = jnp.where(lane == (row + count_y - 1) % count_y, 1.0, 0.0).astype(BF16)
    return same, above, below


def spread(rows_ref, kind, row, mask):
    count_y, lanes = mask.shape
    blocks = []
    for ra in range(6):
        line = rows_ref[kind, ra, pl.ds(row, 1), :lanes]
        blocks.append(jnp.broadcast_to(line, (count_y, lanes)).astype(BF16) * mask)
    return jnp.concatenate(blocks, axis=0)


def fraction(component, coords, length):
    return jnp.mod(component * coords, length).astype(F32) / length


def table_kernel(lengths, deep, place_ref, momenta_ref, table_ref):
    length_x, length_z, length_y = lengths
    half = table_ref.shape[0] // 2
    shape = 2 * half, table_ref.shape[2]
    row = lax.broadcasted_iota(jnp.int32, shape, 0)
    lane = lax.broadcasted_iota(jnp.int32, shape, 1)
    x_at = row // 2
    x = place_ref[1] + jnp.where(x_at == 2, -1, x_at)
    plane = lane // length_y
    above = deep + (shape[1] // length_y - deep) // 2
    z = place_ref[2] + jnp.where(plane < deep, plane, jnp.where(plane < above, deep, deep - 1))
    y = lane % length_y
    first = row % 2 == 0
    m_x, m_y, m_z = (jnp.where(first, momenta_ref[0, i], momenta_ref[1, i]) for i in range(3))
    angle = 2.0 * math.pi * (
        (fraction(m_x, x, length_x) + fraction(m_y, y, length_y)) + fraction(m_z, z, length_z)
    )
    for first, values in ((0, jnp.cos(angle)), (half, jnp.sin(angle))):
        for at in range(2 * half):
            table_ref[first + at // 2, at % 2 : at % 2 + 1] = values[at : at + 1]


def write_phased(planes_of, table, x_at, table_first, blocks, out_ref, first, colour_stride):
    for b in range(3):
        for block in range(blocks):
            real = planes_of(0, b, block).T.astype(F32)
            imag = planes_of(1, b, block).T.astype(F32)
            nev, sites = real.shape
            at = first + b * colour_stride + block * sites
            put_phased(real, imag, table, x_at, table_first + block * sites, out_ref, at)


def put_phased(real, imag, table, x_at, table_at, out_ref, at):
    nev, sites = real.shape
    for p in range(2):
        cosine, sine = (table[half + x_at, p : p + 1, pl.ds(table_at, sites)] for half in (0, table.shape[0] // 2))
        out_ref[2 * p * nev : (2 * p + 1) * nev, at : at + sites] = (cosine * real - sine * imag).astype(BF16)
        out_ref[(2 * p + 1) * nev : (2 * p + 2) * nev, at : at + sites] = (sine * real + cosine * imag).astype(BF16)


def put_displaced(out_ref, z, terms, count_y, nev):
    for r in range(2):
        for a in range(3):
            rows = terms[(r * 3 + a) * count_y : (r * 3 + a + 1) * count_y]
            out_ref[a, z, :, r * nev : (r + 1) * nev] = rows.astype(BF16)


def combine(products, nev):
    real, imag = [], []
    for p in range(2):
        rr = products[2 * p * nev : (2 * p + 1) * nev, :nev]
        ri = products[2 * p * nev : (2 * p + 1) * nev, nev:]
        ir = products[(2 * p + 1) * nev : (2 * p + 2) * nev, :nev]
        ii = products[(2 * p + 1) * nev : (2 * p + 2) * nev, nev:]
        real.append(rr + ii)
        imag.append(ri - ir)
    return real + imag


def by_owner(first, second):
    nev, lanes = first.shape
    a = first.reshape(nev // 8, 8, lanes)
    b = second.reshape(nev // 8, 8, lanes)
    upper = lax.broadcasted_iota(jnp.int32, a.shape, 1) < 4
    even = jnp.where(upper, a, pltpu.roll(b, 4, 1))
    odd = jnp.where(upper, pltpu.roll(a, 4, 1), b)
    return jnp.stack([even, odd], axis=1).reshape(nev // 4, 8, lanes)


def partial_rows(parts):
    return jnp.concatenate([by_owner(parts[0], parts[1]), by_owner(parts[2], parts[3])], axis=1)


def packed_plane(packed, depth, q, b, z, count, count_y):
    first = ((q * 3 + b) * depth + z) * count_y
    return packed[first : first + count * count_y]


def link_planes(nev, count_z, count_y):
    return -(-18 * count_y * count_z // (nev * count_y))


def packed_link(packed, depth, k, e, count_z, count_y):
    nev = packed.shape[1]
    per_row = nev // count_y
    first = (6 * depth + k * link_planes(nev, count_z, count_y)) * count_y + e // per_row * count_z
    lane = e % per_row * count_y
    return packed[first : first + count_z, lane : lane + count_y]


def put_links(out_ref, at, first_plane, link, count_z, count_y, nev):
    per_row = nev // count_y
    per_plane = count_y // count_z
    for row in range(link_planes(nev, count_z, count_y) * per_plane):
        held = [link(e) for e in range(row * per_row, min(18, (row + 1) * per_row))]
        held += [jnp.zeros((count_z, count_y), BF16)] * (per_row - len(held))
        first = row % per_plane * count_z
        out_ref[at, first_plane + row // per_plane, first : first + count_z] = jnp.concatenate(held, axis=1)


def pack_kernel(place_ref, v_ref, link_ref, first_ref, second_ref, given_ref):
    count_z, count_y, nev = v_ref.shape[3:]
    core, odd = place_ref[0], place_ref[3]
    planes = link_planes(nev, count_z, count_y)
    for out_ref, at, t in (
        (first_ref, 0, core + 2 * (1 - odd)),
        (second_ref, 0, core + 2 * odd),
        (given_ref, 0, 1 - core),
        (given_ref, 1, 3 - core),
    ):
        for held in range(6):
            out_ref[at, held * count_z : (held + 1) * count_z] = v_ref[held // 3, held % 3, t]
    for out_ref, at, t, directions in (
        (first_ref, 0, core + 2 * (1 - odd), 1),
        (second_ref, 0, core + 2 * odd, 1),
        (given_ref, 0, 1 - core, 3),
        (given_ref, 1, 3 - core, 3),
    ):
        for k in range(directions):
            put_links(
                out_ref, at, 6 * count_z + k * planes, lambda e, k=k, t=t: link_ref[k, e, t], count_z, count_y, nev
            )


def split(place_ref, swap_ref, start, count_z, out_refs):
    odd = place_ref[3]
    for i, out_ref in enumerate(out_refs):
        m = odd if i else 1 - odd
        behind = out_ref.shape[1] % 6
        depth = out_ref.shape[1] // 6
        for held in range(6):
            first = held * count_z + start
            out_ref[0, held * depth : (held + 1) * depth] = swap_ref[m, first : first + depth]
        if behind:
            out_ref[0, 6 * depth :] = swap_ref[m, 6 * count_z : 6 * count_z + behind]


def split_first_kernel(count_z, place_ref, swap_ref, v_ref, first_ref, second_ref, lowest_ref):
    split(place_ref, swap_ref, 0, count_z, (first_ref, second_ref))
    core = place_ref[0]
    for m in range(2):
        for i in range(6):
            own = v_ref[i // 3, i % 3, core + 2 * m, 0]
            lowest_ref[m, i] = jnp.where(core == 0, own, swap_ref[m, i * count_z])


def split_last_kernel(count_z, place_ref, swap_ref, first_ref, second_ref):
    split(place_ref, swap_ref, count_z - first_ref.shape[1] // 6, count_z, (first_ref, second_ref))


def yz_kernel(place_ref, v_ref, swap_ref, link_ref, table_ref, out_ref, top_ref, line_ref,
              rows, padded, phased, moved_y, moved_z):
    core = place_ref[0]
    step_m = pl.program_id(0)
    t = core + 2 * step_m
    count_z, count_y, nev = v_ref.shape[3:]
    deep = 2 * count_z
    lanes = 6 * count_y
    sites = deep * count_y
    same, above, below = site_masks(count_y, lanes)
    mine = pl.multiple_of(core * count_z, count_z)
    theirs = pl.multiple_of((1 - core) * count_z, count_z)
    wide = rows.shape[3]
    lane = lax.broadcasted_iota(jnp.int32, (count_z, wide), 1) % count_y

    def fill_rows(link, start):
        at = pl.ds(start, count_z)
        link_y = [0.5 * link(1, e).astype(F32) for e in range(18)]
        for ra, line in enumerate(link_rows(link_y, False, wide)):
            rows[0, ra, at, :] = jnp.where(
                lane == 0, pltpu.roll(line, wide - (count_y - 1), 1), pltpu.roll(line, 1, 1)
            )
        for ra, line in enumerate(link_rows(link_y, True, wide)):
            rows[1, ra, at, :] = -line
        link_z = [0.5 * link(2, e).astype(F32) for e in range(18)]
        for ra, line in enumerate(link_rows(link_z, False, wide)):
            rows[2, ra, at, :] = line
        for ra, line in enumerate(link_rows(link_z, True, wide)):
            rows[3, ra, at, :] = -line

    padded[:, :, pl.ds(mine, count_z)] = v_ref[:, :, t]
    swapped = swap_ref.at[step_m]
    for q in range(2):
        for b in range(3):
            block = packed_plane(swapped, count_z, q, b, 0, count_z, count_y)
            padded[q, b, pl.ds(theirs, count_z)] = block.reshape(count_z, count_y, nev)
    fill_rows(lambda k, e: packed_link(swapped, count_z, k, e, count_z, count_y), theirs)
    fill_rows(lambda k, e: link_ref[k, e, t], mine)

    table = table_ref
    step = nev // count_y
    write_phased(
        lambda q, b, block: padded[q, b, block * step : (block + 1) * step].reshape(nev, nev),
        table, 0, 0, sites // nev, phased, 0, sites,
    )
    def forward(z):
        return jnp.dot(
            spread(rows, 2, z, same), padded[:, :, z + 1].reshape(lanes, nev), preferred_element_type=F32
        )

    def backward(z):
        return jnp.dot(
            spread(rows, 3, z - 1, same), padded[:, :, z - 1].reshape(lanes, nev), preferred_element_type=F32
        )

    for z in range(deep):
        in_y = spread(rows, 0, z, above) + spread(rows, 1, z, below)
        terms = jnp.dot(in_y, padded[:, :, z].reshape(lanes, nev), preferred_element_type=F32)
        put_displaced(moved_y, z, terms, count_y, nev)
        terms = forward(z) if z + 1 < deep else 0.0
        if z > 0:
            terms += backward(z)
        put_displaced(moved_z, z, terms, count_y, nev)
    for at, moved in enumerate((moved_y, moved_z)):
        products = jnp.dot(phased[...], moved[...].reshape(3 * sites, 2 * nev), preferred_element_type=F32)
        out_ref[:, 0, :, at * nev : (at + 1) * nev] = partial_rows(combine(products, nev)).astype(BF16)
    top_ref[0] = padded[:, :, deep - 1].reshape(lanes, nev)
    for kind in range(2):
        for ra in range(6):
            line_ref[0, kind * 8 + ra : kind * 8 + ra + 1] = rows[2 + kind, ra, deep - 1 : deep]


def from_rows(ref, depth, count_y, first=0):
    return lambda q, b, z, count: packed_plane(ref, depth, q, b, first + z, count, count_y)


def from_times(ref, t):
    count_y, nev = ref.shape[4:]
    return lambda q, b, z, count: ref[q, b, t, z : z + count].reshape(count * count_y, nev)


def x_terms(odd, at, own, received, own_link, received_link, link_first, table, table_first, rows, phased, moved):
    lanes = rows.shape[3]
    count_z, count_y = moved.shape[2:4]
    nev = moved.shape[4] // 2
    below = odd if at else 1 - odd
    same = site_masks(count_y, lanes)[0]
    entries = [0.5 * jnp.where(below == 1, own_link(e), received_link(e)).astype(F32) for e in range(18)]
    for ra, line in enumerate(link_rows(entries, False, lanes)):
        rows[below, ra] = line
    for ra, line in enumerate(link_rows(entries, True, lanes)):
        rows[1 - below, ra] = -line
    sites = count_z * count_y
    step = nev // count_y
    for vectors, x_at, first in ((own, 0, 0), (received, 2 - below, 3 * sites)):
        write_phased(
            lambda q, b, block: vectors(q, b, block * step, step),
            table, x_at, table_first, sites // nev, phased, first, sites,
        )

    def plane(vectors, z):
        return jnp.concatenate([vectors(q, b, z, 1) for q in range(2) for b in range(3)], axis=0)

    for z in range(count_z):
        line = link_first + z
        terms = jnp.dot(spread(rows, 1, line, same), plane(received, z), preferred_element_type=F32)
        put_displaced(moved.at[0], z, terms, count_y, nev)
        terms = jnp.dot(spread(rows, 0, line, same), plane(own, z), preferred_element_type=F32)
        put_displaced(moved.at[1], z, terms, count_y, nev)
    products = jnp.dot(phased[...], moved[...].reshape(6 * sites, 2 * nev), preferred_element_type=F32)
    return combine(products, nev)


def x_first_kernel(place_ref, v_ref, link_ref, first_ref, second_ref, table, out_ref, rows, phased, moved):
    count_z, count_y = link_ref.shape[3:]
    core, odd = place_ref[0], place_ref[3]
    at_table = pl.multiple_of(core * (count_z * count_y), count_z * count_y)
    for at, got in enumerate((first_ref.at[0], second_ref.at[0])):
        m = 1 - odd if at else odd
        t = core + 2 * m
        parts = x_terms(
            odd, at, from_times(v_ref, t), from_rows(got, count_z, count_y),
            lambda e, t=t: link_ref[0, e, t], lambda e, got=got: packed_link(got, count_z, 0, e, count_z, count_y),
            0, table, at_table, rows, phased, moved,
        )
        for i, part in enumerate(parts):
            out_ref[m, i] = part


def x_part(first, at, place_ref, swap_ref, got, received_link, table, rows, phased, moved):
    held_z = rows.shape[2]
    depth, count_y = moved.shape[2:4]
    odd = place_ref[3]
    at_table = pl.multiple_of((1 - place_ref[0]) * (held_z * count_y) + first * count_y, moved.shape[4] // 2)
    own = swap_ref.at[1 - odd if at else odd]
    return x_terms(
        odd, at, from_rows(own, held_z, count_y, first), from_rows(got, depth, count_y),
        lambda e: packed_link(own, held_z, 0, e, held_z, count_y), received_link,
        first, table, at_table, rows, phased, moved,
    )


def x_middle_kernel(place_ref, swap_ref, first_ref, second_ref, table, before, out_ref, links_ref, *scratch):
    held_z = scratch[0].shape[2]
    depth, count_y = scratch[2].shape[2:4]
    odd = place_ref[3]
    for at, got in enumerate((first_ref.at[0], second_ref.at[0])):
        m = 1 - odd if at else odd
        links_ref[at] = got[got.shape[0] - links_ref.shape[1] :]
        parts = x_part(
            0, at, place_ref, swap_ref, got,
            lambda e, got=got: packed_link(got, depth, 0, e, held_z, count_y), table, *scratch,
        )
        for i, part in enumerate(parts):
            out_ref[m, i] = part + before[m, i]


def boundary(top, halo, lines, table, edge):
    lanes, nev = top.shape
    count_y = lanes // 6
    wide = lanes // 2
    same = site_masks(count_y, lanes)[0]

    def matrix(kind):
        blocks = []
        for ra in range(6):
            line = lines[kind * 8 + ra : kind * 8 + ra + 1, :lanes]
            blocks.append(jnp.broadcast_to(line, (count_y, lanes)).astype(BF16) * same)
        return jnp.concatenate(blocks, axis=0)

    products = 0.0
    for at, (phased, moved, kind) in enumerate(((top, halo, 0), (halo, top, 1))):
        put_phased(
            phased[:wide].T.astype(F32), phased[wide:].T.astype(F32), table, 0,
            table.shape[2] - (at + 1) * nev, edge, at * nev,
        )
        terms = jnp.dot(matrix(kind), moved[...], preferred_element_type=F32).astype(BF16)
        displaced = jnp.concatenate([terms[:wide], terms[wide:]], axis=1)
        products += jnp.dot(edge[:, at * nev : at * nev + wide], displaced, preferred_element_type=F32)
    return combine(products, nev)


def x_last_kernel(place_ref, swap_ref, first_ref, second_ref, link_rows_ref, table, before, sent_ref,
                  top_ref, halo_ref, line_ref, out_ref, rows, phased, moved, edge):
    nev = before.shape[3]
    held_z = rows.shape[2]
    depth, count_y = moved.shape[2:4]
    odd = place_ref[3]
    out_ref[:, :, :, :nev] = sent_ref[:, :, :, :nev]
    for m in range(2):
        above = partial_rows(boundary(top_ref.at[m], halo_ref.at[m], line_ref.at[m], table, edge))
        out_ref[:, m, :, nev : 2 * nev] = (sent_ref[:, m, :, nev:].astype(F32) + above).astype(BF16)
    for at, got in enumerate((first_ref.at[0], second_ref.at[0])):
        m = 1 - odd if at else odd
        parts = x_part(
            held_z - depth, at, place_ref, swap_ref, got,
            lambda e, at=at: packed_link(link_rows_ref.at[at], 0, 0, e, held_z, count_y), table,
            rows, phased, moved,
        )
        parts = [part + before[m, i] for i, part in enumerate(parts)]
        out_ref[:, m, :, 2 * nev :] = partial_rows(parts).astype(BF16)


def total_kernel(directions_ref, got_ref, out_ref, total_ref):
    step = pl.program_id(0)
    part = jnp.sum(got_ref[...].astype(F32), axis=0)

    @pl.when(step == 0)
    def _():
        total_ref[...] = part

    @pl.when(step > 0)
    def _():
        total_ref[...] += part

    @pl.when(step == pl.num_programs(0) - 1)
    def _():
        total = total_ref[...]
        nev = total.shape[1] // 3
        group = out_ref.shape[0]
        in_y, in_z, in_x = (total[:, k * nev : (k + 1) * nev] for k in range(3))
        for d in range(3):
            direction = directions_ref[d]
            chosen = jnp.where(direction == 0, in_x, jnp.where(direction == 1, in_y, in_z))
            for r in range(2):
                for p in range(2):
                    for i in range(group):
                        row = (r * 2 + p) * group + i
                        out_ref[i, 0, p, r : r + 1, d * nev : (d + 1) * nev] = chosen[row : row + 1]


def exchange(first, second):
    count = lax.axis_size("ts")
    got = [None, None]
    for at, array in ((1, second), (0, first)):
        pairs = [(i, (i + 1 if (i + at) % 2 == 0 else i - 1) % count) for i in range(count)]
        got[at] = lax.ppermute(array.reshape(1, -1, array.shape[-1]), "ts", pairs)
    return got


def shards(eigvecs, gauge_links, momenta, directions):
    _, _, count_t, _, count_z, count_y, nev = eigvecs.shape
    vectors = eigvecs.reshape(2, 3, count_t, count_z, count_y, nev)
    links = gauge_links.reshape(3, 18, count_t, count_z, count_y)
    size_x, size_g = lax.axis_size("ts"), lax.axis_size("gz")
    x, g = lax.axis_index("ts"), lax.axis_index("gz")
    core, chip = g % 2, g // 2
    deep = 2 * count_z
    sites = count_z * count_y
    group = nev // size_x

    small = pl.CostEstimate(flops=1_000_000, bytes_accessed=100_000, transcendentals=0)
    limit = pltpu.CompilerParams(vmem_limit_bytes=28 * 1024 * 1024)
    in_vmem = pl.BlockSpec(memory_space=pltpu.VMEM)
    in_smem = pl.BlockSpec(memory_space=pltpu.SMEM)
    planes = link_planes(nev, count_z, count_y)

    place = jnp.stack([core, x, chip * deep, x % 2]).astype(jnp.int32)

    def planes_of(times, depth, directions):
        return jax.ShapeDtypeStruct((times, 6 * depth + directions * planes, count_y, nev), BF16)

    def call(kernel, name, out_shape, scratch_shapes, *operands):
        in_specs = [in_smem] + [in_vmem] * (len(operands) - 1)
        return pl.pallas_call(
            kernel,
            in_specs=in_specs,
            out_specs=jax.tree.map(lambda _: in_vmem, out_shape),
            out_shape=out_shape,
            scratch_shapes=scratch_shapes,
            compiler_params=limit,
            cost_estimate=small,
            name=name,
        )(*operands)

    *mine, given = call(
        pack_kernel, "pack", [planes_of(1, count_z, 1)] * 2 + [planes_of(2, count_z, 3)], [],
        place, vectors, links,
    )
    got_first = exchange(*mine)
    swapped = lax.ppermute(given, "gz", [(0, 1), (1, 0), (2, 3), (3, 2)])
    tail = nev // count_y
    lead = count_z - tail
    table = pl.pallas_call(
        functools.partial(table_kernel, (size_x, count_z * size_g, count_y), deep),
        in_specs=[in_smem, in_smem],
        out_specs=in_vmem,
        out_shape=jax.ShapeDtypeStruct((8, 2, 2 * sites + 2 * nev), F32),
        compiler_params=limit,
        cost_estimate=pl.CostEstimate(flops=10_000_000_000, bytes_accessed=100_000, transcendentals=0),
        name="phase_table",
    )(place, momenta)
    after, _ = lax.optimization_barrier((place, table))
    shapes = [planes_of(1, lead, 1)] * 2 + [jax.ShapeDtypeStruct((2, 6, count_y, nev), BF16)]
    *mine, lowest = call(
        functools.partial(split_first_kernel, count_z), "split_first", shapes, [], after, swapped, vectors
    )
    got_second = exchange(*mine)
    halo = lax.ppermute(lowest.reshape(2, 6 * count_y, nev), "gz", [(0, 2), (2, 0), (1, 3), (3, 1)])

    after, _ = lax.optimization_barrier((place, lowest))
    swapped_rows = swapped.reshape(2, -1, nev)
    sent, top, lines = pl.pallas_call(
        yz_kernel,
        grid=(2,),
        in_specs=[in_smem] + [in_vmem] * 4,
        out_specs=[
            pl.BlockSpec((size_x, 1, 4 * group, 2 * nev), lambda m: (0, m, 0, 0)),
            pl.BlockSpec((1, 6 * count_y, nev), lambda m: (m, 0, 0)),
            pl.BlockSpec((1, 16, 2 * nev), lambda m: (m, 0, 0)),
        ],
        out_shape=[
            jax.ShapeDtypeStruct((size_x, 2, 4 * group, 2 * nev), BF16),
            jax.ShapeDtypeStruct((2, 6 * count_y, nev), BF16),
            jax.ShapeDtypeStruct((2, 16, 2 * nev), F32),
        ],
        scratch_shapes=[
            pltpu.VMEM((4, 6, deep, 2 * nev), F32),
            pltpu.VMEM((2, 3, deep, count_y, nev), BF16),
            pltpu.VMEM((4 * nev, 6 * sites), BF16),
            pltpu.VMEM((3, deep, count_y, 2 * nev), BF16),
            pltpu.VMEM((3, deep, count_y, 2 * nev), BF16),
        ],
        compiler_params=limit,
        cost_estimate=small,
        name="yz_terms",
    )(after, vectors, swapped_rows, links, table)

    after, _, got_first[1] = lax.optimization_barrier((place, sent, got_first[1]))
    mine = call(
        functools.partial(split_last_kernel, count_z), "split_last", [planes_of(1, tail, 0)] * 2, [], after, swapped
    )
    got_last = exchange(*mine)

    def scratch(depth):
        return [
            pltpu.VMEM((2, 6, count_z, 6 * count_y), F32),
            pltpu.VMEM((4 * nev, 6 * depth * count_y), BF16),
            pltpu.VMEM((2, 3, depth, count_y, 2 * nev), BF16),
        ]

    parts = jax.ShapeDtypeStruct((2, 4, nev, nev), F32)
    (part,) = call(
        x_first_kernel, "x_first", [parts], scratch(count_z), after, vectors, links, *got_first, table
    )
    part, links_down = call(
        x_middle_kernel, "x_middle", [parts, jax.ShapeDtypeStruct((2, planes * count_y, nev), BF16)],
        scratch(lead), after, swapped_rows, *got_second, table, part,
    )
    (sent,) = call(
        x_last_kernel, "x_last", [jax.ShapeDtypeStruct((size_x, 2, 4 * group, 3 * nev), BF16)],
        scratch(tail) + [pltpu.VMEM((4 * nev, 2 * nev), BF16)],
        after, swapped_rows, *got_last, links_down, table, part, sent, top, halo, lines,
    )

    pieces = sent.reshape(2 * size_x, 4 * group, 3 * nev)
    groups = [[(ts * 2 + h) * 2 + c for ts in range(size_x) for h in range(2)] for c in range(2)]
    got = lax.all_to_all(pieces, ("ts", "gz"), 0, 0, tiled=True, axis_index_groups=groups)
    out_shape = (group, 1, 2, 2, 3 * nev)
    return pl.pallas_call(
        total_kernel,
        grid=(4,),
        in_specs=[in_smem, pl.BlockSpec((size_x // 2, 4 * group, 3 * nev), lambda i: (i, 0, 0))],
        out_specs=pl.BlockSpec(out_shape, lambda i: (0, 0, 0, 0, 0)),
        out_shape=jax.ShapeDtypeStruct(out_shape, F32),
        scratch_shapes=[pltpu.VMEM((4 * group, 3 * nev), F32)],
        compiler_params=limit,
        name="total",
    )(directions, got)


def solution(mesh):
    in_specs = (
        P(None, None, None, "ts", "gz", None, None),
        P(None, None, None, "ts", "gz", None),
        P(),
        P(),
    )
    out_specs = P("ts", "gz", None, None, None)
    return jax.shard_map(shards, mesh=mesh, in_specs=in_specs, out_specs=out_specs, check_vma=False)
```

time: 81.8 us -> 77.8 us (0.951)
  waiting for transfers between devices: 0.02 us -> 4.35 us
  starting transfers between devices: 22.9 us -> 18.8 us
  Pallas kernels: 31.9 us -> 29 us
  local copies, waits for them, and re-layouts: 6.18 us -> 4.16 us
    ppermute x7, waiting for transfers between devices: 0.02 us -> 4.34 us  [the longest x6 3.68 us: exchange(): got[at] = lax.ppermute(array.reshape(1, -1, array.shape[-1]), 'ts', pairs)]
    ppermute x7, starting transfers between devices: 22.9 us -> 18.8 us  [the longest x6 16 us: exchange(): got[at] = lax.ppermute(array.reshape(1, -1, array.shape[-1]), 'ts', pairs)]
    pallas_call x9, Pallas kernels: 31.9 us -> 29 us  [the longest x6 16.4 us: call(): pl.pallas_call(kernel, in_specs=in_specs, out_specs=jax.tree.map(lambda _...]
    unnamed x18 -> x10, local copies, waits for them, and re-layouts: 6.18 us -> 4.16 us
  transfers between devices with their start and end apart: 8 -> 8, of which waited for: 0 -> 2; matrix products, arithmetic and copies ran while one was open for 0% -> 0% of each run, Pallas kernels for 32% -> 31%
where the time goes in v5:
time: 77.8 us; the launch traced here: 77.5 us
  Pallas kernels  29 us (37%)
  blocking collectives  20.9 us (27%)
  starting transfers between devices  18.8 us (24%)
  waiting for transfers between devices  4.35 us (6%)
  local copies, waits for them, and re-layouts  4.16 us (5%)
    all_to_all x1, blocking collectives, shards(): lax.all_to_all(pieces, ('ts', 'gz'), 0, 0, tiled=True, axis_index_groups=...  20.9 us
    pallas_call x6, Pallas kernels, call(): pl.pallas_call(kernel, in_specs=in_specs, out_specs=jax.tree.map(lambda _...  16.4 us
    ppermute x6, starting transfers between devices, exchange(): got[at] = lax.ppermute(array.reshape(1, -1, array.shape[-1]), 'ts', pairs)  16 us
    pallas_call x1, Pallas kernels, shards(): pl.pallas_call(yz_kernel, grid=(2,), in_specs=[in_smem] + [in_vmem] * 4,...  10.5 us
    unnamed x10, local copies, waits for them, and re-layouts  4.16 us
    ppermute x6, waiting for transfers between devices, exchange(): got[at] = lax.ppermute(array.reshape(1, -1, array.shape[-1]), 'ts', pairs)  3.68 us
    ppermute x1, starting transfers between devices, shards(): lax.ppermute(lowest.reshape(2, 6 * count_y, nev), 'gz', [(0, 2), (2, 0),...  2.73 us
  transfers between devices with their start and end apart: 8, of which 2 were waited for; matrix products, arithmetic and copies ran while one was open for 0% of the time, Pallas kernels for 31%

profile of v5, /device:TPU:0, one launch (start us, length us, event | category | flops | bytes accessed | tf_op | source)
XLA Modules:
  0.0 77.5 jit_solution(5239065875209864587)
XLA Ops:
  0.0 0.1 pad_add_fusion.place_ref
  0.1 1.9 %copy-done = bf16[2,3,4,1,16,32,128]{6,5,4,3,2,1,0:T(8,128)(2,1)S(1)} copy-done((bf16[2,3,4,1,16,32,128]{6,5,4,3,2,1,0:T(8,128)(2,1)S(1)}, bf16[2,3,4,1,16,32,128]{6,5,4,3,2,1,0:T(8,128)(2,1)}, u32[]{:S(2)}) %copy-start) | copy-done | bytes 3145752
  2.0 1.2 %copy-done.2 = bf16[3,18,4,1,16,32]{5,4,3,2,1,0:T(8,128)(2,1)S(1)} copy-done((bf16[3,18,4,1,16,32]{5,4,3,2,1,0:T(8,128)(2,1)S(1)}, bf16[3,18,4,1,16,32]{5,4,3,2,1,0:T(8,128)(2,1)}, u32[]{:S(2)}) %copy-start.2) | copy-done | bytes 221208
  3.1 0.9 %pack.1 = (bf16[1,99,32,128]{3,2,1,0:T(8,128)(2,1)S(1)}, bf16[1,99,32,128]{3,2,1,0:T(8,128)(2,1)S(1)}, bf16[2,105,32,128]{3,2,1,0:T(8,128)(2,1)S(1)}) custom-call(s32[4]{0:T(128)S(1)} %pad_add_fusion.place_ref, bf16[2,3,4,16,32,128]{5,4,3,2,1,0:T(8,128)(2,1)S(1)} %bitcast.15, bf16[3,18,4,16,32]{4,3,2,1,0:T(8,128)(2,1)S(1)} %bitcast.22), custom_call_target="tpu_custom_call" | custom-call | flops 1000000 | bytes 100000 | tf_op jit(solution)/shard_map/pack/pallas_call | solution.py:472
  4.1 0.1 collective-permute-start
  4.2 7.6 %collective-permute-start.1 = (bf16[1,3168,128]{2,1,0:T(8,128)(2,1)S(1)}, bf16[1,3168,128]{2,1,0:T(8,128)(2,1)S(1)}, u32[]{:S(2)}, u32[]{:S(2)}) collective-permute-start(bf16[1,3168,128]{2,1,0:T(8,128)(2,1)S(1)} %bitcast.27), channel_id=1, source_target_pairs={{0,124},{4,8},{8,4},{12,16},{16,12},{20,24},{24,20},{28,32},{32,28... | collective-permute-start | bytes 2433032 | tf_op jit(solution)/shard_map/ppermute | solution.py:444
  11.7 0.0 collective-permute-start.6
  11.7 0.8 phase_table.1.table_ref.table
  12.5 0.0 collective-permute-done.swap_ref
  12.5 1.1 %copy-done.1 = bf16[2,3,4,1,16,32,128]{6,5,4,3,2,1,0:T(8,128)(2,1)S(1)} copy-done((bf16[2,3,4,1,16,32,128]{6,5,4,3,2,1,0:T(8,128)(2,1)S(1)}, bf16[2,3,4,1,16,32,128]{6,5,4,3,2,1,0:T(8,128)(2,1)}, u32[]{:S(2)}) %copy-start.1) | copy-done | bytes 3145752
  13.6 0.7 split_first.1
  14.3 1.7 %collective-permute-start.5 = (bf16[1,2400,128]{2,1,0:T(8,128)(2,1)S(1)}, bf16[1,2400,128]{2,1,0:T(8,128)(2,1)S(1)}, u32[]{:S(2)}, u32[]{:S(2)}) collective-permute-start(bf16[1,2400,128]{2,1,0:T(8,128)(2,1)S(1)} %bitcast.29), channel_id=1, source_target_pairs={{0,124},{4,8},{8,4},{12,16},{16,12},{20,24},{24,20},{28,32},{32,28... | collective-permute-start | bytes 1843208 | tf_op jit(solution)/shard_map/ppermute | solution.py:444
  16.0 0.5 collective-permute-start.4
  16.5 10.5 %yz_terms.1 = (bf16[32,2,16,256]{3,2,1,0:T(8,128)(2,1)S(1)}, bf16[2,192,128]{2,1,0:T(8,128)(2,1)S(1)}, f32[2,16,256]{2,1,0:T(8,128)S(1)}) custom-call(s32[4]{0:T(128)S(1)} %pad_add_fusion.place_ref, bf16[2,3,4,16,32,128]{5,4,3,2,1,0:T(8,128)(2,1)S(1)} %bitcast.17, bf16[2,3360,128]{2,1,0:T(8,128)(2,1)S(1)} %bitcast.19, ...), custom_call_target="tpu_custom_call" | custom-call | flops 1000000 | bytes 100000 | tf_op jit(solution)/shard_map/yz_terms/pallas_call | solution.py:510
  27.0 3.7 %collective-permute-done.1.second_ref = bf16[1,3168,128]{2,1,0:T(8,128)(2,1)S(1)} collective-permute-done((bf16[1,3168,128]{2,1,0:T(8,128)(2,1)S(1)}, bf16[1,3168,128]{2,1,0:T(8,128)(2,1)S(1)}, u32[]{:S(2)}, u32[]{:S(2)}) %collective-permute-start.1) | collective-permute-done | bytes 811040 | tf_op jit(solution)/shard_map/ppermute | solution.py:444
  30.6 0.6 split_last.1
  31.2 6.3 %collective-permute-start.3 = (bf16[1,768,128]{2,1,0:T(8,128)(2,1)S(1)}, bf16[1,768,128]{2,1,0:T(8,128)(2,1)S(1)}, u32[]{:S(2)}, u32[]{:S(2)}) collective-permute-start(bf16[1,768,128]{2,1,0:T(8,128)(2,1)S(1)} %bitcast.31), channel_id=1, source_target_pairs={{0,124},{4,8},{8,4},{12,16},{16,12},{20,24},{24,20},{28,32},{32,28... | collective-permute-start | bytes 589832 | tf_op jit(solution)/shard_map/ppermute | solution.py:444
  37.5 2.7 %collective-permute-start.7 = (bf16[2,192,128]{2,1,0:T(8,128)(2,1)S(1)}, bf16[2,192,128]{2,1,0:T(8,128)(2,1)S(1)}, u32[]{:S(2)}, u32[]{:S(2)}) collective-permute-start(bf16[2,192,128]{2,1,0:T(8,128)(2,1)S(1)} %bitcast.32), channel_id=1, source_target_pairs={{0,2},{2,0},{1,3},{3,1},{4,6},{6,4},{5,7},{7,5},{8,10},{10,8},{9,1... | collective-permute-start | bytes 294920 | tf_op jit(solution)/shard_map/ppermute | solution.py:506
  40.2 6.5 %x_first.1.before = f32[2,4,128,128]{3,2,1,0:T(8,128)S(1)} custom-call(s32[4]{0:T(128)S(1)} %pad_add_fusion.place_ref, bf16[2,3,4,16,32,128]{5,4,3,2,1,0:T(8,128)(2,1)S(1)} %bitcast.18, bf16[3,18,4,16,32]{4,3,2,1,0:T(8,128)(2,1)S(1)} %bitcast.24, bf16[1,3168,128]{2,1,0:T(8,128)(2,1)S(1)} %collective-permute-done.6.first_ref, ...), custom_call_target="tpu_custom_call" | custom-call | flops 1000000 | bytes 100000 | tf_op jit(solution)/shard_map/x_first/pallas_call | solution.py:472
  46.8 4.9 %x_middle.1 = (f32[2,4,128,128]{3,2,1,0:T(8,128)S(1)}, bf16[2,96,128]{2,1,0:T(8,128)(2,1)S(1)}) custom-call(s32[4]{0:T(128)S(1)} %pad_add_fusion.place_ref, bf16[2,3360,128]{2,1,0:T(8,128)(2,1)S(1)} %bitcast.20, bf16[1,2400,128]{2,1,0:T(8,128)(2,1)S(1)} %collective-permute-done.4.first_ref, bf16[1,2400,128]{2,1,0:T(8,128)(2,1)S(1)} %collective-permute-done.5.second_ref, ...), custom_call_target="tpu_custom_call" | custom-call | flops 1000000 | bytes 100000 | tf_op jit(solution)/shard_map/x_middle/pallas_call | solution.py:472
  51.7 0.7 collective-permute-done.7.halo_ref
  52.3 2.8 %x_last.1 = bf16[32,2,16,384]{3,2,1,0:T(8,128)(2,1)S(1)} custom-call(s32[4]{0:T(128)S(1)} %pad_add_fusion.place_ref, bf16[2,3360,128]{2,1,0:T(8,128)(2,1)S(1)} %bitcast.21, bf16[1,768,128]{2,1,0:T(8,128)(2,1)S(1)} %collective-permute-done.2.first_ref, bf16[1,768,128]{2,1,0:T(8,128)(2,1)S(1)} %collective-permute-done.3.second_ref, ...), custom_call_target="tpu_custom_call" | custom-call | flops 1000000 | bytes 100000 | tf_op jit(solution)/shard_map/x_last/pallas_call | solution.py:472
  55.2 20.9 %all_to_all.5.got_ref = bf16[64,16,384]{2,1,0:T(8,128)(2,1)S(1)} all-to-all(bf16[64,16,384]{2,1,0:T(8,128)(2,1)S(1)} %bitcast.25), channel_id=1, replica_groups={{0,2,4,6,8,10,12,14,16,18,20,22,24,26,28,30,32,34,36,38,40,42,44,46,48,..., dimensions={0} | all-to-all | bytes 1572864 | tf_op jit(solution)/shard_map/all_to_all | solution.py:565
  76.1 1.4 %total.1 = f32[4,1,2,2,384]{4,3,2,1,0:T(2,128)} custom-call(s32[3]{0:T(128)S(1)} %copy-done.3, bf16[64,16,384]{2,1,0:T(8,128)(2,1)S(1)} %all_to_all.5.got_ref), custom_call_target="tpu_custom_call" | custom-call | tf_op jit(solution)/shard_map/total/pallas_call | solution.py:567
  (13 shorter events, 0.0 us)
Async XLA Ops:
  0.1 1.9 %copy-start = (bf16[2,3,4,1,16,32,128]{6,5,4,3,2,1,0:T(8,128)(2,1)S(1)}, bf16[2,3,4,1,16,32,128]{6,5,4,3,2,1,0:T(8,128)(2,1)}, u32[]{:S(2)}) copy-start(bf16[2,3,4,1,16,32,128]{6,5,4,3,2,1,0:T(8,128)(2,1)} %param.4) | copy-start | bytes 9437188
  2.0 1.2 %copy-start.2 = (bf16[3,18,4,1,16,32]{5,4,3,2,1,0:T(8,128)(2,1)S(1)}, bf16[3,18,4,1,16,32]{5,4,3,2,1,0:T(8,128)(2,1)}, u32[]{:S(2)}) copy-start(bf16[3,18,4,1,16,32]{5,4,3,2,1,0:T(8,128)(2,1)} %param.5) | copy-start | bytes 663556
  3.1 8.6 %copy-start.4 = (s32[2,3]{1,0:T(2,128)S(1)}, s32[2,3]{1,0:T(2,128)}, u32[]{:S(2)}) copy-start(s32[2,3]{1,0:T(2,128)} %momenta_ref.1) | copy-start | bytes 76
  4.1 8.5 %collective-permute-start = (bf16[2,105,32,128]{3,2,1,0:T(8,128)(2,1)S(1)}, bf16[2,105,32,128]{3,2,1,0:T(8,128)(2,1)S(1)}, u32[]{:S(2)}, u32[]{:S(2)}) collective-permute-start(bf16[2,105,32,128]{3,2,1,0:T(8,128)(2,1)S(1)} %get-tuple-element.23), channel_id=1, source_target_pairs={{0,1},{1,0},{2,3},{3,2},{4,5},{5,4},{6,7},{7,6},{8,9},{9,8},{10,11... | collective-permute-start | bytes 5160968 | tf_op jit(solution)/shard_map/ppermute | solution.py:488
  4.2 26.5 %collective-permute-start.1 = (bf16[1,3168,128]{2,1,0:T(8,128)(2,1)S(1)}, bf16[1,3168,128]{2,1,0:T(8,128)(2,1)S(1)}, u32[]{:S(2)}, u32[]{:S(2)}) collective-permute-start(bf16[1,3168,128]{2,1,0:T(8,128)(2,1)S(1)} %bitcast.27), channel_id=1, source_target_pairs={{0,124},{4,8},{8,4},{12,16},{16,12},{20,24},{24,20},{28,32},{32,28... | collective-permute-start | bytes 2433032 | tf_op jit(solution)/shard_map/ppermute | solution.py:444
  11.7 25.8 %collective-permute-start.6 = (bf16[1,3168,128]{2,1,0:T(8,128)(2,1)S(1)}, bf16[1,3168,128]{2,1,0:T(8,128)(2,1)S(1)}, u32[]{:S(2)}, u32[]{:S(2)}) collective-permute-start(bf16[1,3168,128]{2,1,0:T(8,128)(2,1)S(1)} %bitcast.26), channel_id=1, source_target_pairs={{0,4},{4,0},{8,12},{12,8},{16,20},{20,16},{24,28},{28,24},{32,36},... | collective-permute-start | bytes 2433032 | tf_op jit(solution)/shard_map/ppermute | solution.py:444
  11.7 1.9 %copy-start.1 = (bf16[2,3,4,1,16,32,128]{6,5,4,3,2,1,0:T(8,128)(2,1)S(1)}, bf16[2,3,4,1,16,32,128]{6,5,4,3,2,1,0:T(8,128)(2,1)}, u32[]{:S(2)}) copy-start(bf16[2,3,4,1,16,32,128]{6,5,4,3,2,1,0:T(8,128)(2,1)} %param.4) | copy-start | bytes 9437188
  14.3 32.5 %collective-permute-start.5 = (bf16[1,2400,128]{2,1,0:T(8,128)(2,1)S(1)}, bf16[1,2400,128]{2,1,0:T(8,128)(2,1)S(1)}, u32[]{:S(2)}, u32[]{:S(2)}) collective-permute-start(bf16[1,2400,128]{2,1,0:T(8,128)(2,1)S(1)} %bitcast.29), channel_id=1, source_target_pairs={{0,124},{4,8},{8,4},{12,16},{16,12},{20,24},{24,20},{28,32},{32,28... | collective-permute-start | bytes 1843208 | tf_op jit(solution)/shard_map/ppermute | solution.py:444
  16.0 30.7 %collective-permute-start.4 = (bf16[1,2400,128]{2,1,0:T(8,128)(2,1)S(1)}, bf16[1,2400,128]{2,1,0:T(8,128)(2,1)S(1)}, u32[]{:S(2)}, u32[]{:S(2)}) collective-permute-start(bf16[1,2400,128]{2,1,0:T(8,128)(2,1)S(1)} %bitcast.28), channel_id=1, source_target_pairs={{0,4},{4,0},{8,12},{12,8},{16,20},{20,16},{24,28},{28,24},{32,36},... | collective-permute-start | bytes 1843208 | tf_op jit(solution)/shard_map/ppermute | solution.py:444
  31.2 21.1 %collective-permute-start.3 = (bf16[1,768,128]{2,1,0:T(8,128)(2,1)S(1)}, bf16[1,768,128]{2,1,0:T(8,128)(2,1)S(1)}, u32[]{:S(2)}, u32[]{:S(2)}) collective-permute-start(bf16[1,768,128]{2,1,0:T(8,128)(2,1)S(1)} %bitcast.31), channel_id=1, source_target_pairs={{0,124},{4,8},{8,4},{12,16},{16,12},{20,24},{24,20},{28,32},{32,28... | collective-permute-start | bytes 589832 | tf_op jit(solution)/shard_map/ppermute | solution.py:444
  37.5 14.8 %collective-permute-start.2 = (bf16[1,768,128]{2,1,0:T(8,128)(2,1)S(1)}, bf16[1,768,128]{2,1,0:T(8,128)(2,1)S(1)}, u32[]{:S(2)}, u32[]{:S(2)}) collective-permute-start(bf16[1,768,128]{2,1,0:T(8,128)(2,1)S(1)} %bitcast.30), channel_id=1, source_target_pairs={{0,4},{4,0},{8,12},{12,8},{16,20},{20,16},{24,28},{28,24},{32,36},... | collective-permute-start | bytes 589832 | tf_op jit(solution)/shard_map/ppermute | solution.py:444
  37.5 14.8 %collective-permute-start.7 = (bf16[2,192,128]{2,1,0:T(8,128)(2,1)S(1)}, bf16[2,192,128]{2,1,0:T(8,128)(2,1)S(1)}, u32[]{:S(2)}, u32[]{:S(2)}) collective-permute-start(bf16[2,192,128]{2,1,0:T(8,128)(2,1)S(1)} %bitcast.32), channel_id=1, source_target_pairs={{0,2},{2,0},{1,3},{3,1},{4,6},{6,4},{5,7},{7,5},{8,10},{10,8},{9,1... | collective-permute-start | bytes 294920 | tf_op jit(solution)/shard_map/ppermute | solution.py:506
  52.3 23.8 %copy-start.3 = (s32[3]{0:T(128)S(1)}, s32[3]{0:T(128)}, u32[]{:S(2)}) copy-start(s32[3]{0:T(128)} %directions_ref.1) | copy-start | bytes 40

commit v6 on v5

--- a/solution.py
+++ b/solution.py
@@ -155,46 +155,38 @@
         out_ref[at, first_plane + row // per_plane, first : first + count_z] = jnp.concatenate(held, axis=1)
 
 
-def pack_kernel(place_ref, v_ref, link_ref, first_ref, second_ref, given_ref):
+def pack_own_kernel(place_ref, v_ref, link_ref, first_ref, second_ref):
     count_z, count_y, nev = v_ref.shape[3:]
     core, odd = place_ref[0], place_ref[3]
-    planes = link_planes(nev, count_z, count_y)
-    for out_ref, at, t in (
-        (first_ref, 0, core + 2 * (1 - odd)),
-        (second_ref, 0, core + 2 * odd),
-        (given_ref, 0, 1 - core),
-        (given_ref, 1, 3 - core),
-    ):
+    for out_ref, t in ((first_ref, core + 2 * (1 - odd)), (second_ref, core + 2 * odd)):
         for held in range(6):
-            out_ref[at, held * count_z : (held + 1) * count_z] = v_ref[held // 3, held % 3, t]
-    for out_ref, at, t, directions in (
-        (first_ref, 0, core + 2 * (1 - odd), 1),
-        (second_ref, 0, core + 2 * odd, 1),
-        (given_ref, 0, 1 - core, 3),
-        (given_ref, 1, 3 - core, 3),
-    ):
-        for k in range(directions):
-            put_links(
-                out_ref, at, 6 * count_z + k * planes, lambda e, k=k, t=t: link_ref[k, e, t], count_z, count_y, nev
-            )
+            out_ref[0, held * count_z : (held + 1) * count_z] = v_ref[held // 3, held % 3, t]
+        put_links(out_ref, 0, 6 * count_z, lambda e, t=t: link_ref[0, e, t], count_z, count_y, nev)
+
+
+def pack_given_kernel(place_ref, v_ref, given_ref):
+    count_z = v_ref.shape[3]
+    for m in range(2):
+        for held in range(6):
+            given_ref[m, held * count_z : (held + 1) * count_z] = v_ref[held // 3, held % 3, 1 - place_ref[0] + 2 * m]
 
 
 def split(place_ref, swap_ref, start, count_z, out_refs):
     odd = place_ref[3]
+    depth = out_refs[0].shape[1] // 6
     for i, out_ref in enumerate(out_refs):
-        m = odd if i else 1 - odd
-        behind = out_ref.shape[1] % 6
-        depth = out_ref.shape[1] // 6
         for held in range(6):
             first = held * count_z + start
-            out_ref[0, held * depth : (held + 1) * depth] = swap_ref[m, first : first + depth]
-        if behind:
-            out_ref[0, 6 * depth :] = swap_ref[m, 6 * count_z : 6 * count_z + behind]
-
-
-def split_first_kernel(count_z, place_ref, swap_ref, v_ref, first_ref, second_ref, lowest_ref):
+            out_ref[0, held * depth : (held + 1) * depth] = swap_ref[odd if i else 1 - odd, first : first + depth]
+
+
+def split_first_kernel(count_z, place_ref, swap_ref, link_ref, v_ref, first_ref, second_ref, lowest_ref):
+    count_y, nev = v_ref.shape[4:]
     split(place_ref, swap_ref, 0, count_z, (first_ref, second_ref))
-    core = place_ref[0]
+    core, odd = place_ref[0], place_ref[3]
+    for out_ref, t in ((first_ref, core + 2 * (1 - odd)), (second_ref, core + 2 * odd)):
+        depth = out_ref.shape[1] // 6
+        put_links(out_ref, 0, 6 * depth, lambda e, t=t: link_ref[0, e, t], count_z, count_y, nev)
     for m in range(2):
         for i in range(6):
             own = v_ref[i // 3, i % 3, core + 2 * m, 0]
@@ -205,7 +197,7 @@
     split(place_ref, swap_ref, count_z - first_ref.shape[1] // 6, count_z, (first_ref, second_ref))
 
 
-def yz_kernel(place_ref, v_ref, swap_ref, link_ref, table_ref, out_ref, top_ref, line_ref,
+def yz_kernel(place_ref, v_ref, swap_ref, link_ref, other_link_ref, table_ref, out_ref, top_ref, line_ref,
               rows, padded, phased, moved_y, moved_z):
     core = place_ref[0]
     step_m = pl.program_id(0)
@@ -241,7 +233,7 @@
         for b in range(3):
             block = packed_plane(swapped, count_z, q, b, 0, count_z, count_y)
             padded[q, b, pl.ds(theirs, count_z)] = block.reshape(count_z, count_y, nev)
-    fill_rows(lambda k, e: packed_link(swapped, count_z, k, e, count_z, count_y), theirs)
+    fill_rows(lambda k, e: other_link_ref[k, e, t], theirs)
     fill_rows(lambda k, e: link_ref[k, e, t], mine)
 
     table = table_ref
@@ -334,32 +326,17 @@
             out_ref[m, i] = part
 
 
-def x_part(first, at, place_ref, swap_ref, got, received_link, table, rows, phased, moved):
+def x_part(first, at, place_ref, swap_ref, link_ref, got, received_link, table, rows, phased, moved):
     held_z = rows.shape[2]
     depth, count_y = moved.shape[2:4]
-    odd = place_ref[3]
-    at_table = pl.multiple_of((1 - place_ref[0]) * (held_z * count_y) + first * count_y, moved.shape[4] // 2)
-    own = swap_ref.at[1 - odd if at else odd]
+    core, odd = place_ref[0], place_ref[3]
+    m = 1 - odd if at else odd
+    at_table = pl.multiple_of((1 - core) * (held_z * count_y) + first * count_y, moved.shape[4] // 2)
     return x_terms(
-        odd, at, from_rows(own, held_z, count_y, first), from_rows(got, depth, count_y),
-        lambda e: packed_link(own, held_z, 0, e, held_z, count_y), received_link,
+        odd, at, from_rows(swap_ref.at[m], held_z, count_y, first), from_rows(got, depth, count_y),
+        lambda e: link_ref[0, e, core + 2 * m], received_link,
         first, table, at_table, rows, phased, moved,
     )
-
-
-def x_middle_kernel(place_ref, swap_ref, first_ref, second_ref, table, before, out_ref, links_ref, *scratch):
-    held_z = scratch[0].shape[2]
-    depth, count_y = scratch[2].shape[2:4]
-    odd = place_ref[3]
-    for at, got in enumerate((first_ref.at[0], second_ref.at[0])):
-        m = 1 - odd if at else odd
-        links_ref[at] = got[got.shape[0] - links_ref.shape[1] :]
-        parts = x_part(
-            0, at, place_ref, swap_ref, got,
-            lambda e, got=got: packed_link(got, depth, 0, e, held_z, count_y), table, *scratch,
-        )
-        for i, part in enumerate(parts):
-            out_ref[m, i] = part + before[m, i]
 
 
 def boundary(top, halo, lines, table, edge):
@@ -387,25 +364,45 @@
     return combine(products, nev)
 
 
-def x_last_kernel(place_ref, swap_ref, first_ref, second_ref, link_rows_ref, table, before, sent_ref,
-                  top_ref, halo_ref, line_ref, out_ref, rows, phased, moved, edge):
-    nev = before.shape[3]
+def x_middle(at, place_ref, swap_ref, link_ref, got_ref, table, before, out_ref, links_ref, *scratch):
+    held_z = scratch[0].shape[2]
+    depth, count_y = scratch[2].shape[2:4]
+    odd = place_ref[3]
+    got = got_ref.at[0]
+    links_ref[...] = got[got.shape[0] - links_ref.shape[0] :]
+    parts = x_part(
+        0, at, place_ref, swap_ref, link_ref, got,
+        lambda e: packed_link(got, depth, 0, e, held_z, count_y), table, *scratch,
+    )
+    for i, part in enumerate(parts):
+        out_ref[i] = part + before[1 - odd if at else odd, i]
+
+
+def x_last(at, place_ref, swap_ref, link_ref, got_ref, links_ref, table, before, pieces_ref, rows, phased, moved):
+    nev = before.shape[2]
     held_z = rows.shape[2]
     depth, count_y = moved.shape[2:4]
     odd = place_ref[3]
-    out_ref[:, :, :, :nev] = sent_ref[:, :, :, :nev]
+    parts = x_part(
+        held_z - depth, at, place_ref, swap_ref, link_ref, got_ref.at[0],
+        lambda e: packed_link(links_ref, 0, 0, e, held_z, count_y), table, rows, phased, moved,
+    )
+    parts = [part + before[i] for i, part in enumerate(parts)]
+    pieces_ref[:, 1 - odd if at else odd, :, 2 * nev :] = partial_rows(parts).astype(BF16)
+
+
+def x_last_first(place_ref, swap_ref, link_ref, got_ref, links_ref, table, before, sent_ref, pieces_ref, *scratch):
+    pieces_ref[:, :, :, : sent_ref.shape[3]] = sent_ref[...]
+    x_last(0, place_ref, swap_ref, link_ref, got_ref, links_ref, table, before, pieces_ref, *scratch)
+
+
+def x_last_second(place_ref, swap_ref, link_ref, got_ref, links_ref, table, before, top_ref, halo_ref, line_ref, sent_ref,
+                  pieces_ref, rows, phased, moved, edge):
+    nev = before.shape[2]
     for m in range(2):
         above = partial_rows(boundary(top_ref.at[m], halo_ref.at[m], line_ref.at[m], table, edge))
-        out_ref[:, m, :, nev : 2 * nev] = (sent_ref[:, m, :, nev:].astype(F32) + above).astype(BF16)
-    for at, got in enumerate((first_ref.at[0], second_ref.at[0])):
-        m = 1 - odd if at else odd
-        parts = x_part(
-            held_z - depth, at, place_ref, swap_ref, got,
-            lambda e, at=at: packed_link(link_rows_ref.at[at], 0, 0, e, held_z, count_y), table,
-            rows, phased, moved,
-        )
-        parts = [part + before[m, i] for i, part in enumerate(parts)]
-        out_ref[:, m, :, 2 * nev :] = partial_rows(parts).astype(BF16)
+        pieces_ref[:, m, :, nev : 2 * nev] = (sent_ref[:, m, :, nev : 2 * nev].astype(F32) + above).astype(BF16)
+    x_last(1, place_ref, swap_ref, link_ref, got_ref, links_ref, table, before, pieces_ref, rows, phased, moved)
 
 
 def total_kernel(directions_ref, got_ref, out_ref, total_ref):
@@ -439,7 +436,7 @@
 def exchange(first, second):
     count = lax.axis_size("ts")
     got = [None, None]
-    for at, array in ((1, second), (0, first)):
+    for at, array in ((0, first), (1, second)):
         pairs = [(i, (i + 1 if (i + at) % 2 == 0 else i - 1) % count) for i in range(count)]
         got[at] = lax.ppermute(array.reshape(1, -1, array.shape[-1]), "ts", pairs)
     return got
@@ -457,7 +454,7 @@
     group = nev // size_x
 
     small = pl.CostEstimate(flops=1_000_000, bytes_accessed=100_000, transcendentals=0)
-    limit = pltpu.CompilerParams(vmem_limit_bytes=28 * 1024 * 1024)
+    limit = pltpu.CompilerParams(vmem_limit_bytes=20 * 1024 * 1024)
     in_vmem = pl.BlockSpec(memory_space=pltpu.VMEM)
     in_smem = pl.BlockSpec(memory_space=pltpu.SMEM)
     planes = link_planes(nev, count_z, count_y)
@@ -467,7 +464,7 @@
     def planes_of(times, depth, directions):
         return jax.ShapeDtypeStruct((times, 6 * depth + directions * planes, count_y, nev), BF16)
 
-    def call(kernel, name, out_shape, scratch_shapes, *operands):
+    def call(kernel, name, out_shape, scratch_shapes, *operands, aliases={}):
         in_specs = [in_smem] + [in_vmem] * (len(operands) - 1)
         return pl.pallas_call(
             kernel,
@@ -475,17 +472,19 @@
             out_specs=jax.tree.map(lambda _: in_vmem, out_shape),
             out_shape=out_shape,
             scratch_shapes=scratch_shapes,
+            input_output_aliases=aliases,
             compiler_params=limit,
             cost_estimate=small,
             name=name,
         )(*operands)
 
-    *mine, given = call(
-        pack_kernel, "pack", [planes_of(1, count_z, 1)] * 2 + [planes_of(2, count_z, 3)], [],
-        place, vectors, links,
-    )
+    swap = [(0, 1), (1, 0), (2, 3), (3, 2)]
+    other_links = lax.ppermute(gauge_links, "gz", swap).reshape(links.shape)
+    mine = call(pack_own_kernel, "pack_own", [planes_of(1, count_z, 1)] * 2, [], place, vectors, links)
     got_first = exchange(*mine)
-    swapped = lax.ppermute(given, "gz", [(0, 1), (1, 0), (2, 3), (3, 2)])
+    after, other_links, _ = lax.optimization_barrier((place, other_links, mine[0]))
+    (given,) = call(pack_given_kernel, "pack_given", [planes_of(2, count_z, 0)], [], after, vectors)
+    swapped = lax.ppermute(given, "gz", swap)
     tail = nev // count_y
     lead = count_z - tail
     table = pl.pallas_call(
@@ -494,13 +493,13 @@
         out_specs=in_vmem,
         out_shape=jax.ShapeDtypeStruct((8, 2, 2 * sites + 2 * nev), F32),
         compiler_params=limit,
-        cost_estimate=pl.CostEstimate(flops=10_000_000_000, bytes_accessed=100_000, transcendentals=0),
+        cost_estimate=pl.CostEstimate(flops=20_000_000_000, bytes_accessed=100_000, transcendentals=0),
         name="phase_table",
     )(place, momenta)
     after, _ = lax.optimization_barrier((place, table))
     shapes = [planes_of(1, lead, 1)] * 2 + [jax.ShapeDtypeStruct((2, 6, count_y, nev), BF16)]
     *mine, lowest = call(
-        functools.partial(split_first_kernel, count_z), "split_first", shapes, [], after, swapped, vectors
+        functools.partial(split_first_kernel, count_z), "split_first", shapes, [], after, swapped, other_links, vectors
     )
     got_second = exchange(*mine)
     halo = lax.ppermute(lowest.reshape(2, 6 * count_y, nev), "gz", [(0, 2), (2, 0), (1, 3), (3, 1)])
@@ -510,7 +509,7 @@
     sent, top, lines = pl.pallas_call(
         yz_kernel,
         grid=(2,),
-        in_specs=[in_smem] + [in_vmem] * 4,
+        in_specs=[in_smem] + [in_vmem] * 5,
         out_specs=[
             pl.BlockSpec((size_x, 1, 4 * group, 2 * nev), lambda m: (0, m, 0, 0)),
             pl.BlockSpec((1, 6 * count_y, nev), lambda m: (m, 0, 0)),
@@ -531,9 +530,9 @@
         compiler_params=limit,
         cost_estimate=small,
         name="yz_terms",
-    )(after, vectors, swapped_rows, links, table)
-
-    after, _, got_first[1] = lax.optimization_barrier((place, sent, got_first[1]))
+    )(after, vectors, swapped_rows, links, other_links, table)
+
+    after, _ = lax.optimization_barrier((place, sent))
     mine = call(
         functools.partial(split_last_kernel, count_z), "split_last", [planes_of(1, tail, 0)] * 2, [], after, swapped
     )
@@ -550,17 +549,26 @@
     (part,) = call(
         x_first_kernel, "x_first", [parts], scratch(count_z), after, vectors, links, *got_first, table
     )
-    part, links_down = call(
-        x_middle_kernel, "x_middle", [parts, jax.ShapeDtypeStruct((2, planes * count_y, nev), BF16)],
-        scratch(lead), after, swapped_rows, *got_second, table, part,
-    )
-    (sent,) = call(
-        x_last_kernel, "x_last", [jax.ShapeDtypeStruct((size_x, 2, 4 * group, 3 * nev), BF16)],
-        scratch(tail) + [pltpu.VMEM((4 * nev, 2 * nev), BF16)],
-        after, swapped_rows, *got_last, links_down, table, part, sent, top, halo, lines,
-    )
-
-    pieces = sent.reshape(2 * size_x, 4 * group, 3 * nev)
+    one = [jax.ShapeDtypeStruct(parts.shape[1:], F32), jax.ShapeDtypeStruct((planes * count_y, nev), BF16)]
+    all_pieces = [jax.ShapeDtypeStruct((size_x, 2, 4 * group, 3 * nev), BF16)]
+    operands = after, swapped_rows, other_links
+    first, first_links = call(
+        functools.partial(x_middle, 0), "x_middle_first", one, scratch(lead), *operands, got_second[0], table, part
+    )
+    (pieces,) = call(
+        x_last_first, "x_last_first", all_pieces, scratch(tail), *operands, got_last[0], first_links, table, first, sent
+    )
+    after, _ = lax.optimization_barrier((after, pieces))
+    operands = after, swapped_rows, other_links
+    second, second_links = call(
+        functools.partial(x_middle, 1), "x_middle_second", one, scratch(lead), *operands, got_second[1], table, part
+    )
+    (pieces,) = call(
+        x_last_second, "x_last_second", all_pieces, scratch(tail) + [pltpu.VMEM((4 * nev, 2 * nev), BF16)],
+        *operands, got_last[1], second_links, table, second, top, halo, lines, pieces, aliases={10: 0},
+    )
+
+    pieces = pieces.reshape(2 * size_x, 4 * group, 3 * nev)
     groups = [[(ts * 2 + h) * 2 + c for ts in range(size_x) for h in range(2)] for c in range(2)]
     got = lax.all_to_all(pieces, ("ts", "gz"), 0, 0, tiled=True, axis_index_groups=groups)
     out_shape = (group, 1, 2, 2, 3 * nev)

time: 77.8 us -> 76.6 us (0.985)
  Pallas kernels: 29 us -> 30.7 us
  starting transfers between devices: 18.8 us -> 17.7 us
  local copies, waits for them, and re-layouts: 4.16 us -> 3.08 us
    ppermute x6, waiting for transfers between devices: 3.68 us -> 0.02 us  [exchange(): got[at] = lax.ppermute(array.reshape(1, -1, array.shape[-1]), 'ts', pairs)]
    ppermute x1 -> x2, waiting for transfers between devices: 0.01 us -> 2.58 us  [the longest x1 2.58 us: shards(): swapped = lax.ppermute(given, 'gz', swap)]
    pallas_call x6 -> x9, Pallas kernels: 16.4 us -> 17.9 us  [call(): pl.pallas_call(kernel, in_specs=in_specs, out_specs=jax.tree.map(lambda _...]
    ppermute x1, waiting for transfers between devices: 0.66 us -> 1.89 us  [shards(): lax.ppermute(lowest.reshape(2, 6 * count_y, nev), 'gz', [(0, 2), (2, 0),...]
    ppermute x6, starting transfers between devices: 16 us -> 14.9 us  [exchange(): got[at] = lax.ppermute(array.reshape(1, -1, array.shape[-1]), 'ts', pairs)]
    unnamed x10 -> x12, local copies, waits for them, and re-layouts: 4.16 us -> 3.08 us
    all_to_all x1, blocking collectives: 20.9 us -> 20.2 us  [shards(): lax.all_to_all(pieces, ('ts', 'gz'), 0, 0, tiled=True, axis_index_groups=...]
  transfers between devices with their start and end apart: 8 -> 9, of which waited for: 2 -> 2; matrix products, arithmetic and copies ran while one was open for 0% -> 0% of each run, Pallas kernels for 31% -> 35%
where the time goes in v6:
time: 76.6 us; the launch traced here: 76.4 us
  Pallas kernels  30.7 us (40%)
  blocking collectives  20.2 us (26%)
  starting transfers between devices  17.7 us (23%)
  waiting for transfers between devices  4.49 us (6%)
  local copies, waits for them, and re-layouts  3.08 us (4%)
    all_to_all x1, blocking collectives, shards(): lax.all_to_all(pieces, ('ts', 'gz'), 0, 0, tiled=True, axis_index_groups=...  20.2 us
    pallas_call x9, Pallas kernels, call(): pl.pallas_call(kernel, in_specs=in_specs, out_specs=jax.tree.map(lambda _...  17.9 us
    ppermute x6, starting transfers between devices, exchange(): got[at] = lax.ppermute(array.reshape(1, -1, array.shape[-1]), 'ts', pairs)  14.9 us
    pallas_call x1, Pallas kernels, shards(): pl.pallas_call(yz_kernel, grid=(2,), in_specs=[in_smem] + [in_vmem] * 5,...  10.6 us
    unnamed x12, local copies, waits for them, and re-layouts  3.08 us
    ppermute x1, starting transfers between devices, shards(): lax.ppermute(lowest.reshape(2, 6 * count_y, nev), 'gz', [(0, 2), (2, 0),...  2.73 us
    ppermute x1, waiting for transfers between devices, shards(): swapped = lax.ppermute(given, 'gz', swap)  2.58 us
    ppermute x1, waiting for transfers between devices, shards(): lax.ppermute(lowest.reshape(2, 6 * count_y, nev), 'gz', [(0, 2), (2, 0),...  1.89 us
  transfers between devices with their start and end apart: 9, of which 2 were waited for; matrix products, arithmetic and copies ran while one was open for 0% of the time, Pallas kernels for 35%

profile of v6, /device:TPU:0, one launch (start us, length us, event | category | flops | bytes accessed | tf_op | source)
XLA Modules:
  0.0 76.4 jit_solution(7930575755232768404)
XLA Ops:
  0.1 1.9 %copy-done = bf16[2,3,4,1,16,32,128]{6,5,4,3,2,1,0:T(8,128)(2,1)S(1)} copy-done((bf16[2,3,4,1,16,32,128]{6,5,4,3,2,1,0:T(8,128)(2,1)S(1)}, bf16[2,3,4,1,16,32,128]{6,5,4,3,2,1,0:T(8,128)(2,1)}, u32[]{:S(2)}) %copy-start) | copy-done | bytes 3145752
  2.0 1.2 %copy-done.2 = bf16[3,18,4,1,16,32]{5,4,3,2,1,0:T(8,128)(2,1)S(1)} copy-done((bf16[3,18,4,1,16,32]{5,4,3,2,1,0:T(8,128)(2,1)S(1)}, bf16[3,18,4,1,16,32]{5,4,3,2,1,0:T(8,128)(2,1)}, u32[]{:S(2)}) %copy-start.2) | copy-done | bytes 221208
  3.1 0.7 pack_own.1
  3.9 1.7 %collective-permute-start.4 = (bf16[1,3168,128]{2,1,0:T(8,128)(2,1)S(1)}, bf16[1,3168,128]{2,1,0:T(8,128)(2,1)S(1)}, u32[]{:S(2)}, u32[]{:S(2)}) collective-permute-start(bf16[1,3168,128]{2,1,0:T(8,128)(2,1)S(1)} %bitcast.39), channel_id=1, source_target_pairs={{0,4},{4,0},{8,12},{12,8},{16,20},{20,16},{24,28},{28,24},{32,36},... | collective-permute-start | bytes 2433032 | tf_op jit(solution)/shard_map/ppermute | solution.py:441
  5.6 6.6 %collective-permute-start.5 = (bf16[1,3168,128]{2,1,0:T(8,128)(2,1)S(1)}, bf16[1,3168,128]{2,1,0:T(8,128)(2,1)S(1)}, u32[]{:S(2)}, u32[]{:S(2)}) collective-permute-start(bf16[1,3168,128]{2,1,0:T(8,128)(2,1)S(1)} %bitcast.38), channel_id=1, source_target_pairs={{0,124},{4,8},{8,4},{12,16},{16,12},{20,24},{24,20},{28,32},{32,28... | collective-permute-start | bytes 2433032 | tf_op jit(solution)/shard_map/ppermute | solution.py:441
  12.2 0.6 pack_given.1
  12.9 0.1 collective-permute-start.1
  13.0 0.8 %phase_table.1.table_ref.table = f32[8,2,1280]{2,1,0:T(2,128)S(1)} custom-call(s32[4]{0:T(128)S(1)} %pad_add_fusion.place_ref, s32[2,3]{1,0:T(2,128)S(1)} %copy-done.5), custom_call_target="tpu_custom_call" | custom-call | flops 20000000000 | bytes 100000 | tf_op jit(solution)/shard_map/phase_table/pallas_call | solution.py:490
  13.8 2.6 %collective-permute-done.1.swap_ref = bf16[2,96,32,128]{3,2,1,0:T(8,128)(2,1)S(1)} collective-permute-done((bf16[2,96,32,128]{3,2,1,0:T(8,128)(2,1)S(1)}, bf16[2,96,32,128]{3,2,1,0:T(8,128)(2,1)S(1)}, u32[]{:S(2)}, u32[]{:S(2)}) %collective-permute-start.1) | collective-permute-done | bytes 1572896 | tf_op jit(solution)/shard_map/ppermute | solution.py:487
  16.4 0.7 split_first.1
  17.1 1.3 %collective-permute-start.7 = (bf16[1,2400,128]{2,1,0:T(8,128)(2,1)S(1)}, bf16[1,2400,128]{2,1,0:T(8,128)(2,1)S(1)}, u32[]{:S(2)}, u32[]{:S(2)}) collective-permute-start(bf16[1,2400,128]{2,1,0:T(8,128)(2,1)S(1)} %bitcast.40), channel_id=1, source_target_pairs={{0,124},{4,8},{8,4},{12,16},{16,12},{20,24},{24,20},{28,32},{32,28... | collective-permute-start | bytes 1843208 | tf_op jit(solution)/shard_map/ppermute | solution.py:441
  18.4 10.6 %yz_terms.1 = (bf16[32,2,16,256]{3,2,1,0:T(8,128)(2,1)S(1)}, bf16[2,192,128]{2,1,0:T(8,128)(2,1)S(1)}, f32[2,16,256]{2,1,0:T(8,128)S(1)}) custom-call(s32[4]{0:T(128)S(1)} %pad_add_fusion.place_ref, bf16[2,3,4,16,32,128]{5,4,3,2,1,0:T(8,128)(2,1)S(1)} %bitcast.20, bf16[2,3072,128]{2,1,0:T(8,128)(2,1)S(1)} %bitcast.22, ...), custom_call_target="tpu_custom_call" | custom-call | flops 1000000 | bytes 100000 | tf_op jit(solution)/shard_map/yz_terms/pallas_call | solution.py:509
  29.0 0.6 split_last.1
  29.6 0.8 %collective-permute-start.2 = (bf16[1,768,128]{2,1,0:T(8,128)(2,1)S(1)}, bf16[1,768,128]{2,1,0:T(8,128)(2,1)S(1)}, u32[]{:S(2)}, u32[]{:S(2)}) collective-permute-start(bf16[1,768,128]{2,1,0:T(8,128)(2,1)S(1)} %bitcast.43), channel_id=1, source_target_pairs={{0,4},{4,0},{8,12},{12,8},{16,20},{20,16},{24,28},{28,24},{32,36},... | collective-permute-start | bytes 589832 | tf_op jit(solution)/shard_map/ppermute | solution.py:441
  30.4 4.4 %collective-permute-start.6 = (bf16[1,768,128]{2,1,0:T(8,128)(2,1)S(1)}, bf16[1,768,128]{2,1,0:T(8,128)(2,1)S(1)}, u32[]{:S(2)}, u32[]{:S(2)}) collective-permute-start(bf16[1,768,128]{2,1,0:T(8,128)(2,1)S(1)} %bitcast.42), channel_id=1, source_target_pairs={{0,124},{4,8},{8,4},{12,16},{16,12},{20,24},{24,20},{28,32},{32,28... | collective-permute-start | bytes 589832 | tf_op jit(solution)/shard_map/ppermute | solution.py:441
  34.9 2.7 %collective-permute-start.8 = (bf16[2,192,128]{2,1,0:T(8,128)(2,1)S(1)}, bf16[2,192,128]{2,1,0:T(8,128)(2,1)S(1)}, u32[]{:S(2)}, u32[]{:S(2)}) collective-permute-start(bf16[2,192,128]{2,1,0:T(8,128)(2,1)S(1)} %bitcast.44), channel_id=1, source_target_pairs={{0,2},{2,0},{1,3},{3,1},{4,6},{6,4},{5,7},{7,5},{8,10},{10,8},{9,1... | collective-permute-start | bytes 294920 | tf_op jit(solution)/shard_map/ppermute | solution.py:505
  37.6 6.5 %x_first.1.before = f32[2,4,128,128]{3,2,1,0:T(8,128)S(1)} custom-call(s32[4]{0:T(128)S(1)} %pad_add_fusion.place_ref, bf16[2,3,4,16,32,128]{5,4,3,2,1,0:T(8,128)(2,1)S(1)} %bitcast.21, bf16[3,18,4,16,32]{4,3,2,1,0:T(8,128)(2,1)S(1)} %bitcast.36, bf16[1,3168,128]{2,1,0:T(8,128)(2,1)S(1)} %collective-permute-done.4.first_ref, ...), custom_call_target="tpu_custom_call" | custom-call | flops 1000000 | bytes 100000 | tf_op jit(solution)/shard_map/x_first/pallas_call | solution.py:469
  44.1 2.5 %x_middle_first.1 = (f32[4,128,128]{2,1,0:T(8,128)S(1)}, bf16[96,128]{1,0:T(8,128)(2,1)S(1)}) custom-call(s32[4]{0:T(128)S(1)} %pad_add_fusion.place_ref, bf16[2,3072,128]{2,1,0:T(8,128)(2,1)S(1)} %bitcast.23, bf16[3,18,4,16,32]{4,3,2,1,0:T(8,128)(2,1)S(1)} %bitcast.29, bf16[1,2400,128]{2,1,0:T(8,128)(2,1)S(1)} %collective-permute-done.3.got_ref, ...), custom_call_target="tpu_custom_call" | custom-call | flops 1000000 | bytes 100000 | tf_op jit(solution)/shard_map/x_middle_first/pallas_call | solution.py:469
  46.6 1.6 %x_last_first.1.sent_ref = bf16[32,2,16,384]{3,2,1,0:T(8,128)(2,1)S(1)} custom-call(s32[4]{0:T(128)S(1)} %pad_add_fusion.place_ref, bf16[2,3072,128]{2,1,0:T(8,128)(2,1)S(1)} %bitcast.24, bf16[3,18,4,16,32]{4,3,2,1,0:T(8,128)(2,1)S(1)} %bitcast.30, bf16[1,768,128]{2,1,0:T(8,128)(2,1)S(1)} %collective-permute-done.2.got_ref, ...), custom_call_target="tpu_custom_call" | custom-call | flops 1000000 | bytes 100000 | tf_op jit(solution)/shard_map/x_last_first/pallas_call | solution.py:469
  48.2 2.5 %x_middle_second.1 = (f32[4,128,128]{2,1,0:T(8,128)S(1)}, bf16[96,128]{1,0:T(8,128)(2,1)S(1)}) custom-call(s32[4]{0:T(128)S(1)} %pad_add_fusion.place_ref, bf16[2,3072,128]{2,1,0:T(8,128)(2,1)S(1)} %bitcast.25, bf16[3,18,4,16,32]{4,3,2,1,0:T(8,128)(2,1)S(1)} %bitcast.31, bf16[1,2400,128]{2,1,0:T(8,128)(2,1)S(1)} %collective-permute-done.7.got_ref, ...), custom_call_target="tpu_custom_call" | custom-call | flops 1000000 | bytes 100000 | tf_op jit(solution)/shard_map/x_middle_second/pallas_call | solution.py:469
  50.7 1.9 %collective-permute-done.8.halo_ref = bf16[2,192,128]{2,1,0:T(8,128)(2,1)S(1)} collective-permute-done((bf16[2,192,128]{2,1,0:T(8,128)(2,1)S(1)}, bf16[2,192,128]{2,1,0:T(8,128)(2,1)S(1)}, u32[]{:S(2)}, u32[]{:S(2)}) %collective-permute-start.8) | collective-permute-done | bytes 98336 | tf_op jit(solution)/shard_map/ppermute | solution.py:505
  52.6 2.2 %x_last_second.1 = bf16[32,2,16,384]{3,2,1,0:T(8,128)(2,1)S(1)} custom-call(s32[4]{0:T(128)S(1)} %pad_add_fusion.place_ref, bf16[2,3072,128]{2,1,0:T(8,128)(2,1)S(1)} %bitcast.26, bf16[3,18,4,16,32]{4,3,2,1,0:T(8,128)(2,1)S(1)} %bitcast.32, bf16[1,768,128]{2,1,0:T(8,128)(2,1)S(1)} %collective-permute-done.6.got_ref, ...), custom_call_target="tpu_custom_call", output_to_operand_aliasing={{}: (10, {})} | custom-call | flops 1000000 | bytes 100000 | tf_op jit(solution)/shard_map/x_last_second/pallas_call | solution.py:469
  54.8 20.2 %all_to_all.5.got_ref = bf16[64,16,384]{2,1,0:T(8,128)(2,1)S(1)} all-to-all(bf16[64,16,384]{2,1,0:T(8,128)(2,1)S(1)} %bitcast.37), channel_id=1, replica_groups={{0,2,4,6,8,10,12,14,16,18,20,22,24,26,28,30,32,34,36,38,40,42,44,46,48,..., dimensions={0} | all-to-all | bytes 1572864 | tf_op jit(solution)/shard_map/all_to_all | solution.py:573
  75.0 1.4 %total.1 = f32[4,1,2,2,384]{4,3,2,1,0:T(2,128)} custom-call(s32[3]{0:T(128)S(1)} %copy-done.4, bf16[64,16,384]{2,1,0:T(8,128)(2,1)S(1)} %all_to_all.5.got_ref), custom_call_target="tpu_custom_call" | custom-call | tf_op jit(solution)/shard_map/total/pallas_call | solution.py:575
  (20 shorter events, 0.2 us)
Async XLA Ops:
  0.0 12.2 %collective-permute-start = (bf16[3,18,4,1,16,32]{5,4,2,1,0,3:T(8,128)(2,1)}, bf16[3,18,4,1,16,32]{5,4,2,1,0,3:T(8,128)(2,1)S(1)}, u32[]{:S(2)}, u32[]{:S(2)}) collective-permute-start(bf16[3,18,4,1,16,32]{5,4,2,1,0,3:T(8,128)(2,1)} %bitcast.33), channel_id=1, source_target_pairs={{0,1},{1,0},{2,3},{3,2},{4,5},{5,4},{6,7},{7,6},{8,9},{9,8},{10,11... | collective-permute-start | bytes 663560 | tf_op jit(solution)/shard_map/ppermute | solution.py:482
  0.1 1.9 %copy-start = (bf16[2,3,4,1,16,32,128]{6,5,4,3,2,1,0:T(8,128)(2,1)S(1)}, bf16[2,3,4,1,16,32,128]{6,5,4,3,2,1,0:T(8,128)(2,1)}, u32[]{:S(2)}) copy-start(bf16[2,3,4,1,16,32,128]{6,5,4,3,2,1,0:T(8,128)(2,1)} %param.4) | copy-start | bytes 9437188
  2.0 1.2 %copy-start.2 = (bf16[3,18,4,1,16,32]{5,4,3,2,1,0:T(8,128)(2,1)S(1)}, bf16[3,18,4,1,16,32]{5,4,3,2,1,0:T(8,128)(2,1)}, u32[]{:S(2)}) copy-start(bf16[3,18,4,1,16,32]{5,4,3,2,1,0:T(8,128)(2,1)} %param.5) | copy-start | bytes 663556
  3.9 26.6 %collective-permute-start.4 = (bf16[1,3168,128]{2,1,0:T(8,128)(2,1)S(1)}, bf16[1,3168,128]{2,1,0:T(8,128)(2,1)S(1)}, u32[]{:S(2)}, u32[]{:S(2)}) collective-permute-start(bf16[1,3168,128]{2,1,0:T(8,128)(2,1)S(1)} %bitcast.39), channel_id=1, source_target_pairs={{0,4},{4,0},{8,12},{12,8},{16,20},{20,16},{24,28},{28,24},{32,36},... | collective-permute-start | bytes 2433032 | tf_op jit(solution)/shard_map/ppermute | solution.py:441
  5.6 29.2 %collective-permute-start.5 = (bf16[1,3168,128]{2,1,0:T(8,128)(2,1)S(1)}, bf16[1,3168,128]{2,1,0:T(8,128)(2,1)S(1)}, u32[]{:S(2)}, u32[]{:S(2)}) collective-permute-start(bf16[1,3168,128]{2,1,0:T(8,128)(2,1)S(1)} %bitcast.38), channel_id=1, source_target_pairs={{0,124},{4,8},{8,4},{12,16},{16,12},{20,24},{24,20},{28,32},{32,28... | collective-permute-start | bytes 2433032 | tf_op jit(solution)/shard_map/ppermute | solution.py:441
  12.2 0.8 copy-start.5
  12.9 3.5 %collective-permute-start.1 = (bf16[2,96,32,128]{3,2,1,0:T(8,128)(2,1)S(1)}, bf16[2,96,32,128]{3,2,1,0:T(8,128)(2,1)S(1)}, u32[]{:S(2)}, u32[]{:S(2)}) collective-permute-start(bf16[2,96,32,128]{3,2,1,0:T(8,128)(2,1)S(1)} %pack_given.1), channel_id=1, source_target_pairs={{0,1},{1,0},{2,3},{3,2},{4,5},{5,4},{6,7},{7,6},{8,9},{9,8},{10,11... | collective-permute-start | bytes 4718600 | tf_op jit(solution)/shard_map/ppermute | solution.py:487
  13.0 3.4 %copy-start.1 = (bf16[2,3,4,1,16,32,128]{6,5,4,3,2,1,0:T(8,128)(2,1)S(1)}, bf16[2,3,4,1,16,32,128]{6,5,4,3,2,1,0:T(8,128)(2,1)}, u32[]{:S(2)}) copy-start(bf16[2,3,4,1,16,32,128]{6,5,4,3,2,1,0:T(8,128)(2,1)} %param.4) | copy-start | bytes 9437188
  13.8 4.6 %copy-start.3 = (bf16[3,18,4,1,16,32]{5,4,3,2,1,0:T(8,128)(2,1)S(1)}, bf16[3,18,4,1,16,32]{5,4,3,2,1,0:T(8,128)(2,1)}, u32[]{:S(2)}) copy-start(bf16[3,18,4,1,16,32]{5,4,3,2,1,0:T(8,128)(2,1)} %param.5) | copy-start | bytes 663556
  17.0 27.1 %collective-permute-start.3 = (bf16[1,2400,128]{2,1,0:T(8,128)(2,1)S(1)}, bf16[1,2400,128]{2,1,0:T(8,128)(2,1)S(1)}, u32[]{:S(2)}, u32[]{:S(2)}) collective-permute-start(bf16[1,2400,128]{2,1,0:T(8,128)(2,1)S(1)} %bitcast.41), channel_id=1, source_target_pairs={{0,4},{4,0},{8,12},{12,8},{16,20},{20,16},{24,28},{28,24},{32,36},... | collective-permute-start | bytes 1843208 | tf_op jit(solution)/shard_map/ppermute | solution.py:441
  17.1 31.1 %collective-permute-start.7 = (bf16[1,2400,128]{2,1,0:T(8,128)(2,1)S(1)}, bf16[1,2400,128]{2,1,0:T(8,128)(2,1)S(1)}, u32[]{:S(2)}, u32[]{:S(2)}) collective-permute-start(bf16[1,2400,128]{2,1,0:T(8,128)(2,1)S(1)} %bitcast.40), channel_id=1, source_target_pairs={{0,124},{4,8},{8,4},{12,16},{16,12},{20,24},{24,20},{28,32},{32,28... | collective-permute-start | bytes 1843208 | tf_op jit(solution)/shard_map/ppermute | solution.py:441
  29.6 17.0 %collective-permute-start.2 = (bf16[1,768,128]{2,1,0:T(8,128)(2,1)S(1)}, bf16[1,768,128]{2,1,0:T(8,128)(2,1)S(1)}, u32[]{:S(2)}, u32[]{:S(2)}) collective-permute-start(bf16[1,768,128]{2,1,0:T(8,128)(2,1)S(1)} %bitcast.43), channel_id=1, source_target_pairs={{0,4},{4,0},{8,12},{12,8},{16,20},{20,16},{24,28},{28,24},{32,36},... | collective-permute-start | bytes 589832 | tf_op jit(solution)/shard_map/ppermute | solution.py:441
  30.4 22.2 %collective-permute-start.6 = (bf16[1,768,128]{2,1,0:T(8,128)(2,1)S(1)}, bf16[1,768,128]{2,1,0:T(8,128)(2,1)S(1)}, u32[]{:S(2)}, u32[]{:S(2)}) collective-permute-start(bf16[1,768,128]{2,1,0:T(8,128)(2,1)S(1)} %bitcast.42), channel_id=1, source_target_pairs={{0,124},{4,8},{8,4},{12,16},{16,12},{20,24},{24,20},{28,32},{32,28... | collective-permute-start | bytes 589832 | tf_op jit(solution)/shard_map/ppermute | solution.py:441
  34.9 17.7 %collective-permute-start.8 = (bf16[2,192,128]{2,1,0:T(8,128)(2,1)S(1)}, bf16[2,192,128]{2,1,0:T(8,128)(2,1)S(1)}, u32[]{:S(2)}, u32[]{:S(2)}) collective-permute-start(bf16[2,192,128]{2,1,0:T(8,128)(2,1)S(1)} %bitcast.44), channel_id=1, source_target_pairs={{0,2},{2,0},{1,3},{3,1},{4,6},{6,4},{5,7},{7,5},{8,10},{10,8},{9,1... | collective-permute-start | bytes 294920 | tf_op jit(solution)/shard_map/ppermute | solution.py:505
  54.8 20.2 %copy-start.4 = (s32[3]{0:T(128)S(1)}, s32[3]{0:T(128)}, u32[]{:S(2)}) copy-start(s32[3]{0:T(128)} %directions_ref.1) | copy-start | bytes 40

commit v7 on v6

--- a/solution.py
+++ b/solution.py
@@ -278,17 +278,21 @@
     return lambda q, b, z, count: ref[q, b, t, z : z + count].reshape(count * count_y, nev)
 
 
-def x_terms(odd, at, own, received, own_link, received_link, link_first, table, table_first, rows, phased, moved):
+def pair_rows(odd, at, own_link, received_link, rows):
+    below = odd if at else 1 - odd
+    entries = [0.5 * jnp.where(below == 1, own_link(e), received_link(e)).astype(F32) for e in range(18)]
+    for ra, line in enumerate(link_rows(entries, False, rows.shape[3])):
+        rows[below, ra] = line
+    for ra, line in enumerate(link_rows(entries, True, rows.shape[3])):
+        rows[1 - below, ra] = -line
+
+
+def x_terms(odd, at, own, received, link_first, table, table_first, rows, phased, moved):
     lanes = rows.shape[3]
     count_z, count_y = moved.shape[2:4]
     nev = moved.shape[4] // 2
     below = odd if at else 1 - odd
     same = site_masks(count_y, lanes)[0]
-    entries = [0.5 * jnp.where(below == 1, own_link(e), received_link(e)).astype(F32) for e in range(18)]
-    for ra, line in enumerate(link_rows(entries, False, lanes)):
-        rows[below, ra] = line
-    for ra, line in enumerate(link_rows(entries, True, lanes)):
-        rows[1 - below, ra] = -line
     sites = count_z * count_y
     step = nev // count_y
     for vectors, x_at, first in ((own, 0, 0), (received, 2 - below, 3 * sites)):
@@ -317,29 +321,29 @@
     for at, got in enumerate((first_ref.at[0], second_ref.at[0])):
         m = 1 - odd if at else odd
         t = core + 2 * m
+        pair_rows(
+            odd, at, lambda e, t=t: link_ref[0, e, t],
+            lambda e, got=got: packed_link(got, count_z, 0, e, count_z, count_y), rows,
+        )
         parts = x_terms(
-            odd, at, from_times(v_ref, t), from_rows(got, count_z, count_y),
-            lambda e, t=t: link_ref[0, e, t], lambda e, got=got: packed_link(got, count_z, 0, e, count_z, count_y),
-            0, table, at_table, rows, phased, moved,
+            odd, at, from_times(v_ref, t), from_rows(got, count_z, count_y), 0, table, at_table, rows, phased, moved
         )
         for i, part in enumerate(parts):
             out_ref[m, i] = part
 
 
-def x_part(first, at, place_ref, swap_ref, link_ref, got, received_link, table, rows, phased, moved):
+def x_part(first, at, place_ref, swap_ref, got, table, rows, phased, moved):
     held_z = rows.shape[2]
     depth, count_y = moved.shape[2:4]
     core, odd = place_ref[0], place_ref[3]
-    m = 1 - odd if at else odd
     at_table = pl.multiple_of((1 - core) * (held_z * count_y) + first * count_y, moved.shape[4] // 2)
     return x_terms(
-        odd, at, from_rows(swap_ref.at[m], held_z, count_y, first), from_rows(got, depth, count_y),
-        lambda e: link_ref[0, e, core + 2 * m], received_link,
+        odd, at, from_rows(swap_ref.at[1 - odd if at else odd], held_z, count_y, first), from_rows(got, depth, count_y),
         first, table, at_table, rows, phased, moved,
     )
 
 
-def boundary(top, halo, lines, table, edge):
+def boundary_below(top, lines, table, phased, displaced, forward):
     lanes, nev = top.shape
     count_y = lanes // 6
     wide = lanes // 2
@@ -352,57 +356,68 @@
             blocks.append(jnp.broadcast_to(line, (count_y, lanes)).astype(BF16) * same)
         return jnp.concatenate(blocks, axis=0)
 
-    products = 0.0
-    for at, (phased, moved, kind) in enumerate(((top, halo, 0), (halo, top, 1))):
-        put_phased(
-            phased[:wide].T.astype(F32), phased[wide:].T.astype(F32), table, 0,
-            table.shape[2] - (at + 1) * nev, edge, at * nev,
+    put_phased(top[:wide].T.astype(F32), top[wide:].T.astype(F32), table, 0, table.shape[2] - nev, phased, 0)
+    terms = jnp.dot(matrix(1), top[...], preferred_element_type=F32).astype(BF16)
+    displaced[...] = jnp.concatenate([terms[:wide], terms[wide:]], axis=1)
+    forward[:, :lanes] = matrix(0)
+
+
+def boundary(halo, phased, displaced, forward, table, edge):
+    lanes, nev = halo.shape
+    wide = lanes // 2
+    put_phased(halo[:wide].T.astype(F32), halo[wide:].T.astype(F32), table, 0, table.shape[2] - 2 * nev, edge, 0)
+    products = jnp.dot(edge[:, :wide], displaced[...], preferred_element_type=F32)
+    terms = jnp.dot(forward[:, :lanes], halo[...], preferred_element_type=F32).astype(BF16)
+    terms = jnp.concatenate([terms[:wide], terms[wide:]], axis=1)
+    products += jnp.dot(phased[:, :wide], terms, preferred_element_type=F32)
+    return combine(products, nev)
+
+
+def x_middle(at, place_ref, swap_ref, link_ref, got_ref, table, before, out_ref, rows_ref, *scratch):
+    held_z = rows_ref.shape[2]
+    depth, count_y = scratch[1].shape[2:4]
+    core, odd = place_ref[0], place_ref[3]
+    m = 1 - odd if at else odd
+    got = got_ref.at[0]
+    pair_rows(
+        odd, at, lambda e: link_ref[0, e, core + 2 * m], lambda e: packed_link(got, depth, 0, e, held_z, count_y), rows_ref
+    )
+    parts = x_part(0, at, place_ref, swap_ref, got, table, rows_ref, *scratch)
+    for i, part in enumerate(parts):
+        out_ref[i] = part + before[m, i]
+
+
+def x_middle_first(place_ref, swap_ref, link_ref, got_ref, table, before, top_ref, line_ref,
+                   out_ref, rows_ref, phased_ref, displaced_ref, forward_ref, *scratch):
+    for m in range(2):
+        boundary_below(
+            top_ref.at[m], line_ref.at[m], table, phased_ref.at[m], displaced_ref.at[m], forward_ref.at[m]
         )
-        terms = jnp.dot(matrix(kind), moved[...], preferred_element_type=F32).astype(BF16)
-        displaced = jnp.concatenate([terms[:wide], terms[wide:]], axis=1)
-        products += jnp.dot(edge[:, at * nev : at * nev + wide], displaced, preferred_element_type=F32)
-    return combine(products, nev)
-
-
-def x_middle(at, place_ref, swap_ref, link_ref, got_ref, table, before, out_ref, links_ref, *scratch):
-    held_z = scratch[0].shape[2]
-    depth, count_y = scratch[2].shape[2:4]
+    x_middle(0, place_ref, swap_ref, link_ref, got_ref, table, before, out_ref, rows_ref, *scratch)
+
+
+def x_last(at, place_ref, swap_ref, got_ref, rows_ref, table, before, pieces_ref, *scratch):
+    nev = before.shape[2]
     odd = place_ref[3]
-    got = got_ref.at[0]
-    links_ref[...] = got[got.shape[0] - links_ref.shape[0] :]
-    parts = x_part(
-        0, at, place_ref, swap_ref, link_ref, got,
-        lambda e: packed_link(got, depth, 0, e, held_z, count_y), table, *scratch,
-    )
-    for i, part in enumerate(parts):
-        out_ref[i] = part + before[1 - odd if at else odd, i]
-
-
-def x_last(at, place_ref, swap_ref, link_ref, got_ref, links_ref, table, before, pieces_ref, rows, phased, moved):
-    nev = before.shape[2]
-    held_z = rows.shape[2]
-    depth, count_y = moved.shape[2:4]
-    odd = place_ref[3]
-    parts = x_part(
-        held_z - depth, at, place_ref, swap_ref, link_ref, got_ref.at[0],
-        lambda e: packed_link(links_ref, 0, 0, e, held_z, count_y), table, rows, phased, moved,
-    )
+    first = rows_ref.shape[2] - scratch[1].shape[2]
+    parts = x_part(first, at, place_ref, swap_ref, got_ref.at[0], table, rows_ref, *scratch)
     parts = [part + before[i] for i, part in enumerate(parts)]
     pieces_ref[:, 1 - odd if at else odd, :, 2 * nev :] = partial_rows(parts).astype(BF16)
 
 
-def x_last_first(place_ref, swap_ref, link_ref, got_ref, links_ref, table, before, sent_ref, pieces_ref, *scratch):
+def x_last_first(place_ref, swap_ref, got_ref, rows_ref, table, before, sent_ref, pieces_ref, *scratch):
     pieces_ref[:, :, :, : sent_ref.shape[3]] = sent_ref[...]
-    x_last(0, place_ref, swap_ref, link_ref, got_ref, links_ref, table, before, pieces_ref, *scratch)
-
-
-def x_last_second(place_ref, swap_ref, link_ref, got_ref, links_ref, table, before, top_ref, halo_ref, line_ref, sent_ref,
-                  pieces_ref, rows, phased, moved, edge):
+    x_last(0, place_ref, swap_ref, got_ref, rows_ref, table, before, pieces_ref, *scratch)
+
+
+def x_last_second(place_ref, swap_ref, got_ref, rows_ref, table, before, halo_ref, phased_ref, displaced_ref,
+                  forward_ref, sent_ref, pieces_ref, phased, moved, edge):
     nev = before.shape[2]
     for m in range(2):
-        above = partial_rows(boundary(top_ref.at[m], halo_ref.at[m], line_ref.at[m], table, edge))
+        parts = boundary(halo_ref.at[m], phased_ref.at[m], displaced_ref.at[m], forward_ref.at[m], table, edge.at[m])
+        above = partial_rows(parts)
         pieces_ref[:, m, :, nev : 2 * nev] = (sent_ref[:, m, :, nev : 2 * nev].astype(F32) + above).astype(BF16)
-    x_last(1, place_ref, swap_ref, link_ref, got_ref, links_ref, table, before, pieces_ref, rows, phased, moved)
+    x_last(1, place_ref, swap_ref, got_ref, rows_ref, table, before, pieces_ref, phased, moved)
 
 
 def total_kernel(directions_ref, got_ref, out_ref, total_ref):
@@ -540,32 +555,40 @@
 
     def scratch(depth):
         return [
-            pltpu.VMEM((2, 6, count_z, 6 * count_y), F32),
             pltpu.VMEM((4 * nev, 6 * depth * count_y), BF16),
             pltpu.VMEM((2, 3, depth, count_y, 2 * nev), BF16),
         ]
 
     parts = jax.ShapeDtypeStruct((2, 4, nev, nev), F32)
+    rows_shape = (2, 6, count_z, 6 * count_y)
     (part,) = call(
-        x_first_kernel, "x_first", [parts], scratch(count_z), after, vectors, links, *got_first, table
-    )
-    one = [jax.ShapeDtypeStruct(parts.shape[1:], F32), jax.ShapeDtypeStruct((planes * count_y, nev), BF16)]
+        x_first_kernel, "x_first", [parts], [pltpu.VMEM(rows_shape, F32)] + scratch(count_z), after, vectors, links, *got_first, table
+    )
+    one = [jax.ShapeDtypeStruct(parts.shape[1:], F32), jax.ShapeDtypeStruct(rows_shape, F32)]
     all_pieces = [jax.ShapeDtypeStruct((size_x, 2, 4 * group, 3 * nev), BF16)]
     operands = after, swapped_rows, other_links
-    first, first_links = call(
-        functools.partial(x_middle, 0), "x_middle_first", one, scratch(lead), *operands, got_second[0], table, part
-    )
+    edges = [
+        jax.ShapeDtypeStruct((2, 4 * nev, nev), BF16),
+        jax.ShapeDtypeStruct((2, 3 * count_y, 2 * nev), BF16),
+        jax.ShapeDtypeStruct((2, 6 * count_y, 2 * nev), BF16),
+    ]
+    first, first_rows, *edges = call(
+        x_middle_first, "x_middle_first", one + edges, scratch(lead),
+        *operands, got_second[0], table, part, top, lines,
+    )
+    after, _ = lax.optimization_barrier((after, first_rows))
+    operands = after, swapped_rows, other_links
+    second, second_rows = call(
+        functools.partial(x_middle, 1), "x_middle_second", one, scratch(lead), *operands, got_second[1], table, part
+    )
+    after, _ = lax.optimization_barrier((after, second_rows))
+    operands = after, swapped_rows, other_links
     (pieces,) = call(
-        x_last_first, "x_last_first", all_pieces, scratch(tail), *operands, got_last[0], first_links, table, first, sent
-    )
-    after, _ = lax.optimization_barrier((after, pieces))
-    operands = after, swapped_rows, other_links
-    second, second_links = call(
-        functools.partial(x_middle, 1), "x_middle_second", one, scratch(lead), *operands, got_second[1], table, part
+        x_last_first, "x_last_first", all_pieces, scratch(tail), *operands[:2], got_last[0], first_rows, table, first, sent
     )
     (pieces,) = call(
-        x_last_second, "x_last_second", all_pieces, scratch(tail) + [pltpu.VMEM((4 * nev, 2 * nev), BF16)],
-        *operands, got_last[1], second_links, table, second, top, halo, lines, pieces, aliases={10: 0},
+        x_last_second, "x_last_second", all_pieces, scratch(tail) + [pltpu.VMEM((2, 4 * nev, nev), BF16)],
+        *operands[:2], got_last[1], second_rows, table, second, halo, *edges, pieces, aliases={10: 0},
     )
 
     pieces = pieces.reshape(2 * size_x, 4 * group, 3 * nev)

time: 76.6 us -> 76.3 us (level)
  no operation moved by 1% of the time
where the time goes in v7:
time: 76.3 us; the launch traced here: 76.1 us
  Pallas kernels  30.4 us (40%)
  blocking collectives  20 us (26%)
  starting transfers between devices  17.7 us (23%)
  waiting for transfers between devices  4.65 us (6%)
  local copies, waits for them, and re-layouts  3.08 us (4%)
    all_to_all x1, blocking collectives, shards(): lax.all_to_all(pieces, ('ts', 'gz'), 0, 0, tiled=True, axis_index_groups=...  20 us
    pallas_call x9, Pallas kernels, call(): pl.pallas_call(kernel, in_specs=in_specs, out_specs=jax.tree.map(lambda _...  17.6 us
    ppermute x6, starting transfers between devices, exchange(): got[at] = lax.ppermute(array.reshape(1, -1, array.shape[-1]), 'ts', pairs)  14.9 us
    pallas_call x1, Pallas kernels, shards(): pl.pallas_call(yz_kernel, grid=(2,), in_specs=[in_smem] + [in_vmem] * 5,...  10.6 us
    unnamed x12, local copies, waits for them, and re-layouts  3.08 us
    ppermute x1, starting transfers between devices, shards(): lax.ppermute(lowest.reshape(2, 6 * count_y, nev), 'gz', [(0, 2), (2, 0),...  2.73 us
    ppermute x1, waiting for transfers between devices, shards(): swapped = lax.ppermute(given, 'gz', swap)  2.58 us
    ppermute x1, waiting for transfers between devices, shards(): lax.ppermute(lowest.reshape(2, 6 * count_y, nev), 'gz', [(0, 2), (2, 0),...  2.05 us
  transfers between devices with their start and end apart: 9, of which 2 were waited for; matrix products, arithmetic and copies ran while one was open for 0% of the time, Pallas kernels for 35%

profile of v7, /device:TPU:0, one launch (start us, length us, event | category | flops | bytes accessed | tf_op | source)
XLA Modules:
  0.0 76.1 jit_solution(211427190575714963)
XLA Ops:
  0.1 1.9 %copy-done = bf16[2,3,4,1,16,32,128]{6,5,4,3,2,1,0:T(8,128)(2,1)S(1)} copy-done((bf16[2,3,4,1,16,32,128]{6,5,4,3,2,1,0:T(8,128)(2,1)S(1)}, bf16[2,3,4,1,16,32,128]{6,5,4,3,2,1,0:T(8,128)(2,1)}, u32[]{:S(2)}) %copy-start) | copy-done | bytes 3145752
  2.0 1.2 %copy-done.2 = bf16[3,18,4,1,16,32]{5,4,3,2,1,0:T(8,128)(2,1)S(1)} copy-done((bf16[3,18,4,1,16,32]{5,4,3,2,1,0:T(8,128)(2,1)S(1)}, bf16[3,18,4,1,16,32]{5,4,3,2,1,0:T(8,128)(2,1)}, u32[]{:S(2)}) %copy-start.2) | copy-done | bytes 221208
  3.1 0.7 pack_own.1
  3.9 1.7 %collective-permute-start.3 = (bf16[1,3168,128]{2,1,0:T(8,128)(2,1)S(1)}, bf16[1,3168,128]{2,1,0:T(8,128)(2,1)S(1)}, u32[]{:S(2)}, u32[]{:S(2)}) collective-permute-start(bf16[1,3168,128]{2,1,0:T(8,128)(2,1)S(1)} %bitcast.37), channel_id=1, source_target_pairs={{0,4},{4,0},{8,12},{12,8},{16,20},{20,16},{24,28},{28,24},{32,36},... | collective-permute-start | bytes 2433032 | tf_op jit(solution)/shard_map/ppermute | solution.py:456
  5.6 6.6 %collective-permute-start.4 = (bf16[1,3168,128]{2,1,0:T(8,128)(2,1)S(1)}, bf16[1,3168,128]{2,1,0:T(8,128)(2,1)S(1)}, u32[]{:S(2)}, u32[]{:S(2)}) collective-permute-start(bf16[1,3168,128]{2,1,0:T(8,128)(2,1)S(1)} %bitcast.36), channel_id=1, source_target_pairs={{0,124},{4,8},{8,4},{12,16},{16,12},{20,24},{24,20},{28,32},{32,28... | collective-permute-start | bytes 2433032 | tf_op jit(solution)/shard_map/ppermute | solution.py:456
  12.2 0.6 pack_given.1
  12.9 0.1 collective-permute-start.1
  13.0 0.8 %phase_table.1.table_ref.table = f32[8,2,1280]{2,1,0:T(2,128)S(1)} custom-call(s32[4]{0:T(128)S(1)} %pad_add_fusion.place_ref, s32[2,3]{1,0:T(2,128)S(1)} %copy-done.5), custom_call_target="tpu_custom_call" | custom-call | flops 20000000000 | bytes 100000 | tf_op jit(solution)/shard_map/phase_table/pallas_call | solution.py:505
  13.8 2.6 %collective-permute-done.1.swap_ref = bf16[2,96,32,128]{3,2,1,0:T(8,128)(2,1)S(1)} collective-permute-done((bf16[2,96,32,128]{3,2,1,0:T(8,128)(2,1)S(1)}, bf16[2,96,32,128]{3,2,1,0:T(8,128)(2,1)S(1)}, u32[]{:S(2)}, u32[]{:S(2)}) %collective-permute-start.1) | collective-permute-done | bytes 1572896 | tf_op jit(solution)/shard_map/ppermute | solution.py:502
  16.4 0.7 split_first.1
  17.1 1.3 %collective-permute-start.5 = (bf16[1,2400,128]{2,1,0:T(8,128)(2,1)S(1)}, bf16[1,2400,128]{2,1,0:T(8,128)(2,1)S(1)}, u32[]{:S(2)}, u32[]{:S(2)}) collective-permute-start(bf16[1,2400,128]{2,1,0:T(8,128)(2,1)S(1)} %bitcast.38), channel_id=1, source_target_pairs={{0,124},{4,8},{8,4},{12,16},{16,12},{20,24},{24,20},{28,32},{32,28... | collective-permute-start | bytes 1843208 | tf_op jit(solution)/shard_map/ppermute | solution.py:456
  18.4 10.6 %yz_terms.1 = (bf16[32,2,16,256]{3,2,1,0:T(8,128)(2,1)S(1)}, bf16[2,192,128]{2,1,0:T(8,128)(2,1)S(1)}, f32[2,16,256]{2,1,0:T(8,128)S(1)}) custom-call(s32[4]{0:T(128)S(1)} %pad_add_fusion.place_ref, bf16[2,3,4,16,32,128]{5,4,3,2,1,0:T(8,128)(2,1)S(1)} %bitcast.20, bf16[2,3072,128]{2,1,0:T(8,128)(2,1)S(1)} %bitcast.22, ...), custom_call_target="tpu_custom_call" | custom-call | flops 1000000 | bytes 100000 | tf_op jit(solution)/shard_map/yz_terms/pallas_call | solution.py:524
  29.0 0.6 split_last.1
  29.6 0.8 %collective-permute-start.8 = (bf16[1,768,128]{2,1,0:T(8,128)(2,1)S(1)}, bf16[1,768,128]{2,1,0:T(8,128)(2,1)S(1)}, u32[]{:S(2)}, u32[]{:S(2)}) collective-permute-start(bf16[1,768,128]{2,1,0:T(8,128)(2,1)S(1)} %bitcast.41), channel_id=1, source_target_pairs={{0,4},{4,0},{8,12},{12,8},{16,20},{20,16},{24,28},{28,24},{32,36},... | collective-permute-start | bytes 589832 | tf_op jit(solution)/shard_map/ppermute | solution.py:456
  30.4 4.4 %collective-permute-start.6 = (bf16[1,768,128]{2,1,0:T(8,128)(2,1)S(1)}, bf16[1,768,128]{2,1,0:T(8,128)(2,1)S(1)}, u32[]{:S(2)}, u32[]{:S(2)}) collective-permute-start(bf16[1,768,128]{2,1,0:T(8,128)(2,1)S(1)} %bitcast.40), channel_id=1, source_target_pairs={{0,124},{4,8},{8,4},{12,16},{16,12},{20,24},{24,20},{28,32},{32,28... | collective-permute-start | bytes 589832 | tf_op jit(solution)/shard_map/ppermute | solution.py:456
  34.9 2.7 %collective-permute-start.7 = (bf16[2,192,128]{2,1,0:T(8,128)(2,1)S(1)}, bf16[2,192,128]{2,1,0:T(8,128)(2,1)S(1)}, u32[]{:S(2)}, u32[]{:S(2)}) collective-permute-start(bf16[2,192,128]{2,1,0:T(8,128)(2,1)S(1)} %bitcast.42), channel_id=1, source_target_pairs={{0,2},{2,0},{1,3},{3,1},{4,6},{6,4},{5,7},{7,5},{8,10},{10,8},{9,1... | collective-permute-start | bytes 294920 | tf_op jit(solution)/shard_map/ppermute | solution.py:520
  37.6 6.5 %x_first.1.before = f32[2,4,128,128]{3,2,1,0:T(8,128)S(1)} custom-call(s32[4]{0:T(128)S(1)} %pad_add_fusion.place_ref, bf16[2,3,4,16,32,128]{5,4,3,2,1,0:T(8,128)(2,1)S(1)} %bitcast.21, bf16[3,18,4,16,32]{4,3,2,1,0:T(8,128)(2,1)S(1)} %bitcast.34, bf16[1,3168,128]{2,1,0:T(8,128)(2,1)S(1)} %collective-permute-done.3.first_ref, ...), custom_call_target="tpu_custom_call" | custom-call | flops 1000000 | bytes 100000 | tf_op jit(solution)/shard_map/x_first/pallas_call | solution.py:484
  44.1 2.5 %x_middle_first.1 = (f32[4,128,128]{2,1,0:T(8,128)S(1)}, f32[2,6,16,192]{3,2,1,0:T(8,128)S(1)}, bf16[2,512,128]{2,1,0:T(8,128)(2,1)S(1)}, bf16[2,96,256]{2,1,0:T(8,128)(2,1)S(1)}, bf16[2,192,256]{2,1,0:T(8,128)(2,1)S(1)}) custom-call(s32[4]{0:T(128)S(1)} %pad_add_fusion.place_ref, bf16[2,3072,128]{2,1,0:T(8,128)(2,1)S(1)} %bitcast.23, ...), custom_call_target="tpu_custom_call" | custom-call | flops 1000000 | bytes 100000 | tf_op jit(solution)/shard_map/x_middle_first/pallas_call | solution.py:484
  46.7 2.5 %x_middle_second.1 = (f32[4,128,128]{2,1,0:T(8,128)S(1)}, f32[2,6,16,192]{3,2,1,0:T(8,128)S(1)}) custom-call(s32[4]{0:T(128)S(1)} %pad_add_fusion.place_ref, bf16[2,3072,128]{2,1,0:T(8,128)(2,1)S(1)} %bitcast.24, bf16[3,18,4,16,32]{4,3,2,1,0:T(8,128)(2,1)S(1)} %bitcast.30, bf16[1,2400,128]{2,1,0:T(8,128)(2,1)S(1)} %collective-permute-done.5.got_ref, ...), custom_call_target="tpu_custom_call" | custom-call | flops 1000000 | bytes 100000 | tf_op jit(solution)/shard_map/x_middle_second/pallas_call | solution.py:484
  49.2 1.3 %x_last_first.1.sent_ref = bf16[32,2,16,384]{3,2,1,0:T(8,128)(2,1)S(1)} custom-call(s32[4]{0:T(128)S(1)} %pad_add_fusion.place_ref, bf16[2,3072,128]{2,1,0:T(8,128)(2,1)S(1)} %bitcast.25, bf16[1,768,128]{2,1,0:T(8,128)(2,1)S(1)} %collective-permute-done.8.got_ref, f32[2,6,16,192]{3,2,1,0:T(8,128)S(1)} %get-tuple-element.41.rows_ref, ...), custom_call_target="tpu_custom_call" | custom-call | flops 1000000 | bytes 100000 | tf_op jit(solution)/shard_map/x_last_first/pallas_call | solution.py:484
  50.5 2.0 %collective-permute-done.7.halo_ref = bf16[2,192,128]{2,1,0:T(8,128)(2,1)S(1)} collective-permute-done((bf16[2,192,128]{2,1,0:T(8,128)(2,1)S(1)}, bf16[2,192,128]{2,1,0:T(8,128)(2,1)S(1)}, u32[]{:S(2)}, u32[]{:S(2)}) %collective-permute-start.7) | collective-permute-done | bytes 98336 | tf_op jit(solution)/shard_map/ppermute | solution.py:520
  52.6 2.1 %x_last_second.1 = bf16[32,2,16,384]{3,2,1,0:T(8,128)(2,1)S(1)} custom-call(s32[4]{0:T(128)S(1)} %pad_add_fusion.place_ref, bf16[2,3072,128]{2,1,0:T(8,128)(2,1)S(1)} %bitcast.26, bf16[1,768,128]{2,1,0:T(8,128)(2,1)S(1)} %collective-permute-done.6.got_ref, f32[2,6,16,192]{3,2,1,0:T(8,128)S(1)} %get-tuple-element.44.rows_ref, ...), custom_call_target="tpu_custom_call", output_to_operand_aliasing={{}: (10, {})} | custom-call | flops 1000000 | bytes 100000 | tf_op jit(solution)/shard_map/x_last_second/pallas_call | solution.py:484
  54.7 20.0 %all_to_all.5.got_ref = bf16[64,16,384]{2,1,0:T(8,128)(2,1)S(1)} all-to-all(bf16[64,16,384]{2,1,0:T(8,128)(2,1)S(1)} %bitcast.35), channel_id=1, replica_groups={{0,2,4,6,8,10,12,14,16,18,20,22,24,26,28,30,32,34,36,38,40,42,44,46,48,..., dimensions={0} | all-to-all | bytes 1572864 | tf_op jit(solution)/shard_map/all_to_all | solution.py:596
  74.7 1.4 %total.1 = f32[4,1,2,2,384]{4,3,2,1,0:T(2,128)} custom-call(s32[3]{0:T(128)S(1)} %copy-done.4, bf16[64,16,384]{2,1,0:T(8,128)(2,1)S(1)} %all_to_all.5.got_ref), custom_call_target="tpu_custom_call" | custom-call | tf_op jit(solution)/shard_map/total/pallas_call | solution.py:598
  (20 shorter events, 0.2 us)
Async XLA Ops:
  0.0 12.2 %collective-permute-start = (bf16[3,18,4,1,16,32]{5,4,2,1,0,3:T(8,128)(2,1)}, bf16[3,18,4,1,16,32]{5,4,2,1,0,3:T(8,128)(2,1)S(1)}, u32[]{:S(2)}, u32[]{:S(2)}) collective-permute-start(bf16[3,18,4,1,16,32]{5,4,2,1,0,3:T(8,128)(2,1)} %bitcast.31), channel_id=1, source_target_pairs={{0,1},{1,0},{2,3},{3,2},{4,5},{5,4},{6,7},{7,6},{8,9},{9,8},{10,11... | collective-permute-start | bytes 663560 | tf_op jit(solution)/shard_map/ppermute | solution.py:497
  0.1 1.9 %copy-start = (bf16[2,3,4,1,16,32,128]{6,5,4,3,2,1,0:T(8,128)(2,1)S(1)}, bf16[2,3,4,1,16,32,128]{6,5,4,3,2,1,0:T(8,128)(2,1)}, u32[]{:S(2)}) copy-start(bf16[2,3,4,1,16,32,128]{6,5,4,3,2,1,0:T(8,128)(2,1)} %param.4) | copy-start | bytes 9437188
  2.0 1.2 %copy-start.2 = (bf16[3,18,4,1,16,32]{5,4,3,2,1,0:T(8,128)(2,1)S(1)}, bf16[3,18,4,1,16,32]{5,4,3,2,1,0:T(8,128)(2,1)}, u32[]{:S(2)}) copy-start(bf16[3,18,4,1,16,32]{5,4,3,2,1,0:T(8,128)(2,1)} %param.5) | copy-start | bytes 663556
  3.9 26.6 %collective-permute-start.3 = (bf16[1,3168,128]{2,1,0:T(8,128)(2,1)S(1)}, bf16[1,3168,128]{2,1,0:T(8,128)(2,1)S(1)}, u32[]{:S(2)}, u32[]{:S(2)}) collective-permute-start(bf16[1,3168,128]{2,1,0:T(8,128)(2,1)S(1)} %bitcast.37), channel_id=1, source_target_pairs={{0,4},{4,0},{8,12},{12,8},{16,20},{20,16},{24,28},{28,24},{32,36},... | collective-permute-start | bytes 2433032 | tf_op jit(solution)/shard_map/ppermute | solution.py:456
  5.6 29.2 %collective-permute-start.4 = (bf16[1,3168,128]{2,1,0:T(8,128)(2,1)S(1)}, bf16[1,3168,128]{2,1,0:T(8,128)(2,1)S(1)}, u32[]{:S(2)}, u32[]{:S(2)}) collective-permute-start(bf16[1,3168,128]{2,1,0:T(8,128)(2,1)S(1)} %bitcast.36), channel_id=1, source_target_pairs={{0,124},{4,8},{8,4},{12,16},{16,12},{20,24},{24,20},{28,32},{32,28... | collective-permute-start | bytes 2433032 | tf_op jit(solution)/shard_map/ppermute | solution.py:456
  12.2 0.8 copy-start.5
  12.9 3.5 %collective-permute-start.1 = (bf16[2,96,32,128]{3,2,1,0:T(8,128)(2,1)S(1)}, bf16[2,96,32,128]{3,2,1,0:T(8,128)(2,1)S(1)}, u32[]{:S(2)}, u32[]{:S(2)}) collective-permute-start(bf16[2,96,32,128]{3,2,1,0:T(8,128)(2,1)S(1)} %pack_given.1), channel_id=1, source_target_pairs={{0,1},{1,0},{2,3},{3,2},{4,5},{5,4},{6,7},{7,6},{8,9},{9,8},{10,11... | collective-permute-start | bytes 4718600 | tf_op jit(solution)/shard_map/ppermute | solution.py:502
  13.0 3.4 %copy-start.1 = (bf16[2,3,4,1,16,32,128]{6,5,4,3,2,1,0:T(8,128)(2,1)S(1)}, bf16[2,3,4,1,16,32,128]{6,5,4,3,2,1,0:T(8,128)(2,1)}, u32[]{:S(2)}) copy-start(bf16[2,3,4,1,16,32,128]{6,5,4,3,2,1,0:T(8,128)(2,1)} %param.4) | copy-start | bytes 9437188
  13.8 4.6 %copy-start.3 = (bf16[3,18,4,1,16,32]{5,4,3,2,1,0:T(8,128)(2,1)S(1)}, bf16[3,18,4,1,16,32]{5,4,3,2,1,0:T(8,128)(2,1)}, u32[]{:S(2)}) copy-start(bf16[3,18,4,1,16,32]{5,4,3,2,1,0:T(8,128)(2,1)} %param.5) | copy-start | bytes 663556
  17.0 27.1 %collective-permute-start.2 = (bf16[1,2400,128]{2,1,0:T(8,128)(2,1)S(1)}, bf16[1,2400,128]{2,1,0:T(8,128)(2,1)S(1)}, u32[]{:S(2)}, u32[]{:S(2)}) collective-permute-start(bf16[1,2400,128]{2,1,0:T(8,128)(2,1)S(1)} %bitcast.39), channel_id=1, source_target_pairs={{0,4},{4,0},{8,12},{12,8},{16,20},{20,16},{24,28},{28,24},{32,36},... | collective-permute-start | bytes 1843208 | tf_op jit(solution)/shard_map/ppermute | solution.py:456
  17.1 29.5 %collective-permute-start.5 = (bf16[1,2400,128]{2,1,0:T(8,128)(2,1)S(1)}, bf16[1,2400,128]{2,1,0:T(8,128)(2,1)S(1)}, u32[]{:S(2)}, u32[]{:S(2)}) collective-permute-start(bf16[1,2400,128]{2,1,0:T(8,128)(2,1)S(1)} %bitcast.38), channel_id=1, source_target_pairs={{0,124},{4,8},{8,4},{12,16},{16,12},{20,24},{24,20},{28,32},{32,28... | collective-permute-start | bytes 1843208 | tf_op jit(solution)/shard_map/ppermute | solution.py:456
  29.6 19.6 %collective-permute-start.8 = (bf16[1,768,128]{2,1,0:T(8,128)(2,1)S(1)}, bf16[1,768,128]{2,1,0:T(8,128)(2,1)S(1)}, u32[]{:S(2)}, u32[]{:S(2)}) collective-permute-start(bf16[1,768,128]{2,1,0:T(8,128)(2,1)S(1)} %bitcast.41), channel_id=1, source_target_pairs={{0,4},{4,0},{8,12},{12,8},{16,20},{20,16},{24,28},{28,24},{32,36},... | collective-permute-start | bytes 589832 | tf_op jit(solution)/shard_map/ppermute | solution.py:456
  30.4 22.2 %collective-permute-start.6 = (bf16[1,768,128]{2,1,0:T(8,128)(2,1)S(1)}, bf16[1,768,128]{2,1,0:T(8,128)(2,1)S(1)}, u32[]{:S(2)}, u32[]{:S(2)}) collective-permute-start(bf16[1,768,128]{2,1,0:T(8,128)(2,1)S(1)} %bitcast.40), channel_id=1, source_target_pairs={{0,124},{4,8},{8,4},{12,16},{16,12},{20,24},{24,20},{28,32},{32,28... | collective-permute-start | bytes 589832 | tf_op jit(solution)/shard_map/ppermute | solution.py:456
  34.9 17.7 %collective-permute-start.7 = (bf16[2,192,128]{2,1,0:T(8,128)(2,1)S(1)}, bf16[2,192,128]{2,1,0:T(8,128)(2,1)S(1)}, u32[]{:S(2)}, u32[]{:S(2)}) collective-permute-start(bf16[2,192,128]{2,1,0:T(8,128)(2,1)S(1)} %bitcast.42), channel_id=1, source_target_pairs={{0,2},{2,0},{1,3},{3,1},{4,6},{6,4},{5,7},{7,5},{8,10},{10,8},{9,1... | collective-permute-start | bytes 294920 | tf_op jit(solution)/shard_map/ppermute | solution.py:520
  54.7 20.0 %copy-start.4 = (s32[3]{0:T(128)S(1)}, s32[3]{0:T(128)}, u32[]{:S(2)}) copy-start(s32[3]{0:T(128)} %directions_ref.1) | copy-start | bytes 40

commit v8 on v7

--- a/solution.py
+++ b/solution.py
@@ -164,11 +164,17 @@
         put_links(out_ref, 0, 6 * count_z, lambda e, t=t: link_ref[0, e, t], count_z, count_y, nev)
 
 
-def pack_given_kernel(place_ref, v_ref, given_ref):
-    count_z = v_ref.shape[3]
+def pack_given_kernel(place_ref, v_ref, link_ref, given_ref):
+    count_z, count_y, nev = v_ref.shape[3:]
+    planes = link_planes(nev, count_z, count_y)
     for m in range(2):
+        t = 1 - place_ref[0] + 2 * m
         for held in range(6):
-            given_ref[m, held * count_z : (held + 1) * count_z] = v_ref[held // 3, held % 3, 1 - place_ref[0] + 2 * m]
+            given_ref[m, held * count_z : (held + 1) * count_z] = v_ref[held // 3, held % 3, t]
+        for k in range(3):
+            put_links(
+                given_ref, m, 6 * count_z + k * planes, lambda e, k=k, t=t: link_ref[k, e, t], count_z, count_y, nev
+            )
 
 
 def split(place_ref, swap_ref, start, count_z, out_refs):
@@ -180,13 +186,13 @@
             out_ref[0, held * depth : (held + 1) * depth] = swap_ref[odd if i else 1 - odd, first : first + depth]
 
 
-def split_first_kernel(count_z, place_ref, swap_ref, link_ref, v_ref, first_ref, second_ref, lowest_ref):
-    count_y, nev = v_ref.shape[4:]
+def split_first_kernel(count_z, place_ref, swap_ref, v_ref, first_ref, second_ref, lowest_ref):
     split(place_ref, swap_ref, 0, count_z, (first_ref, second_ref))
     core, odd = place_ref[0], place_ref[3]
-    for out_ref, t in ((first_ref, core + 2 * (1 - odd)), (second_ref, core + 2 * odd)):
+    for out_ref, m in ((first_ref, 1 - odd), (second_ref, odd)):
         depth = out_ref.shape[1] // 6
-        put_links(out_ref, 0, 6 * depth, lambda e, t=t: link_ref[0, e, t], count_z, count_y, nev)
+        planes = out_ref.shape[1] - 6 * depth
+        out_ref[0, 6 * depth :] = swap_ref[m, 6 * count_z : 6 * count_z + planes]
     for m in range(2):
         for i in range(6):
             own = v_ref[i // 3, i % 3, core + 2 * m, 0]
@@ -197,7 +203,7 @@
     split(place_ref, swap_ref, count_z - first_ref.shape[1] // 6, count_z, (first_ref, second_ref))
 
 
-def yz_kernel(place_ref, v_ref, swap_ref, link_ref, other_link_ref, table_ref, out_ref, top_ref, line_ref,
+def yz_kernel(place_ref, v_ref, swap_ref, link_ref, table_ref, out_ref, top_ref, line_ref,
               rows, padded, phased, moved_y, moved_z):
     core = place_ref[0]
     step_m = pl.program_id(0)
@@ -233,7 +239,7 @@
         for b in range(3):
             block = packed_plane(swapped, count_z, q, b, 0, count_z, count_y)
             padded[q, b, pl.ds(theirs, count_z)] = block.reshape(count_z, count_y, nev)
-    fill_rows(lambda k, e: other_link_ref[k, e, t], theirs)
+    fill_rows(lambda k, e: packed_link(swapped, count_z, k, e, count_z, count_y), theirs)
     fill_rows(lambda k, e: link_ref[k, e, t], mine)
 
     table = table_ref
@@ -373,27 +379,28 @@
     return combine(products, nev)
 
 
-def x_middle(at, place_ref, swap_ref, link_ref, got_ref, table, before, out_ref, rows_ref, *scratch):
+def x_middle(at, place_ref, swap_ref, got_ref, table, before, out_ref, rows_ref, *scratch):
     held_z = rows_ref.shape[2]
     depth, count_y = scratch[1].shape[2:4]
-    core, odd = place_ref[0], place_ref[3]
+    odd = place_ref[3]
     m = 1 - odd if at else odd
-    got = got_ref.at[0]
+    own, got = swap_ref.at[m], got_ref.at[0]
     pair_rows(
-        odd, at, lambda e: link_ref[0, e, core + 2 * m], lambda e: packed_link(got, depth, 0, e, held_z, count_y), rows_ref
+        odd, at, lambda e: packed_link(own, held_z, 0, e, held_z, count_y),
+        lambda e: packed_link(got, depth, 0, e, held_z, count_y), rows_ref,
     )
     parts = x_part(0, at, place_ref, swap_ref, got, table, rows_ref, *scratch)
     for i, part in enumerate(parts):
         out_ref[i] = part + before[m, i]
 
 
-def x_middle_first(place_ref, swap_ref, link_ref, got_ref, table, before, top_ref, line_ref,
+def x_middle_first(place_ref, swap_ref, got_ref, table, before, top_ref, line_ref,
                    out_ref, rows_ref, phased_ref, displaced_ref, forward_ref, *scratch):
     for m in range(2):
         boundary_below(
             top_ref.at[m], line_ref.at[m], table, phased_ref.at[m], displaced_ref.at[m], forward_ref.at[m]
         )
-    x_middle(0, place_ref, swap_ref, link_ref, got_ref, table, before, out_ref, rows_ref, *scratch)
+    x_middle(0, place_ref, swap_ref, got_ref, table, before, out_ref, rows_ref, *scratch)
 
 
 def x_last(at, place_ref, swap_ref, got_ref, rows_ref, table, before, pieces_ref, *scratch):
@@ -494,11 +501,10 @@
         )(*operands)
 
     swap = [(0, 1), (1, 0), (2, 3), (3, 2)]
-    other_links = lax.ppermute(gauge_links, "gz", swap).reshape(links.shape)
     mine = call(pack_own_kernel, "pack_own", [planes_of(1, count_z, 1)] * 2, [], place, vectors, links)
     got_first = exchange(*mine)
-    after, other_links, _ = lax.optimization_barrier((place, other_links, mine[0]))
-    (given,) = call(pack_given_kernel, "pack_given", [planes_of(2, count_z, 0)], [], after, vectors)
+    after, _ = lax.optimization_barrier((place, mine[0]))
+    (given,) = call(pack_given_kernel, "pack_given", [planes_of(2, count_z, 3)], [], after, vectors, links)
     swapped = lax.ppermute(given, "gz", swap)
     tail = nev // count_y
     lead = count_z - tail
@@ -514,7 +520,7 @@
     after, _ = lax.optimization_barrier((place, table))
     shapes = [planes_of(1, lead, 1)] * 2 + [jax.ShapeDtypeStruct((2, 6, count_y, nev), BF16)]
     *mine, lowest = call(
-        functools.partial(split_first_kernel, count_z), "split_first", shapes, [], after, swapped, other_links, vectors
+        functools.partial(split_first_kernel, count_z), "split_first", shapes, [], after, swapped, vectors
     )
     got_second = exchange(*mine)
     halo = lax.ppermute(lowest.reshape(2, 6 * count_y, nev), "gz", [(0, 2), (2, 0), (1, 3), (3, 1)])
@@ -524,7 +530,7 @@
     sent, top, lines = pl.pallas_call(
         yz_kernel,
         grid=(2,),
-        in_specs=[in_smem] + [in_vmem] * 5,
+        in_specs=[in_smem] + [in_vmem] * 4,
         out_specs=[
             pl.BlockSpec((size_x, 1, 4 * group, 2 * nev), lambda m: (0, m, 0, 0)),
             pl.BlockSpec((1, 6 * count_y, nev), lambda m: (m, 0, 0)),
@@ -545,7 +551,7 @@
         compiler_params=limit,
         cost_estimate=small,
         name="yz_terms",
-    )(after, vectors, swapped_rows, links, other_links, table)
+    )(after, vectors, swapped_rows, links, table)
 
     after, _ = lax.optimization_barrier((place, sent))
     mine = call(
@@ -566,7 +572,7 @@
     )
     one = [jax.ShapeDtypeStruct(parts.shape[1:], F32), jax.ShapeDtypeStruct(rows_shape, F32)]
     all_pieces = [jax.ShapeDtypeStruct((size_x, 2, 4 * group, 3 * nev), BF16)]
-    operands = after, swapped_rows, other_links
+    operands = after, swapped_rows
     edges = [
         jax.ShapeDtypeStruct((2, 4 * nev, nev), BF16),
         jax.ShapeDtypeStruct((2, 3 * count_y, 2 * nev), BF16),
@@ -577,18 +583,18 @@
         *operands, got_second[0], table, part, top, lines,
     )
     after, _ = lax.optimization_barrier((after, first_rows))
-    operands = after, swapped_rows, other_links
+    operands = after, swapped_rows
     second, second_rows = call(
         functools.partial(x_middle, 1), "x_middle_second", one, scratch(lead), *operands, got_second[1], table, part
     )
     after, _ = lax.optimization_barrier((after, second_rows))
-    operands = after, swapped_rows, other_links
+    operands = after, swapped_rows
     (pieces,) = call(
-        x_last_first, "x_last_first", all_pieces, scratch(tail), *operands[:2], got_last[0], first_rows, table, first, sent
+        x_last_first, "x_last_first", all_pieces, scratch(tail), *operands, got_last[0], first_rows, table, first, sent
     )
     (pieces,) = call(
         x_last_second, "x_last_second", all_pieces, scratch(tail) + [pltpu.VMEM((2, 4 * nev, nev), BF16)],
-        *operands[:2], got_last[1], second_rows, table, second, halo, *edges, pieces, aliases={10: 0},
+        *operands, got_last[1], second_rows, table, second, halo, *edges, pieces, aliases={10: 0},
     )
 
     pieces = pieces.reshape(2 * size_x, 4 * group, 3 * nev)

time: 76.3 us -> 74.8 us (0.980)
  blocking collectives: 20 us -> 19.2 us
    unnamed x12 -> x10, local copies, waits for them, and re-layouts: 3.08 us -> 3.07 us
  transfers between devices with their start and end apart: 9 -> 8, of which waited for: 2 -> 2; matrix products, arithmetic and copies ran while one was open for 0% -> 0% of each run, Pallas kernels for 35% -> 35%
where the time goes in v8:
time: 74.8 us; the launch traced here: 74.6 us
  Pallas kernels  30.2 us (40%)
  blocking collectives  19.2 us (26%)
  starting transfers between devices  17.7 us (24%)
  waiting for transfers between devices  4.23 us (6%)
  local copies, waits for them, and re-layouts  3.07 us (4%)
    all_to_all x1, blocking collectives, shards(): lax.all_to_all(pieces, ('ts', 'gz'), 0, 0, tiled=True, axis_index_groups=...  19.2 us
    pallas_call x9, Pallas kernels, call(): pl.pallas_call(kernel, in_specs=in_specs, out_specs=jax.tree.map(lambda _...  17.5 us
    ppermute x6, starting transfers between devices, exchange(): got[at] = lax.ppermute(array.reshape(1, -1, array.shape[-1]), 'ts', pairs)  14.9 us
    pallas_call x1, Pallas kernels, shards(): pl.pallas_call(yz_kernel, grid=(2,), in_specs=[in_smem] + [in_vmem] * 4,...  10.5 us
    unnamed x10, local copies, waits for them, and re-layouts  3.07 us
    ppermute x1, waiting for transfers between devices, shards(): swapped = lax.ppermute(given, 'gz', swap)  2.8 us
    ppermute x1, starting transfers between devices, shards(): lax.ppermute(lowest.reshape(2, 6 * count_y, nev), 'gz', [(0, 2), (2, 0),...  2.73 us
  transfers between devices with their start and end apart: 8, of which 2 were waited for; matrix products, arithmetic and copies ran while one was open for 0% of the time, Pallas kernels for 35%

profile of v8, /device:TPU:0, one launch (start us, length us, event | category | flops | bytes accessed | tf_op | source)
XLA Modules:
  0.0 74.6 jit_solution(6882616044469827535)
XLA Ops:
  0.1 1.9 %copy-done = bf16[2,3,4,1,16,32,128]{6,5,4,3,2,1,0:T(8,128)(2,1)S(1)} copy-done((bf16[2,3,4,1,16,32,128]{6,5,4,3,2,1,0:T(8,128)(2,1)S(1)}, bf16[2,3,4,1,16,32,128]{6,5,4,3,2,1,0:T(8,128)(2,1)}, u32[]{:S(2)}) %copy-start) | copy-done | bytes 3145752
  2.0 1.2 %copy-done.2 = bf16[3,18,4,1,16,32]{5,4,3,2,1,0:T(8,128)(2,1)S(1)} copy-done((bf16[3,18,4,1,16,32]{5,4,3,2,1,0:T(8,128)(2,1)S(1)}, bf16[3,18,4,1,16,32]{5,4,3,2,1,0:T(8,128)(2,1)}, u32[]{:S(2)}) %copy-start.2) | copy-done | bytes 221208
  3.1 0.7 pack_own.1
  3.9 1.7 %collective-permute-start.2 = (bf16[1,3168,128]{2,1,0:T(8,128)(2,1)S(1)}, bf16[1,3168,128]{2,1,0:T(8,128)(2,1)S(1)}, u32[]{:S(2)}, u32[]{:S(2)}) collective-permute-start(bf16[1,3168,128]{2,1,0:T(8,128)(2,1)S(1)} %bitcast.31), channel_id=1, source_target_pairs={{0,4},{4,0},{8,12},{12,8},{16,20},{20,16},{24,28},{28,24},{32,36},... | collective-permute-start | bytes 2433032 | tf_op jit(solution)/shard_map/ppermute | solution.py:463
  5.6 6.6 %collective-permute-start.3 = (bf16[1,3168,128]{2,1,0:T(8,128)(2,1)S(1)}, bf16[1,3168,128]{2,1,0:T(8,128)(2,1)S(1)}, u32[]{:S(2)}, u32[]{:S(2)}) collective-permute-start(bf16[1,3168,128]{2,1,0:T(8,128)(2,1)S(1)} %bitcast.30), channel_id=1, source_target_pairs={{0,124},{4,8},{8,4},{12,16},{16,12},{20,24},{24,20},{28,32},{32,28... | collective-permute-start | bytes 2433032 | tf_op jit(solution)/shard_map/ppermute | solution.py:463
  12.2 0.8 %pack_given.1 = bf16[2,105,32,128]{3,2,1,0:T(8,128)(2,1)S(1)} custom-call(s32[4]{0:T(128)S(1)} %pad_add_fusion.place_ref, bf16[2,3,4,16,32,128]{5,4,3,2,1,0:T(8,128)(2,1)S(1)} %bitcast.21, bf16[3,18,4,16,32]{4,3,2,1,0:T(8,128)(2,1)S(1)} %bitcast.26), custom_call_target="tpu_custom_call" | custom-call | flops 1000000 | bytes 100000 | tf_op jit(solution)/shard_map/pack_given/pallas_call | solution.py:491
  13.0 0.1 collective-permute-start
  13.1 0.8 %phase_table.1.table_ref.table = f32[8,2,1280]{2,1,0:T(2,128)S(1)} custom-call(s32[4]{0:T(128)S(1)} %pad_add_fusion.place_ref, s32[2,3]{1,0:T(2,128)S(1)} %copy-done.4), custom_call_target="tpu_custom_call" | custom-call | flops 20000000000 | bytes 100000 | tf_op jit(solution)/shard_map/phase_table/pallas_call | solution.py:511
  13.9 2.8 %collective-permute-done.swap_ref = bf16[2,105,32,128]{3,2,1,0:T(8,128)(2,1)S(1)} collective-permute-done((bf16[2,105,32,128]{3,2,1,0:T(8,128)(2,1)S(1)}, bf16[2,105,32,128]{3,2,1,0:T(8,128)(2,1)S(1)}, u32[]{:S(2)}, u32[]{:S(2)}) %collective-permute-start) | collective-permute-done | bytes 1720352 | tf_op jit(solution)/shard_map/ppermute | solution.py:508
  16.7 0.7 split_first.1
  17.4 1.3 %collective-permute-start.4 = (bf16[1,2400,128]{2,1,0:T(8,128)(2,1)S(1)}, bf16[1,2400,128]{2,1,0:T(8,128)(2,1)S(1)}, u32[]{:S(2)}, u32[]{:S(2)}) collective-permute-start(bf16[1,2400,128]{2,1,0:T(8,128)(2,1)S(1)} %bitcast.32), channel_id=1, source_target_pairs={{0,124},{4,8},{8,4},{12,16},{16,12},{20,24},{24,20},{28,32},{32,28... | collective-permute-start | bytes 1843208 | tf_op jit(solution)/shard_map/ppermute | solution.py:463
  18.7 10.5 %yz_terms.1 = (bf16[32,2,16,256]{3,2,1,0:T(8,128)(2,1)S(1)}, bf16[2,192,128]{2,1,0:T(8,128)(2,1)S(1)}, f32[2,16,256]{2,1,0:T(8,128)S(1)}) custom-call(s32[4]{0:T(128)S(1)} %pad_add_fusion.place_ref, bf16[2,3,4,16,32,128]{5,4,3,2,1,0:T(8,128)(2,1)S(1)} %bitcast.23, bf16[2,3360,128]{2,1,0:T(8,128)(2,1)S(1)} %bitcast.15, ...), custom_call_target="tpu_custom_call" | custom-call | flops 1000000 | bytes 100000 | tf_op jit(solution)/shard_map/yz_terms/pallas_call | solution.py:530
  29.2 0.6 split_last.1
  29.8 0.8 %collective-permute-start.7 = (bf16[1,768,128]{2,1,0:T(8,128)(2,1)S(1)}, bf16[1,768,128]{2,1,0:T(8,128)(2,1)S(1)}, u32[]{:S(2)}, u32[]{:S(2)}) collective-permute-start(bf16[1,768,128]{2,1,0:T(8,128)(2,1)S(1)} %bitcast.35), channel_id=1, source_target_pairs={{0,4},{4,0},{8,12},{12,8},{16,20},{20,16},{24,28},{28,24},{32,36},... | collective-permute-start | bytes 589832 | tf_op jit(solution)/shard_map/ppermute | solution.py:463
  30.6 4.4 %collective-permute-start.5 = (bf16[1,768,128]{2,1,0:T(8,128)(2,1)S(1)}, bf16[1,768,128]{2,1,0:T(8,128)(2,1)S(1)}, u32[]{:S(2)}, u32[]{:S(2)}) collective-permute-start(bf16[1,768,128]{2,1,0:T(8,128)(2,1)S(1)} %bitcast.34), channel_id=1, source_target_pairs={{0,124},{4,8},{8,4},{12,16},{16,12},{20,24},{24,20},{28,32},{32,28... | collective-permute-start | bytes 589832 | tf_op jit(solution)/shard_map/ppermute | solution.py:463
  35.0 2.7 %collective-permute-start.6 = (bf16[2,192,128]{2,1,0:T(8,128)(2,1)S(1)}, bf16[2,192,128]{2,1,0:T(8,128)(2,1)S(1)}, u32[]{:S(2)}, u32[]{:S(2)}) collective-permute-start(bf16[2,192,128]{2,1,0:T(8,128)(2,1)S(1)} %bitcast.36), channel_id=1, source_target_pairs={{0,2},{2,0},{1,3},{3,1},{4,6},{6,4},{5,7},{7,5},{8,10},{10,8},{9,1... | collective-permute-start | bytes 294920 | tf_op jit(solution)/shard_map/ppermute | solution.py:526
  37.8 6.5 %x_first.1.before = f32[2,4,128,128]{3,2,1,0:T(8,128)S(1)} custom-call(s32[4]{0:T(128)S(1)} %pad_add_fusion.place_ref, bf16[2,3,4,16,32,128]{5,4,3,2,1,0:T(8,128)(2,1)S(1)} %bitcast.24, bf16[3,18,4,16,32]{4,3,2,1,0:T(8,128)(2,1)S(1)} %bitcast.28, bf16[1,3168,128]{2,1,0:T(8,128)(2,1)S(1)} %collective-permute-done.2.first_ref, ...), custom_call_target="tpu_custom_call" | custom-call | flops 1000000 | bytes 100000 | tf_op jit(solution)/shard_map/x_first/pallas_call | solution.py:491
  44.3 2.4 %x_middle_first.1 = (f32[4,128,128]{2,1,0:T(8,128)S(1)}, f32[2,6,16,192]{3,2,1,0:T(8,128)S(1)}, bf16[2,512,128]{2,1,0:T(8,128)(2,1)S(1)}, bf16[2,96,256]{2,1,0:T(8,128)(2,1)S(1)}, bf16[2,192,256]{2,1,0:T(8,128)(2,1)S(1)}) custom-call(s32[4]{0:T(128)S(1)} %pad_add_fusion.place_ref, bf16[2,3360,128]{2,1,0:T(8,128)(2,1)S(1)} %bitcast.16, ...), custom_call_target="tpu_custom_call" | custom-call | flops 1000000 | bytes 100000 | tf_op jit(solution)/shard_map/x_middle_first/pallas_call | solution.py:491
  46.7 2.4 %x_middle_second.1 = (f32[4,128,128]{2,1,0:T(8,128)S(1)}, f32[2,6,16,192]{3,2,1,0:T(8,128)S(1)}) custom-call(s32[4]{0:T(128)S(1)} %pad_add_fusion.place_ref, bf16[2,3360,128]{2,1,0:T(8,128)(2,1)S(1)} %bitcast.17, bf16[1,2400,128]{2,1,0:T(8,128)(2,1)S(1)} %collective-permute-done.4.got_ref, f32[8,2,1280]{2,1,0:T(2,128)S(1)} %phase_table.1.table_ref.table, ...), custom_call_target="tpu_custom_call" | custom-call | flops 1000000 | bytes 100000 | tf_op jit(solution)/shard_map/x_middle_second/pallas_call | solution.py:491
  49.2 1.3 %x_last_first.1.sent_ref = bf16[32,2,16,384]{3,2,1,0:T(8,128)(2,1)S(1)} custom-call(s32[4]{0:T(128)S(1)} %pad_add_fusion.place_ref, bf16[2,3360,128]{2,1,0:T(8,128)(2,1)S(1)} %bitcast.18, bf16[1,768,128]{2,1,0:T(8,128)(2,1)S(1)} %collective-permute-done.7.got_ref, f32[2,6,16,192]{3,2,1,0:T(8,128)S(1)} %get-tuple-element.39.rows_ref, ...), custom_call_target="tpu_custom_call" | custom-call | flops 1000000 | bytes 100000 | tf_op jit(solution)/shard_map/x_last_first/pallas_call | solution.py:491
  50.5 1.4 %collective-permute-done.6.halo_ref = bf16[2,192,128]{2,1,0:T(8,128)(2,1)S(1)} collective-permute-done((bf16[2,192,128]{2,1,0:T(8,128)(2,1)S(1)}, bf16[2,192,128]{2,1,0:T(8,128)(2,1)S(1)}, u32[]{:S(2)}, u32[]{:S(2)}) %collective-permute-start.6) | collective-permute-done | bytes 98336 | tf_op jit(solution)/shard_map/ppermute | solution.py:526
  51.9 2.1 %x_last_second.1 = bf16[32,2,16,384]{3,2,1,0:T(8,128)(2,1)S(1)} custom-call(s32[4]{0:T(128)S(1)} %pad_add_fusion.place_ref, bf16[2,3360,128]{2,1,0:T(8,128)(2,1)S(1)} %bitcast.19, bf16[1,768,128]{2,1,0:T(8,128)(2,1)S(1)} %collective-permute-done.5.got_ref, f32[2,6,16,192]{3,2,1,0:T(8,128)S(1)} %get-tuple-element.42.rows_ref, ...), custom_call_target="tpu_custom_call", output_to_operand_aliasing={{}: (10, {})} | custom-call | flops 1000000 | bytes 100000 | tf_op jit(solution)/shard_map/x_last_second/pallas_call | solution.py:491
  54.0 19.2 %all_to_all.5.got_ref = bf16[64,16,384]{2,1,0:T(8,128)(2,1)S(1)} all-to-all(bf16[64,16,384]{2,1,0:T(8,128)(2,1)S(1)} %bitcast.29), channel_id=1, replica_groups={{0,2,4,6,8,10,12,14,16,18,20,22,24,26,28,30,32,34,36,38,40,42,44,46,48,..., dimensions={0} | all-to-all | bytes 1572864 | tf_op jit(solution)/shard_map/all_to_all | solution.py:602
  73.2 1.4 %total.1 = f32[4,1,2,2,384]{4,3,2,1,0:T(2,128)} custom-call(s32[3]{0:T(128)S(1)} %copy-done.3, bf16[64,16,384]{2,1,0:T(8,128)(2,1)S(1)} %all_to_all.5.got_ref), custom_call_target="tpu_custom_call" | custom-call | tf_op jit(solution)/shard_map/total/pallas_call | solution.py:604
  (16 shorter events, 0.2 us)
Async XLA Ops:
  0.1 1.9 %copy-start = (bf16[2,3,4,1,16,32,128]{6,5,4,3,2,1,0:T(8,128)(2,1)S(1)}, bf16[2,3,4,1,16,32,128]{6,5,4,3,2,1,0:T(8,128)(2,1)}, u32[]{:S(2)}) copy-start(bf16[2,3,4,1,16,32,128]{6,5,4,3,2,1,0:T(8,128)(2,1)} %param.4) | copy-start | bytes 9437188
  2.0 1.2 %copy-start.2 = (bf16[3,18,4,1,16,32]{5,4,3,2,1,0:T(8,128)(2,1)S(1)}, bf16[3,18,4,1,16,32]{5,4,3,2,1,0:T(8,128)(2,1)}, u32[]{:S(2)}) copy-start(bf16[3,18,4,1,16,32]{5,4,3,2,1,0:T(8,128)(2,1)} %param.5) | copy-start | bytes 663556
  3.9 26.7 %collective-permute-start.2 = (bf16[1,3168,128]{2,1,0:T(8,128)(2,1)S(1)}, bf16[1,3168,128]{2,1,0:T(8,128)(2,1)S(1)}, u32[]{:S(2)}, u32[]{:S(2)}) collective-permute-start(bf16[1,3168,128]{2,1,0:T(8,128)(2,1)S(1)} %bitcast.31), channel_id=1, source_target_pairs={{0,4},{4,0},{8,12},{12,8},{16,20},{20,16},{24,28},{28,24},{32,36},... | collective-permute-start | bytes 2433032 | tf_op jit(solution)/shard_map/ppermute | solution.py:463
  5.6 7.5 %copy-start.4 = (s32[2,3]{1,0:T(2,128)S(1)}, s32[2,3]{1,0:T(2,128)}, u32[]{:S(2)}) copy-start(s32[2,3]{1,0:T(2,128)} %momenta_ref.1) | copy-start | bytes 76
  5.6 29.4 %collective-permute-start.3 = (bf16[1,3168,128]{2,1,0:T(8,128)(2,1)S(1)}, bf16[1,3168,128]{2,1,0:T(8,128)(2,1)S(1)}, u32[]{:S(2)}, u32[]{:S(2)}) collective-permute-start(bf16[1,3168,128]{2,1,0:T(8,128)(2,1)S(1)} %bitcast.30), channel_id=1, source_target_pairs={{0,124},{4,8},{8,4},{12,16},{16,12},{20,24},{24,20},{28,32},{32,28... | collective-permute-start | bytes 2433032 | tf_op jit(solution)/shard_map/ppermute | solution.py:463
  13.0 3.7 %collective-permute-start = (bf16[2,105,32,128]{3,2,1,0:T(8,128)(2,1)S(1)}, bf16[2,105,32,128]{3,2,1,0:T(8,128)(2,1)S(1)}, u32[]{:S(2)}, u32[]{:S(2)}) collective-permute-start(bf16[2,105,32,128]{3,2,1,0:T(8,128)(2,1)S(1)} %pack_given.1), channel_id=1, source_target_pairs={{0,1},{1,0},{2,3},{3,2},{4,5},{5,4},{6,7},{7,6},{8,9},{9,8},{10,11... | collective-permute-start | bytes 5160968 | tf_op jit(solution)/shard_map/ppermute | solution.py:508
  13.1 3.6 %copy-start.1 = (bf16[2,3,4,1,16,32,128]{6,5,4,3,2,1,0:T(8,128)(2,1)S(1)}, bf16[2,3,4,1,16,32,128]{6,5,4,3,2,1,0:T(8,128)(2,1)}, u32[]{:S(2)}) copy-start(bf16[2,3,4,1,16,32,128]{6,5,4,3,2,1,0:T(8,128)(2,1)} %param.4) | copy-start | bytes 9437188
  17.3 26.9 %collective-permute-start.1 = (bf16[1,2400,128]{2,1,0:T(8,128)(2,1)S(1)}, bf16[1,2400,128]{2,1,0:T(8,128)(2,1)S(1)}, u32[]{:S(2)}, u32[]{:S(2)}) collective-permute-start(bf16[1,2400,128]{2,1,0:T(8,128)(2,1)S(1)} %bitcast.33), channel_id=1, source_target_pairs={{0,4},{4,0},{8,12},{12,8},{16,20},{20,16},{24,28},{28,24},{32,36},... | collective-permute-start | bytes 1843208 | tf_op jit(solution)/shard_map/ppermute | solution.py:463
  17.4 29.3 %collective-permute-start.4 = (bf16[1,2400,128]{2,1,0:T(8,128)(2,1)S(1)}, bf16[1,2400,128]{2,1,0:T(8,128)(2,1)S(1)}, u32[]{:S(2)}, u32[]{:S(2)}) collective-permute-start(bf16[1,2400,128]{2,1,0:T(8,128)(2,1)S(1)} %bitcast.32), channel_id=1, source_target_pairs={{0,124},{4,8},{8,4},{12,16},{16,12},{20,24},{24,20},{28,32},{32,28... | collective-permute-start | bytes 1843208 | tf_op jit(solution)/shard_map/ppermute | solution.py:463
  29.8 19.4 %collective-permute-start.7 = (bf16[1,768,128]{2,1,0:T(8,128)(2,1)S(1)}, bf16[1,768,128]{2,1,0:T(8,128)(2,1)S(1)}, u32[]{:S(2)}, u32[]{:S(2)}) collective-permute-start(bf16[1,768,128]{2,1,0:T(8,128)(2,1)S(1)} %bitcast.35), channel_id=1, source_target_pairs={{0,4},{4,0},{8,12},{12,8},{16,20},{20,16},{24,28},{28,24},{32,36},... | collective-permute-start | bytes 589832 | tf_op jit(solution)/shard_map/ppermute | solution.py:463
  30.6 21.3 %collective-permute-start.5 = (bf16[1,768,128]{2,1,0:T(8,128)(2,1)S(1)}, bf16[1,768,128]{2,1,0:T(8,128)(2,1)S(1)}, u32[]{:S(2)}, u32[]{:S(2)}) collective-permute-start(bf16[1,768,128]{2,1,0:T(8,128)(2,1)S(1)} %bitcast.34), channel_id=1, source_target_pairs={{0,124},{4,8},{8,4},{12,16},{16,12},{20,24},{24,20},{28,32},{32,28... | collective-permute-start | bytes 589832 | tf_op jit(solution)/shard_map/ppermute | solution.py:463
  35.0 16.9 %collective-permute-start.6 = (bf16[2,192,128]{2,1,0:T(8,128)(2,1)S(1)}, bf16[2,192,128]{2,1,0:T(8,128)(2,1)S(1)}, u32[]{:S(2)}, u32[]{:S(2)}) collective-permute-start(bf16[2,192,128]{2,1,0:T(8,128)(2,1)S(1)} %bitcast.36), channel_id=1, source_target_pairs={{0,2},{2,0},{1,3},{3,1},{4,6},{6,4},{5,7},{7,5},{8,10},{10,8},{9,1... | collective-permute-start | bytes 294920 | tf_op jit(solution)/shard_map/ppermute | solution.py:526
  51.9 21.3 %copy-start.3 = (s32[3]{0:T(128)S(1)}, s32[3]{0:T(128)}, u32[]{:S(2)}) copy-start(s32[3]{0:T(128)} %directions_ref.1) | copy-start | bytes 40

commit v9 on v8

--- a/solution.py
+++ b/solution.py
@@ -412,19 +412,54 @@
     pieces_ref[:, 1 - odd if at else odd, :, 2 * nev :] = partial_rows(parts).astype(BF16)
 
 
-def x_last_first(place_ref, swap_ref, got_ref, rows_ref, table, before, sent_ref, pieces_ref, *scratch):
+def one_side(vectors, x_at, kind, at_table, first, rows, table, phased, displaced):
+    depth, count_y, lanes = displaced.shape[1:]
+    nev = lanes // 2
+    sites = depth * count_y
+    step = nev // count_y
+    same = site_masks(count_y, rows.shape[3])[0]
+    write_phased(
+        lambda q, b, block: vectors(q, b, block * step, step), table, x_at, at_table, sites // nev, phased, 0, sites
+    )
+    for z in range(depth):
+        plane = jnp.concatenate([vectors(q, b, z, 1) for q in range(2) for b in range(3)], axis=0)
+        terms = jnp.dot(spread(rows, kind, first + z, same), plane, preferred_element_type=F32)
+        put_displaced(displaced, z, terms, count_y, nev)
+
+
+def last_place(place_ref, rows_ref, displaced):
+    held_z = rows_ref.shape[2]
+    depth, count_y, lanes = displaced.shape[1:]
+    first = held_z - depth
+    at = pl.multiple_of((1 - place_ref[0]) * (held_z * count_y) + first * count_y, lanes // 2)
+    return held_z, depth, count_y, first, at
+
+
+def x_last_first(place_ref, swap_ref, got_ref, rows_ref, second_rows, table, before, sent_ref,
+                 pieces_ref, own_phased, own_displaced, *scratch):
     pieces_ref[:, :, :, : sent_ref.shape[3]] = sent_ref[...]
     x_last(0, place_ref, swap_ref, got_ref, rows_ref, table, before, pieces_ref, *scratch)
-
-
-def x_last_second(place_ref, swap_ref, got_ref, rows_ref, table, before, halo_ref, phased_ref, displaced_ref,
-                  forward_ref, sent_ref, pieces_ref, phased, moved, edge):
+    held_z, depth, count_y, first, at_table = last_place(place_ref, second_rows, own_displaced)
+    own = from_rows(swap_ref.at[1 - place_ref[3]], held_z, count_y, first)
+    one_side(own, 0, 0, at_table, first, second_rows, table, own_phased, own_displaced)
+
+
+def x_last_second(place_ref, got_ref, rows_ref, own_phased, own_displaced, table, before, halo_ref, phased_ref,
+                  displaced_ref, forward_ref, sent_ref, pieces_ref, phased, displaced, edge):
     nev = before.shape[2]
+    odd = place_ref[3]
     for m in range(2):
         parts = boundary(halo_ref.at[m], phased_ref.at[m], displaced_ref.at[m], forward_ref.at[m], table, edge.at[m])
         above = partial_rows(parts)
         pieces_ref[:, m, :, nev : 2 * nev] = (sent_ref[:, m, :, nev : 2 * nev].astype(F32) + above).astype(BF16)
-    x_last(1, place_ref, swap_ref, got_ref, rows_ref, table, before, pieces_ref, phased, moved)
+    held_z, depth, count_y, first, at_table = last_place(place_ref, rows_ref, displaced)
+    received = from_rows(got_ref.at[0], depth, count_y)
+    one_side(received, 2 - odd, 1, at_table, first, rows_ref, table, phased, displaced)
+    sites = 3 * depth * count_y
+    products = jnp.dot(own_phased[...], displaced[...].reshape(sites, 2 * nev), preferred_element_type=F32)
+    products += jnp.dot(phased[...], own_displaced[...].reshape(sites, 2 * nev), preferred_element_type=F32)
+    parts = [part + before[i] for i, part in enumerate(combine(products, nev))]
+    pieces_ref[:, 1 - odd, :, 2 * nev :] = partial_rows(parts).astype(BF16)
 
 
 def total_kernel(directions_ref, got_ref, out_ref, total_ref):
@@ -589,12 +624,15 @@
     )
     after, _ = lax.optimization_barrier((after, second_rows))
     operands = after, swapped_rows
+    sides = [(4 * nev, 3 * tail * count_y), (3, tail, count_y, 2 * nev)]
+    pieces, *own_side = call(
+        x_last_first, "x_last_first", all_pieces + [jax.ShapeDtypeStruct(side, BF16) for side in sides], scratch(tail),
+        *operands, got_last[0], first_rows, second_rows, table, first, sent,
+    )
     (pieces,) = call(
-        x_last_first, "x_last_first", all_pieces, scratch(tail), *operands, got_last[0], first_rows, table, first, sent
-    )
-    (pieces,) = call(
-        x_last_second, "x_last_second", all_pieces, scratch(tail) + [pltpu.VMEM((2, 4 * nev, nev), BF16)],
-        *operands, got_last[1], second_rows, table, second, halo, *edges, pieces, aliases={10: 0},
+        x_last_second, "x_last_second", all_pieces,
+        [pltpu.VMEM(side, BF16) for side in sides] + [pltpu.VMEM((2, 4 * nev, nev), BF16)],
+        after, got_last[1], second_rows, *own_side, table, second, halo, *edges, pieces, aliases={11: 0},
     )
 
     pieces = pieces.reshape(2 * size_x, 4 * group, 3 * nev)

time: 74.8 us -> 74.6 us (level)
  no operation moved by 1% of the time
where the time goes in v9:
time: 74.6 us; the launch traced here: 74.4 us
  Pallas kernels  30.1 us (40%)
  blocking collectives  19.2 us (26%)
  starting transfers between devices  17.7 us (24%)
  waiting for transfers between devices  4.06 us (5%)
  local copies, waits for them, and re-layouts  3.07 us (4%)
    all_to_all x1, blocking collectives, shards(): lax.all_to_all(pieces, ('ts', 'gz'), 0, 0, tiled=True, axis_index_groups=...  19.2 us
    pallas_call x9, Pallas kernels, call(): pl.pallas_call(kernel, in_specs=in_specs, out_specs=jax.tree.map(lambda _...  17.4 us
    ppermute x6, starting transfers between devices, exchange(): got[at] = lax.ppermute(array.reshape(1, -1, array.shape[-1]), 'ts', pairs)  14.9 us
    pallas_call x1, Pallas kernels, shards(): pl.pallas_call(yz_kernel, grid=(2,), in_specs=[in_smem] + [in_vmem] * 4,...  10.5 us
    unnamed x10, local copies, waits for them, and re-layouts  3.07 us
    ppermute x1, waiting for transfers between devices, shards(): swapped = lax.ppermute(given, 'gz', swap)  2.8 us
    ppermute x1, starting transfers between devices, shards(): lax.ppermute(lowest.reshape(2, 6 * count_y, nev), 'gz', [(0, 2), (2, 0),...  2.73 us
  transfers between devices with their start and end apart: 8, of which 2 were waited for; matrix products, arithmetic and copies ran while one was open for 0% of the time, Pallas kernels for 35%

profile of v9, /device:TPU:0, one launch (start us, length us, event | category | flops | bytes accessed | tf_op | source)
XLA Modules:
  0.0 74.4 jit_solution(11338896005892411336)
XLA Ops:
  0.1 1.9 %copy-done = bf16[2,3,4,1,16,32,128]{6,5,4,3,2,1,0:T(8,128)(2,1)S(1)} copy-done((bf16[2,3,4,1,16,32,128]{6,5,4,3,2,1,0:T(8,128)(2,1)S(1)}, bf16[2,3,4,1,16,32,128]{6,5,4,3,2,1,0:T(8,128)(2,1)}, u32[]{:S(2)}) %copy-start) | copy-done | bytes 3145752
  2.0 1.2 %copy-done.2 = bf16[3,18,4,1,16,32]{5,4,3,2,1,0:T(8,128)(2,1)S(1)} copy-done((bf16[3,18,4,1,16,32]{5,4,3,2,1,0:T(8,128)(2,1)S(1)}, bf16[3,18,4,1,16,32]{5,4,3,2,1,0:T(8,128)(2,1)}, u32[]{:S(2)}) %copy-start.2) | copy-done | bytes 221208
  3.1 0.7 pack_own.1
  3.9 1.7 %collective-permute-start.2 = (bf16[1,3168,128]{2,1,0:T(8,128)(2,1)S(1)}, bf16[1,3168,128]{2,1,0:T(8,128)(2,1)S(1)}, u32[]{:S(2)}, u32[]{:S(2)}) collective-permute-start(bf16[1,3168,128]{2,1,0:T(8,128)(2,1)S(1)} %bitcast.30), channel_id=1, source_target_pairs={{0,4},{4,0},{8,12},{12,8},{16,20},{20,16},{24,28},{28,24},{32,36},... | collective-permute-start | bytes 2433032 | tf_op jit(solution)/shard_map/ppermute | solution.py:498
  5.6 6.6 %collective-permute-start.3 = (bf16[1,3168,128]{2,1,0:T(8,128)(2,1)S(1)}, bf16[1,3168,128]{2,1,0:T(8,128)(2,1)S(1)}, u32[]{:S(2)}, u32[]{:S(2)}) collective-permute-start(bf16[1,3168,128]{2,1,0:T(8,128)(2,1)S(1)} %bitcast.29), channel_id=1, source_target_pairs={{0,124},{4,8},{8,4},{12,16},{16,12},{20,24},{24,20},{28,32},{32,28... | collective-permute-start | bytes 2433032 | tf_op jit(solution)/shard_map/ppermute | solution.py:498
  12.2 0.8 %pack_given.1 = bf16[2,105,32,128]{3,2,1,0:T(8,128)(2,1)S(1)} custom-call(s32[4]{0:T(128)S(1)} %pad_add_fusion.place_ref, bf16[2,3,4,16,32,128]{5,4,3,2,1,0:T(8,128)(2,1)S(1)} %bitcast.16, bf16[3,18,4,16,32]{4,3,2,1,0:T(8,128)(2,1)S(1)} %bitcast.25), custom_call_target="tpu_custom_call" | custom-call | flops 1000000 | bytes 100000 | tf_op jit(solution)/shard_map/pack_given/pallas_call | solution.py:526
  13.0 0.1 collective-permute-start
  13.1 0.8 %phase_table.1.table_ref.table = f32[8,2,1280]{2,1,0:T(2,128)S(1)} custom-call(s32[4]{0:T(128)S(1)} %pad_add_fusion.place_ref, s32[2,3]{1,0:T(2,128)S(1)} %copy-done.4), custom_call_target="tpu_custom_call" | custom-call | flops 20000000000 | bytes 100000 | tf_op jit(solution)/shard_map/phase_table/pallas_call | solution.py:546
  13.9 2.8 %collective-permute-done.swap_ref = bf16[2,105,32,128]{3,2,1,0:T(8,128)(2,1)S(1)} collective-permute-done((bf16[2,105,32,128]{3,2,1,0:T(8,128)(2,1)S(1)}, bf16[2,105,32,128]{3,2,1,0:T(8,128)(2,1)S(1)}, u32[]{:S(2)}, u32[]{:S(2)}) %collective-permute-start) | collective-permute-done | bytes 1720352 | tf_op jit(solution)/shard_map/ppermute | solution.py:543
  16.7 0.7 split_first.1
  17.4 1.3 %collective-permute-start.4 = (bf16[1,2400,128]{2,1,0:T(8,128)(2,1)S(1)}, bf16[1,2400,128]{2,1,0:T(8,128)(2,1)S(1)}, u32[]{:S(2)}, u32[]{:S(2)}) collective-permute-start(bf16[1,2400,128]{2,1,0:T(8,128)(2,1)S(1)} %bitcast.31), channel_id=1, source_target_pairs={{0,124},{4,8},{8,4},{12,16},{16,12},{20,24},{24,20},{28,32},{32,28... | collective-permute-start | bytes 1843208 | tf_op jit(solution)/shard_map/ppermute | solution.py:498
  18.7 10.5 %yz_terms.1 = (bf16[32,2,16,256]{3,2,1,0:T(8,128)(2,1)S(1)}, bf16[2,192,128]{2,1,0:T(8,128)(2,1)S(1)}, f32[2,16,256]{2,1,0:T(8,128)S(1)}) custom-call(s32[4]{0:T(128)S(1)} %pad_add_fusion.place_ref, bf16[2,3,4,16,32,128]{5,4,3,2,1,0:T(8,128)(2,1)S(1)} %bitcast.18, bf16[2,3360,128]{2,1,0:T(8,128)(2,1)S(1)} %bitcast.20, ...), custom_call_target="tpu_custom_call" | custom-call | flops 1000000 | bytes 100000 | tf_op jit(solution)/shard_map/yz_terms/pallas_call | solution.py:565
  29.2 0.6 split_last.1
  29.8 0.8 %collective-permute-start.6 = (bf16[1,768,128]{2,1,0:T(8,128)(2,1)S(1)}, bf16[1,768,128]{2,1,0:T(8,128)(2,1)S(1)}, u32[]{:S(2)}, u32[]{:S(2)}) collective-permute-start(bf16[1,768,128]{2,1,0:T(8,128)(2,1)S(1)} %bitcast.34), channel_id=1, source_target_pairs={{0,4},{4,0},{8,12},{12,8},{16,20},{20,16},{24,28},{28,24},{32,36},... | collective-permute-start | bytes 589832 | tf_op jit(solution)/shard_map/ppermute | solution.py:498
  30.6 4.4 %collective-permute-start.5 = (bf16[1,768,128]{2,1,0:T(8,128)(2,1)S(1)}, bf16[1,768,128]{2,1,0:T(8,128)(2,1)S(1)}, u32[]{:S(2)}, u32[]{:S(2)}) collective-permute-start(bf16[1,768,128]{2,1,0:T(8,128)(2,1)S(1)} %bitcast.33), channel_id=1, source_target_pairs={{0,124},{4,8},{8,4},{12,16},{16,12},{20,24},{24,20},{28,32},{32,28... | collective-permute-start | bytes 589832 | tf_op jit(solution)/shard_map/ppermute | solution.py:498
  35.0 2.7 %collective-permute-start.7 = (bf16[2,192,128]{2,1,0:T(8,128)(2,1)S(1)}, bf16[2,192,128]{2,1,0:T(8,128)(2,1)S(1)}, u32[]{:S(2)}, u32[]{:S(2)}) collective-permute-start(bf16[2,192,128]{2,1,0:T(8,128)(2,1)S(1)} %bitcast.35), channel_id=1, source_target_pairs={{0,2},{2,0},{1,3},{3,1},{4,6},{6,4},{5,7},{7,5},{8,10},{10,8},{9,1... | collective-permute-start | bytes 294920 | tf_op jit(solution)/shard_map/ppermute | solution.py:561
  37.8 6.5 %x_first.1.before = f32[2,4,128,128]{3,2,1,0:T(8,128)S(1)} custom-call(s32[4]{0:T(128)S(1)} %pad_add_fusion.place_ref, bf16[2,3,4,16,32,128]{5,4,3,2,1,0:T(8,128)(2,1)S(1)} %bitcast.19, bf16[3,18,4,16,32]{4,3,2,1,0:T(8,128)(2,1)S(1)} %bitcast.27, bf16[1,3168,128]{2,1,0:T(8,128)(2,1)S(1)} %collective-permute-done.2.first_ref, ...), custom_call_target="tpu_custom_call" | custom-call | flops 1000000 | bytes 100000 | tf_op jit(solution)/shard_map/x_first/pallas_call | solution.py:526
  44.3 2.4 %x_middle_first.1 = (f32[4,128,128]{2,1,0:T(8,128)S(1)}, f32[2,6,16,192]{3,2,1,0:T(8,128)S(1)}, bf16[2,512,128]{2,1,0:T(8,128)(2,1)S(1)}, bf16[2,96,256]{2,1,0:T(8,128)(2,1)S(1)}, bf16[2,192,256]{2,1,0:T(8,128)(2,1)S(1)}) custom-call(s32[4]{0:T(128)S(1)} %pad_add_fusion.place_ref, bf16[2,3360,128]{2,1,0:T(8,128)(2,1)S(1)} %bitcast.21, ...), custom_call_target="tpu_custom_call" | custom-call | flops 1000000 | bytes 100000 | tf_op jit(solution)/shard_map/x_middle_first/pallas_call | solution.py:526
  46.7 2.4 %x_middle_second.1 = (f32[4,128,128]{2,1,0:T(8,128)S(1)}, f32[2,6,16,192]{3,2,1,0:T(8,128)S(1)}) custom-call(s32[4]{0:T(128)S(1)} %pad_add_fusion.place_ref, bf16[2,3360,128]{2,1,0:T(8,128)(2,1)S(1)} %bitcast.22, bf16[1,2400,128]{2,1,0:T(8,128)(2,1)S(1)} %collective-permute-done.4.got_ref, f32[8,2,1280]{2,1,0:T(2,128)S(1)} %phase_table.1.table_ref.table, ...), custom_call_target="tpu_custom_call" | custom-call | flops 1000000 | bytes 100000 | tf_op jit(solution)/shard_map/x_middle_second/pallas_call | solution.py:526
  49.2 1.5 %x_last_first.1 = (bf16[32,2,16,384]{3,2,1,0:T(8,128)(2,1)S(1)}, bf16[512,384]{1,0:T(8,128)(2,1)S(1)}, bf16[3,4,32,256]{3,2,1,0:T(8,128)(2,1)S(1)}) custom-call(s32[4]{0:T(128)S(1)} %pad_add_fusion.place_ref, bf16[2,3360,128]{2,1,0:T(8,128)(2,1)S(1)} %bitcast.23, bf16[1,768,128]{2,1,0:T(8,128)(2,1)S(1)} %collective-permute-done.6.got_ref, ...), custom_call_target="tpu_custom_call" | custom-call | flops 1000000 | bytes 100000 | tf_op jit(solution)/shard_map/x_last_first/pallas_call | solution.py:526
  50.7 1.2 %collective-permute-done.7.halo_ref = bf16[2,192,128]{2,1,0:T(8,128)(2,1)S(1)} collective-permute-done((bf16[2,192,128]{2,1,0:T(8,128)(2,1)S(1)}, bf16[2,192,128]{2,1,0:T(8,128)(2,1)S(1)}, u32[]{:S(2)}, u32[]{:S(2)}) %collective-permute-start.7) | collective-permute-done | bytes 98336 | tf_op jit(solution)/shard_map/ppermute | solution.py:561
  51.9 1.8 %x_last_second.1 = bf16[32,2,16,384]{3,2,1,0:T(8,128)(2,1)S(1)} custom-call(s32[4]{0:T(128)S(1)} %pad_add_fusion.place_ref, bf16[1,768,128]{2,1,0:T(8,128)(2,1)S(1)} %collective-permute-done.5.got_ref, f32[2,6,16,192]{3,2,1,0:T(8,128)S(1)} %get-tuple-element.45.second_rows.rows_ref, ...), custom_call_target="tpu_custom_call", output_to_operand_aliasing={{}: (11, {})} | custom-call | flops 1000000 | bytes 100000 | tf_op jit(solution)/shard_map/x_last_second/pallas_call | solution.py:526
  53.8 19.2 %all_to_all.5.got_ref = bf16[64,16,384]{2,1,0:T(8,128)(2,1)S(1)} all-to-all(bf16[64,16,384]{2,1,0:T(8,128)(2,1)S(1)} %bitcast.28), channel_id=1, replica_groups={{0,2,4,6,8,10,12,14,16,18,20,22,24,26,28,30,32,34,36,38,40,42,44,46,48,..., dimensions={0} | all-to-all | bytes 1572864 | tf_op jit(solution)/shard_map/all_to_all | solution.py:640
  73.0 1.4 %total.1 = f32[4,1,2,2,384]{4,3,2,1,0:T(2,128)} custom-call(s32[3]{0:T(128)S(1)} %copy-done.3, bf16[64,16,384]{2,1,0:T(8,128)(2,1)S(1)} %all_to_all.5.got_ref), custom_call_target="tpu_custom_call" | custom-call | tf_op jit(solution)/shard_map/total/pallas_call | solution.py:642
  (16 shorter events, 0.2 us)
Async XLA Ops:
  0.1 1.9 %copy-start = (bf16[2,3,4,1,16,32,128]{6,5,4,3,2,1,0:T(8,128)(2,1)S(1)}, bf16[2,3,4,1,16,32,128]{6,5,4,3,2,1,0:T(8,128)(2,1)}, u32[]{:S(2)}) copy-start(bf16[2,3,4,1,16,32,128]{6,5,4,3,2,1,0:T(8,128)(2,1)} %param.4) | copy-start | bytes 9437188
  2.0 1.2 %copy-start.2 = (bf16[3,18,4,1,16,32]{5,4,3,2,1,0:T(8,128)(2,1)S(1)}, bf16[3,18,4,1,16,32]{5,4,3,2,1,0:T(8,128)(2,1)}, u32[]{:S(2)}) copy-start(bf16[3,18,4,1,16,32]{5,4,3,2,1,0:T(8,128)(2,1)} %param.5) | copy-start | bytes 663556
  3.9 26.7 %collective-permute-start.2 = (bf16[1,3168,128]{2,1,0:T(8,128)(2,1)S(1)}, bf16[1,3168,128]{2,1,0:T(8,128)(2,1)S(1)}, u32[]{:S(2)}, u32[]{:S(2)}) collective-permute-start(bf16[1,3168,128]{2,1,0:T(8,128)(2,1)S(1)} %bitcast.30), channel_id=1, source_target_pairs={{0,4},{4,0},{8,12},{12,8},{16,20},{20,16},{24,28},{28,24},{32,36},... | collective-permute-start | bytes 2433032 | tf_op jit(solution)/shard_map/ppermute | solution.py:498
  5.6 7.5 %copy-start.4 = (s32[2,3]{1,0:T(2,128)S(1)}, s32[2,3]{1,0:T(2,128)}, u32[]{:S(2)}) copy-start(s32[2,3]{1,0:T(2,128)} %momenta_ref.1) | copy-start | bytes 76
  5.6 29.4 %collective-permute-start.3 = (bf16[1,3168,128]{2,1,0:T(8,128)(2,1)S(1)}, bf16[1,3168,128]{2,1,0:T(8,128)(2,1)S(1)}, u32[]{:S(2)}, u32[]{:S(2)}) collective-permute-start(bf16[1,3168,128]{2,1,0:T(8,128)(2,1)S(1)} %bitcast.29), channel_id=1, source_target_pairs={{0,124},{4,8},{8,4},{12,16},{16,12},{20,24},{24,20},{28,32},{32,28... | collective-permute-start | bytes 2433032 | tf_op jit(solution)/shard_map/ppermute | solution.py:498
  13.0 3.7 %collective-permute-start = (bf16[2,105,32,128]{3,2,1,0:T(8,128)(2,1)S(1)}, bf16[2,105,32,128]{3,2,1,0:T(8,128)(2,1)S(1)}, u32[]{:S(2)}, u32[]{:S(2)}) collective-permute-start(bf16[2,105,32,128]{3,2,1,0:T(8,128)(2,1)S(1)} %pack_given.1), channel_id=1, source_target_pairs={{0,1},{1,0},{2,3},{3,2},{4,5},{5,4},{6,7},{7,6},{8,9},{9,8},{10,11... | collective-permute-start | bytes 5160968 | tf_op jit(solution)/shard_map/ppermute | solution.py:543
  13.1 3.6 %copy-start.1 = (bf16[2,3,4,1,16,32,128]{6,5,4,3,2,1,0:T(8,128)(2,1)S(1)}, bf16[2,3,4,1,16,32,128]{6,5,4,3,2,1,0:T(8,128)(2,1)}, u32[]{:S(2)}) copy-start(bf16[2,3,4,1,16,32,128]{6,5,4,3,2,1,0:T(8,128)(2,1)} %param.4) | copy-start | bytes 9437188
  17.3 26.9 %collective-permute-start.1 = (bf16[1,2400,128]{2,1,0:T(8,128)(2,1)S(1)}, bf16[1,2400,128]{2,1,0:T(8,128)(2,1)S(1)}, u32[]{:S(2)}, u32[]{:S(2)}) collective-permute-start(bf16[1,2400,128]{2,1,0:T(8,128)(2,1)S(1)} %bitcast.32), channel_id=1, source_target_pairs={{0,4},{4,0},{8,12},{12,8},{16,20},{20,16},{24,28},{28,24},{32,36},... | collective-permute-start | bytes 1843208 | tf_op jit(solution)/shard_map/ppermute | solution.py:498
  17.4 29.3 %collective-permute-start.4 = (bf16[1,2400,128]{2,1,0:T(8,128)(2,1)S(1)}, bf16[1,2400,128]{2,1,0:T(8,128)(2,1)S(1)}, u32[]{:S(2)}, u32[]{:S(2)}) collective-permute-start(bf16[1,2400,128]{2,1,0:T(8,128)(2,1)S(1)} %bitcast.31), channel_id=1, source_target_pairs={{0,124},{4,8},{8,4},{12,16},{16,12},{20,24},{24,20},{28,32},{32,28... | collective-permute-start | bytes 1843208 | tf_op jit(solution)/shard_map/ppermute | solution.py:498
  29.8 19.4 %collective-permute-start.6 = (bf16[1,768,128]{2,1,0:T(8,128)(2,1)S(1)}, bf16[1,768,128]{2,1,0:T(8,128)(2,1)S(1)}, u32[]{:S(2)}, u32[]{:S(2)}) collective-permute-start(bf16[1,768,128]{2,1,0:T(8,128)(2,1)S(1)} %bitcast.34), channel_id=1, source_target_pairs={{0,4},{4,0},{8,12},{12,8},{16,20},{20,16},{24,28},{28,24},{32,36},... | collective-permute-start | bytes 589832 | tf_op jit(solution)/shard_map/ppermute | solution.py:498
  30.6 21.3 %collective-permute-start.5 = (bf16[1,768,128]{2,1,0:T(8,128)(2,1)S(1)}, bf16[1,768,128]{2,1,0:T(8,128)(2,1)S(1)}, u32[]{:S(2)}, u32[]{:S(2)}) collective-permute-start(bf16[1,768,128]{2,1,0:T(8,128)(2,1)S(1)} %bitcast.33), channel_id=1, source_target_pairs={{0,124},{4,8},{8,4},{12,16},{16,12},{20,24},{24,20},{28,32},{32,28... | collective-permute-start | bytes 589832 | tf_op jit(solution)/shard_map/ppermute | solution.py:498
  35.0 16.9 %collective-permute-start.7 = (bf16[2,192,128]{2,1,0:T(8,128)(2,1)S(1)}, bf16[2,192,128]{2,1,0:T(8,128)(2,1)S(1)}, u32[]{:S(2)}, u32[]{:S(2)}) collective-permute-start(bf16[2,192,128]{2,1,0:T(8,128)(2,1)S(1)} %bitcast.35), channel_id=1, source_target_pairs={{0,2},{2,0},{1,3},{3,1},{4,6},{6,4},{5,7},{7,5},{8,10},{10,8},{9,1... | collective-permute-start | bytes 294920 | tf_op jit(solution)/shard_map/ppermute | solution.py:561
  51.9 21.0 %copy-start.3 = (s32[3]{0:T(128)S(1)}, s32[3]{0:T(128)}, u32[]{:S(2)}) copy-start(s32[3]{0:T(128)} %directions_ref.1) | copy-start | bytes 40

commit v10 on v9

--- a/solution.py
+++ b/solution.py
@@ -462,32 +462,19 @@
     pieces_ref[:, 1 - odd, :, 2 * nev :] = partial_rows(parts).astype(BF16)
 
 
-def total_kernel(directions_ref, got_ref, out_ref, total_ref):
-    step = pl.program_id(0)
-    part = jnp.sum(got_ref[...].astype(F32), axis=0)
-
-    @pl.when(step == 0)
-    def _():
-        total_ref[...] = part
-
-    @pl.when(step > 0)
-    def _():
-        total_ref[...] += part
-
-    @pl.when(step == pl.num_programs(0) - 1)
-    def _():
-        total = total_ref[...]
-        nev = total.shape[1] // 3
-        group = out_ref.shape[0]
-        in_y, in_z, in_x = (total[:, k * nev : (k + 1) * nev] for k in range(3))
-        for d in range(3):
-            direction = directions_ref[d]
-            chosen = jnp.where(direction == 0, in_x, jnp.where(direction == 1, in_y, in_z))
-            for r in range(2):
-                for p in range(2):
-                    for i in range(group):
-                        row = (r * 2 + p) * group + i
-                        out_ref[i, 0, p, r : r + 1, d * nev : (d + 1) * nev] = chosen[row : row + 1]
+def total_kernel(directions_ref, got_ref, out_ref):
+    total = jnp.sum(got_ref[...].astype(F32), axis=0)
+    nev = total.shape[1] // 3
+    group = out_ref.shape[0]
+    in_y, in_z, in_x = (total[:, k * nev : (k + 1) * nev] for k in range(3))
+    for d in range(3):
+        direction = directions_ref[d]
+        chosen = jnp.where(direction == 0, in_x, jnp.where(direction == 1, in_y, in_z))
+        for r in range(2):
+            for p in range(2):
+                for i in range(group):
+                    row = (r * 2 + p) * group + i
+                    out_ref[i, 0, p, r : r + 1, d * nev : (d + 1) * nev] = chosen[row : row + 1]
 
 
 def exchange(first, second):
@@ -638,17 +625,10 @@
     pieces = pieces.reshape(2 * size_x, 4 * group, 3 * nev)
     groups = [[(ts * 2 + h) * 2 + c for ts in range(size_x) for h in range(2)] for c in range(2)]
     got = lax.all_to_all(pieces, ("ts", "gz"), 0, 0, tiled=True, axis_index_groups=groups)
-    out_shape = (group, 1, 2, 2, 3 * nev)
-    return pl.pallas_call(
-        total_kernel,
-        grid=(4,),
-        in_specs=[in_smem, pl.BlockSpec((size_x // 2, 4 * group, 3 * nev), lambda i: (i, 0, 0))],
-        out_specs=pl.BlockSpec(out_shape, lambda i: (0, 0, 0, 0, 0)),
-        out_shape=jax.ShapeDtypeStruct(out_shape, F32),
-        scratch_shapes=[pltpu.VMEM((4 * group, 3 * nev), F32)],
-        compiler_params=limit,
-        name="total",
-    )(directions, got)
+    (out,) = call(
+        total_kernel, "total", [jax.ShapeDtypeStruct((group, 1, 2, 2, 3 * nev), F32)], [], directions, got
+    )
+    return out
 
 
 def solution(mesh):

time: 74.6 us -> 74.5 us (level)
    pallas_call x1 -> x0, Pallas kernels: 1.4 us -> none  [shards(): pl.pallas_call(total_kernel, grid=(4,), in_specs=[in_smem, pl.BlockSpec((...]
    pallas_call x9 -> x10, Pallas kernels: 17.4 us -> 18.7 us  [call(): pl.pallas_call(kernel, in_specs=in_specs, out_specs=jax.tree.map(lambda _...]
where the time goes in v10:
time: 74.5 us; the launch traced here: 74.3 us
  Pallas kernels  30 us (40%)
  blocking collectives  19.2 us (26%)
  starting transfers between devices  17.7 us (24%)
  waiting for transfers between devices  4.06 us (5%)
  local copies, waits for them, and re-layouts  3.07 us (4%)
    all_to_all x1, blocking collectives, shards(): lax.all_to_all(pieces, ('ts', 'gz'), 0, 0, tiled=True, axis_index_groups=...  19.2 us
    pallas_call x10, Pallas kernels, call(): pl.pallas_call(kernel, in_specs=in_specs, out_specs=jax.tree.map(lambda _...  18.7 us
    ppermute x6, starting transfers between devices, exchange(): got[at] = lax.ppermute(array.reshape(1, -1, array.shape[-1]), 'ts', pairs)  14.9 us
    pallas_call x1, Pallas kernels, shards(): pl.pallas_call(yz_kernel, grid=(2,), in_specs=[in_smem] + [in_vmem] * 4,...  10.5 us
    unnamed x10, local copies, waits for them, and re-layouts  3.07 us
    ppermute x1, waiting for transfers between devices, shards(): swapped = lax.ppermute(given, 'gz', swap)  2.8 us
    ppermute x1, starting transfers between devices, shards(): lax.ppermute(lowest.reshape(2, 6 * count_y, nev), 'gz', [(0, 2), (2, 0),...  2.73 us
  transfers between devices with their start and end apart: 8, of which 2 were waited for; matrix products, arithmetic and copies ran while one was open for 0% of the time, Pallas kernels for 35%

profile of v10, /device:TPU:0, one launch (start us, length us, event | category | flops | bytes accessed | tf_op | source)
XLA Modules:
  0.0 74.3 jit_solution(9254876094498001240)
XLA Ops:
  0.1 1.9 %copy-done = bf16[2,3,4,1,16,32,128]{6,5,4,3,2,1,0:T(8,128)(2,1)S(1)} copy-done((bf16[2,3,4,1,16,32,128]{6,5,4,3,2,1,0:T(8,128)(2,1)S(1)}, bf16[2,3,4,1,16,32,128]{6,5,4,3,2,1,0:T(8,128)(2,1)}, u32[]{:S(2)}) %copy-start) | copy-done | bytes 3145752
  2.0 1.2 %copy-done.2 = bf16[3,18,4,1,16,32]{5,4,3,2,1,0:T(8,128)(2,1)S(1)} copy-done((bf16[3,18,4,1,16,32]{5,4,3,2,1,0:T(8,128)(2,1)S(1)}, bf16[3,18,4,1,16,32]{5,4,3,2,1,0:T(8,128)(2,1)}, u32[]{:S(2)}) %copy-start.2) | copy-done | bytes 221208
  3.1 0.7 pack_own.1
  3.9 1.7 %collective-permute-start.2 = (bf16[1,3168,128]{2,1,0:T(8,128)(2,1)S(1)}, bf16[1,3168,128]{2,1,0:T(8,128)(2,1)S(1)}, u32[]{:S(2)}, u32[]{:S(2)}) collective-permute-start(bf16[1,3168,128]{2,1,0:T(8,128)(2,1)S(1)} %bitcast.30), channel_id=1, source_target_pairs={{0,4},{4,0},{8,12},{12,8},{16,20},{20,16},{24,28},{28,24},{32,36},... | collective-permute-start | bytes 2433032 | tf_op jit(solution)/shard_map/ppermute | solution.py:485
  5.6 6.6 %collective-permute-start.3 = (bf16[1,3168,128]{2,1,0:T(8,128)(2,1)S(1)}, bf16[1,3168,128]{2,1,0:T(8,128)(2,1)S(1)}, u32[]{:S(2)}, u32[]{:S(2)}) collective-permute-start(bf16[1,3168,128]{2,1,0:T(8,128)(2,1)S(1)} %bitcast.29), channel_id=1, source_target_pairs={{0,124},{4,8},{8,4},{12,16},{16,12},{20,24},{24,20},{28,32},{32,28... | collective-permute-start | bytes 2433032 | tf_op jit(solution)/shard_map/ppermute | solution.py:485
  12.2 0.8 %pack_given.1 = bf16[2,105,32,128]{3,2,1,0:T(8,128)(2,1)S(1)} custom-call(s32[4]{0:T(128)S(1)} %pad_add_fusion.place_ref, bf16[2,3,4,16,32,128]{5,4,3,2,1,0:T(8,128)(2,1)S(1)} %bitcast.16, bf16[3,18,4,16,32]{4,3,2,1,0:T(8,128)(2,1)S(1)} %bitcast.25), custom_call_target="tpu_custom_call" | custom-call | flops 1000000 | bytes 100000 | tf_op jit(solution)/shard_map/pack_given/pallas_call | solution.py:513
  13.0 0.1 collective-permute-start
  13.1 0.8 %phase_table.1.table_ref.table = f32[8,2,1280]{2,1,0:T(2,128)S(1)} custom-call(s32[4]{0:T(128)S(1)} %pad_add_fusion.place_ref, s32[2,3]{1,0:T(2,128)S(1)} %copy-done.4), custom_call_target="tpu_custom_call" | custom-call | flops 20000000000 | bytes 100000 | tf_op jit(solution)/shard_map/phase_table/pallas_call | solution.py:533
  13.9 2.8 %collective-permute-done.swap_ref = bf16[2,105,32,128]{3,2,1,0:T(8,128)(2,1)S(1)} collective-permute-done((bf16[2,105,32,128]{3,2,1,0:T(8,128)(2,1)S(1)}, bf16[2,105,32,128]{3,2,1,0:T(8,128)(2,1)S(1)}, u32[]{:S(2)}, u32[]{:S(2)}) %collective-permute-start) | collective-permute-done | bytes 1720352 | tf_op jit(solution)/shard_map/ppermute | solution.py:530
  16.7 0.7 split_first.1
  17.4 1.3 %collective-permute-start.4 = (bf16[1,2400,128]{2,1,0:T(8,128)(2,1)S(1)}, bf16[1,2400,128]{2,1,0:T(8,128)(2,1)S(1)}, u32[]{:S(2)}, u32[]{:S(2)}) collective-permute-start(bf16[1,2400,128]{2,1,0:T(8,128)(2,1)S(1)} %bitcast.31), channel_id=1, source_target_pairs={{0,124},{4,8},{8,4},{12,16},{16,12},{20,24},{24,20},{28,32},{32,28... | collective-permute-start | bytes 1843208 | tf_op jit(solution)/shard_map/ppermute | solution.py:485
  18.7 10.5 %yz_terms.1 = (bf16[32,2,16,256]{3,2,1,0:T(8,128)(2,1)S(1)}, bf16[2,192,128]{2,1,0:T(8,128)(2,1)S(1)}, f32[2,16,256]{2,1,0:T(8,128)S(1)}) custom-call(s32[4]{0:T(128)S(1)} %pad_add_fusion.place_ref, bf16[2,3,4,16,32,128]{5,4,3,2,1,0:T(8,128)(2,1)S(1)} %bitcast.18, bf16[2,3360,128]{2,1,0:T(8,128)(2,1)S(1)} %bitcast.20, ...), custom_call_target="tpu_custom_call" | custom-call | flops 1000000 | bytes 100000 | tf_op jit(solution)/shard_map/yz_terms/pallas_call | solution.py:552
  29.2 0.6 split_last.1
  29.8 0.8 %collective-permute-start.6 = (bf16[1,768,128]{2,1,0:T(8,128)(2,1)S(1)}, bf16[1,768,128]{2,1,0:T(8,128)(2,1)S(1)}, u32[]{:S(2)}, u32[]{:S(2)}) collective-permute-start(bf16[1,768,128]{2,1,0:T(8,128)(2,1)S(1)} %bitcast.34), channel_id=1, source_target_pairs={{0,4},{4,0},{8,12},{12,8},{16,20},{20,16},{24,28},{28,24},{32,36},... | collective-permute-start | bytes 589832 | tf_op jit(solution)/shard_map/ppermute | solution.py:485
  30.6 4.4 %collective-permute-start.5 = (bf16[1,768,128]{2,1,0:T(8,128)(2,1)S(1)}, bf16[1,768,128]{2,1,0:T(8,128)(2,1)S(1)}, u32[]{:S(2)}, u32[]{:S(2)}) collective-permute-start(bf16[1,768,128]{2,1,0:T(8,128)(2,1)S(1)} %bitcast.33), channel_id=1, source_target_pairs={{0,124},{4,8},{8,4},{12,16},{16,12},{20,24},{24,20},{28,32},{32,28... | collective-permute-start | bytes 589832 | tf_op jit(solution)/shard_map/ppermute | solution.py:485
  35.0 2.7 %collective-permute-start.7 = (bf16[2,192,128]{2,1,0:T(8,128)(2,1)S(1)}, bf16[2,192,128]{2,1,0:T(8,128)(2,1)S(1)}, u32[]{:S(2)}, u32[]{:S(2)}) collective-permute-start(bf16[2,192,128]{2,1,0:T(8,128)(2,1)S(1)} %bitcast.35), channel_id=1, source_target_pairs={{0,2},{2,0},{1,3},{3,1},{4,6},{6,4},{5,7},{7,5},{8,10},{10,8},{9,1... | collective-permute-start | bytes 294920 | tf_op jit(solution)/shard_map/ppermute | solution.py:548
  37.8 6.5 %x_first.1.before = f32[2,4,128,128]{3,2,1,0:T(8,128)S(1)} custom-call(s32[4]{0:T(128)S(1)} %pad_add_fusion.place_ref, bf16[2,3,4,16,32,128]{5,4,3,2,1,0:T(8,128)(2,1)S(1)} %bitcast.19, bf16[3,18,4,16,32]{4,3,2,1,0:T(8,128)(2,1)S(1)} %bitcast.27, bf16[1,3168,128]{2,1,0:T(8,128)(2,1)S(1)} %collective-permute-done.2.first_ref, ...), custom_call_target="tpu_custom_call" | custom-call | flops 1000000 | bytes 100000 | tf_op jit(solution)/shard_map/x_first/pallas_call | solution.py:513
  44.3 2.4 %x_middle_first.1 = (f32[4,128,128]{2,1,0:T(8,128)S(1)}, f32[2,6,16,192]{3,2,1,0:T(8,128)S(1)}, bf16[2,512,128]{2,1,0:T(8,128)(2,1)S(1)}, bf16[2,96,256]{2,1,0:T(8,128)(2,1)S(1)}, bf16[2,192,256]{2,1,0:T(8,128)(2,1)S(1)}) custom-call(s32[4]{0:T(128)S(1)} %pad_add_fusion.place_ref, bf16[2,3360,128]{2,1,0:T(8,128)(2,1)S(1)} %bitcast.21, ...), custom_call_target="tpu_custom_call" | custom-call | flops 1000000 | bytes 100000 | tf_op jit(solution)/shard_map/x_middle_first/pallas_call | solution.py:513
  46.7 2.4 %x_middle_second.1 = (f32[4,128,128]{2,1,0:T(8,128)S(1)}, f32[2,6,16,192]{3,2,1,0:T(8,128)S(1)}) custom-call(s32[4]{0:T(128)S(1)} %pad_add_fusion.place_ref, bf16[2,3360,128]{2,1,0:T(8,128)(2,1)S(1)} %bitcast.22, bf16[1,2400,128]{2,1,0:T(8,128)(2,1)S(1)} %collective-permute-done.4.got_ref, f32[8,2,1280]{2,1,0:T(2,128)S(1)} %phase_table.1.table_ref.table, ...), custom_call_target="tpu_custom_call" | custom-call | flops 1000000 | bytes 100000 | tf_op jit(solution)/shard_map/x_middle_second/pallas_call | solution.py:513
  49.2 1.5 %x_last_first.1 = (bf16[32,2,16,384]{3,2,1,0:T(8,128)(2,1)S(1)}, bf16[512,384]{1,0:T(8,128)(2,1)S(1)}, bf16[3,4,32,256]{3,2,1,0:T(8,128)(2,1)S(1)}) custom-call(s32[4]{0:T(128)S(1)} %pad_add_fusion.place_ref, bf16[2,3360,128]{2,1,0:T(8,128)(2,1)S(1)} %bitcast.23, bf16[1,768,128]{2,1,0:T(8,128)(2,1)S(1)} %collective-permute-done.6.got_ref, ...), custom_call_target="tpu_custom_call" | custom-call | flops 1000000 | bytes 100000 | tf_op jit(solution)/shard_map/x_last_first/pallas_call | solution.py:513
  50.7 1.2 %collective-permute-done.7.halo_ref = bf16[2,192,128]{2,1,0:T(8,128)(2,1)S(1)} collective-permute-done((bf16[2,192,128]{2,1,0:T(8,128)(2,1)S(1)}, bf16[2,192,128]{2,1,0:T(8,128)(2,1)S(1)}, u32[]{:S(2)}, u32[]{:S(2)}) %collective-permute-start.7) | collective-permute-done | bytes 98336 | tf_op jit(solution)/shard_map/ppermute | solution.py:548
  51.9 1.8 %x_last_second.1 = bf16[32,2,16,384]{3,2,1,0:T(8,128)(2,1)S(1)} custom-call(s32[4]{0:T(128)S(1)} %pad_add_fusion.place_ref, bf16[1,768,128]{2,1,0:T(8,128)(2,1)S(1)} %collective-permute-done.5.got_ref, f32[2,6,16,192]{3,2,1,0:T(8,128)S(1)} %get-tuple-element.45.second_rows.rows_ref, ...), custom_call_target="tpu_custom_call", output_to_operand_aliasing={{}: (11, {})} | custom-call | flops 1000000 | bytes 100000 | tf_op jit(solution)/shard_map/x_last_second/pallas_call | solution.py:513
  53.8 19.2 %all_to_all.5.got_ref = bf16[64,16,384]{2,1,0:T(8,128)(2,1)S(1)} all-to-all(bf16[64,16,384]{2,1,0:T(8,128)(2,1)S(1)} %bitcast.28), channel_id=1, replica_groups={{0,2,4,6,8,10,12,14,16,18,20,22,24,26,28,30,32,34,36,38,40,42,44,46,48,..., dimensions={0} | all-to-all | bytes 1572864 | tf_op jit(solution)/shard_map/all_to_all | solution.py:627
  73.0 1.3 %total.1 = f32[4,1,2,2,384]{4,3,2,1,0:T(2,128)} custom-call(s32[3]{0:T(128)S(1)} %copy-done.3, bf16[64,16,384]{2,1,0:T(8,128)(2,1)S(1)} %all_to_all.5.got_ref), custom_call_target="tpu_custom_call" | custom-call | flops 1000000 | bytes 100000 | tf_op jit(solution)/shard_map/total/pallas_call | solution.py:513
  (16 shorter events, 0.2 us)
Async XLA Ops:
  0.1 1.9 %copy-start = (bf16[2,3,4,1,16,32,128]{6,5,4,3,2,1,0:T(8,128)(2,1)S(1)}, bf16[2,3,4,1,16,32,128]{6,5,4,3,2,1,0:T(8,128)(2,1)}, u32[]{:S(2)}) copy-start(bf16[2,3,4,1,16,32,128]{6,5,4,3,2,1,0:T(8,128)(2,1)} %param.4) | copy-start | bytes 9437188
  2.0 1.2 %copy-start.2 = (bf16[3,18,4,1,16,32]{5,4,3,2,1,0:T(8,128)(2,1)S(1)}, bf16[3,18,4,1,16,32]{5,4,3,2,1,0:T(8,128)(2,1)}, u32[]{:S(2)}) copy-start(bf16[3,18,4,1,16,32]{5,4,3,2,1,0:T(8,128)(2,1)} %param.5) | copy-start | bytes 663556
  3.9 26.7 %collective-permute-start.2 = (bf16[1,3168,128]{2,1,0:T(8,128)(2,1)S(1)}, bf16[1,3168,128]{2,1,0:T(8,128)(2,1)S(1)}, u32[]{:S(2)}, u32[]{:S(2)}) collective-permute-start(bf16[1,3168,128]{2,1,0:T(8,128)(2,1)S(1)} %bitcast.30), channel_id=1, source_target_pairs={{0,4},{4,0},{8,12},{12,8},{16,20},{20,16},{24,28},{28,24},{32,36},... | collective-permute-start | bytes 2433032 | tf_op jit(solution)/shard_map/ppermute | solution.py:485
  5.6 7.5 %copy-start.4 = (s32[2,3]{1,0:T(2,128)S(1)}, s32[2,3]{1,0:T(2,128)}, u32[]{:S(2)}) copy-start(s32[2,3]{1,0:T(2,128)} %momenta_ref.1) | copy-start | bytes 76
  5.6 29.4 %collective-permute-start.3 = (bf16[1,3168,128]{2,1,0:T(8,128)(2,1)S(1)}, bf16[1,3168,128]{2,1,0:T(8,128)(2,1)S(1)}, u32[]{:S(2)}, u32[]{:S(2)}) collective-permute-start(bf16[1,3168,128]{2,1,0:T(8,128)(2,1)S(1)} %bitcast.29), channel_id=1, source_target_pairs={{0,124},{4,8},{8,4},{12,16},{16,12},{20,24},{24,20},{28,32},{32,28... | collective-permute-start | bytes 2433032 | tf_op jit(solution)/shard_map/ppermute | solution.py:485
  13.0 3.7 %collective-permute-start = (bf16[2,105,32,128]{3,2,1,0:T(8,128)(2,1)S(1)}, bf16[2,105,32,128]{3,2,1,0:T(8,128)(2,1)S(1)}, u32[]{:S(2)}, u32[]{:S(2)}) collective-permute-start(bf16[2,105,32,128]{3,2,1,0:T(8,128)(2,1)S(1)} %pack_given.1), channel_id=1, source_target_pairs={{0,1},{1,0},{2,3},{3,2},{4,5},{5,4},{6,7},{7,6},{8,9},{9,8},{10,11... | collective-permute-start | bytes 5160968 | tf_op jit(solution)/shard_map/ppermute | solution.py:530
  13.1 3.6 %copy-start.1 = (bf16[2,3,4,1,16,32,128]{6,5,4,3,2,1,0:T(8,128)(2,1)S(1)}, bf16[2,3,4,1,16,32,128]{6,5,4,3,2,1,0:T(8,128)(2,1)}, u32[]{:S(2)}) copy-start(bf16[2,3,4,1,16,32,128]{6,5,4,3,2,1,0:T(8,128)(2,1)} %param.4) | copy-start | bytes 9437188
  17.3 26.9 %collective-permute-start.1 = (bf16[1,2400,128]{2,1,0:T(8,128)(2,1)S(1)}, bf16[1,2400,128]{2,1,0:T(8,128)(2,1)S(1)}, u32[]{:S(2)}, u32[]{:S(2)}) collective-permute-start(bf16[1,2400,128]{2,1,0:T(8,128)(2,1)S(1)} %bitcast.32), channel_id=1, source_target_pairs={{0,4},{4,0},{8,12},{12,8},{16,20},{20,16},{24,28},{28,24},{32,36},... | collective-permute-start | bytes 1843208 | tf_op jit(solution)/shard_map/ppermute | solution.py:485
  17.4 29.3 %collective-permute-start.4 = (bf16[1,2400,128]{2,1,0:T(8,128)(2,1)S(1)}, bf16[1,2400,128]{2,1,0:T(8,128)(2,1)S(1)}, u32[]{:S(2)}, u32[]{:S(2)}) collective-permute-start(bf16[1,2400,128]{2,1,0:T(8,128)(2,1)S(1)} %bitcast.31), channel_id=1, source_target_pairs={{0,124},{4,8},{8,4},{12,16},{16,12},{20,24},{24,20},{28,32},{32,28... | collective-permute-start | bytes 1843208 | tf_op jit(solution)/shard_map/ppermute | solution.py:485
  29.8 19.4 %collective-permute-start.6 = (bf16[1,768,128]{2,1,0:T(8,128)(2,1)S(1)}, bf16[1,768,128]{2,1,0:T(8,128)(2,1)S(1)}, u32[]{:S(2)}, u32[]{:S(2)}) collective-permute-start(bf16[1,768,128]{2,1,0:T(8,128)(2,1)S(1)} %bitcast.34), channel_id=1, source_target_pairs={{0,4},{4,0},{8,12},{12,8},{16,20},{20,16},{24,28},{28,24},{32,36},... | collective-permute-start | bytes 589832 | tf_op jit(solution)/shard_map/ppermute | solution.py:485
  30.6 21.3 %collective-permute-start.5 = (bf16[1,768,128]{2,1,0:T(8,128)(2,1)S(1)}, bf16[1,768,128]{2,1,0:T(8,128)(2,1)S(1)}, u32[]{:S(2)}, u32[]{:S(2)}) collective-permute-start(bf16[1,768,128]{2,1,0:T(8,128)(2,1)S(1)} %bitcast.33), channel_id=1, source_target_pairs={{0,124},{4,8},{8,4},{12,16},{16,12},{20,24},{24,20},{28,32},{32,28... | collective-permute-start | bytes 589832 | tf_op jit(solution)/shard_map/ppermute | solution.py:485
  35.0 16.9 %collective-permute-start.7 = (bf16[2,192,128]{2,1,0:T(8,128)(2,1)S(1)}, bf16[2,192,128]{2,1,0:T(8,128)(2,1)S(1)}, u32[]{:S(2)}, u32[]{:S(2)}) collective-permute-start(bf16[2,192,128]{2,1,0:T(8,128)(2,1)S(1)} %bitcast.35), channel_id=1, source_target_pairs={{0,2},{2,0},{1,3},{3,1},{4,6},{6,4},{5,7},{7,5},{8,10},{10,8},{9,1... | collective-permute-start | bytes 294920 | tf_op jit(solution)/shard_map/ppermute | solution.py:548
  51.9 21.0 %copy-start.3 = (s32[3]{0:T(128)S(1)}, s32[3]{0:T(128)}, u32[]{:S(2)}) copy-start(s32[3]{0:T(128)} %directions_ref.1) | copy-start | bytes 40
